TPU v7x, 32 devices: a whole 2x2x4 slice. The times are simulated.
32 devices in a mesh: seq: 8 (over z, x), ch: 4 (over y, core).
Axes of the slice: x: 2, y: 2, z: 4, core: 2. Of those that a mesh axis runs over, the one named last changes fastest.
Arguments:
- inputs: bfloat16 [8192, 768], P('seq')
- cotangent: bfloat16 [8192, 768], P('seq')
- starts: int32 [8], replicated, may hold values from 1 to 8191, as said below
- master_conv: float32 [3, 768, 384], P(None, 'seq', 'ch'), may hold values from -0.125 to 0.125
- first_conv: float32 [3, 768, 384], P(None, 'seq', 'ch')
- second_conv: float32 [3, 768, 384], P(None, 'seq', 'ch')
- master_point: float32 [384, 768], P('ch', 'seq'), may hold values from -0.3125 to 0.3125
- first_point: float32 [384, 768], P('ch', 'seq')
- second_point: float32 [384, 768], P('ch', 'seq')
- norm_in: float32 [2, 768], replicated
- first_in: float32 [2, 768], replicated
- second_in: float32 [2, 768], replicated
- norm_mid: float32 [2, 384], P(None, 'ch')
- first_mid: float32 [2, 384], P(None, 'ch')
- second_mid: float32 [2, 384], P(None, 'ch')
Outputs:
- block_out: bfloat16 [8192, 768], P('seq')
- input_grad: float32 [8192, 768], P('seq')
- first_conv_new: float32 [3, 768, 384], P(None, 'seq', 'ch')
- second_conv_new: float32 [3, 768, 384], P(None, 'seq', 'ch')
- conv_new: float32 [3, 768, 384], P(None, 'seq', 'ch')
- first_point_new: float32 [384, 768], P('ch', 'seq')
- second_point_new: float32 [384, 768], P('ch', 'seq')
- point_new: float32 [384, 768], P('ch', 'seq')
- first_in_new: float32 [2, 768], replicated
- second_in_new: float32 [2, 768], replicated
- norm_in_new: float32 [2, 768], replicated
- first_mid_new: float32 [2, 384], P(None, 'ch')
- second_mid_new: float32 [2, 384], P(None, 'ch')
- norm_mid_new: float32 [2, 384], P(None, 'ch')
Inputs may be any that keep to these rules, and one draw needn't show every extreme that they name: starts[k] = starts[0] + k * 1024, with starts[0] between 1 and min(1024, 1024) - 1.
All inputs are finite; a program needn't handle non-finite values.
Results may differ from a plain program's by a relative error of at most 0.0068.
Values may be sent and summed in bfloat16 or wider, within the bound.
No kernel may reach another device: no remote copies, remote signals or barrier semaphores. Data moves between devices by JAX's collectives and lax.ppermute only.
A program may use at most 64 MiB of HBM per device.

v0:
```python
import jax
import jax.numpy as jnp
from jax import lax
from jax.sharding import PartitionSpec as P

KERNEL_WIDTH = 3
DILATION_BINS = 9
STEP = 10


NORM_EPS = 1e-05
ADAM_EPS = 1e-08
BETA_ONE = 0.9
BETA_TWO = 0.999
RATE_WEIGHT = 0.05
RATE_NORM = 0.5
DECAY_WEIGHT = 0.01


def padded(x, sides, width):
    for axis, dim in sides:
        size, length = (lax.axis_size(axis), x.shape[dim])
        up = [(i, (i + 1) % size) for i in range(size - 1)]
        down = [(j, i) for i, j in up]
        last = lax.slice_in_dim(x, length - width, length, axis=dim)
        first = lax.slice_in_dim(x, 0, width, axis=dim)
        before = lax.ppermute(last, axis, up)
        after = lax.ppermute(first, axis, down)
        x = jnp.concatenate([before, x, after], axis=dim)
    return x


def window_masks(starts, positions, bin_count):

    def window_of(neighbors):
        return jnp.sum((neighbors[:, None] >= starts[None, :]).astype(jnp.int32), axis=1)

    own_window = window_of(positions)
    mask_list = []
    for kernel_index in range(KERNEL_WIDTH):
        bin_shift = (kernel_index - KERNEL_WIDTH // 2) * DILATION_BINS
        neighbors = positions + bin_shift
        inside = (neighbors >= 0) & (neighbors < bin_count) & (window_of(neighbors) == own_window)
        mask_list.append(inside.astype(jnp.float32))
    return mask_list


def normalize(values, params, bin_count):
    totals = lax.psum((jnp.sum(values, axis=0), jnp.sum(values * values, axis=0)), "seq")
    average = totals[0] / bin_count
    variance = totals[1] / bin_count - average * average
    inv_root = lax.rsqrt(variance + NORM_EPS)
    centered = (values - average) * inv_root
    return (centered, inv_root, centered * params[0] + params[1])


def norm_back(upstream, centered, inv_root, params, bin_count):
    totals = lax.psum((jnp.sum(upstream * centered, axis=0), jnp.sum(upstream, axis=0)), "seq")
    grads = (
        inv_root * params[0] * (upstream - totals[1] / bin_count - centered * totals[0] / bin_count)
    )
    return (grads, jnp.stack([totals[0], totals[1]]))


def gelu_back(pre_act, upstream):
    return jax.vjp(jax.nn.gelu, pre_act)[1](upstream)[0]


def adamw(weights_old, first_moment_state, second_mom, gradient, step_rate, decay_rate):
    first_next = BETA_ONE * first_moment_state + (1.0 - BETA_ONE) * gradient
    second_next = BETA_TWO * second_mom + (1.0 - BETA_TWO) * gradient * gradient
    corrected = (
        first_next
        / (1.0 - BETA_ONE**STEP)
        / (jnp.sqrt(second_next / (1.0 - BETA_TWO**STEP)) + ADAM_EPS)
    )
    weights_new = weights_old - step_rate * (corrected + decay_rate * weights_old)
    return (first_next, second_next, weights_new)


def input_terms(rimmed, kernel, mask_list, row_count, receptive_span):
    upstream_part = jnp.zeros((row_count, kernel.shape[1]), jnp.float32)
    for kernel_index in range(KERNEL_WIDTH):
        bin_shift = (kernel_index - KERNEL_WIDTH // 2) * DILATION_BINS
        back_window = rimmed[receptive_span - bin_shift : receptive_span - bin_shift + row_count]
        back_product = lax.dot_general(
            back_window,
            kernel[kernel_index],
            (((1,), (1,)), ((), ())),
            preferred_element_type=jnp.float32,
        )
        upstream_part = (
            upstream_part + back_product * mask_list[KERNEL_WIDTH - 1 - kernel_index][:, None]
        )
    return upstream_part


def shards(
    inputs,
    cotangent,
    starts,
    master_conv,
    first_conv,
    second_conv,
    master_point,
    first_point,
    second_point,
    norm_in,
    first_in,
    second_in,
    norm_mid,
    first_mid,
    second_mid,
):
    row_count = inputs.shape[0]
    bin_count = row_count * lax.axis_size("seq")
    receptive_span = DILATION_BINS * (KERNEL_WIDTH // 2)
    conv_full, point_full = (
        lax.all_gather(master_conv.astype(jnp.bfloat16), "seq", axis=1, tiled=True),
        lax.all_gather(master_point.astype(jnp.bfloat16), "seq", axis=1, tiled=True),
    )
    positions = lax.axis_index("seq") * row_count + jnp.arange(row_count, dtype=jnp.int32)
    mask_list = window_masks(starts, positions, bin_count)
    values = inputs.astype(jnp.float32)
    centered_input, root_in, pre_in = normalize(values, norm_in, bin_count)
    hidden_in = jax.nn.gelu(pre_in).astype(jnp.bfloat16)
    features = padded(hidden_in, (("seq", 0),), receptive_span)
    conv_out = jnp.zeros((row_count, conv_full.shape[2]), jnp.float32)
    for kernel_index in range(KERNEL_WIDTH):
        bin_shift = (kernel_index - KERNEL_WIDTH // 2) * DILATION_BINS
        window = features[receptive_span + bin_shift : receptive_span + bin_shift + row_count]
        product = jnp.dot(window, conv_full[kernel_index], preferred_element_type=jnp.float32)
        conv_out = conv_out + product * mask_list[kernel_index][:, None]
    centered_mid, root_mid, pre_mid = normalize(conv_out, norm_mid, bin_count)
    hidden_mid = jax.nn.gelu(pre_mid).astype(jnp.bfloat16)
    partial_value = jnp.dot(hidden_mid, point_full, preferred_element_type=jnp.float32)
    branch = lax.psum(partial_value, "ch")
    block_out = (values + branch).astype(jnp.bfloat16)
    grad_point = lax.dot_general(
        hidden_mid, cotangent, (((0,), (0,)), ((), ())), preferred_element_type=jnp.float32
    )
    upstream_mid = lax.dot_general(
        cotangent, point_full, (((1,), (1,)), ((), ())), preferred_element_type=jnp.float32
    )
    grad_conv_out, grad_mid = norm_back(
        gelu_back(pre_mid, upstream_mid), centered_mid, root_mid, norm_mid, bin_count
    )
    low_conv_out = grad_conv_out.astype(jnp.bfloat16)
    rimmed_back = padded(low_conv_out, (("seq", 0),), receptive_span)
    conv_terms = []
    for kernel_index in range(KERNEL_WIDTH):
        bin_shift = (kernel_index - KERNEL_WIDTH // 2) * DILATION_BINS
        window = features[receptive_span + bin_shift : receptive_span + bin_shift + row_count]
        masked = low_conv_out * mask_list[kernel_index][:, None].astype(jnp.bfloat16)
        conv_terms.append(
            lax.dot_general(
                window, masked, (((0,), (0,)), ((), ())), preferred_element_type=jnp.float32
            )
        )
    grad_conv = jnp.stack(conv_terms)
    upstream_part = input_terms(rimmed_back, conv_full, mask_list, row_count, receptive_span)
    upstream_in = lax.psum(upstream_part, "ch")
    grad_branch_in, grad_in = norm_back(
        gelu_back(pre_in, upstream_in), centered_input, root_in, norm_in, bin_count
    )
    input_grad = cotangent.astype(jnp.float32) + grad_branch_in
    convolution_sum, point_sum = (
        lax.psum_scatter(grad_conv, "seq", scatter_dimension=1, tiled=True),
        lax.psum_scatter(grad_point, "seq", scatter_dimension=1, tiled=True),
    )
    conv_first, conv_second, conv_next = adamw(
        master_conv, first_conv, second_conv, convolution_sum, RATE_WEIGHT, DECAY_WEIGHT
    )
    point_first, point_second, point_next = adamw(
        master_point, first_point, second_point, point_sum, RATE_WEIGHT, DECAY_WEIGHT
    )
    in_first, in_second, in_next = adamw(norm_in, first_in, second_in, grad_in, RATE_NORM, 0.0)
    mid_first, mid_second, mid_next = adamw(
        norm_mid, first_mid, second_mid, grad_mid, RATE_NORM, 0.0
    )
    return (
        block_out,
        input_grad,
        conv_first,
        conv_second,
        conv_next,
        point_first,
        point_second,
        point_next,
        in_first,
        in_second,
        in_next,
        mid_first,
        mid_second,
        mid_next,
    )


def solution(mesh):
    in_specs = (
        P("seq", None),
        P("seq", None),
        P(),
        P(None, "seq", "ch"),
        P(None, "seq", "ch"),
        P(None, "seq", "ch"),
        P("ch", "seq"),
        P("ch", "seq"),
        P("ch", "seq"),
        P(),
        P(),
        P(),
        P(None, "ch"),
        P(None, "ch"),
        P(None, "ch"),
    )
    out_specs = (
        P("seq", None),
        P("seq", None),
        P(None, "seq", "ch"),
        P(None, "seq", "ch"),
        P(None, "seq", "ch"),
        P("ch", "seq"),
        P("ch", "seq"),
        P("ch", "seq"),
        P(),
        P(),
        P(),
        P(None, "ch"),
        P(None, "ch"),
        P(None, "ch"),
    )
    return jax.shard_map(shards, mesh=mesh, in_specs=in_specs, out_specs=out_specs, check_vma=False)
```

profile of v0, /device:TPU:0, one launch (start us, length us, event | category | flops | bytes accessed | tf_op | source)
XLA Modules:
  0.0 326.9 jit_solution(6080414549231704102)
XLA Ops:
  8.1 0.8 slice_reduce_fusion.1
  8.9 1.9 convert_reduce_fusion
  10.8 23.3 %all-reduce.3 = (f32[768]{0:T(1024)S(1)}, f32[768]{0:T(1024)S(1)}) all-reduce(f32[768]{0:T(1024)S(1)} %get-tuple-element.59, f32[768]{0:T(1024)S(1)} %get-tuple-element.58), channel_id=1, replica_groups=mesh['seq'=8,'ch'=4] {'seq'}, use_global_device_ids=true, to_apply=%region_3.0 | all-reduce | flops 1536 | bytes 12288 | tf_op jit(solution)/shard_map/psum | solution.py:49
  34.1 2.9 fusion.15
  37.1 1.3 collective-permute-start
  38.4 1.3 collective-permute-start.1
  39.9 31.6 %all_gather.6 = bf16[3,768,96]{2,1,0:T(8,128)(2,1)S(1)} all-gather(bf16[3,96,96]{2,1,0:T(8,128)(2,1)S(1)} %convert_element_type.90), channel_id=1, replica_groups=mesh['seq'=8,'ch'=4] {'seq'}, dimensions={1}, use_global_device_ids=true | all-gather | bytes 497664 | tf_op jit(solution)/shard_map/all_gather | solution.py:119
  72.2 30.6 %all_gather.7 = bf16[96,768]{0,1:T(8,128)(2,1)S(1)} all-gather(bf16[96,96]{0,1:T(8,128)(2,1)S(1)} %copy.44), channel_id=1, replica_groups=mesh['seq'=8,'ch'=4] {'seq'}, dimensions={1}, use_global_device_ids=true | all-gather | bytes 165888 | tf_op jit(solution)/shard_map/all_gather | solution.py:120
  103.5 0.8 fusion.63
  104.3 20.0 %all-reduce.2 = (f32[96]{0:T(128)S(1)}, f32[96]{0:T(128)S(1)}) all-reduce(f32[96]{0:T(128)S(1)} %get-tuple-element.63, f32[96]{0:T(128)S(1)} %get-tuple-element.62), channel_id=1, replica_groups=mesh['seq'=8,'ch'=4] {'seq'}, use_global_device_ids=true, to_apply=%region_10.0 | all-reduce | flops 192 | bytes 1536 | tf_op jit(solution)/shard_map/psum | solution.py:49
  124.4 3.0 convolution_bitcast_fusion
  127.5 2.3 fusion.62
  129.8 17.2 %all-reduce.1 = (f32[96]{0:T(128)S(1)}, f32[96]{0:T(128)S(1)}) all-reduce(f32[96]{0:T(128)S(1)} %get-tuple-element.61, f32[96]{0:T(128)S(1)} %get-tuple-element.60), channel_id=1, replica_groups=mesh['seq'=8,'ch'=4] {'seq'}, use_global_device_ids=true, to_apply=%region_15.0 | all-reduce | flops 192 | bytes 1536 | tf_op jit(solution)/shard_map/psum | solution.py:58
  148.9 0.7 copy.52
  149.6 1.5 reshape.99
  151.3 1.3 collective-permute-start.2
  152.6 2.4 fusion.60
  155.6 4.7 %collective-permute-start.3 = (bf16[9,96]{0,1:T(8,128)(2,1)S(1)}, bf16[9,96]{0,1:T(8,128)(2,1)S(1)}, u32[]{:S(2)}, u32[]{:S(2)}) collective-permute-start(bf16[9,96]{0,1:T(8,128)(2,1)S(1)} %get-tuple-element.101), channel_id=1, source_target_pairs={{0,4},{4,8},{8,12},{12,16},{16,20},{20,24},{24,28},{1,5},{5,9},{9,... | collective-permute-start | bytes 5192 | tf_op jit(solution)/shard_map/ppermute | solution.py:27
  160.4 0.7 fusion.32
  161.7 2.7 multiply_add_fusion
  164.5 0.8 copy-done.5
  166.3 20.0 %reduce-scatter.9.cloned.1.call-done = f32[96,96]{1,0:T(8,128)} async-done(((f32[768,96]{1,0:T(8,128)}), f32[96,96]{1,0:T(8,128)}) %reduce-scatter.9.cloned.1.call-update) | async-done | bytes 36880
  186.3 0.9 copy.55
  187.9 65.4 %reduce-scatter.7.cloned.1.call-done = f32[96,288]{1,0:T(8,128)} async-done(((f32[768,288]{1,0:T(8,128)}), f32[96,288]{1,0:T(8,128)}) %reduce-scatter.7.cloned.1.call-update) | async-done | bytes 110608
  253.3 1.1 reshape.100
  254.6 0.8 copy.51
  255.4 0.8 copy.50
  256.2 0.8 copy.49
  257.0 28.4 %all-reduce.7.cloned.1.call-done = (f32[1024,768]{1,0:T(8,128)}, f32[1024,768]{1,0:T(8,128)}) async-done(((f32[1024,768]{1,0:T(8,128)}, f32[1024,768]{1,0:T(8,128)}), (f32[1024,768]{1,0:T(8,128)}, f32[1024,768]{1,0:T(8,128)})) %all-reduce.7.cloned.1.call-update) | async-done | bytes 6291472 | tf_op jit(solution)/shard_map/psum | solution.py:137
  285.4 5.6 %fusion.61 = (f32[768]{0:T(1024)S(1)}, f32[768]{0:T(1024)S(1)}, f32[1024,768]{1,0:T(8,128)}) fusion(f32[768]{0:T(1024)S(1)} %get-tuple-element.104, f32[768]{0:T(1024)S(1)} %get-tuple-element.105, bf16[1024,768]{1,0:T(8,128)(2,1)S(1)} %copy-done, f32[1024,768]{1,0:T(8,128)} %get-tuple-element.78, f32[768]{0:T(1024)S(1)} %get-tuple-element.65, ...), kind=kLoop, calls=%fused_computation.121 | loop fusion | flops 21232128 | bytes 7882752 | tf_op jit(solution)/shard_map/reduce_sum | solution.py:58
  290.9 21.6 %all-reduce = (f32[768]{0:T(1024)S(1)}, f32[768]{0:T(1024)S(1)}) all-reduce(f32[768]{0:T(1024)S(1)} %get-tuple-element.57, f32[768]{0:T(1024)S(1)} %get-tuple-element.56), channel_id=1, replica_groups=mesh['seq'=8,'ch'=4] {'seq'}, use_global_device_ids=true, to_apply=%region_20.0 | all-reduce | flops 1536 | bytes 12288 | tf_op jit(solution)/shard_map/psum | solution.py:58
  312.6 6.2 %fusion.20 = (f32[1024,768]{1,0:T(8,128)}, bf16[1024,768]{1,0:T(8,128)(2,1)}) fusion(bf16[1024,768]{1,0:T(8,128)(2,1)S(1)} %copy-done, f32[1024,768]{1,0:T(8,128)} %get-tuple-element.95, bf16[1024,768]{1,0:T(8,128)(2,1)S(1)} %copy-done.1, f32[768]{0:T(1024)S(1)} %get-tuple-element.69, f32[768]{0:T(1024)S(1)} %broadcast_multiply_fusion, ...), kind=kLoop, calls=%fused_computation.26 | loop fusion | flops 9437184 | bytes 14171136 | tf_op jit(solution)/shard_map/add | solution.py:166
  (86 shorter events, 7.3 us)
Async XLA Ops:
  8.0 31.7 %copy-start.12 = (f32[2,96]{1,0:T(2,128)S(1)}, f32[2,96]{1,0:T(2,128)}, u32[]{:S(2)}) copy-start(f32[2,96]{1,0:T(2,128)} %param.27) | copy-start | bytes 2308
  8.0 31.7 %copy-start.6 = (f32[96,96]{1,0:T(8,128)S(1)}, f32[96,96]{1,0:T(8,128)}, u32[]{:S(2)}) copy-start(f32[96,96]{1,0:T(8,128)} %param.21) | copy-start | bytes 110596
  8.0 31.8 %copy-start.4 = (f32[3,96,96]{2,1,0:T(8,128)S(1)}, f32[3,96,96]{2,1,0:T(8,128)}, u32[]{:S(2)}) copy-start(f32[3,96,96]{2,1,0:T(8,128)} %param.18) | copy-start | bytes 331780
  8.0 178.3 %reduce-scatter.9.cloned.1.call-start = ((), (), s32[]{:S(2)}) async-start(), calls=%async_computation.3 | async-start | bytes 442368
  34.1 38.0 %copy-start.17 = (s32[8]{0:T(128)S(1)}, s32[8]{0:T(128)}, u32[]{:S(2)}) copy-start(s32[8]{0:T(128)} %param.17) | copy-start | bytes 100
  37.1 66.4 %collective-permute-start = (bf16[9,768]{1,0:T(8,128)(2,1)S(1)}, bf16[9,768]{1,0:T(8,128)(2,1)S(1)}, u32[]{:S(2)}, u32[]{:S(2)}) collective-permute-start(bf16[9,768]{1,0:T(8,128)(2,1)S(1)} %get-tuple-element.99), channel_id=1, source_target_pairs={{0,4},{4,8},{8,12},{12,16},{16,20},{20,24},{24,28},{1,5},{5,9},{9,... | collective-permute-start | bytes 41480 | tf_op jit(solution)/shard_map/ppermute | solution.py:27
  38.4 64.5 %collective-permute-start.1 = (bf16[9,768]{1,0:T(8,128)(2,1)S(1)}, bf16[9,768]{1,0:T(8,128)(2,1)S(1)}, u32[]{:S(2)}, u32[]{:S(2)}) collective-permute-start(bf16[9,768]{1,0:T(8,128)(2,1)S(1)} %get-tuple-element.100), channel_id=1, source_target_pairs={{4,0},{8,4},{12,8},{16,12},{20,16},{24,20},{28,24},{5,1},{9,5},{13... | collective-permute-start | bytes 41480 | tf_op jit(solution)/shard_map/ppermute | solution.py:28
  102.9 1.4 copy-start.20
  103.5 0.8 copy-start.18
  104.3 42.8 %copy-start.2 = (f32[1024,96]{0,1:T(8,128)}, f32[1024,96]{0,1:T(8,128)S(1)}, u32[]{:S(2)}) copy-start(f32[1024,96]{0,1:T(8,128)S(1)} %get-tuple-element.113) | copy-start | bytes 1179652
  127.4 19.9 %copy-start.19 = (bf16[9,768]{1,0:T(8,128)(2,1)S(1)}, bf16[9,768]{1,0:T(8,128)(2,1)}, u32[]{:S(2)}) copy-start(bf16[9,768]{1,0:T(8,128)(2,1)} %copy-done.18) | copy-start | bytes 41476
  127.4 20.4 %copy-start.21 = (bf16[9,768]{1,0:T(8,128)(2,1)S(1)}, bf16[9,768]{1,0:T(8,128)(2,1)}, u32[]{:S(2)}) copy-start(bf16[9,768]{1,0:T(8,128)(2,1)} %copy-done.20) | copy-start | bytes 41476
  127.4 125.9 %reduce-scatter.7.cloned.1.call-start = ((), (), s32[]{:S(2)}) async-start(), calls=%async_computation.2 | async-start | bytes 1327104
  149.6 3.0 copy-start.3
  151.1 134.3 %all-reduce.7.cloned.1.call-start = ((), (), s32[]{:S(2)}) async-start(), calls=%async_computation.4 | async-start | bytes 12582912 | tf_op jit(solution)/shard_map/psum | solution.py:137
  151.3 9.1 %collective-permute-start.2 = (bf16[9,96]{0,1:T(8,128)(2,1)S(1)}, bf16[9,96]{0,1:T(8,128)(2,1)S(1)}, u32[]{:S(2)}, u32[]{:S(2)}) collective-permute-start(bf16[9,96]{0,1:T(8,128)(2,1)S(1)} %get-tuple-element.102), channel_id=1, source_target_pairs={{4,0},{8,4},{12,8},{16,12},{20,16},{24,20},{28,24},{5,1},{9,5},{13... | collective-permute-start | bytes 5192 | tf_op jit(solution)/shard_map/ppermute | solution.py:28
  155.6 6.1 %collective-permute-start.3 = (bf16[9,96]{0,1:T(8,128)(2,1)S(1)}, bf16[9,96]{0,1:T(8,128)(2,1)S(1)}, u32[]{:S(2)}, u32[]{:S(2)}) collective-permute-start(bf16[9,96]{0,1:T(8,128)(2,1)S(1)} %get-tuple-element.101), channel_id=1, source_target_pairs={{0,4},{4,8},{8,12},{12,16},{16,20},{20,24},{24,28},{1,5},{5,9},{9,... | collective-permute-start | bytes 5192 | tf_op jit(solution)/shard_map/ppermute | solution.py:27
  164.4 0.9 copy-start.5
  164.4 1.0 copy-start.7
  164.4 1.1 copy-start.8
  164.4 1.3 copy-start.15
  164.4 1.3 copy-start.16
  164.4 22.8 %copy-start.9 = (f32[96,96]{1,0:T(8,128)S(1)}, f32[96,96]{1,0:T(8,128)}, u32[]{:S(2)}) copy-start(f32[96,96]{1,0:T(8,128)} %param.23) | copy-start | bytes 110596
  164.4 22.8 %copy-start.10 = (f32[96,96]{1,0:T(8,128)S(1)}, f32[96,96]{1,0:T(8,128)}, u32[]{:S(2)}) copy-start(f32[96,96]{1,0:T(8,128)} %param.22) | copy-start | bytes 110596
  165.3 120.1 %copy-start = (bf16[1024,768]{1,0:T(8,128)(2,1)S(1)}, bf16[1024,768]{1,0:T(8,128)(2,1)}, u32[]{:S(2)}) copy-start(bf16[1024,768]{1,0:T(8,128)(2,1)} %param.15) | copy-start | bytes 4718596
  285.4 27.2 %copy-start.1 = (bf16[1024,768]{1,0:T(8,128)(2,1)S(1)}, bf16[1024,768]{1,0:T(8,128)(2,1)}, u32[]{:S(2)}) copy-start(bf16[1024,768]{1,0:T(8,128)(2,1)} %param.16) | copy-start | bytes 4718596
  312.6 6.3 %copy-start.11 = (f32[2,768]{1,0:T(2,128)S(1)}, f32[2,768]{1,0:T(2,128)}, u32[]{:S(2)}) copy-start(f32[2,768]{1,0:T(2,128)} %param.24) | copy-start | bytes 18436
  312.6 6.3 %copy-start.13 = (f32[2,768]{1,0:T(2,128)S(1)}, f32[2,768]{1,0:T(2,128)}, u32[]{:S(2)}) copy-start(f32[2,768]{1,0:T(2,128)} %param.26) | copy-start | bytes 18436
  312.6 6.2 %copy-start.14 = (f32[2,768]{1,0:T(2,128)S(1)}, f32[2,768]{1,0:T(2,128)}, u32[]{:S(2)}) copy-start(f32[2,768]{1,0:T(2,128)} %param.25) | copy-start | bytes 18436
Sparse Core Ops, SparseCore 0:
  127.5 58.7 reduce-scatter.8
  190.3 62.9 reduce-scatter.6
Sparse Core Ops, SparseCore 1:
  164.5 120.8 all-reduce.6
where the time goes:
time: 327 us
  blocking collectives  144 us (44%)
  waiting for transfers between devices  115 us (35%)
  other arithmetic  19 us (6%)
  between operations  16 us (5%)
  matrix products  15.3 us (5%)
  local copies, waits for them, and re-layouts  8.88 us (3%)
  starting transfers between devices  8.71 us (3%)
    unnamed x5, waiting for transfers between devices  85.5 us
    psum x2, blocking collectives, normalize(): lax.psum((jnp.sum(values, axis=0), jnp.sum(values * values, axis=0)), 'seq')  43.4 us
    psum x2, blocking collectives, norm_back(): lax.psum((jnp.sum(upstream * centered, axis=0), jnp.sum(upstream, axis=0)...  38.8 us
    all_gather x1, blocking collectives, shards(): lax.all_gather(master_conv.astype(jnp.bfloat16), 'seq', axis=1, tiled=True)  31.6 us
    all_gather x1, blocking collectives, shards(): lax.all_gather(master_point.astype(jnp.bfloat16), 'seq', axis=1, tiled=True)  30.6 us
    psum x1, waiting for transfers between devices, shards(): branch = lax.psum(partial_value, 'ch')  28.4 us
    unnamed x56, local copies, waits for them, and re-layouts  7.99 us
  transfers between devices with their start and end apart: 7, of which 4 were waited for; matrix products, arithmetic and copies ran while one was open for 6% of the time, Pallas kernels for 0%

commit v1 on v0

v1 whole, which is shorter than its diff:
```python
import jax
import jax.numpy as jnp
from jax import lax
from jax.sharding import PartitionSpec as P

KERNEL_WIDTH = 3
DILATION_BINS = 9
STEP = 10


NORM_EPS = 1e-05
ADAM_EPS = 1e-08
BETA_ONE = 0.9
BETA_TWO = 0.999
RATE_WEIGHT = 0.05
RATE_NORM = 0.5
DECAY_WEIGHT = 0.01


def gather_blocks(x, axis):
    size, own = lax.axis_size(axis), lax.axis_index(axis)
    blocks = x[None]
    reach = size // 2
    while reach:
        other = lax.ppermute(blocks, axis, [(i, i ^ reach) for i in range(size)])
        high = (own // reach) % 2 == 1
        pair = [jnp.where(high, other, blocks), jnp.where(high, blocks, other)]
        blocks = jnp.stack(pair, axis=1).reshape((-1,) + x.shape)
        reach //= 2
    return blocks


def scatter_sum(blocks, axis):
    size, own = lax.axis_size(axis), lax.axis_index(axis)
    reach = 1
    while reach < size:
        pairs = blocks.reshape((-1, 2) + blocks.shape[1:])
        high = (own // reach) % 2 == 1
        kept = jnp.where(high, pairs[:, 1], pairs[:, 0])
        sent = jnp.where(high, pairs[:, 0], pairs[:, 1]).astype(jnp.bfloat16)
        got = lax.ppermute(sent, axis, [(i, i ^ reach) for i in range(size)])
        blocks = kept + got.astype(jnp.float32)
        reach *= 2
    return blocks[0]


def each(x, axes):
    size = lax.axis_size(axes)
    copies = jnp.broadcast_to(x[None], (size,) + x.shape)
    return lax.all_to_all(copies, axes, 0, 0, tiled=True)


def moments(total, bin_count):
    average = total[0] / bin_count
    variance = total[1] / bin_count - average * average
    return average, lax.rsqrt(variance + NORM_EPS)


def window_masks(starts, positions, bin_count):

    def window_of(neighbors):
        return jnp.sum((neighbors[:, None] >= starts[None, :]).astype(jnp.int32), axis=1)

    own_window = window_of(positions)
    mask_list = []
    for kernel_index in range(KERNEL_WIDTH):
        bin_shift = (kernel_index - KERNEL_WIDTH // 2) * DILATION_BINS
        neighbors = positions + bin_shift
        inside = (neighbors >= 0) & (neighbors < bin_count) & (window_of(neighbors) == own_window)
        mask_list.append(inside.astype(jnp.float32))
    return mask_list


def adamw(weights_old, first_moment_state, second_mom, gradient, step_rate, decay_rate):
    first_next = BETA_ONE * first_moment_state + (1.0 - BETA_ONE) * gradient
    second_next = BETA_TWO * second_mom + (1.0 - BETA_TWO) * gradient * gradient
    corrected = (
        first_next
        / (1.0 - BETA_ONE**STEP)
        / (jnp.sqrt(second_next / (1.0 - BETA_TWO**STEP)) + ADAM_EPS)
    )
    weights_new = weights_old - step_rate * (corrected + decay_rate * weights_old)
    return (first_next, second_next, weights_new)


def shards(
    inputs, cotangent, starts,
    master_conv, first_conv, second_conv,
    master_point, first_point, second_point,
    norm_in, first_in, second_in,
    norm_mid, first_mid, second_mid,
):
    rows, width = inputs.shape
    seq_size, ch_size = lax.axis_size("seq"), lax.axis_size("ch")
    own_ch = lax.axis_index("ch")
    bin_count = rows * seq_size
    span = DILATION_BINS * (KERNEL_WIDTH // 2)
    slim = master_conv.shape[2]
    mid = slim * ch_size
    shifts = [(j - KERNEL_WIDTH // 2) * DILATION_BINS for j in range(KERNEL_WIDTH)]

    up = [(i, i + 1) for i in range(seq_size - 1)]
    down = [(j, i) for i, j in up]
    last = jnp.concatenate([inputs[rows - 2 * span :], cotangent[rows - span :]])
    first = jnp.concatenate([inputs[: 2 * span], cotangent[:span]])
    before = lax.ppermute(last, "seq", up)
    after = lax.ppermute(first, "seq", down)
    x_ext = jnp.concatenate([before[: 2 * span], inputs, after[: 2 * span]]).astype(jnp.float32)
    cot_ext = jnp.concatenate([before[2 * span :], cotangent, after[2 * span :]])

    positions = lax.axis_index("seq") * rows - span + jnp.arange(rows + 2 * span, dtype=jnp.int32)
    masks = window_masks(starts, positions, bin_count)
    masks = [mask * ((positions >= 0) & (positions < bin_count)) for mask in masks]

    conv_low = jnp.concatenate(list(master_conv.astype(jnp.bfloat16)), axis=1)
    conv_own = gather_blocks(conv_low, "seq").reshape(width, KERNEL_WIDTH * slim)
    point_own = gather_blocks(master_point.astype(jnp.bfloat16).T, "seq").reshape(width, slim)

    values = inputs.astype(jnp.float32)
    total_in = each(jnp.stack([jnp.sum(values, 0), jnp.sum(values * values, 0)]), "seq").sum(0)
    mean_in, root_in = moments(total_in, bin_count)
    pre_in = (x_ext - mean_in) * root_in * norm_in[0] + norm_in[1]
    hidden_in = jax.nn.gelu(pre_in).astype(jnp.bfloat16)

    products = jnp.dot(hidden_in, conv_own, preferred_element_type=jnp.float32)
    conv_out = 0.0
    for j, shift in enumerate(shifts):
        part = products[span + shift : span + shift + rows + 2 * span, j * slim : (j + 1) * slim]
        conv_out = conv_out + part * masks[j][:, None]
    mine = conv_out[span : span + rows]
    sums = jnp.stack([jnp.sum(mine, 0), jnp.sum(mine * mine, 0)])
    local_mean = sums[0] / rows
    conv_rest = (conv_out - local_mean).astype(jnp.bfloat16)

    all_rest = gather_blocks(conv_rest, "ch")
    all_rest = jnp.concatenate([all_rest[q] for q in range(ch_size)], axis=1)
    all_sums = each(sums, ("seq", "ch")).reshape(seq_size, ch_size, 2, slim)
    all_sums = jnp.transpose(all_sums, (0, 2, 1, 3)).reshape(seq_size, 2, mid)
    mean_mid, root_mid = moments(jnp.sum(all_sums, 0), bin_count)
    local_mean_all = lax.dynamic_index_in_dim(all_sums, lax.axis_index("seq"), 0, False)[0] / rows

    point_all = gather_blocks(point_own, "ch")
    point_all = jnp.concatenate([point_all[q] for q in range(ch_size)], axis=1)
    conv_all = gather_blocks(conv_own, "ch")

    params_mid = gather_blocks(norm_mid, "ch")
    params_mid = jnp.concatenate([params_mid[q] for q in range(ch_size)], axis=1)
    centered_mid = (all_rest.astype(jnp.float32) - (mean_mid - local_mean_all)) * root_mid
    pre_mid = centered_mid * params_mid[0] + params_mid[1]
    upstream_mid = jnp.dot(cot_ext, point_all, preferred_element_type=jnp.float32)
    gelu_mid, pull_mid = jax.vjp(jax.nn.gelu, pre_mid)
    d_mid = pull_mid(upstream_mid)[0]
    hidden_mid = gelu_mid[span : span + rows].astype(jnp.bfloat16)
    d_own, c_own = d_mid[span : span + rows], centered_mid[span : span + rows]
    total_mid = each(jnp.stack([jnp.sum(d_own * c_own, 0), jnp.sum(d_own, 0)]), "seq").sum(0)

    branch = lax.dot_general(
        hidden_mid, point_all, (((1,), (1,)), ((), ())), preferred_element_type=jnp.float32
    )
    block_out = (values + branch).astype(jnp.bfloat16)
    hidden_slim = lax.dynamic_slice_in_dim(hidden_mid, own_ch * slim, slim, axis=1)
    grad_point = lax.dot_general(
        cotangent, hidden_slim, (((0,), (0,)), ((), ())), preferred_element_type=jnp.float32
    )

    grad_out = root_mid * params_mid[0] * (
        d_mid - total_mid[1] / bin_count - centered_mid * total_mid[0] / bin_count
    )
    terms = []
    for j, shift in enumerate(shifts):
        masked = grad_out * masks[j][:, None]
        terms.append(masked[span - shift : span - shift + rows].astype(jnp.bfloat16))
    hidden_own = hidden_in[2 * span : 2 * span + rows]
    slim_terms = [lax.dynamic_slice_in_dim(t, own_ch * slim, slim, axis=1) for t in terms]
    grad_conv = lax.dot_general(
        hidden_own,
        jnp.concatenate(slim_terms, axis=1),
        (((0,), (0,)), ((), ())),
        preferred_element_type=jnp.float32,
    )
    upstream_in = 0.0
    for j in range(KERNEL_WIDTH):
        taps = [conv_all[q][:, j * slim : (j + 1) * slim] for q in range(ch_size)]
        upstream_in = upstream_in + lax.dot_general(
            terms[j],
            jnp.concatenate(taps, axis=1),
            (((1,), (1,)), ((), ())),
            preferred_element_type=jnp.float32,
        )
    d_in = jax.vjp(jax.nn.gelu, pre_in[2 * span : 2 * span + rows])[1](upstream_in)[0]
    centered_in = (values - mean_in) * root_in
    grad_in = each(jnp.stack([jnp.sum(d_in * centered_in, 0), jnp.sum(d_in, 0)]), "seq").sum(0)
    input_grad = cotangent.astype(jnp.float32) + root_in * norm_in[0] * (
        d_in - grad_in[1] / bin_count - centered_in * grad_in[0] / bin_count
    )

    both = jnp.concatenate([grad_conv, grad_point], axis=1)
    both = scatter_sum(both.reshape(seq_size, width // seq_size, -1), "seq")
    conv_sum = jnp.stack([both[:, j * slim : (j + 1) * slim] for j in range(KERNEL_WIDTH)])
    point_sum = both[:, KERNEL_WIDTH * slim :].T

    grad_mid = lax.dynamic_slice_in_dim(total_mid, own_ch * slim, slim, axis=1)
    conv_new = adamw(master_conv, first_conv, second_conv, conv_sum, RATE_WEIGHT, DECAY_WEIGHT)
    point_new = adamw(
        master_point, first_point, second_point, point_sum, RATE_WEIGHT, DECAY_WEIGHT
    )
    in_new = adamw(norm_in, first_in, second_in, grad_in, RATE_NORM, 0.0)
    mid_new = adamw(norm_mid, first_mid, second_mid, grad_mid, RATE_NORM, 0.0)
    return (block_out, input_grad) + conv_new + point_new + in_new + mid_new


def solution(mesh):
    in_specs = (
        P("seq", None),
        P("seq", None),
        P(),
        P(None, "seq", "ch"),
        P(None, "seq", "ch"),
        P(None, "seq", "ch"),
        P("ch", "seq"),
        P("ch", "seq"),
        P("ch", "seq"),
        P(),
        P(),
        P(),
        P(None, "ch"),
        P(None, "ch"),
        P(None, "ch"),
    )
    out_specs = (
        P("seq", None),
        P("seq", None),
        P(None, "seq", "ch"),
        P(None, "seq", "ch"),
        P(None, "seq", "ch"),
        P("ch", "seq"),
        P("ch", "seq"),
        P("ch", "seq"),
        P(),
        P(),
        P(),
        P(None, "ch"),
        P(None, "ch"),
        P(None, "ch"),
    )
    return jax.shard_map(shards, mesh=mesh, in_specs=in_specs, out_specs=out_specs, check_vma=False)
```

time: 327 us -> 179 us (0.55)
  blocking collectives: 144 us -> 0 us
  waiting for transfers between devices: 115 us -> 28.7 us
  starting transfers between devices: 8.71 us -> 44.7 us
  local copies, waits for them, and re-layouts: 8.88 us -> 44 us
  other arithmetic: 19 us -> 41.9 us
  between operations: 16 us -> 1.86 us
    unnamed x5 -> x0, waiting for transfers between devices: 85.5 us -> none
    psum x4 -> x0, blocking collectives: 82.2 us -> none  [the longest x2 43.4 us: normalize(): lax.psum((jnp.sum(values, axis=0), jnp.sum(values * values, axis=0)), 'seq')]
    all_gather x2 -> x0, blocking collectives: 62.2 us -> none  [the longest x1 31.6 us: shards(): lax.all_gather(master_conv.astype(jnp.bfloat16), 'seq', axis=1, tiled=True)]
    psum x1 -> x0, waiting for transfers between devices: 28.4 us -> none  [shards(): branch = lax.psum(partial_value, 'ch')]
    ppermute x4 -> x19, waiting for transfers between devices: 0.58 us -> 22.2 us  [the longest x3 12 us: scatter_sum(): got = lax.ppermute(sent, axis, [(i, i ^ reach) for i in range(size)])]
    concatenate x0 -> x3, local copies, waits for them, and re-layouts: none -> 21.2 us  [the longest x1 9.31 us: shards(): jnp.concatenate([before[:2 * span], inputs, after[:2 * span]])]
    all_to_all x0 -> x4, starting transfers between devices: none -> 21.2 us  [each(): return lax.all_to_all(copies, axes, 0, 0, tiled=True)]
    ppermute x4 -> x19, starting transfers between devices: 8.59 us -> 23.6 us  [the longest x14 15.3 us: gather_blocks(): other = lax.ppermute(blocks, axis, [(i, i ^ reach) for i in range(size)])]
  transfers between devices with their start and end apart: 7 -> 23, of which waited for: 4 -> 10; matrix products, arithmetic and copies ran while one was open for 6% -> 47% of each run, Pallas kernels for 0% -> 0%
where the time goes in v1:
time: 179 us; the launch traced here: 177 us
  starting transfers between devices  44.7 us (25%)
  local copies, waits for them, and re-layouts  44 us (25%)
  other arithmetic  41.9 us (23%)
  waiting for transfers between devices  28.7 us (16%)
  matrix products  15.4 us (9%)
  between operations  1.86 us (1%)
    all_to_all x4, starting transfers between devices, each(): return lax.all_to_all(copies, axes, 0, 0, tiled=True)  21.2 us
    ppermute x14, starting transfers between devices, gather_blocks(): other = lax.ppermute(blocks, axis, [(i, i ^ reach) for i in range(size)])  15.3 us
    ppermute x3, waiting for transfers between devices, scatter_sum(): got = lax.ppermute(sent, axis, [(i, i ^ reach) for i in range(size)])  12 us
    unnamed x120, local copies, waits for them, and re-layouts  11.1 us
    ppermute x14, waiting for transfers between devices, gather_blocks(): other = lax.ppermute(blocks, axis, [(i, i ^ reach) for i in range(size)])  10.1 us
    concatenate x1, local copies, waits for them, and re-layouts, shards(): jnp.concatenate([before[:2 * span], inputs, after[:2 * span]])  9.31 us
    concatenate x1, local copies, waits for them, and re-layouts, shards(): cot_ext = jnp.concatenate([before[2 * span:], cotangent, after[2 * span:]])  9.24 us
    all_to_all x4, waiting for transfers between devices, each(): return lax.all_to_all(copies, axes, 0, 0, tiled=True)  6.51 us
  transfers between devices with their start and end apart: 23, of which 10 were waited for; matrix products, arithmetic and copies ran while one was open for 47% of the time, Pallas kernels for 0%

profile of v1, /device:TPU:0, one launch (start us, length us, event | category | flops | bytes accessed | tf_op | source)
XLA Modules:
  0.0 176.5 jit_solution(5498494029504796063)
XLA Ops:
  1.7 4.1 %collective-permute-start.9 = (bf16[1,96,96]{2,1,0:T(8,128)(2,1)S(1)}, bf16[1,96,96]{2,1,0:T(8,128)(2,1)S(1)}, u32[]{:S(2)}, u32[]{:S(2)}) collective-permute-start(bf16[1,96,96]{2,1,0:T(8,128)(2,1)S(1)} %convert_bitcast_fusion), channel_id=1, source_target_pairs={{0,16},{4,20},{8,24},{12,28},{16,0},{20,4},{24,8},{28,12},{1,17},{... | collective-permute-start | bytes 55304 | tf_op jit(solution)/shard_map/ppermute | solution.py:25
  7.5 1.9 %convert_reduce_fusion = (f32[768]{0:T(1024)S(1)}, f32[768]{0:T(1024)S(1)}) fusion(bf16[1024,768]{1,0:T(8,128)(2,1)} %param.15), kind=kLoop, calls=%fused_computation.3 | loop fusion | flops 3144192 | bytes 1579008 | tf_op jit(solution)/shard_map/reduce_sum | solution.py:120
  10.0 6.1 %all-to-all-start = ((f32[8,2,768]{2,1,0:T(2,128)}), f32[8,2,768]{2,1,0:T(2,128)S(1)}, u32[]{:S(2)}, u32[]{:S(2)}) async-start(f32[8,2,768]{2,1,0:T(2,128)} %broadcast_in_dim.16), calls=%async_computation | async-start | bytes 98304 | tf_op jit(solution)/shard_map/all_to_all | solution.py:50
  17.0 3.9 %collective-permute-start = (bf16[27,768]{1,0:T(8,128)(2,1)S(1)}, bf16[27,768]{1,0:T(8,128)(2,1)S(1)}, u32[]{:S(2)}, u32[]{:S(2)}) collective-permute-start(bf16[27,768]{1,0:T(8,128)(2,1)S(1)} %pad_maximum_fusion.14), channel_id=1, source_target_pairs={{0,4},{4,8},{8,12},{12,16},{16,20},{20,24},{24,28},{1,5},{5,9},{9,... | collective-permute-start | bytes 124424 | tf_op jit(solution)/shard_map/ppermute | solution.py:106
  24.1 1.8 %collective-permute-done.7 = f32[1,2,96]{2,1,0:T(2,128)S(1)} collective-permute-done((f32[1,2,96]{2,1,0:T(2,128)S(1)}, f32[1,2,96]{2,1,0:T(2,128)S(1)}, u32[]{:S(2)}, u32[]{:S(2)}) %collective-permute-start.7) | collective-permute-done | bytes 800 | tf_op jit(solution)/shard_map/ppermute | solution.py:25
  30.1 3.5 %collective-permute-start.10 = (bf16[2,96,96]{2,1,0:T(8,128)(2,1)}, bf16[2,96,96]{2,1,0:T(8,128)(2,1)}, u32[]{:S(2)}, u32[]{:S(2)}) collective-permute-start(bf16[2,96,96]{2,1,0:T(8,128)(2,1)} %maximum_bitcast_fusion.5), channel_id=1, source_target_pairs={{0,8},{4,12},{8,0},{12,4},{16,24},{20,28},{24,16},{28,20},{1,9},{5... | collective-permute-start | bytes 110600 | tf_op jit(solution)/shard_map/ppermute | solution.py:25
  34.3 9.3 %concatenate.41 = bf16[1060,768]{1,0:T(8,128)(2,1)} concatenate(bf16[18,768]{1,0:T(8,128)(2,1)S(1)} %slice.307, bf16[1024,768]{1,0:T(8,128)(2,1)S(1)} %copy-done, bf16[18,768]{1,0:T(8,128)(2,1)S(1)} %slice.308), dimensions={0} | concatenate | bytes 3256320 | tf_op jit(solution)/shard_map/concatenate | solution.py:108
  43.7 9.2 %concatenate.46 = bf16[1042,768]{1,0:T(8,128)(2,1)} concatenate(bf16[9,768]{1,0:T(8,128)(2,1)S(1)} %slice.333, bf16[1024,768]{1,0:T(8,128)(2,1)S(1)} %copy-done.1, bf16[9,768]{1,0:T(8,128)(2,1)S(1)} %slice.334), dimensions={0} | concatenate | bytes 3201024 | tf_op jit(solution)/shard_map/concatenate | solution.py:109
  56.8 5.2 %multiply_add_fusion = (f32[1060,768]{1,0:T(8,128)}, bf16[1060,768]{1,0:T(8,128)(2,1)}) fusion(bf16[1060,768]{1,0:T(8,128)(2,1)} %concatenate.41, f32[768]{0:T(1024)S(1)} %get-tuple-element.108, f32[768]{0:T(1024)S(1)} %get-tuple-element.107, f32[768]{0:T(1024)S(1)} %get-tuple-element.111, f32[768]{0:T(1024)S(1)} %get-tuple-element.200), kind=kLoop, calls=%fused_computation.15 | loop fusion | flops 11397120 | bytes 6524928 | tf_op jit(solution)/shard_map/add | solution.py:122
  65.1 2.7 %collective-permute-done.12 = bf16[1,768,96]{1,2,0:T(8,128)(2,1)S(1)} collective-permute-done((bf16[1,768,96]{1,2,0:T(8,128)(2,1)S(1)}, bf16[1,768,96]{1,2,0:T(8,128)(2,1)S(1)}, u32[]{:S(2)}, u32[]{:S(2)}) %collective-permute-start.12) | collective-permute-done | bytes 147488 | tf_op jit(solution)/shard_map/ppermute | solution.py:25
  68.7 3.7 %collective-permute-done.4 = bf16[4,96,288]{2,1,0:T(8,128)(2,1)S(1)} collective-permute-done((bf16[4,96,288]{2,1,0:T(8,128)(2,1)S(1)}, bf16[4,96,288]{2,1,0:T(8,128)(2,1)S(1)}, u32[]{:S(2)}, u32[]{:S(2)}) %collective-permute-start.4) | collective-permute-done | bytes 221216 | tf_op jit(solution)/shard_map/ppermute | solution.py:25
  74.5 2.3 %fusion.111 = f32[1060,288]{0,1:T(8,128)S(1)} fusion(bf16[1060,768]{1,0:T(8,128)(2,1)} %get-tuple-element.139, bf16[768,288]{0,1:T(8,128)(2,1)} %reshape_reshape.6), kind=kOutput, calls=%fused_computation.256 | convolution fusion | flops 468910080 | bytes 3291648 | tf_op jit(solution)/shard_map/dot_general | solution.py:125
  78.6 4.8 %all-to-all-start.1 = ((f32[32,2,96]{2,1,0:T(2,128)}), f32[32,2,96]{2,1,0:T(2,128)}, u32[]{:S(2)}, u32[]{:S(2)}) async-start(f32[32,2,96]{2,1,0:T(2,128)} %broadcast_in_dim.19), calls=%async_computation.1 | async-start | bytes 65536 | tf_op jit(solution)/shard_map/all_to_all | solution.py:50
  83.4 1.7 fusion.72
  88.4 2.0 %all-to-all-done.1 = f32[32,2,96]{2,1,0:T(2,128)} async-done(((f32[32,2,96]{2,1,0:T(2,128)}), f32[32,2,96]{2,1,0:T(2,128)}, u32[]{:S(2)}, u32[]{:S(2)}) %all-to-all-start.1) | async-done | bytes 24608 | tf_op jit(solution)/shard_map/all_to_all | solution.py:50
  93.2 1.8 %collective-permute-done.5 = bf16[1,1042,96]{1,2,0:T(8,128)(2,1)S(1)} collective-permute-done((bf16[1,1042,96]{1,2,0:T(8,128)(2,1)}, bf16[1,1042,96]{1,2,0:T(8,128)(2,1)S(1)}, u32[]{:S(2)}, u32[]{:S(2)}) %collective-permute-start.5) | collective-permute-done | bytes 200096 | tf_op jit(solution)/shard_map/ppermute | solution.py:25
  99.2 2.8 %multiply_add_fusion.1 = (f32[1042,384]{1,0:T(8,128)}, f32[1042,384]{1,0:T(8,128)}, f32[1042,384]{1,0:T(8,128)S(1)}) fusion(f32[384]{0:T(512)S(1)} %get-tuple-element.113, f32[384]{0:T(512)S(1)} %get-tuple-element.114, f32[384]{0:T(512)S(1)} %get-tuple-element.212, f32[384]{0:T(512)S(1)} %get-tuple-element.211, bf16[1042,96]{1,0:T(8,128)(2,1)S(1)} %bitcast.254, ...), kind=kLoop, calls=%fused_computation.42 | loop fusion | flops 7602432 | bytes 5607936 | tf_op jit(solution)/shard_map/add | solution.py:149
  102.0 2.1 %fusion.29 = f32[1042,384]{1,0:T(8,128)S(1)} fusion(bf16[1042,768]{1,0:T(8,128)(2,1)S(1)} %copy-done.14, bf16[768,96]{0,1:T(8,128)(2,1)S(1)} %get-tuple-element.159, bf16[768,96]{0,1:T(8,128)(2,1)S(1)} %get-tuple-element.160, bf16[768,96]{0,1:T(8,128)(2,1)S(1)} %copy-done.35, bf16[768,96]{0,1:T(8,128)(2,1)S(1)} %get-tuple-element.158, ...), kind=kOutput, calls=%fused_computation.40 | convolution fusion | flops 629359872 | bytes 4597248 | tf_op jit(solution)/shard_map/dot_general | solution.py:150
  106.0 5.5 %all-to-all-start.2 = ((f32[8,2,384]{2,1,0:T(2,128)}), f32[8,2,384]{2,1,0:T(2,128)S(1)}, u32[]{:S(2)}, u32[]{:S(2)}) async-start(f32[8,2,384]{2,1,0:T(2,128)} %broadcast_in_dim.22), calls=%async_computation.2 | async-start | bytes 49152 | tf_op jit(solution)/shard_map/all_to_all | solution.py:50
  111.5 2.3 %fusion.36 = bf16[1024,384]{1,0:T(8,128)(2,1)S(1)} fusion(f32[1042,384]{1,0:T(8,128)} %get-tuple-element.148, f32[1042,384]{1,0:T(8,128)} %get-tuple-element.147), kind=kLoop, calls=%fused_computation.55 | loop fusion | flops 786432 | bytes 3932160 | tf_op jit(solution)/shard_map/convert.3
  115.9 2.2 %all-to-all-done.2 = f32[8,2,384]{2,1,0:T(2,128)S(1)} async-done(((f32[8,2,384]{2,1,0:T(2,128)}), f32[8,2,384]{2,1,0:T(2,128)S(1)}, u32[]{:S(2)}, u32[]{:S(2)}) %all-to-all-start.2) | async-done | bytes 24608 | tf_op jit(solution)/shard_map/all_to_all | solution.py:50
  118.2 2.4 %subtract_multiply_fusion = f32[1042,384]{1,0:T(8,128)S(1)} fusion(f32[1042,384]{1,0:T(8,128)} %copy-done.5, f32[384]{0:T(512)S(1)} %get-tuple-element.116, f32[384]{0:T(512)S(1)} %get-tuple-element.115, f32[384]{0:T(512)S(1)} %get-tuple-element.112, f32[384]{0:T(512)S(1)} %get-tuple-element.212, f32[384]{0:T(512)S(1)} %get-tuple-element.211, ...), kind=kLoop, calls=%fused_computation.41 | loop fusion | flops 6001920 | bytes 4008960 | tf_op jit(solution)/shard_map/mul | solution.py:166
  124.4 2.7 %copy.164 = f32[768,384]{1,0:T(8,128)} copy(f32[768,384]{0,1:T(8,128)} %pad_maximum_fusion.1) | data formatting | bytes 2359296 | tf_op jit(solution)/shard_map/concatenate | solution.py:197
  130.3 6.0 %collective-permute-done.16 = bf16[4,96,384]{2,1,0:T(8,128)(2,1)S(1)} collective-permute-done((bf16[4,96,384]{2,1,0:T(8,128)(2,1)S(1)}, bf16[4,96,384]{2,1,0:T(8,128)(2,1)S(1)}, u32[]{:S(2)}, u32[]{:S(2)}) %collective-permute-start.16) | collective-permute-done | bytes 294944 | tf_op jit(solution)/shard_map/ppermute | solution.py:41
  137.3 2.1 %fusion.15 = bf16[1024,768]{1,0:T(8,128)(2,1)} fusion(bf16[1024,768]{1,0:T(8,128)(2,1)S(1)} %copy-done, bf16[1024,384]{1,0:T(8,128)(2,1)S(1)} %copy-done.18, bf16[768,96]{0,1:T(8,128)(2,1)S(1)} %copy-done.32, bf16[768,96]{0,1:T(8,128)(2,1)S(1)} %copy-done.34, bf16[768,96]{0,1:T(8,128)(2,1)S(1)} %copy-done.36, bf16[768,96]{0,1:T(8,128)(2,1)S(1)} %copy-done.30), kind=kOutput, calls=%fused_computation.23 | convolution fusion | flops 608698368 | bytes 4521984 | tf_op jit(solution)/shard_map/dot_general | solution.py:157
  139.4 2.3 %collective-permute-done.17 = bf16[2,96,384]{2,1,0:T(8,128)(2,1)S(1)} collective-permute-done((bf16[2,96,384]{2,1,0:T(8,128)(2,1)S(1)}, bf16[2,96,384]{2,1,0:T(8,128)(2,1)S(1)}, u32[]{:S(2)}, u32[]{:S(2)}) %collective-permute-start.17) | collective-permute-done | bytes 147488 | tf_op jit(solution)/shard_map/ppermute | solution.py:41
  141.8 1.7 collective-permute-start.18
  144.1 3.8 %collective-permute-done.18 = bf16[1,96,384]{2,1,0:T(8,128)(2,1)S(1)} collective-permute-done((bf16[1,96,384]{2,1,0:T(8,128)(2,1)S(1)}, bf16[1,96,384]{2,1,0:T(8,128)(2,1)S(1)}, u32[]{:S(2)}, u32[]{:S(2)}) %collective-permute-start.18) | collective-permute-done | bytes 73760 | tf_op jit(solution)/shard_map/ppermute | solution.py:41
  153.8 4.5 %fusion.19 = (f32[768]{0:T(1024)S(1)}, f32[768]{0:T(1024)S(1)}, f32[1024,768]{1,0:T(8,128)}) fusion(bf16[1024,768]{1,0:T(8,128)(2,1)S(1)} %copy-done, f32[768]{0:T(1024)S(1)} %copy-done.42, f32[768]{0:T(1024)S(1)} %copy-done.44, f32[1060,768]{1,0:T(8,128)S(1)} %copy-done.10, bf16[1024,384]{1,0:T(8,128)(2,1)S(1)} %copy-done.16, ...), kind=kOutput, calls=%fused_computation.27 | convolution fusion | flops 627571200 | bytes 15544320 | tf_op jit(solution)/shard_map/dot_general | solution.py:184
  159.1 4.7 %all-to-all-start.3 = ((f32[8,2,768]{2,1,0:T(2,128)}), f32[8,2,768]{2,1,0:T(2,128)S(1)}, u32[]{:S(2)}, u32[]{:S(2)}) async-start(f32[8,2,768]{2,1,0:T(2,128)} %broadcast_in_dim.23), calls=%async_computation.3 | async-start | bytes 98304 | tf_op jit(solution)/shard_map/all_to_all | solution.py:50
  168.2 2.3 %all-to-all-done.3 = f32[8,2,768]{2,1,0:T(2,128)S(1)} async-done(((f32[8,2,768]{2,1,0:T(2,128)}), f32[8,2,768]{2,1,0:T(2,128)S(1)}, u32[]{:S(2)}, u32[]{:S(2)}) %all-to-all-start.3) | async-done | bytes 49184 | tf_op jit(solution)/shard_map/all_to_all | solution.py:50
  171.9 4.6 %fusion.23 = f32[1024,768]{1,0:T(8,128)} fusion(bf16[1024,768]{1,0:T(8,128)(2,1)S(1)} %copy-done, f32[1024,768]{1,0:T(8,128)} %get-tuple-element.215, bf16[1024,768]{1,0:T(8,128)(2,1)S(1)} %copy-done.2, f32[768]{0:T(1024)S(1)} %get-tuple-element.110, f32[768]{0:T(1024)S(1)} %get-tuple-element.109, f32[768]{0:T(1024)S(1)} %copy-done.42, ...), kind=kLoop, calls=%fused_computation.31 | loop fusion | flops 7864320 | bytes 9452544 | tf_op jit(solution)/shard_map/add | solution.py:193
  (267 shorter events, 58.5 us)
Async XLA Ops:
  0.6 15.5 %copy-start = (bf16[1024,768]{1,0:T(8,128)(2,1)S(1)}, bf16[1024,768]{1,0:T(8,128)(2,1)}, u32[]{:S(2)}) copy-start(bf16[1024,768]{1,0:T(8,128)(2,1)} %param.15) | copy-start | bytes 4718596
  0.7 21.6 %copy-start.50 = (f32[2,96]{1,0:T(2,128)S(1)}, f32[2,96]{1,0:T(2,128)}, u32[]{:S(2)}) copy-start(f32[2,96]{1,0:T(2,128)} %param.27) | copy-start | bytes 2308
  0.7 23.2 %copy-start.54 = (s32[8]{0:T(128)S(1)}, s32[8]{0:T(128)}, u32[]{:S(2)}) copy-start(s32[8]{0:T(128)} %param.17) | copy-start | bytes 100
  1.7 26.3 %copy-start.39 = (f32[96,96]{1,0:T(8,128)S(1)}, f32[96,96]{1,0:T(8,128)}, u32[]{:S(2)}) copy-start(f32[96,96]{1,0:T(8,128)} %param.22) | copy-start | bytes 110596
  1.7 26.9 %copy-start.40 = (f32[96,96]{1,0:T(8,128)S(1)}, f32[96,96]{1,0:T(8,128)}, u32[]{:S(2)}) copy-start(f32[96,96]{1,0:T(8,128)} %param.23) | copy-start | bytes 110596
  1.7 27.7 %collective-permute-start.9 = (bf16[1,96,96]{2,1,0:T(8,128)(2,1)S(1)}, bf16[1,96,96]{2,1,0:T(8,128)(2,1)S(1)}, u32[]{:S(2)}, u32[]{:S(2)}) collective-permute-start(bf16[1,96,96]{2,1,0:T(8,128)(2,1)S(1)} %convert_bitcast_fusion), channel_id=1, source_target_pairs={{0,16},{4,20},{8,24},{12,28},{16,0},{20,4},{24,8},{28,12},{1,17},{... | collective-permute-start | bytes 55304 | tf_op jit(solution)/shard_map/ppermute | solution.py:25
  7.5 46.9 %collective-permute-start.2 = (bf16[1,96,288]{2,1,0:T(8,128)(2,1)}, bf16[1,96,288]{2,1,0:T(8,128)(2,1)}, u32[]{:S(2)}, u32[]{:S(2)}) collective-permute-start(bf16[1,96,288]{2,1,0:T(8,128)(2,1)} %maximum_bitcast_fusion.4), channel_id=1, source_target_pairs={{0,16},{4,20},{8,24},{12,28},{16,0},{20,4},{24,8},{28,12},{1,17},{... | collective-permute-start | bytes 165896 | tf_op jit(solution)/shard_map/ppermute | solution.py:25
  10.0 46.0 %all-to-all-start = ((f32[8,2,768]{2,1,0:T(2,128)}), f32[8,2,768]{2,1,0:T(2,128)S(1)}, u32[]{:S(2)}, u32[]{:S(2)}) async-start(f32[8,2,768]{2,1,0:T(2,128)} %broadcast_in_dim.16), calls=%async_computation | async-start | bytes 98304 | tf_op jit(solution)/shard_map/all_to_all | solution.py:50
  17.0 17.3 %collective-permute-start = (bf16[27,768]{1,0:T(8,128)(2,1)S(1)}, bf16[27,768]{1,0:T(8,128)(2,1)S(1)}, u32[]{:S(2)}, u32[]{:S(2)}) collective-permute-start(bf16[27,768]{1,0:T(8,128)(2,1)S(1)} %pad_maximum_fusion.14), channel_id=1, source_target_pairs={{0,4},{4,8},{8,12},{12,16},{16,20},{20,24},{24,28},{1,5},{5,9},{9,... | collective-permute-start | bytes 124424 | tf_op jit(solution)/shard_map/ppermute | solution.py:106
  20.9 13.4 %collective-permute-start.1 = (bf16[27,768]{1,0:T(8,128)(2,1)S(1)}, bf16[27,768]{1,0:T(8,128)(2,1)S(1)}, u32[]{:S(2)}, u32[]{:S(2)}) collective-permute-start(bf16[27,768]{1,0:T(8,128)(2,1)S(1)} %pad_maximum_fusion.15), channel_id=1, source_target_pairs={{4,0},{8,4},{12,8},{16,12},{20,16},{24,20},{28,24},{5,1},{9,5},{13... | collective-permute-start | bytes 124424 | tf_op jit(solution)/shard_map/ppermute | solution.py:107
  22.2 3.6 %collective-permute-start.7 = (f32[1,2,96]{2,1,0:T(2,128)S(1)}, f32[1,2,96]{2,1,0:T(2,128)S(1)}, u32[]{:S(2)}, u32[]{:S(2)}) collective-permute-start(f32[1,2,96]{2,1,0:T(2,128)S(1)} %bitcast.262), channel_id=1, source_target_pairs={{0,2},{1,3},{2,0},{3,1},{4,6},{5,7},{6,4},{7,5},{8,10},{9,11},{10,... | collective-permute-start | bytes 2312 | tf_op jit(solution)/shard_map/ppermute | solution.py:25
  25.9 3.5 %collective-permute-start.8 = (f32[2,2,96]{2,1,0:T(2,128)S(1)}, f32[2,2,96]{2,1,0:T(2,128)S(1)}, u32[]{:S(2)}, u32[]{:S(2)}) collective-permute-start(f32[2,2,96]{2,1,0:T(2,128)S(1)} %maximum_bitcast_fusion.6), channel_id=1, source_target_pairs={{0,1},{1,0},{2,3},{3,2},{4,5},{5,4},{6,7},{7,6},{8,9},{9,8},{10,11... | collective-permute-start | bytes 4616 | tf_op jit(solution)/shard_map/ppermute | solution.py:25
  30.1 22.8 %collective-permute-start.10 = (bf16[2,96,96]{2,1,0:T(8,128)(2,1)}, bf16[2,96,96]{2,1,0:T(8,128)(2,1)}, u32[]{:S(2)}, u32[]{:S(2)}) collective-permute-start(bf16[2,96,96]{2,1,0:T(8,128)(2,1)} %maximum_bitcast_fusion.5), channel_id=1, source_target_pairs={{0,8},{4,12},{8,0},{12,4},{16,24},{20,28},{24,16},{28,20},{1,9},{5... | collective-permute-start | bytes 110600 | tf_op jit(solution)/shard_map/ppermute | solution.py:25
  43.7 12.5 %copy-start.45 = (f32[2,768]{1,0:T(2,128)S(1)}, f32[2,768]{1,0:T(2,128)}, u32[]{:S(2)}) copy-start(f32[2,768]{1,0:T(2,128)} %param.24) | copy-start | bytes 18436
  53.8 8.2 %collective-permute-start.11 = (bf16[4,96,96]{2,1,0:T(8,128)(2,1)S(1)}, bf16[4,96,96]{2,1,0:T(8,128)(2,1)S(1)}, u32[]{:S(2)}, u32[]{:S(2)}) collective-permute-start(bf16[4,96,96]{2,1,0:T(8,128)(2,1)S(1)} %bitcast.259), channel_id=1, source_target_pairs={{0,4},{4,0},{8,12},{12,8},{16,20},{20,16},{24,28},{28,24},{1,5},{5... | collective-permute-start | bytes 221192 | tf_op jit(solution)/shard_map/ppermute | solution.py:25
  55.4 8.5 %collective-permute-start.3 = (bf16[2,96,288]{2,1,0:T(8,128)(2,1)S(1)}, bf16[2,96,288]{2,1,0:T(8,128)(2,1)S(1)}, u32[]{:S(2)}, u32[]{:S(2)}) collective-permute-start(bf16[2,96,288]{2,1,0:T(8,128)(2,1)S(1)} %maximum_bitcast_fusion.3), channel_id=1, source_target_pairs={{0,8},{4,12},{8,0},{12,4},{16,24},{20,28},{24,16},{28,20},{1,9},{5... | collective-permute-start | bytes 331784 | tf_op jit(solution)/shard_map/ppermute | solution.py:25
  62.4 5.4 %collective-permute-start.12 = (bf16[1,768,96]{1,2,0:T(8,128)(2,1)S(1)}, bf16[1,768,96]{1,2,0:T(8,128)(2,1)S(1)}, u32[]{:S(2)}, u32[]{:S(2)}) collective-permute-start(bf16[1,768,96]{1,2,0:T(8,128)(2,1)S(1)} %broadcast_in_dim_reshape_reshape.6), channel_id=1, source_target_pairs={{0,2},{1,3},{2,0},{3,1},{4,6},{5,7},{6,4},{7,5},{8,10},{9,11},{10,... | collective-permute-start | bytes 442376 | tf_op jit(solution)/shard_map/ppermute | solution.py:25
  64.1 8.3 %collective-permute-start.4 = (bf16[4,96,288]{2,1,0:T(8,128)(2,1)S(1)}, bf16[4,96,288]{2,1,0:T(8,128)(2,1)S(1)}, u32[]{:S(2)}, u32[]{:S(2)}) collective-permute-start(bf16[4,96,288]{2,1,0:T(8,128)(2,1)S(1)} %bitcast.258), channel_id=1, source_target_pairs={{0,4},{4,0},{8,12},{12,8},{16,20},{20,16},{24,28},{28,24},{1,5},{5... | collective-permute-start | bytes 663560 | tf_op jit(solution)/shard_map/ppermute | solution.py:25
  68.7 27.5 %collective-permute-start.13 = (bf16[2,768,96]{1,2,0:T(8,128)(2,1)}, bf16[2,768,96]{1,2,0:T(8,128)(2,1)}, u32[]{:S(2)}, u32[]{:S(2)}) collective-permute-start(bf16[2,768,96]{1,2,0:T(8,128)(2,1)} %maximum_bitcast_fusion.2), channel_id=1, source_target_pairs={{0,1},{1,0},{2,3},{3,2},{4,5},{5,4},{6,7},{7,6},{8,9},{9,8},{10,11... | collective-permute-start | bytes 884744 | tf_op jit(solution)/shard_map/ppermute | solution.py:25
  78.6 11.9 %all-to-all-start.1 = ((f32[32,2,96]{2,1,0:T(2,128)}), f32[32,2,96]{2,1,0:T(2,128)}, u32[]{:S(2)}, u32[]{:S(2)}) async-start(f32[32,2,96]{2,1,0:T(2,128)} %broadcast_in_dim.19), calls=%async_computation.1 | async-start | bytes 65536 | tf_op jit(solution)/shard_map/all_to_all | solution.py:50
  86.4 8.5 %collective-permute-start.5 = (bf16[1,1042,96]{1,2,0:T(8,128)(2,1)}, bf16[1,1042,96]{1,2,0:T(8,128)(2,1)S(1)}, u32[]{:S(2)}, u32[]{:S(2)}) collective-permute-start(bf16[1,1042,96]{1,2,0:T(8,128)(2,1)} %fusion.72), channel_id=1, source_target_pairs={{0,2},{1,3},{2,0},{3,1},{4,6},{5,7},{6,4},{7,5},{8,10},{9,11},{10,... | collective-permute-start | bytes 600200 | tf_op jit(solution)/shard_map/ppermute | solution.py:25
  87.9 40.9 %collective-permute-start.14 = (bf16[1,768,288]{1,2,0:T(8,128)(2,1)}, bf16[1,768,288]{1,2,0:T(8,128)(2,1)}, u32[]{:S(2)}, u32[]{:S(2)}) collective-permute-start(bf16[1,768,288]{1,2,0:T(8,128)(2,1)} %broadcast_in_dim_reshape_reshape.7), channel_id=1, source_target_pairs={{0,2},{1,3},{2,0},{3,1},{4,6},{5,7},{6,4},{7,5},{8,10},{9,11},{10,... | collective-permute-start | bytes 1327112 | tf_op jit(solution)/shard_map/ppermute | solution.py:25
  96.1 1.9 %collective-permute-start.6 = (bf16[2,1042,96]{1,2,0:T(8,128)(2,1)S(1)}, bf16[2,1042,96]{1,2,0:T(8,128)(2,1)S(1)}, u32[]{:S(2)}, u32[]{:S(2)}) collective-permute-start(bf16[2,1042,96]{1,2,0:T(8,128)(2,1)S(1)} %maximum_bitcast_fusion.1), channel_id=1, source_target_pairs={{0,1},{1,0},{2,3},{3,2},{4,5},{5,4},{6,7},{7,6},{8,9},{9,8},{10,11... | collective-permute-start | bytes 1200392 | tf_op jit(solution)/shard_map/ppermute | solution.py:25
  106.0 12.2 %all-to-all-start.2 = ((f32[8,2,384]{2,1,0:T(2,128)}), f32[8,2,384]{2,1,0:T(2,128)S(1)}, u32[]{:S(2)}, u32[]{:S(2)}) async-start(f32[8,2,384]{2,1,0:T(2,128)} %broadcast_in_dim.22), calls=%async_computation.2 | async-start | bytes 49152 | tf_op jit(solution)/shard_map/all_to_all | solution.py:50
  128.3 8.0 %collective-permute-start.16 = (bf16[4,96,384]{2,1,0:T(8,128)(2,1)S(1)}, bf16[4,96,384]{2,1,0:T(8,128)(2,1)S(1)}, u32[]{:S(2)}, u32[]{:S(2)}) collective-permute-start(bf16[4,96,384]{2,1,0:T(8,128)(2,1)S(1)} %fusion.67), channel_id=1, source_target_pairs={{0,4},{4,0},{8,12},{12,8},{16,20},{20,16},{24,28},{28,24},{1,5},{5... | collective-permute-start | bytes 884744 | tf_op jit(solution)/shard_map/ppermute | solution.py:41
  130.3 18.6 %collective-permute-start.15 = (bf16[2,768,288]{1,2,0:T(8,128)(2,1)S(1)}, bf16[2,768,288]{1,2,0:T(8,128)(2,1)S(1)}, u32[]{:S(2)}, u32[]{:S(2)}) collective-permute-start(bf16[2,768,288]{1,2,0:T(8,128)(2,1)S(1)} %maximum_bitcast_fusion), channel_id=1, source_target_pairs={{0,1},{1,0},{2,3},{3,2},{4,5},{5,4},{6,7},{7,6},{8,9},{9,8},{10,11... | collective-permute-start | bytes 2654216 | tf_op jit(solution)/shard_map/ppermute | solution.py:25
  136.5 5.2 %collective-permute-start.17 = (bf16[2,96,384]{2,1,0:T(8,128)(2,1)S(1)}, bf16[2,96,384]{2,1,0:T(8,128)(2,1)S(1)}, u32[]{:S(2)}, u32[]{:S(2)}) collective-permute-start(bf16[2,96,384]{2,1,0:T(8,128)(2,1)S(1)} %fusion.74), channel_id=1, source_target_pairs={{0,8},{4,12},{8,0},{12,4},{16,24},{20,28},{24,16},{28,20},{1,9},{5... | collective-permute-start | bytes 442376 | tf_op jit(solution)/shard_map/ppermute | solution.py:41
  141.8 6.1 %collective-permute-start.18 = (bf16[1,96,384]{2,1,0:T(8,128)(2,1)S(1)}, bf16[1,96,384]{2,1,0:T(8,128)(2,1)S(1)}, u32[]{:S(2)}, u32[]{:S(2)}) collective-permute-start(bf16[1,96,384]{2,1,0:T(8,128)(2,1)S(1)} %fusion.77), channel_id=1, source_target_pairs={{0,16},{4,20},{8,24},{12,28},{16,0},{20,4},{24,8},{28,12},{1,17},{... | collective-permute-start | bytes 221192 | tf_op jit(solution)/shard_map/ppermute | solution.py:41
  153.8 9.9 %copy-start.25 = (f32[96,96]{0,1:T(8,128)S(1)}, f32[96,96]{0,1:T(8,128)}, u32[]{:S(2)}) copy-start(f32[96,96]{0,1:T(8,128)} %copy.169) | copy-start | bytes 110596
  153.8 9.9 %copy-start.26 = (f32[96,96]{0,1:T(8,128)S(1)}, f32[96,96]{0,1:T(8,128)}, u32[]{:S(2)}) copy-start(f32[96,96]{0,1:T(8,128)} %copy.170) | copy-start | bytes 110596
  153.8 16.8 %copy-start.46 = (f32[2,768]{1,0:T(2,128)S(1)}, f32[2,768]{1,0:T(2,128)}, u32[]{:S(2)}) copy-start(f32[2,768]{1,0:T(2,128)} %param.24) | copy-start | bytes 18436
  159.1 11.5 %all-to-all-start.3 = ((f32[8,2,768]{2,1,0:T(2,128)}), f32[8,2,768]{2,1,0:T(2,128)S(1)}, u32[]{:S(2)}, u32[]{:S(2)}) async-start(f32[8,2,768]{2,1,0:T(2,128)} %broadcast_in_dim.23), calls=%async_computation.3 | async-start | bytes 98304 | tf_op jit(solution)/shard_map/all_to_all | solution.py:50
  (46 other events, 204.9 us)

commit v2 on v0

v2 whole, which is shorter than its diff:
```python
import functools

import jax
import jax.numpy as jnp
from jax import lax
from jax.experimental import pallas as pl
from jax.experimental.pallas import tpu as pltpu
from jax.sharding import PartitionSpec as P

KERNEL_WIDTH = 3
DILATION_BINS = 9
WIN = 1024
STEP = 10

NORM_EPS = 1e-05
ADAM_EPS = 1e-08
BETA_ONE = 0.9
BETA_TWO = 0.999
RATE_WEIGHT = 0.05
RATE_NORM = 0.5
DECAY_WEIGHT = 0.01

LANES = 128
EDGE = 16
RIM = 2 * EDGE
GELU_A = 0.7978845608028654
GELU_B = 0.044715
SHIFTS = [(j - KERNEL_WIDTH // 2) * DILATION_BINS for j in range(KERNEL_WIDTH)]
ROW_DIMS = (((0,), (0,)), ((), ()))
LANE_DIMS = (((1,), (1,)), ((), ()))
F32, BF16 = jnp.float32, jnp.bfloat16


def call(body, outs, args, scratch=(), smem=(), flops=0, limit=24):
    spaces = [pltpu.SMEM if k in smem else pltpu.VMEM for k in range(len(args))]
    size = lambda a: a.size * a.dtype.itemsize
    return pl.pallas_call(
        body,
        out_shape=[jax.ShapeDtypeStruct(s, t) for s, t in outs],
        in_specs=[pl.BlockSpec(memory_space=s) for s in spaces],
        out_specs=[pl.BlockSpec(memory_space=pltpu.VMEM) for _ in outs],
        scratch_shapes=[pltpu.VMEM(s, t) for s, t in scratch],
        compiler_params=pltpu.CompilerParams(vmem_limit_bytes=limit * 2**20),
        cost_estimate=pl.CostEstimate(
            flops=flops, bytes_accessed=sum(size(a) for a in args), transcendentals=0
        ),
    )(*args)


def up_to(size, step):
    return -(-size // step) * step


def split_three(v):
    high = v.astype(BF16).astype(F32)
    rest = v - high
    middle = rest.astype(BF16).astype(F32)
    return high, middle, rest - middle


def gelu_and_slope(v):
    square = v * v
    t = jnp.tanh(v * (GELU_A + (GELU_A * GELU_B) * square))
    half = 0.5 * (1.0 + t)
    slope = half + (0.5 * v) * (1.0 - t * t) * (GELU_A + (3.0 * GELU_A * GELU_B) * square)
    return v * half, slope


def reach_of(first, count, shift, start, bin_count):
    here = first + lax.broadcasted_iota(jnp.int32, (count, LANES), 0)
    there = here + shift
    inside = (here >= 0) & (here < bin_count) & (there >= 0) & (there < bin_count)
    return inside & (((here - start) >> 10) == ((there - start) >> 10))


def pack_kernel(conv_ref, out_ref):
    depth, slim = conv_ref.shape[1:]
    out_ref[...] = jnp.zeros_like(out_ref)
    for j in range(KERNEL_WIDTH):
        out_ref[:depth, j * LANES : j * LANES + slim] = conv_ref[j].astype(BF16)


def stats_kernel(x_ref, head_ref, tail_ref, point_ref, sent_ref, last_ref, first_ref, sum_ref):
    rows, width = x_ref.shape
    tiles = width // LANES
    slim, depth = point_ref.shape

    def step(k, carry):
        v = x_ref[pl.ds(pl.multiple_of(k * 32, 32), 32), :].astype(F32)
        v = v.reshape(4, 8, width)
        return carry[0] + v.sum(0), carry[1] + (v * v).sum(0)

    zero = jnp.zeros((8, width), F32)
    one, two = lax.fori_loop(0, rows // 32, step, (zero, zero), unroll=4)
    sum_ref[...] = jnp.zeros_like(sum_ref)
    for stat, total in enumerate((one, two)):
        parts = split_three(jnp.sum(total, 0, keepdims=True))
        for k in range(tiles):
            for p, part in enumerate(parts):
                row = p * 2 * tiles + stat * tiles + k
                sum_ref[row : row + 1, :] = part[:, k * LANES : (k + 1) * LANES]
    base = sent_ref.shape[1] - sum_ref.shape[0]
    sent_ref[...] = jnp.zeros_like(sent_ref)
    turned = point_ref[...].T.astype(BF16)
    sums = sum_ref[...].astype(BF16)
    for d in range(sent_ref.shape[0]):
        sent_ref[d, :depth, :slim] = turned
        sent_ref[d, base:, :] = sums
    last_ref[:RIM, :] = x_ref[rows - RIM :, :]
    last_ref[RIM:, :] = tail_ref[...]
    first_ref[:RIM, :] = x_ref[:RIM, :]
    first_ref[RIM:, :] = head_ref[...]


def act_kernel(x_ref, before_ref, after_ref, got_ref, norm_ref, hid_ref, slope_ref, vec_ref, point_ref, *, bin_count, depth):
    rows, width = x_ref.shape
    tiles = width // LANES
    count, height = got_ref.shape[:2]
    area = up_to(6 * tiles, 16)
    total = got_ref[0, height - area :, :].astype(F32)
    for d in range(1, count):
        total = total + got_ref[d, height - area :, :].astype(F32)
    total = total[: 2 * tiles] + total[2 * tiles : 4 * tiles] + total[4 * tiles : 6 * tiles]
    for d in range(count):
        point_ref[d] = got_ref[d, :depth, :]
    for k in range(tiles):
        lanes = slice(k * LANES, (k + 1) * LANES)
        mean = total[k : k + 1] / bin_count
        square = total[tiles + k : tiles + k + 1] / bin_count
        root = lax.rsqrt(square - mean * mean + NORM_EPS)
        gain = root * norm_ref[0:1, lanes]
        vec_ref[0:1, lanes] = root
        vec_ref[1:2, lanes] = -mean * root
        vec_ref[2:3, lanes] = gain
        vec_ref[3:4, lanes] = norm_ref[1:2, lanes] - mean * gain

    gain, bias = vec_ref[2:3, :], vec_ref[3:4, :]
    for src, at in ((before_ref, 0), (after_ref, RIM + rows)):
        for k in range(0, RIM, 16):
            hidden, _ = gelu_and_slope(src[k : k + 16, :].astype(F32) * gain + bias)
            hid_ref[at + k : at + k + 16, :] = hidden.astype(BF16)

    def step(k, carry):
        at = pl.multiple_of(k * 16, 16)
        v = x_ref[pl.ds(at, 16), :].astype(F32) * vec_ref[2:3, :] + vec_ref[3:4, :]
        hidden, slope = gelu_and_slope(v)
        hid_ref[pl.ds(pl.multiple_of(at + RIM, 16), 16), :] = hidden.astype(BF16)
        slope_ref[pl.ds(at, 16), :] = slope
        return carry

    lax.fori_loop(0, rows // 16, step, 0, unroll=2)


def conv_kernel(start_ref, hid_ref, *refs, relatives, bin_count):
    pieces, (norm_ref, weight_ref, rest_ref, sent_ref, stack, prod, out) = refs[:-7], refs[-7:]
    width = hid_ref.shape[1]
    rows = hid_ref.shape[0] - 2 * RIM
    slim = norm_ref.shape[1]
    own = lax.axis_index("seq")
    at = 0
    for piece in pieces:
        for k in range(piece.shape[0]):
            stack[own ^ relatives[at]] = piece[k].astype(stack.dtype)
            at += 1
    weight_ref[...] = stack[...].reshape(width, -1).astype(BF16)
    chunk = (rows + 2 * RIM) // 4
    for k in range(4):
        prod[k * chunk : (k + 1) * chunk, :] = jnp.dot(
            hid_ref[k * chunk : (k + 1) * chunk, :], weight_ref[...], preferred_element_type=F32
        )
    first = own * rows
    start = start_ref[0]

    def rows_of(begin, count):
        value = 0.0
        for j, shift in enumerate(SHIFTS):
            part = prod[begin + EDGE + shift : begin + EDGE + shift + count, j * LANES : (j + 1) * LANES]
            mask = reach_of(first + begin - EDGE, count, shift, start, bin_count)
            value = value + jnp.where(mask, part, 0.0)
        out[begin : begin + count, :] = value
        return value

    rows_of(0, EDGE)
    rows_of(EDGE + rows, EDGE)
    one = two = jnp.zeros((8, LANES), F32)
    step = 128
    for k in range(rows // step):
        value = rows_of(EDGE + k * step, step).reshape(step // 8, 8, LANES)
        one = one + value.sum(0)
        two = two + (value * value).sum(0)
    one, two = jnp.sum(one, 0, keepdims=True), jnp.sum(two, 0, keepdims=True)
    sent_ref[...] = jnp.zeros_like(sent_ref)
    for d in range(sent_ref.shape[0]):
        sent_ref[d, 0:1, :] = one
        sent_ref[d, 1:2, :] = two
        sent_ref[d, 2:4, :slim] = norm_ref[...]
    mean = one / rows
    rest_ref[...] = (out[...] - mean).astype(BF16)


def upstream_kernel(cot_ref, before_ref, after_ref, *refs):
    pieces, (up_ref, point_ref) = refs[:-2], refs[-2:]
    rows, width = cot_ref.shape
    at = 0
    for piece in pieces:
        for k in range(piece.shape[0]):
            point_ref[:, at * LANES : (at + 1) * LANES] = piece[k]
            at += 1
    point = point_ref[...]
    up_ref[:EDGE, :] = jnp.dot(before_ref[RIM:, :], point, preferred_element_type=F32)
    up_ref[EDGE + rows :, :] = jnp.dot(after_ref[RIM:, :], point, preferred_element_type=F32)
    chunk = rows // 4
    for k in range(4):
        up_ref[EDGE + k * chunk : EDGE + (k + 1) * chunk, :] = jnp.dot(
            cot_ref[k * chunk : (k + 1) * chunk, :], point, preferred_element_type=F32
        )


def mid_kernel(got_ref, up_ref, *refs, relatives, bin_count, seq_size):
    pieces, (hid_ref, d_ref, sent_ref, vec_ref) = refs[:-4], refs[-4:]
    rows = hid_ref.shape[0]
    ch_size = len(relatives)
    own_seq, own_ch = lax.axis_index("seq"), lax.axis_index("ch")
    blocks = [(piece, k) for piece in pieces for k in range(piece.shape[0])]
    for r, (piece, k) in enumerate(blocks):
        lanes = slice(r * LANES, (r + 1) * LANES)
        q = own_ch ^ relatives[r]
        total = got_ref[q]
        for s in range(1, seq_size):
            total = total + got_ref[s * ch_size + q]
        mine = got_ref[own_seq * ch_size + q]
        mean = total[0:1] / bin_count
        root = lax.rsqrt(total[1:2] / bin_count - mean * mean + NORM_EPS)
        offset = (mine[0:1] / rows - mean) * root
        gain, bias = mine[2:3], mine[3:4]
        vec_ref[0:1, lanes] = root
        vec_ref[1:2, lanes] = offset
        vec_ref[2:3, lanes] = gain
        vec_ref[3:4, lanes] = bias

        def rows_of(begin, count):
            centered = piece[k, pl.ds(begin, count), :].astype(F32) * root + offset
            hidden, slope = gelu_and_slope(centered * gain + bias)
            d = up_ref[pl.ds(begin, count), lanes] * slope
            d_ref[pl.ds(begin, count), lanes] = d
            return centered, hidden, d

        rows_of(0, EDGE)
        rows_of(EDGE + rows, EDGE)
        step = 64

        def body(i, carry):
            begin = pl.multiple_of(EDGE + i * step, 16)
            centered, hidden, d = rows_of(begin, step)
            hid_ref[pl.ds(pl.multiple_of(i * step, 16), step), lanes] = hidden.astype(BF16)
            d = d.reshape(step // 8, 8, LANES)
            return carry[0] + (d * centered.reshape(d.shape)).sum(0), carry[1] + d.sum(0)

        zero = jnp.zeros((8, LANES), F32)
        gain_sum, bias_sum = lax.fori_loop(0, rows // step, body, (zero, zero))
        gain_sum = jnp.sum(gain_sum, 0, keepdims=True)
        bias_sum = jnp.sum(bias_sum, 0, keepdims=True)
        for d in range(seq_size):
            sent_ref[d, 0:1, lanes] = gain_sum
            sent_ref[d, 1:2, lanes] = bias_sum


def out_kernel(x_ref, cot_ref, hid_ref, point_ref, out_ref, grad_ref):
    rows = x_ref.shape[0]
    chunk = rows // 4
    point = point_ref[...]
    for k in range(4):
        part = slice(k * chunk, (k + 1) * chunk)
        branch = lax.dot_general(hid_ref[part, :], point, LANE_DIMS, preferred_element_type=F32)
        out_ref[part, :] = (x_ref[part, :].astype(F32) + branch).astype(BF16)
    grad_ref[...] = lax.dot_general(
        cot_ref[...], hid_ref[:, :LANES], ROW_DIMS, preferred_element_type=F32
    )


def weight_grad_kernel(start_ref, got_ref, vec_ref, d_ref, hid_ref, point_ref, *refs, bin_count, depth):
    pieces, (term_ref, kept_ref, sent_ref, total_ref, grad, full) = refs[:-6], refs[-6:]
    rows = term_ref.shape[0]
    blocks = [(piece, k) for piece in pieces for k in range(piece.shape[0])]
    own = lax.axis_index("seq")
    first = own * rows
    start = start_ref[0]
    total = got_ref[0]
    for s in range(1, got_ref.shape[0]):
        total = total + got_ref[s]
    total_ref[...] = total
    step = 64
    for r, (piece, k) in enumerate(blocks):
        lanes = slice(r * LANES, (r + 1) * LANES)
        root, offset, gain = vec_ref[0:1, lanes], vec_ref[1:2, lanes], vec_ref[2:3, lanes]
        scale = root * gain
        pull = scale * total[0:1, lanes] / bin_count
        slant = pull * root
        level = scale * total[1:2, lanes] / bin_count + pull * offset
        for begin in range(0, rows + RIM, 96):
            part = slice(begin, min(begin + 96, rows + RIM))
            rest = piece[k, part, :].astype(F32)
            grad[part, :] = d_ref[part, lanes] * scale - (rest * slant + level)
        for j, shift in enumerate(SHIFTS):
            at = (r * KERNEL_WIDTH + j) * LANES
            for begin in range(0, rows, step):
                mask = reach_of(first + begin - shift, step, shift, start, bin_count)
                value = grad[EDGE + begin - shift : EDGE + begin - shift + step, :]
                term_ref[begin : begin + step, at : at + LANES] = jnp.where(mask, value, 0.0).astype(BF16)
    wide = KERNEL_WIDTH * LANES
    full[:, :wide] = lax.dot_general(
        hid_ref[RIM : RIM + rows, :], term_ref[:, :wide], ROW_DIMS, preferred_element_type=F32
    )
    full[:, wide:] = point_ref[...]
    low = own % 2
    for k in range(kept_ref.shape[0]):
        kept_ref[k] = full[pl.ds(pl.multiple_of((2 * k + low) * depth, 8), depth), :]
        sent_ref[k] = full[pl.ds(pl.multiple_of((2 * k + 1 - low) * depth, 8), depth), :].astype(BF16)


def input_grad_kernel(x_ref, slope_ref, vec_ref, term_ref, weight_ref, d_ref, sent_ref):
    rows, width = x_ref.shape
    root, offset = vec_ref[0:1, :], vec_ref[1:2, :]
    one = two = jnp.zeros((8, width), F32)
    step = 128
    for k in range(rows // step):
        part = slice(k * step, (k + 1) * step)
        up = lax.dot_general(term_ref[part, :], weight_ref[...], LANE_DIMS, preferred_element_type=F32)
        d = up * slope_ref[part, :]
        d_ref[part, :] = d
        centered = x_ref[part, :].astype(F32) * root + offset
        one = one + (d * centered).reshape(step // 8, 8, width).sum(0)
        two = two + d.reshape(step // 8, 8, width).sum(0)
    one, two = jnp.sum(one, 0, keepdims=True), jnp.sum(two, 0, keepdims=True)
    for d in range(sent_ref.shape[0]):
        sent_ref[d, 0:1, :] = one
        sent_ref[d, 1:2, :] = two


def final_kernel(x_ref, cot_ref, d_ref, vec_ref, got_ref, out_ref, total_ref, *, bin_count):
    rows, width = x_ref.shape
    total = got_ref[0]
    for s in range(1, got_ref.shape[0]):
        total = total + got_ref[s]
    total_ref[...] = total
    root, offset, scale = vec_ref[0:1, :], vec_ref[1:2, :], vec_ref[2:3, :]
    pull = scale * total[0:1] / bin_count
    slant = pull * root
    level = scale * total[1:2] / bin_count + pull * offset
    step = 16

    def body(i, carry):
        at = pl.ds(pl.multiple_of(i * step, 16), step)
        value = x_ref[at, :].astype(F32) * slant + level
        out_ref[at, :] = cot_ref[at, :].astype(F32) + (d_ref[at, :] * scale - value)
        return carry

    lax.fori_loop(0, rows // step, body, 0, unroll=4)


def flip(axis, reach):
    return [(i, i ^ reach) for i in range(lax.axis_size(axis))]


def relatives_of(size):
    found, reach = [0], size // 2
    while reach:
        found, reach = found + [r ^ reach for r in found], reach // 2
    return found


def gather_pieces(x, axis):
    pieces, reach = [x[None]], lax.axis_size(axis) // 2
    while reach:
        held = pieces[0] if len(pieces) == 1 else jnp.concatenate(pieces)
        pieces.append(lax.ppermute(held, axis, flip(axis, reach)))
        reach //= 2
    return pieces


def spread(copies, axes):
    return lax.all_to_all(copies, axes, 0, 0, tiled=True)


def adamw(weights_old, first_moment_state, second_mom, gradient, step_rate, decay_rate):
    first_next = BETA_ONE * first_moment_state + (1.0 - BETA_ONE) * gradient
    second_next = BETA_TWO * second_mom + (1.0 - BETA_TWO) * gradient * gradient
    corrected = (
        first_next
        / (1.0 - BETA_ONE**STEP)
        / (jnp.sqrt(second_next / (1.0 - BETA_TWO**STEP)) + ADAM_EPS)
    )
    weights_new = weights_old - step_rate * (corrected + decay_rate * weights_old)
    return (first_next, second_next, weights_new)


def shards(
    inputs,
    cotangent,
    starts,
    master_conv,
    first_conv,
    second_conv,
    master_point,
    first_point,
    second_point,
    norm_in,
    first_in,
    second_in,
    norm_mid,
    first_mid,
    second_mid,
):
    rows, width = inputs.shape
    seq_size, ch_size = lax.axis_size("seq"), lax.axis_size("ch")
    bin_count = rows * seq_size
    depth, slim = master_conv.shape[1:]
    tiles = width // LANES
    wide = KERNEL_WIDTH * LANES
    seq_relatives, ch_relatives = relatives_of(seq_size), relatives_of(ch_size)
    mid = ch_size * LANES
    ext = rows + 2 * EDGE

    (conv_low,) = call(pack_kernel, [((depth, wide), BF16)], [master_conv])
    area = up_to(6 * tiles, 16)
    height = up_to(depth, 16) + area
    sent_in, last, first = call(
        stats_kernel,
        [((seq_size, height, LANES), BF16)] + [((RIM + EDGE, width), BF16)] * 2,
        [inputs, cotangent[:EDGE], cotangent[rows - EDGE :], master_point],
        scratch=[((area, LANES), F32)],
    )
    conv_pieces = gather_pieces(conv_low, "seq")
    got_in = spread(sent_in, "seq")
    up = [(i, i + 1) for i in range(seq_size - 1)]
    down = [(j, i) for i, j in up]
    before = lax.ppermute(last, "seq", up)
    after = lax.ppermute(first, "seq", down)
    hidden_in, slope_in, vec_in, point_own = call(
        functools.partial(act_kernel, bin_count=bin_count, depth=depth),
        [
            ((rows + 2 * RIM, width), BF16),
            ((rows, width), F32),
            ((8, width), F32),
            ((seq_size, depth, LANES), BF16),
        ],
        [inputs, before, after, got_in, norm_in],
        flops=40 * rows * width,
    )
    point_pieces = gather_pieces(point_own.reshape(width, LANES), "ch")

    stack_type = BF16 if depth % 16 == 0 else F32
    conv_own, rest, sent_mid = call(
        functools.partial(conv_kernel, relatives=seq_relatives, bin_count=bin_count),
        [
            ((width, wide), BF16),
            ((ext, LANES), BF16),
            ((seq_size * ch_size, 4, LANES), F32),
        ],
        [starts, hidden_in] + conv_pieces + [norm_mid],
        scratch=[
            ((seq_size, depth, wide), stack_type),
            ((rows + 2 * RIM, wide), F32),
            ((ext, LANES), F32),
        ],
        smem=(0,),
        flops=2 * rows * width * wide,
    )
    rest_pieces = gather_pieces(rest, "ch")
    got_mid = spread(sent_mid, ("seq", "ch"))
    upstream, point_all = call(
        upstream_kernel,
        [((ext, mid), F32), ((width, mid), BF16)],
        [cotangent, before, after] + point_pieces,
        flops=2 * rows * width * mid,
    )
    conv_all = jnp.concatenate(
        [piece[k] for piece in gather_pieces(conv_own, "ch") for k in range(piece.shape[0])], axis=1
    )
    hidden_mid, d_mid, sent_back, vec_mid = call(
        functools.partial(
            mid_kernel, relatives=ch_relatives, bin_count=bin_count, seq_size=seq_size
        ),
        [((rows, mid), BF16), ((ext, mid), F32), ((seq_size, 2, mid), F32), ((8, mid), F32)],
        [got_mid, upstream] + rest_pieces,
        flops=40 * rows * mid,
    )
    got_back = spread(sent_back, "seq")
    block_out, grad_point = call(
        out_kernel,
        [((rows, width), BF16), ((width, LANES), F32)],
        [inputs, cotangent, hidden_mid, point_all],
        flops=2 * rows * width * (mid + LANES),
    )
    terms, kept, sent, total_mid = call(
        functools.partial(weight_grad_kernel, bin_count=bin_count, depth=depth),
        [
            ((rows, ch_size * wide), BF16),
            ((seq_size // 2, depth, wide + LANES), F32),
            ((seq_size // 2, depth, wide + LANES), BF16),
            ((2, mid), F32),
        ],
        [starts, got_back, vec_mid, d_mid, hidden_in, grad_point] + rest_pieces,
        scratch=[((ext, LANES), F32), ((width, wide + LANES), F32)],
        smem=(0,),
        flops=2 * rows * width * wide,
    )
    d_in, sent_first = call(
        input_grad_kernel,
        [((rows, width), F32), ((seq_size, 2, width), F32)],
        [inputs, slope_in, vec_in, terms, conv_all],
        flops=2 * rows * width * ch_size * wide,
    )
    got_first = spread(sent_first, "seq")
    input_grad, total_in = call(
        functools.partial(final_kernel, bin_count=bin_count),
        [((rows, width), F32), ((2, width), F32)],
        [inputs, cotangent, d_in, vec_in, got_first],
        flops=10 * rows * width,
    )

    own = lax.axis_index("seq")
    reach = 1
    while True:
        got = lax.ppermute(sent, "seq", flip("seq", reach))
        blocks = kept + got.astype(F32)
        reach *= 2
        if reach == seq_size:
            break
        pairs = blocks.reshape((-1, 2) + blocks.shape[1:])
        high = (own // reach) % 2 == 1
        kept = jnp.where(high, pairs[:, 1], pairs[:, 0])
        sent = jnp.where(high, pairs[:, 0], pairs[:, 1]).astype(BF16)
    both = blocks[0]
    conv_sum = jnp.stack(
        [both[:, j * LANES : j * LANES + slim] for j in range(KERNEL_WIDTH)]
    )
    point_sum = both[:, wide : wide + slim].T

    conv_new = adamw(master_conv, first_conv, second_conv, conv_sum, RATE_WEIGHT, DECAY_WEIGHT)
    point_new = adamw(
        master_point, first_point, second_point, point_sum, RATE_WEIGHT, DECAY_WEIGHT
    )
    in_new = adamw(norm_in, first_in, second_in, total_in, RATE_NORM, 0.0)
    mid_new = adamw(norm_mid, first_mid, second_mid, total_mid[:, :slim], RATE_NORM, 0.0)
    return (block_out, input_grad) + conv_new + point_new + in_new + mid_new


def solution(mesh):
    in_specs = (
        P("seq", None),
        P("seq", None),
        P(),
        P(None, "seq", "ch"),
        P(None, "seq", "ch"),
        P(None, "seq", "ch"),
        P("ch", "seq"),
        P("ch", "seq"),
        P("ch", "seq"),
        P(),
        P(),
        P(),
        P(None, "ch"),
        P(None, "ch"),
        P(None, "ch"),
    )
    out_specs = (
        P("seq", None),
        P("seq", None),
        P(None, "seq", "ch"),
        P(None, "seq", "ch"),
        P(None, "seq", "ch"),
        P("ch", "seq"),
        P("ch", "seq"),
        P("ch", "seq"),
        P(),
        P(),
        P(),
        P(None, "ch"),
        P(None, "ch"),
        P(None, "ch"),
    )
    return jax.shard_map(shards, mesh=mesh, in_specs=in_specs, out_specs=out_specs, check_vma=False)
```

time: 327 us -> 173 us (0.53)
  blocking collectives: 144 us -> 0 us
  waiting for transfers between devices: 115 us -> 32.5 us
  local copies, waits for them, and re-layouts: 8.88 us -> 54.6 us
  starting transfers between devices: 8.71 us -> 42.8 us
  Pallas kernels: 0 us -> 28 us
  matrix products: 15.3 us -> 0 us
  between operations: 16 us -> 1.09 us
  other arithmetic: 19 us -> 12.5 us
    unnamed x5 -> x0, waiting for transfers between devices: 85.5 us -> none
    psum x4 -> x0, blocking collectives: 82.2 us -> none  [the longest x2 43.4 us: normalize(): lax.psum((jnp.sum(values, axis=0), jnp.sum(values * values, axis=0)), 'seq')]
    all_gather x2 -> x0, blocking collectives: 62.2 us -> none  [the longest x1 31.6 us: shards(): lax.all_gather(master_conv.astype(jnp.bfloat16), 'seq', axis=1, tiled=True)]
    unnamed x56 -> x140, local copies, waits for them, and re-layouts: 7.99 us -> 52.9 us
    ppermute x4 -> x14, waiting for transfers between devices: 0.58 us -> 32.3 us  [the longest x3 13.3 us: shards(): got = lax.ppermute(sent, 'seq', flip('seq', reach))]
    psum x1 -> x0, waiting for transfers between devices: 28.4 us -> none  [shards(): branch = lax.psum(partial_value, 'ch')]
    pallas_call x0 -> x10, Pallas kernels: none -> 28 us  [call(): pl.pallas_call(body, out_shape=[jax.ShapeDtypeStruct(s, t) for s, t in ou...]
    all_to_all x0 -> x4, starting transfers between devices: none -> 22.9 us  [spread(): return lax.all_to_all(copies, axes, 0, 0, tiled=True)]
  transfers between devices with their start and end apart: 7 -> 18, of which waited for: 4 -> 8; matrix products, arithmetic and copies ran while one was open for 6% -> 13% of each run, Pallas kernels for 0% -> 5%
where the time goes in v2:
time: 173 us; the launch traced here: 172 us
  local copies, waits for them, and re-layouts  54.6 us (32%)
  starting transfers between devices  42.8 us (25%)
  waiting for transfers between devices  32.5 us (19%)
  Pallas kernels  28 us (16%)
  other arithmetic  12.5 us (7%)
    unnamed x140, local copies, waits for them, and re-layouts  52.9 us
    pallas_call x10, Pallas kernels, call(): pl.pallas_call(body, out_shape=[jax.ShapeDtypeStruct(s, t) for s, t in ou...  28 us
    all_to_all x4, starting transfers between devices, spread(): return lax.all_to_all(copies, axes, 0, 0, tiled=True)  22.9 us
    ppermute x3, waiting for transfers between devices, shards(): got = lax.ppermute(sent, 'seq', flip('seq', reach))  13.3 us
    ppermute x9, waiting for transfers between devices, gather_pieces(): pieces.append(lax.ppermute(held, axis, flip(axis, reach)))  11.5 us
    ppermute x9, starting transfers between devices, gather_pieces(): pieces.append(lax.ppermute(held, axis, flip(axis, reach)))  10.5 us
    ppermute x1, waiting for transfers between devices, shards(): before = lax.ppermute(last, 'seq', up)  7.49 us
    ppermute x3, starting transfers between devices, shards(): got = lax.ppermute(sent, 'seq', flip('seq', reach))  6.15 us
  transfers between devices with their start and end apart: 18, of which 8 were waited for; matrix products, arithmetic and copies ran while one was open for 13% of the time, Pallas kernels for 5%

profile of v2, /device:TPU:0, one launch (start us, length us, event | category | flops | bytes accessed | tf_op | source)
XLA Modules:
  0.0 171.6 jit_solution(3895738355037985438)
XLA Ops:
  1.6 4.1 %collective-permute-start.2 = (bf16[1,96,384]{2,1,0:T(8,128)(2,1)S(1)}, bf16[1,96,384]{2,1,0:T(8,128)(2,1)S(1)}, u32[]{:S(2)}, u32[]{:S(2)}) collective-permute-start(bf16[1,96,384]{2,1,0:T(8,128)(2,1)S(1)} %bitcast.46), channel_id=1, source_target_pairs={{0,16},{4,20},{8,24},{12,28},{16,0},{20,4},{24,8},{28,12},{1,17},{... | collective-permute-start | bytes 221192 | tf_op jit(solution)/shard_map/ppermute | solution.py:376
  5.7 3.9 %collective-permute-done.2.refs_1_ = bf16[1,96,384]{2,1,0:T(8,128)(2,1)S(1)} collective-permute-done((bf16[1,96,384]{2,1,0:T(8,128)(2,1)S(1)}, bf16[1,96,384]{2,1,0:T(8,128)(2,1)S(1)}, u32[]{:S(2)}, u32[]{:S(2)}) %collective-permute-start.2) | collective-permute-done | bytes 73760 | tf_op jit(solution)/shard_map/ppermute | solution.py:376
  14.5 5.6 %all-to-all-start = ((bf16[8,144,128]{2,1,0:T(8,128)(2,1)}), bf16[8,144,128]{2,1,0:T(8,128)(2,1)S(1)}, u32[]{:S(2)}, u32[]{:S(2)}) async-start(bf16[8,144,128]{2,1,0:T(8,128)(2,1)} %get-tuple-element.42), calls=%async_computation | async-start | bytes 589824 | tf_op jit(solution)/shard_map/all_to_all | solution.py:382
  20.9 2.0 %collective-permute-start.4 = (bf16[4,96,384]{2,1,0:T(8,128)(2,1)}, bf16[4,96,384]{2,1,0:T(8,128)(2,1)}, u32[]{:S(2)}, u32[]{:S(2)}) collective-permute-start(bf16[4,96,384]{2,1,0:T(8,128)(2,1)} %pad_maximum_fusion.4), channel_id=1, source_target_pairs={{0,4},{4,0},{8,12},{12,8},{16,20},{20,16},{24,28},{28,24},{1,5},{5... | collective-permute-start | bytes 884744 | tf_op jit(solution)/shard_map/ppermute | solution.py:376
  22.9 1.9 %collective-permute-start = (bf16[48,768]{1,0:T(8,128)(2,1)S(1)}, bf16[48,768]{1,0:T(8,128)(2,1)S(1)}, u32[]{:S(2)}, u32[]{:S(2)}) collective-permute-start(bf16[48,768]{1,0:T(8,128)(2,1)S(1)} %get-tuple-element.40), channel_id=1, source_target_pairs={{0,4},{4,8},{8,12},{12,16},{16,20},{20,24},{24,28},{1,5},{5,9},{9,... | collective-permute-start | bytes 221192 | tf_op jit(solution)/shard_map/ppermute | solution.py:437
  26.1 7.5 %collective-permute-done.before_ref = bf16[48,768]{1,0:T(8,128)(2,1)S(1)} collective-permute-done((bf16[48,768]{1,0:T(8,128)(2,1)S(1)}, bf16[48,768]{1,0:T(8,128)(2,1)S(1)}, u32[]{:S(2)}, u32[]{:S(2)}) %collective-permute-start) | collective-permute-done | bytes 73760 | tf_op jit(solution)/shard_map/ppermute | solution.py:437
  36.7 2.4 %shard_map.255 = (bf16[1088,768]{1,0:T(8,128)(2,1)S(1)}, f32[1024,768]{1,0:T(8,128)S(1)}, f32[8,768]{1,0:T(8,128)S(1)}, bf16[8,96,128]{2,1,0:T(8,128)(2,1)S(1)}) custom-call(bf16[1024,768]{1,0:T(8,128)(2,1)S(1)} %copy-done.1, bf16[48,768]{1,0:T(8,128)(2,1)S(1)} %copy-done.44, bf16[48,768]{1,0:T(8,128)(2,1)S(1)} %copy-done.47, ...), custom_call_target="tpu_custom_call" | custom-call | flops 31457280 | bytes 2021376 | tf_op jit(solution)/shard_map/pallas_call | solution.py:37
  39.1 1.7 copy-done.7
  43.5 2.6 %shard_map.257 = (bf16[768,384]{1,0:T(8,128)(2,1)S(1)}, bf16[1056,128]{1,0:T(8,128)(2,1)S(1)}, f32[32,4,128]{2,1,0:T(4,128)S(1)}) custom-call(s32[8]{0:T(128)S(1)} %copy-done.56, bf16[1088,768]{1,0:T(8,128)(2,1)S(1)} %get-tuple-element.43.hid_ref, bf16[1,96,384]{2,1,0:T(8,128)(2,1)S(1)} %bitcast.49, bf16[1,96,384]{2,1,0:T(8,128)(2,1)S(1)} %copy-done.28, ...), custom_call_target="tpu_custom_call" | custom-call | flops 603979776 | bytes 2261792 | tf_op jit(solution)/shard_map/pallas_call | solution.py:37
  48.2 7.0 %collective-permute-done.7.refs_1_ = bf16[1,1056,128]{2,1,0:T(8,128)(2,1)S(1)} collective-permute-done((bf16[1,1056,128]{2,1,0:T(8,128)(2,1)S(1)}, bf16[1,1056,128]{2,1,0:T(8,128)(2,1)S(1)}, u32[]{:S(2)}, u32[]{:S(2)}) %collective-permute-start.7) | collective-permute-done | bytes 270368 | tf_op jit(solution)/shard_map/ppermute | solution.py:376
  58.2 6.8 %all-to-all-start.1 = ((f32[32,4,128]{2,1,0:T(4,128)}), f32[32,4,128]{2,1,0:T(4,128)}, u32[]{:S(2)}, u32[]{:S(2)}) async-start(f32[32,4,128]{2,1,0:T(4,128)} %copy-done.49), calls=%async_computation.1 | async-start | bytes 131072 | tf_op jit(solution)/shard_map/all_to_all | solution.py:382
  70.1 2.3 %shard_map.258 = (f32[1056,512]{1,0:T(8,128)S(1)}, bf16[768,512]{1,0:T(8,128)(2,1)S(1)}) custom-call(bf16[1024,768]{1,0:T(8,128)(2,1)S(1)} %copy-done.2, bf16[48,768]{1,0:T(8,128)(2,1)S(1)} %copy-done.45, bf16[48,768]{1,0:T(8,128)(2,1)S(1)} %copy-done.48, bf16[1,768,128]{2,1,0:T(8,128)(2,1)S(1)} %bitcast.52, bf16[1,768,128]{2,1,0:T(8,128)(2,1)S(1)} %copy-done.40, ...), custom_call_target="tpu_custom_call" | custom-call | flops 805306368 | bytes 2506752 | tf_op jit(solution)/shard_map/pallas_call | solution.py:37
  77.1 3.7 %shard_map.259 = (bf16[1024,512]{1,0:T(8,128)(2,1)S(1)}, f32[1056,512]{1,0:T(8,128)S(1)}, f32[8,2,512]{2,1,0:T(2,128)S(1)}, f32[8,512]{1,0:T(8,128)S(1)}) custom-call(f32[32,4,128]{2,1,0:T(4,128)} %all-to-all-done.1.got_ref, f32[1056,512]{1,0:T(8,128)S(1)} %copy-done.17, bf16[1,1056,128]{2,1,0:T(8,128)(2,1)S(1)} %bitcast.42, ...), custom_call_target="tpu_custom_call" | custom-call | flops 20971520 | bytes 3309568 | tf_op jit(solution)/shard_map/pallas_call | solution.py:37
  84.3 5.7 %all-to-all-start.2 = ((f32[8,2,512]{2,1,0:T(2,128)}), f32[8,2,512]{2,1,0:T(2,128)S(1)}, u32[]{:S(2)}, u32[]{:S(2)}) async-start(f32[8,2,512]{2,1,0:T(2,128)} %copy-done.50), calls=%async_computation.2 | async-start | bytes 65536 | tf_op jit(solution)/shard_map/all_to_all | solution.py:382
  93.8 2.2 %shard_map.260 = (bf16[1024,768]{1,0:T(8,128)(2,1)}, f32[768,128]{1,0:T(8,128)S(1)}) custom-call(bf16[1024,768]{1,0:T(8,128)(2,1)S(1)} %copy-done.1, bf16[1024,768]{1,0:T(8,128)(2,1)S(1)} %copy-done.3, bf16[1024,512]{1,0:T(8,128)(2,1)S(1)} %copy-done.23, bf16[768,512]{1,0:T(8,128)(2,1)S(1)} %copy-done.25), custom_call_target="tpu_custom_call" | custom-call | flops 1006632960 | bytes 4980736 | tf_op jit(solution)/shard_map/pallas_call | solution.py:37
  101.7 4.1 %shard_map.261 = (bf16[1024,1536]{1,0:T(8,128)(2,1)S(1)}, f32[4,96,512]{2,1,0:T(8,128)S(1)}, bf16[4,96,512]{2,1,0:T(8,128)(2,1)}, f32[2,512]{1,0:T(2,128)S(1)}) custom-call(s32[8]{0:T(128)S(1)} %copy-done.57, f32[8,2,512]{2,1,0:T(2,128)S(1)} %all-to-all-done.2.got_ref, f32[8,512]{1,0:T(8,128)S(1)} %copy-done.53, f32[1056,512]{1,0:T(8,128)S(1)} %copy-done.19, ...), custom_call_target="tpu_custom_call" | custom-call | flops 603979776 | bytes 5357600 | tf_op jit(solution)/shard_map/pallas_call | solution.py:37
  105.8 1.7 copy-done.9
  109.0 2.0 %collective-permute-start.11 = (bf16[4,96,512]{2,1,0:T(8,128)(2,1)}, bf16[4,96,512]{2,1,0:T(8,128)(2,1)S(1)}, u32[]{:S(2)}, u32[]{:S(2)}) collective-permute-start(bf16[4,96,512]{2,1,0:T(8,128)(2,1)} %get-tuple-element.63), channel_id=1, source_target_pairs={{0,4},{4,0},{8,12},{12,8},{16,20},{20,16},{24,28},{28,24},{1,5},{5... | collective-permute-start | bytes 1179656 | tf_op jit(solution)/shard_map/ppermute | solution.py:525
  112.5 7.6 %collective-permute-done.11 = bf16[4,96,512]{2,1,0:T(8,128)(2,1)S(1)} collective-permute-done((bf16[4,96,512]{2,1,0:T(8,128)(2,1)}, bf16[4,96,512]{2,1,0:T(8,128)(2,1)S(1)}, u32[]{:S(2)}, u32[]{:S(2)}) %collective-permute-start.11) | collective-permute-done | bytes 393248 | tf_op jit(solution)/shard_map/ppermute | solution.py:525
  124.4 1.7 %collective-permute-start.12 = (bf16[2,96,512]{1,2,0:T(8,128)(2,1)}, bf16[2,96,512]{1,2,0:T(8,128)(2,1)}, u32[]{:S(2)}, u32[]{:S(2)}) collective-permute-start(bf16[2,96,512]{1,2,0:T(8,128)(2,1)} %fusion.1), channel_id=1, source_target_pairs={{0,8},{4,12},{8,0},{12,4},{16,24},{20,28},{24,16},{28,20},{1,9},{5... | collective-permute-start | bytes 589832 | tf_op jit(solution)/shard_map/ppermute | solution.py:525
  126.9 1.7 copy.32
  128.6 1.7 copy.29
  133.0 2.4 %collective-permute-start.13 = (bf16[1,96,512]{1,2,0:T(8,128)(2,1)S(1)}, bf16[1,96,512]{1,2,0:T(8,128)(2,1)S(1)}, u32[]{:S(2)}, u32[]{:S(2)}) collective-permute-start(bf16[1,96,512]{1,2,0:T(8,128)(2,1)S(1)} %fusion.4), channel_id=1, source_target_pairs={{0,16},{4,20},{8,24},{12,28},{16,0},{20,4},{24,8},{28,12},{1,17},{... | collective-permute-start | bytes 294920 | tf_op jit(solution)/shard_map/ppermute | solution.py:525
  136.7 5.4 %collective-permute-done.13 = bf16[1,96,512]{1,2,0:T(8,128)(2,1)S(1)} collective-permute-done((bf16[1,96,512]{1,2,0:T(8,128)(2,1)S(1)}, bf16[1,96,512]{1,2,0:T(8,128)(2,1)S(1)}, u32[]{:S(2)}, u32[]{:S(2)}) %collective-permute-start.13) | collective-permute-done | bytes 98336 | tf_op jit(solution)/shard_map/ppermute | solution.py:525
  146.2 6.9 %shard_map.262 = (f32[1024,768]{1,0:T(8,128)S(1)}, f32[8,2,768]{2,1,0:T(2,128)}) custom-call(bf16[1024,768]{1,0:T(8,128)(2,1)S(1)} %copy-done.1, f32[1024,768]{1,0:T(8,128)S(1)} %copy-done.8, f32[8,768]{1,0:T(8,128)S(1)} %copy-done.42, bf16[1024,1536]{1,0:T(8,128)(2,1)S(1)} %copy-done.10, bf16[768,1536]{1,0:T(8,128)(2,1)S(1)} %pad_maximum_fusion.weight_ref), custom_call_target="tpu_custom_call" | custom-call | flops 2415919104 | bytes 10248192 | tf_op jit(solution)/shard_map/pallas_call | solution.py:37
  153.1 1.7 copy-done.5
  154.8 4.8 %all-to-all-start.3 = ((f32[8,2,768]{2,1,0:T(2,128)}), f32[8,2,768]{2,1,0:T(2,128)S(1)}, u32[]{:S(2)}, u32[]{:S(2)}) async-start(f32[8,2,768]{2,1,0:T(2,128)} %get-tuple-element.60), calls=%async_computation.3 | async-start | bytes 98304 | tf_op jit(solution)/shard_map/all_to_all | solution.py:382
  161.1 1.7 copy.35
  162.8 1.7 copy.36
  164.5 1.7 copy.37
  166.4 1.9 %copy-done.6 = f32[1024,768]{1,0:T(8,128)S(1)} copy-done((f32[1024,768]{1,0:T(8,128)S(1)}, f32[1024,768]{1,0:T(8,128)}, u32[]{:S(2)}) %copy-start.6) | copy-done | bytes 3145752
  168.3 2.7 %shard_map.263 = (f32[1024,768]{1,0:T(8,128)}, f32[2,768]{1,0:T(2,128)S(1)}) custom-call(bf16[1024,768]{1,0:T(8,128)(2,1)S(1)} %copy-done.1, bf16[1024,768]{1,0:T(8,128)(2,1)S(1)} %copy-done.4, f32[1024,768]{1,0:T(8,128)S(1)} %copy-done.6, f32[8,768]{1,0:T(8,128)S(1)} %copy-done.42, f32[8,2,768]{2,1,0:T(2,128)S(1)} %all-to-all-done.3.got_ref), custom_call_target="tpu_custom_call" | custom-call | flops 7864320 | bytes 6365184 | tf_op jit(solution)/shard_map/pallas_call | solution.py:37
  (173 shorter events, 59.9 us)
Async XLA Ops:
  1.6 33.4 %copy-start.51 = (f32[2,768]{1,0:T(2,128)S(1)}, f32[2,768]{1,0:T(2,128)}, u32[]{:S(2)}) copy-start(f32[2,768]{1,0:T(2,128)} %norm_ref.1) | copy-start | bytes 18436
  1.6 32.7 %copy-start.20 = (bf16[96,384]{1,0:T(8,128)(2,1)}, bf16[96,384]{1,0:T(8,128)(2,1)S(1)}, u32[]{:S(2)}) copy-start(bf16[96,384]{1,0:T(8,128)(2,1)S(1)} %shard_map.256) | copy-start | bytes 221188
  1.6 8.0 %collective-permute-start.2 = (bf16[1,96,384]{2,1,0:T(8,128)(2,1)S(1)}, bf16[1,96,384]{2,1,0:T(8,128)(2,1)S(1)}, u32[]{:S(2)}, u32[]{:S(2)}) collective-permute-start(bf16[1,96,384]{2,1,0:T(8,128)(2,1)S(1)} %bitcast.46), channel_id=1, source_target_pairs={{0,16},{4,20},{8,24},{12,28},{16,0},{20,4},{24,8},{28,12},{1,17},{... | collective-permute-start | bytes 221192 | tf_op jit(solution)/shard_map/ppermute | solution.py:376
  9.6 24.7 %copy-start.27 = (bf16[1,96,384]{2,1,0:T(8,128)(2,1)}, bf16[1,96,384]{2,1,0:T(8,128)(2,1)S(1)}, u32[]{:S(2)}) copy-start(bf16[1,96,384]{2,1,0:T(8,128)(2,1)S(1)} %collective-permute-done.2.refs_1_) | copy-start | bytes 221188
  9.6 10.5 %collective-permute-start.3 = (bf16[2,96,384]{2,1,0:T(8,128)(2,1)S(1)}, bf16[2,96,384]{2,1,0:T(8,128)(2,1)S(1)}, u32[]{:S(2)}, u32[]{:S(2)}) collective-permute-start(bf16[2,96,384]{2,1,0:T(8,128)(2,1)S(1)} %pad_maximum_fusion.5), channel_id=1, source_target_pairs={{0,8},{4,12},{8,0},{12,4},{16,24},{20,28},{24,16},{28,20},{1,9},{5... | collective-permute-start | bytes 442376 | tf_op jit(solution)/shard_map/ppermute | solution.py:376
  13.3 21.6 %copy-start.1 = (bf16[1024,768]{1,0:T(8,128)(2,1)S(1)}, bf16[1024,768]{1,0:T(8,128)(2,1)}, u32[]{:S(2)}) copy-start(bf16[1024,768]{1,0:T(8,128)(2,1)} %x_ref.9) | copy-start | bytes 4718596
  13.3 27.5 %copy-start.54 = (f32[2,96]{1,0:T(2,128)S(1)}, f32[2,96]{1,0:T(2,128)}, u32[]{:S(2)}) copy-start(f32[2,96]{1,0:T(2,128)} %refs_4_.1) | copy-start | bytes 2308
  13.3 27.5 %copy-start.56 = (s32[8]{0:T(128)S(1)}, s32[8]{0:T(128)}, u32[]{:S(2)}) copy-start(s32[8]{0:T(128)} %start_ref.3) | copy-start | bytes 100
  14.5 20.4 %all-to-all-start = ((bf16[8,144,128]{2,1,0:T(8,128)(2,1)}), bf16[8,144,128]{2,1,0:T(8,128)(2,1)S(1)}, u32[]{:S(2)}, u32[]{:S(2)}) async-start(bf16[8,144,128]{2,1,0:T(8,128)(2,1)} %get-tuple-element.42), calls=%async_computation | async-start | bytes 589824 | tf_op jit(solution)/shard_map/all_to_all | solution.py:382
  20.1 14.2 %copy-start.29 = (bf16[2,96,384]{2,1,0:T(8,128)(2,1)}, bf16[2,96,384]{2,1,0:T(8,128)(2,1)S(1)}, u32[]{:S(2)}) copy-start(bf16[2,96,384]{2,1,0:T(8,128)(2,1)S(1)} %collective-permute-done.3.refs_2_) | copy-start | bytes 442372
  20.9 19.9 %collective-permute-start.4 = (bf16[4,96,384]{2,1,0:T(8,128)(2,1)}, bf16[4,96,384]{2,1,0:T(8,128)(2,1)}, u32[]{:S(2)}, u32[]{:S(2)}) collective-permute-start(bf16[4,96,384]{2,1,0:T(8,128)(2,1)} %pad_maximum_fusion.4), channel_id=1, source_target_pairs={{0,4},{4,0},{8,12},{12,8},{16,20},{20,16},{24,28},{28,24},{1,5},{5... | collective-permute-start | bytes 884744 | tf_op jit(solution)/shard_map/ppermute | solution.py:376
  22.9 10.7 %collective-permute-start = (bf16[48,768]{1,0:T(8,128)(2,1)S(1)}, bf16[48,768]{1,0:T(8,128)(2,1)S(1)}, u32[]{:S(2)}, u32[]{:S(2)}) collective-permute-start(bf16[48,768]{1,0:T(8,128)(2,1)S(1)} %get-tuple-element.40), channel_id=1, source_target_pairs={{0,4},{4,8},{8,12},{12,16},{16,20},{20,24},{24,28},{1,5},{5,9},{9,... | collective-permute-start | bytes 221192 | tf_op jit(solution)/shard_map/ppermute | solution.py:437
  24.9 9.4 %collective-permute-start.1 = (bf16[48,768]{1,0:T(8,128)(2,1)S(1)}, bf16[48,768]{1,0:T(8,128)(2,1)S(1)}, u32[]{:S(2)}, u32[]{:S(2)}) collective-permute-start(bf16[48,768]{1,0:T(8,128)(2,1)S(1)} %get-tuple-element.41), channel_id=1, source_target_pairs={{4,0},{8,4},{12,8},{16,12},{20,16},{24,20},{28,24},{5,1},{9,5},{13... | collective-permute-start | bytes 221192 | tf_op jit(solution)/shard_map/ppermute | solution.py:438
  40.8 16.6 %copy-start.37 = (bf16[8,96,128]{2,1,0:T(8,128)(2,1)}, bf16[8,96,128]{2,1,0:T(8,128)(2,1)S(1)}, u32[]{:S(2)}) copy-start(bf16[8,96,128]{2,1,0:T(8,128)(2,1)S(1)} %get-tuple-element.45) | copy-start | bytes 589828
  40.8 17.4 %copy-start.41 = (f32[8,768]{1,0:T(8,128)}, f32[8,768]{1,0:T(8,128)S(1)}, u32[]{:S(2)}) copy-start(f32[8,768]{1,0:T(8,128)S(1)} %get-tuple-element.52.vec_ref) | copy-start | bytes 73732
  46.1 12.1 %copy-start.49 = (f32[32,4,128]{2,1,0:T(4,128)}, f32[32,4,128]{2,1,0:T(4,128)S(1)}, u32[]{:S(2)}) copy-start(f32[32,4,128]{2,1,0:T(4,128)S(1)} %get-tuple-element.44) | copy-start | bytes 196612
  46.1 9.1 %collective-permute-start.7 = (bf16[1,1056,128]{2,1,0:T(8,128)(2,1)S(1)}, bf16[1,1056,128]{2,1,0:T(8,128)(2,1)S(1)}, u32[]{:S(2)}, u32[]{:S(2)}) collective-permute-start(bf16[1,1056,128]{2,1,0:T(8,128)(2,1)S(1)} %bitcast.40), channel_id=1, source_target_pairs={{0,2},{1,3},{2,0},{3,1},{4,6},{5,7},{6,4},{7,5},{8,10},{9,11},{10,... | collective-permute-start | bytes 811016 | tf_op jit(solution)/shard_map/ppermute | solution.py:376
  47.7 9.6 %collective-permute-start.5 = (bf16[1,768,128]{2,1,0:T(8,128)(2,1)S(1)}, bf16[1,768,128]{2,1,0:T(8,128)(2,1)S(1)}, u32[]{:S(2)}, u32[]{:S(2)}) collective-permute-start(bf16[1,768,128]{2,1,0:T(8,128)(2,1)S(1)} %bitcast.50), channel_id=1, source_target_pairs={{0,2},{1,3},{2,0},{3,1},{4,6},{5,7},{6,4},{7,5},{8,10},{9,11},{10,... | collective-permute-start | bytes 589832 | tf_op jit(solution)/shard_map/ppermute | solution.py:376
  56.8 17.7 %collective-permute-start.8 = (bf16[2,1056,128]{2,1,0:T(8,128)(2,1)}, bf16[2,1056,128]{2,1,0:T(8,128)(2,1)}, u32[]{:S(2)}, u32[]{:S(2)}) collective-permute-start(bf16[2,1056,128]{2,1,0:T(8,128)(2,1)} %pad_maximum_fusion.2), channel_id=1, source_target_pairs={{0,1},{1,0},{2,3},{3,2},{4,5},{5,4},{6,7},{7,6},{8,9},{9,8},{10,11... | collective-permute-start | bytes 1622024 | tf_op jit(solution)/shard_map/ppermute | solution.py:376
  58.2 6.8 %collective-permute-start.6 = (bf16[2,768,128]{2,1,0:T(8,128)(2,1)}, bf16[2,768,128]{2,1,0:T(8,128)(2,1)}, u32[]{:S(2)}, u32[]{:S(2)}) collective-permute-start(bf16[2,768,128]{2,1,0:T(8,128)(2,1)} %pad_maximum_fusion.3), channel_id=1, source_target_pairs={{0,1},{1,0},{2,3},{3,2},{4,5},{5,4},{6,7},{7,6},{8,9},{9,8},{10,11... | collective-permute-start | bytes 1179656 | tf_op jit(solution)/shard_map/ppermute | solution.py:376
  58.2 16.3 %all-to-all-start.1 = ((f32[32,4,128]{2,1,0:T(4,128)}), f32[32,4,128]{2,1,0:T(4,128)}, u32[]{:S(2)}, u32[]{:S(2)}) async-start(f32[32,4,128]{2,1,0:T(4,128)} %copy-done.49), calls=%async_computation.1 | async-start | bytes 131072 | tf_op jit(solution)/shard_map/all_to_all | solution.py:382
  84.3 12.4 %all-to-all-start.2 = ((f32[8,2,512]{2,1,0:T(2,128)}), f32[8,2,512]{2,1,0:T(2,128)S(1)}, u32[]{:S(2)}, u32[]{:S(2)}) async-start(f32[8,2,512]{2,1,0:T(2,128)} %copy-done.50), calls=%async_computation.2 | async-start | bytes 65536 | tf_op jit(solution)/shard_map/all_to_all | solution.py:382
  109.0 11.1 %collective-permute-start.11 = (bf16[4,96,512]{2,1,0:T(8,128)(2,1)}, bf16[4,96,512]{2,1,0:T(8,128)(2,1)S(1)}, u32[]{:S(2)}, u32[]{:S(2)}) collective-permute-start(bf16[4,96,512]{2,1,0:T(8,128)(2,1)} %get-tuple-element.63), channel_id=1, source_target_pairs={{0,4},{4,0},{8,12},{12,8},{16,20},{20,16},{24,28},{28,24},{1,5},{5... | collective-permute-start | bytes 1179656 | tf_op jit(solution)/shard_map/ppermute | solution.py:525
  111.0 19.3 %collective-permute-start.9 = (bf16[1,768,384]{2,1,0:T(8,128)(2,1)}, bf16[1,768,384]{2,1,0:T(8,128)(2,1)}, u32[]{:S(2)}, u32[]{:S(2)}) collective-permute-start(bf16[1,768,384]{2,1,0:T(8,128)(2,1)} %bitcast.44), channel_id=1, source_target_pairs={{0,2},{1,3},{2,0},{3,1},{4,6},{5,7},{6,4},{7,5},{8,10},{9,11},{10,... | collective-permute-start | bytes 1769480 | tf_op jit(solution)/shard_map/ppermute | solution.py:376
  124.4 7.6 %collective-permute-start.12 = (bf16[2,96,512]{1,2,0:T(8,128)(2,1)}, bf16[2,96,512]{1,2,0:T(8,128)(2,1)}, u32[]{:S(2)}, u32[]{:S(2)}) collective-permute-start(bf16[2,96,512]{1,2,0:T(8,128)(2,1)} %fusion.1), channel_id=1, source_target_pairs={{0,8},{4,12},{8,0},{12,4},{16,24},{20,28},{24,16},{28,20},{1,9},{5... | collective-permute-start | bytes 589832 | tf_op jit(solution)/shard_map/ppermute | solution.py:525
  130.3 12.0 %copy-start.60 = (f32[3,96,96]{1,2,0:T(8,128)S(1)}, f32[3,96,96]{1,2,0:T(8,128)}, u32[]{:S(2)}) copy-start(f32[3,96,96]{1,2,0:T(8,128)} %copy.32) | copy-start | bytes 331780
  130.3 12.0 %copy-start.61 = (f32[3,96,96]{1,2,0:T(8,128)S(1)}, f32[3,96,96]{1,2,0:T(8,128)}, u32[]{:S(2)}) copy-start(f32[3,96,96]{1,2,0:T(8,128)} %copy.29) | copy-start | bytes 331780
  131.6 11.5 %collective-permute-start.10 = (bf16[2,768,384]{2,1,0:T(8,128)(2,1)S(1)}, bf16[2,768,384]{2,1,0:T(8,128)(2,1)S(1)}, u32[]{:S(2)}, u32[]{:S(2)}) collective-permute-start(bf16[2,768,384]{2,1,0:T(8,128)(2,1)S(1)} %pad_maximum_fusion.1), channel_id=1, source_target_pairs={{0,1},{1,0},{2,3},{3,2},{4,5},{5,4},{6,7},{7,6},{8,9},{9,8},{10,11... | collective-permute-start | bytes 3538952 | tf_op jit(solution)/shard_map/ppermute | solution.py:376
  133.0 9.1 %collective-permute-start.13 = (bf16[1,96,512]{1,2,0:T(8,128)(2,1)S(1)}, bf16[1,96,512]{1,2,0:T(8,128)(2,1)S(1)}, u32[]{:S(2)}, u32[]{:S(2)}) collective-permute-start(bf16[1,96,512]{1,2,0:T(8,128)(2,1)S(1)} %fusion.4), channel_id=1, source_target_pairs={{0,16},{4,20},{8,24},{12,28},{16,0},{20,4},{24,8},{28,12},{1,17},{... | collective-permute-start | bytes 294920 | tf_op jit(solution)/shard_map/ppermute | solution.py:525
  146.2 13.4 %copy-start.36 = (f32[96,96]{1,0:T(8,128)S(1)}, f32[96,96]{1,0:T(8,128)}, u32[]{:S(2)}) copy-start(f32[96,96]{1,0:T(8,128)} %point_ref.1) | copy-start | bytes 110596
  146.2 20.2 %copy-start.4 = (bf16[1024,768]{1,0:T(8,128)(2,1)S(1)}, bf16[1024,768]{1,0:T(8,128)(2,1)}, u32[]{:S(2)}) copy-start(bf16[1024,768]{1,0:T(8,128)(2,1)} %cot_ref.5) | copy-start | bytes 4718596
  154.8 11.6 %all-to-all-start.3 = ((f32[8,2,768]{2,1,0:T(2,128)}), f32[8,2,768]{2,1,0:T(2,128)S(1)}, u32[]{:S(2)}, u32[]{:S(2)}) async-start(f32[8,2,768]{2,1,0:T(2,128)} %get-tuple-element.60), calls=%async_computation.3 | async-start | bytes 98304 | tf_op jit(solution)/shard_map/all_to_all | solution.py:382
  (52 other events, 105.3 us)

commit v3 on v0

v3 whole, which is shorter than its diff:
```python
import functools

import jax
import jax.numpy as jnp
from jax import lax
from jax.experimental import pallas as pl
from jax.experimental.pallas import tpu as pltpu
from jax.sharding import PartitionSpec as P

KERNEL_WIDTH = 3
DILATION_BINS = 9
WIN = 1024
STEP = 10

NORM_EPS = 1e-05
ADAM_EPS = 1e-08
BETA_ONE = 0.9
BETA_TWO = 0.999
RATE_WEIGHT = 0.05
RATE_NORM = 0.5
DECAY_WEIGHT = 0.01

LANES = 128
EDGE = 16
RIM = 2 * EDGE
GELU_A = 0.7978845608028654
GELU_B = 0.044715
SHIFTS = [(j - KERNEL_WIDTH // 2) * DILATION_BINS for j in range(KERNEL_WIDTH)]
ROW_DIMS = (((0,), (0,)), ((), ()))
LANE_DIMS = (((1,), (1,)), ((), ()))
F32, BF16 = jnp.float32, jnp.bfloat16


def call(body, outs, args, scratch=(), smem=(), after=(), flops=0, limit=16):
    spaces = [pltpu.SMEM if k in smem else pltpu.VMEM for k in range(len(args))]
    spaces += [pl.ANY] * len(after)
    size = lambda a: a.size * a.dtype.itemsize

    def kernel(*refs):
        body(*refs[: len(args)], *refs[len(spaces) :])

    return pl.pallas_call(
        kernel,
        out_shape=[jax.ShapeDtypeStruct(s, t) for s, t in outs],
        in_specs=[pl.BlockSpec(memory_space=s) for s in spaces],
        out_specs=[pl.BlockSpec(memory_space=pltpu.VMEM) for _ in outs],
        scratch_shapes=[pltpu.VMEM(s, t) for s, t in scratch],
        compiler_params=pltpu.CompilerParams(vmem_limit_bytes=limit * 2**20),
        cost_estimate=pl.CostEstimate(
            flops=flops, bytes_accessed=sum(size(a) for a in args), transcendentals=0
        ),
        name=getattr(body, "func", body).__name__,
    )(*args, *after)


def up_to(size, step):
    return -(-size // step) * step


def split_three(v):
    high = v.astype(BF16).astype(F32)
    rest = v - high
    middle = rest.astype(BF16).astype(F32)
    return high, middle, rest - middle


def gelu_and_slope(v):
    square = v * v
    t = jnp.tanh(v * (GELU_A + (GELU_A * GELU_B) * square))
    half = 0.5 * (1.0 + t)
    slope = half + (0.5 * v) * (1.0 - t * t) * (GELU_A + (3.0 * GELU_A * GELU_B) * square)
    return v * half, slope


def reach_of(first, count, shift, start, bin_count):
    here = first + lax.broadcasted_iota(jnp.int32, (count, LANES), 0)
    there = here + shift
    inside = (here >= 0) & (here < bin_count) & (there >= 0) & (there < bin_count)
    return inside & (((here - start) >> 10) == ((there - start) >> 10))


def pack_kernel(conv_ref, out_ref):
    depth, slim = conv_ref.shape[1:]
    out_ref[...] = jnp.zeros_like(out_ref)
    for j in range(KERNEL_WIDTH):
        out_ref[:depth, j * LANES : j * LANES + slim] = conv_ref[j].astype(BF16)


def stats_kernel(x_ref, head_ref, tail_ref, point_ref, sum_ref, turned_ref, last_ref, first_ref):
    rows, width = x_ref.shape
    tiles = width // LANES
    slim, depth = point_ref.shape

    def step(k, carry):
        v = x_ref[pl.ds(pl.multiple_of(k * 32, 32), 32), :].astype(F32)
        v = v.reshape(4, 8, width)
        return carry[0] + v.sum(0), carry[1] + (v * v).sum(0)

    zero = jnp.zeros((8, width), F32)
    one, two = lax.fori_loop(0, rows // 32, step, (zero, zero), unroll=4)
    sum_ref[...] = jnp.zeros_like(sum_ref)
    for stat, total in enumerate((one, two)):
        total = jnp.sum(total, 0, keepdims=True)
        for k in range(tiles):
            row = stat * tiles + k
            sum_ref[row : row + 1, :] = total[:, k * LANES : (k + 1) * LANES]
    turned_ref[...] = jnp.zeros_like(turned_ref)
    turned_ref[:, :slim] = point_ref[...].T.astype(BF16)
    last_ref[:RIM, :] = x_ref[rows - RIM :, :]
    last_ref[RIM:, :] = tail_ref[...]
    first_ref[:RIM, :] = x_ref[:RIM, :]
    first_ref[RIM:, :] = head_ref[...]


def act_kernel(
    x_ref, before_ref, after_ref, one_ref, two_ref, norm_ref, hid_ref, slope_ref, vec_ref, *, bin_count
):
    rows, width = x_ref.shape
    tiles = width // LANES
    total = one_ref[...] + two_ref[...]
    for k in range(tiles):
        lanes = slice(k * LANES, (k + 1) * LANES)
        mean = total[k : k + 1, :] / bin_count
        square = total[tiles + k : tiles + k + 1, :] / bin_count
        root = lax.rsqrt(square - mean * mean + NORM_EPS)
        gain = root * norm_ref[0:1, lanes]
        vec_ref[0:1, lanes] = root
        vec_ref[1:2, lanes] = -mean * root
        vec_ref[2:3, lanes] = gain
        vec_ref[3:4, lanes] = norm_ref[1:2, lanes] - mean * gain

    gain, bias = vec_ref[2:3, :], vec_ref[3:4, :]
    for src, at in ((before_ref, 0), (after_ref, RIM + rows)):
        for k in range(0, RIM, 16):
            hidden, _ = gelu_and_slope(src[k : k + 16, :].astype(F32) * gain + bias)
            hid_ref[at + k : at + k + 16, :] = hidden.astype(BF16)

    def step(k, carry):
        at = pl.multiple_of(k * 16, 16)
        v = x_ref[pl.ds(at, 16), :].astype(F32) * vec_ref[2:3, :] + vec_ref[3:4, :]
        hidden, slope = gelu_and_slope(v)
        hid_ref[pl.ds(pl.multiple_of(at + RIM, 16), 16), :] = hidden.astype(BF16)
        slope_ref[pl.ds(at, 16), :] = slope
        return carry

    lax.fori_loop(0, rows // 16, step, 0, unroll=2)


def place(pieces, relatives, stack, own):
    at = 0
    for piece in pieces:
        for k in range(piece.shape[0]):
            stack[own ^ relatives[at]] = piece[k].astype(stack.dtype)
            at += 1
    return stack[...].reshape(-1, stack.shape[2]).astype(BF16)


def place_kernel(*refs, relatives):
    pieces, (out_ref, stack) = refs[:-2], refs[-2:]
    out_ref[...] = place(pieces, relatives, stack, lax.axis_index("seq"))


def conv_kernel(start_ref, hid_ref, *refs, relatives, bin_count):
    pieces, (weight_ref, out_ref, sum_ref, stack, prod) = refs[:-5], refs[-5:]
    rows = hid_ref.shape[0] - 2 * RIM
    own = lax.axis_index("seq")
    weight_ref[...] = place(pieces, relatives, stack, own)
    for at in range(0, weight_ref.shape[1], 256):
        part = slice(at, min(at + 256, weight_ref.shape[1]))
        prod[:, part] = jnp.dot(hid_ref[...], weight_ref[:, part], preferred_element_type=F32)
    first = own * rows
    start = start_ref[0]

    def rows_of(begin, count):
        value = 0.0
        for j, shift in enumerate(SHIFTS):
            part = prod[begin + EDGE + shift : begin + EDGE + shift + count, j * LANES : (j + 1) * LANES]
            mask = reach_of(first + begin - EDGE, count, shift, start, bin_count)
            value = value + jnp.where(mask, part, 0.0)
        out_ref[begin : begin + count, :] = value
        return value

    rows_of(0, EDGE)
    rows_of(EDGE + rows, EDGE)
    one = two = jnp.zeros((8, LANES), F32)
    step = 128
    for k in range(rows // step):
        value = rows_of(EDGE + k * step, step).reshape(step // 8, 8, LANES)
        one = one + value.sum(0)
        two = two + (value * value).sum(0)
    sum_ref[...] = jnp.zeros_like(sum_ref)
    sum_ref[0:1, :] = jnp.sum(one, 0, keepdims=True)
    sum_ref[1:2, :] = jnp.sum(two, 0, keepdims=True)


def upstream_kernel(cot_ref, before_ref, after_ref, *refs, relatives):
    pieces, (up_ref, point_ref, stack) = refs[:-3], refs[-3:]
    rows = cot_ref.shape[0]
    point_ref[...] = place(pieces, relatives, stack, lax.axis_index("seq"))
    for ref, part, at in (
        (before_ref, slice(RIM, RIM + EDGE), 0),
        (cot_ref, slice(0, rows), EDGE),
        (after_ref, slice(RIM, RIM + EDGE), EDGE + rows),
    ):
        value = jnp.dot(ref[part, :], point_ref[...], preferred_element_type=F32)
        up_ref[at : at + value.shape[0], :] = value


def mid_kernel(
    one_ref, two_ref, conv_ref, up_ref, norm_ref, hid_ref, d_ref, cen_ref, sent_ref, vec_ref, *, bin_count
):
    rows = hid_ref.shape[0]
    slim = norm_ref.shape[1]
    total = one_ref[...] + two_ref[...]
    mean = total[0:1] / bin_count
    root = lax.rsqrt(total[1:2] / bin_count - mean * mean + NORM_EPS)
    vec_ref[...] = jnp.zeros_like(vec_ref)
    vec_ref[0:1, :] = root
    vec_ref[1:3, :slim] = norm_ref[...]
    gain, bias = vec_ref[1:2, :], vec_ref[2:3, :]

    def rows_of(begin, count):
        centered = (conv_ref[pl.ds(begin, count), :] - mean) * root
        hidden, slope = gelu_and_slope(centered * gain + bias)
        d = up_ref[pl.ds(begin, count), :] * slope
        cen_ref[pl.ds(begin, count), :] = centered
        d_ref[pl.ds(begin, count), :] = d
        return centered, hidden, d

    rows_of(0, EDGE)
    rows_of(EDGE + rows, EDGE)
    step = 64

    def body(i, carry):
        begin = pl.multiple_of(EDGE + i * step, 16)
        centered, hidden, d = rows_of(begin, step)
        hid_ref[pl.ds(pl.multiple_of(i * step, 16), step), :] = hidden.astype(BF16)
        d = d.reshape(step // 8, 8, LANES)
        return carry[0] + (d * centered.reshape(d.shape)).sum(0), carry[1] + d.sum(0)

    zero = jnp.zeros((8, LANES), F32)
    gain_sum, bias_sum = lax.fori_loop(0, rows // step, body, (zero, zero), unroll=2)
    gain_sum = jnp.sum(gain_sum, 0, keepdims=True)
    bias_sum = jnp.sum(bias_sum, 0, keepdims=True)
    for d in range(sent_ref.shape[0]):
        sent_ref[d, 0:1, :] = gain_sum
        sent_ref[d, 1:2, :] = bias_sum


def conv_back_kernel(got_ref, vec_ref, d_ref, cen_ref, hid_ref, point_ref, grad_ref, total_ref, both_ref, *, bin_count):
    rows = hid_ref.shape[0]
    total = got_ref[0]
    for s in range(1, got_ref.shape[0]):
        total = total + got_ref[s]
    total_ref[...] = total
    scale = vec_ref[0:1, :] * vec_ref[1:2, :]
    pull, level = total[0:1] / bin_count, total[1:2] / bin_count
    for begin in range(0, rows + RIM, 96):
        part = slice(begin, min(begin + 96, rows + RIM))
        grad_ref[part, :] = (scale * (d_ref[part, :] - level - cen_ref[part, :] * pull)).astype(BF16)
    both_ref[:rows, :] = hid_ref[...]
    both_ref[rows:, :] = point_ref[...]


def out_kernel(x_ref, *refs):
    parts, (out_ref, hidden, point) = refs[:-3], refs[-3:]
    rows = x_ref.shape[0]
    for r, part in enumerate(parts):
        hidden[:, r * LANES : (r + 1) * LANES] = part[:rows, :]
        point[:, r * LANES : (r + 1) * LANES] = part[rows:, :]
    for at in range(0, x_ref.shape[1], 256):
        part = slice(at, at + 256)
        branch = lax.dot_general(
            hidden[...], point[part, :], LANE_DIMS, preferred_element_type=F32
        )
        out_ref[:, part] = (x_ref[:, part].astype(F32) + branch).astype(BF16)


def halve(blocks, kept_ref, sent_ref, high):
    for k in range(kept_ref.shape[0]):
        kept_ref[k] = blocks(2 * k + high)
        sent_ref[k] = blocks(2 * k + 1 - high).astype(BF16)


def terms_of(part, grad, term_ref, at, first, start, bin_count):
    rows = term_ref.shape[0]
    step = 64
    grad[...] = part[...].astype(F32)
    for j, shift in enumerate(SHIFTS):
        lanes = slice(at + j * LANES, at + (j + 1) * LANES)
        for begin in range(0, rows, step):
            mask = reach_of(first + begin - shift, step, shift, start, bin_count)
            value = grad[EDGE + begin - shift : EDGE + begin - shift + step, :]
            term_ref[begin : begin + step, lanes] = jnp.where(mask, value, 0.0).astype(BF16)


def weight_grad_kernel(
    start_ref, part_ref, hid_ref, cot_ref, mid_ref, term_ref, kept_ref, sent_ref, grad, full, *, bin_count, depth, slim
):
    rows = term_ref.shape[0]
    own = lax.axis_index("seq")
    terms_of(part_ref, grad, term_ref, 0, own * rows, start_ref[0], bin_count)
    taps = lax.dot_general(
        hid_ref[RIM : RIM + rows, :], term_ref[...], ROW_DIMS, preferred_element_type=F32
    )
    point = lax.dot_general(cot_ref[...], mid_ref[...], ROW_DIMS, preferred_element_type=F32)
    parts = [taps[:, j * LANES : j * LANES + slim] for j in range(KERNEL_WIDTH)] + [point[:, :slim]]
    full[...] = jnp.concatenate(parts, axis=1)
    high = own % 2
    halve(lambda k: full[pl.ds(pl.multiple_of(k * depth, 8), depth), :], kept_ref, sent_ref, high)


def fold_kernel(old_ref, got_ref, kept_ref, sent_ref, *, reach):
    high = (lax.axis_index("seq") // reach) % 2
    halve(lambda k: old_ref[k] + got_ref[k].astype(F32), kept_ref, sent_ref, high)


def adamw(weights_old, first_moment_state, second_mom, gradient, step_rate, decay_rate):
    first_next = BETA_ONE * first_moment_state + (1.0 - BETA_ONE) * gradient
    second_next = BETA_TWO * second_mom + (1.0 - BETA_TWO) * gradient * gradient
    corrected = (
        first_next
        / (1.0 - BETA_ONE**STEP)
        / (jnp.sqrt(second_next / (1.0 - BETA_TWO**STEP)) + ADAM_EPS)
    )
    weights_new = weights_old - step_rate * (corrected + decay_rate * weights_old)
    return (first_next, second_next, weights_new)


def weight_step_kernel(old_ref, got_ref, total_ref, *refs):
    conv, point, mid, outs = refs[:3], refs[3:6], refs[6:9], refs[9:]
    slim = conv[0].shape[2]
    both = old_ref[0] + got_ref[0].astype(F32)
    for j in range(KERNEL_WIDTH):
        grad = both[:, j * slim : (j + 1) * slim]
        new = adamw(*(ref[j] for ref in conv), grad, RATE_WEIGHT, DECAY_WEIGHT)
        for ref, value in zip(outs[:3], new):
            ref[j] = value
    grad = both[:, KERNEL_WIDTH * slim :].T
    new = adamw(*(ref[...] for ref in point), grad, RATE_WEIGHT, DECAY_WEIGHT)
    for ref, value in zip(outs[3:6], new):
        ref[...] = value
    new = adamw(*(ref[...] for ref in mid), total_ref[:, :slim], RATE_NORM, 0.0)
    for ref, value in zip(outs[6:], new):
        ref[...] = value


def first_half_kernel(start_ref, own_ref, *refs, bin_count):
    up_ref, term, weight, grad = refs[-4:]
    count = (len(refs) - 4 + 1) // 2
    grads, weights = refs[: count - 1], refs[count - 1 : -4]
    rows = up_ref.shape[0]
    wide = KERNEL_WIDTH * LANES
    first = lax.axis_index("seq") * rows
    term[:, :wide] = own_ref[...]
    for r, part in enumerate(grads):
        terms_of(part, grad, term, (r + 1) * wide, first, start_ref[0], bin_count)
    for r, piece in enumerate(weights):
        weight[:, r * wide : (r + 1) * wide] = piece[...]
    for at in range(0, up_ref.shape[1], 256):
        part = slice(at, at + 256)
        up_ref[:, part] = lax.dot_general(
            term[...], weight[part, :], LANE_DIMS, preferred_element_type=F32
        )


def second_half_kernel(start_ref, x_ref, slope_ref, vec_ref, part_ref, *refs, bin_count):
    d_ref, sum_ref, term, weight, grad = refs[-5:]
    count = (len(refs) - 5) // 2
    grads, weights = refs[:count], refs[count:-5]
    rows, width = x_ref.shape
    wide = KERNEL_WIDTH * LANES
    first = lax.axis_index("seq") * rows
    for r, part in enumerate(grads):
        terms_of(part, grad, term, r * wide, first, start_ref[0], bin_count)
    for r, piece in enumerate(weights):
        weight[:, r * wide : (r + 1) * wide] = piece[...]
    for at in range(0, width, 256):
        part = slice(at, at + 256)
        up = lax.dot_general(term[...], weight[part, :], LANE_DIMS, preferred_element_type=F32)
        d = (up + part_ref[:, part]) * slope_ref[:, part]
        d_ref[:, part] = d
        centered = x_ref[:, part].astype(F32) * vec_ref[0:1, part] + vec_ref[1:2, part]
        sum_ref[0:1, part] = jnp.sum(d * centered, 0, keepdims=True)
        sum_ref[1:2, part] = jnp.sum(d, 0, keepdims=True)


def final_kernel(x_ref, cot_ref, d_ref, vec_ref, one_ref, two_ref, *refs, bin_count):
    norms, out_ref, news = refs[:3], refs[3], refs[4:]
    rows, width = x_ref.shape
    total = one_ref[...] + two_ref[...]
    new = adamw(*(ref[...] for ref in norms), total, RATE_NORM, 0.0)
    for ref, value in zip(news, new):
        ref[...] = value
    root, offset, scale = vec_ref[0:1, :], vec_ref[1:2, :], vec_ref[2:3, :]
    pull = scale * total[0:1] / bin_count
    slant = pull * root
    level = scale * total[1:2] / bin_count + pull * offset
    step = 16

    def body(i, carry):
        at = pl.ds(pl.multiple_of(i * step, 16), step)
        value = x_ref[at, :].astype(F32) * slant + level
        out_ref[at, :] = cot_ref[at, :].astype(F32) + (d_ref[at, :] * scale - value)
        return carry

    lax.fori_loop(0, rows // step, body, 0, unroll=4)


def flip(axis, reach):
    return [(i, i ^ reach) for i in range(lax.axis_size(axis))]


def relatives_of(order):
    found = [0]
    for reach in order:
        found = found + [r ^ reach for r in found]
    return found


def descending(size):
    return [size >> k for k in range(1, size.bit_length())]


def round_kernel(*refs):
    ins, outs = refs[: 6 + (len(refs) - 9) // 2], refs[6 + (len(refs) - 9) // 2 :]
    for k in range(2):
        one, two, out = ins[2 * k], ins[2 * k + 1], outs[k]
        size = one.shape[0]
        out[:size] = one[...]
        out[size:] = two[...]
    outs[2][...] = ins[4][...] + ins[5][...]
    for src, out in zip(ins[6:], outs[3:]):
        out[...] = src[...]


def add_kernel(one_ref, two_ref, out_ref):
    out_ref[...] = one_ref[...] + two_ref[...]


def add(one, two, after=()):
    return call(add_kernel, [(one.shape, one.dtype)], [one, two], after=after)[0]


def swap(x, axis, reach):
    return lax.ppermute(x, axis, flip(axis, reach))


def gather_parts(x, reaches):
    parts = [x]
    for reach in reaches:
        parts += [swap(part, "ch", reach) for part in parts]
    return parts


def spread(copies, axes):
    return lax.all_to_all(copies, axes, 0, 0, tiled=True)


def shards(
    inputs,
    cotangent,
    starts,
    master_conv,
    first_conv,
    second_conv,
    master_point,
    first_point,
    second_point,
    norm_in,
    first_in,
    second_in,
    norm_mid,
    first_mid,
    second_mid,
):
    rows, width = inputs.shape
    seq_size, ch_size = lax.axis_size("seq"), lax.axis_size("ch")
    bin_count = rows * seq_size
    depth, slim = master_conv.shape[1:]
    tiles = width // LANES
    wide = KERNEL_WIDTH * LANES
    weight_order = descending(seq_size)
    sum_order = weight_order[::-1]
    point_order = [1] + weight_order[:-1]
    ch_order = descending(ch_size)
    ext = rows + 2 * EDGE

    (conv_low,) = call(pack_kernel, [((depth, wide), BF16)], [master_conv])
    sums_in, point_low, last, first = call(
        stats_kernel,
        [((up_to(2 * tiles, 8), LANES), F32), ((depth, LANES), BF16)]
        + [((RIM + EDGE, width), BF16)] * 2,
        [inputs, cotangent[:EDGE], cotangent[rows - EDGE :], master_point],
    )
    up = [(i, i + 1) for i in range(seq_size - 1)]
    down = [(j, i) for i, j in up]
    before = lax.ppermute(last, "seq", up)
    after = lax.ppermute(first, "seq", down)
    held = [conv_low[None], point_low[None], sums_in]
    rounds = len(weight_order)
    top, lower = ch_order[0], ch_order[1:]
    for k in range(rounds):
        got = [
            swap(x, "seq", order[k]) for x, order in zip(held, (weight_order, point_order, sum_order))
        ]
        if k < rounds - 1:
            extra = [before, after] if k == rounds - 2 else []
            shapes = [((2 * x.shape[0],) + x.shape[1:], BF16) for x in held[:2]]
            held = call(
                round_kernel,
                shapes + [(x.shape, x.dtype) for x in [sums_in, *extra]],
                [held[0], got[0], held[1], got[1], held[2], got[2], *extra],
            )
            if extra:
                before, after = held[3:]
                held = held[:3]
    far_one = swap(held[0], "ch", top)
    hidden_in, slope_in, vec_in = call(
        functools.partial(act_kernel, bin_count=bin_count),
        [((rows + 2 * RIM, width), BF16), ((rows, width), F32), ((8, width), F32)],
        [inputs, before, after, held[2], got[2], norm_in],
        flops=40 * rows * width,
    )

    stack_type = BF16 if depth % 16 == 0 else F32
    conv_own, conv_out, sums_mid = call(
        functools.partial(
            conv_kernel, relatives=relatives_of(weight_order), bin_count=bin_count
        ),
        [((width, wide), BF16), ((ext, LANES), F32), ((8, LANES), F32)],
        [starts, hidden_in, held[0], got[0]],
        scratch=[((seq_size, depth, wide), stack_type), ((rows + 2 * RIM, wide), F32)],
        smem=(0,),
        flops=2 * rows * width * wide,
    )
    far_two = swap(got[0], "ch", top)
    upstream, point_own = call(
        functools.partial(upstream_kernel, relatives=relatives_of(point_order)),
        [((ext, LANES), F32), ((width, LANES), BF16)],
        [cotangent, before, after, held[1], got[1]],
        scratch=[((seq_size, depth, LANES), stack_type)],
        after=[sums_mid],
        flops=2 * rows * width * LANES,
    )
    (conv_far,) = call(
        functools.partial(place_kernel, relatives=relatives_of(weight_order)),
        [((width, wide), BF16)],
        [far_one, far_two],
        scratch=[((seq_size, depth, wide), stack_type)],
        after=[upstream],
    )
    total = sums_mid
    for k, reach in enumerate(sum_order):
        total_got = swap(total, "seq", reach)
        if k < rounds - 1:
            total = add(total, total_got, [conv_far] if k == rounds - 2 else [upstream])
    conv_near, conv_far = gather_parts(conv_own, lower), gather_parts(conv_far, lower)
    hidden_mid, d_mid, centered, sent_back, vec_mid = call(
        functools.partial(mid_kernel, bin_count=bin_count),
        [
            ((rows, LANES), BF16),
            ((ext, LANES), F32),
            ((ext, LANES), F32),
            ((seq_size, 2, LANES), F32),
            ((8, LANES), F32),
        ],
        [total, total_got, conv_out, upstream, norm_mid],
        after=[*conv_near[1:], *conv_far[1:]],
        flops=40 * rows * LANES,
    )
    got_back = spread(sent_back, "seq")
    grad_own, total_mid, both = call(
        functools.partial(conv_back_kernel, bin_count=bin_count),
        [((ext, LANES), BF16), ((2, LANES), F32), ((rows + width, LANES), BF16)],
        [got_back, vec_mid, d_mid, centered, hidden_mid, point_own],
    )
    grad_near = gather_parts(grad_own, lower)
    grad_far = gather_parts(swap(grad_own, "ch", top), lower)
    half = seq_size // 2
    terms, kept, sent = call(
        functools.partial(weight_grad_kernel, bin_count=bin_count, depth=depth, slim=slim),
        [
            ((rows, wide), BF16),
            ((half, depth, 4 * slim), F32),
            ((half, depth, 4 * slim), BF16),
        ],
        [starts, grad_own, hidden_in, cotangent, hidden_mid],
        scratch=[((ext, LANES), F32), ((width, 4 * slim), F32)],
        smem=(0,),
        flops=2 * rows * width * (wide + LANES),
    )
    side = ch_size // 2 * wide
    (up_part,) = call(
        functools.partial(first_half_kernel, bin_count=bin_count),
        [((rows, width), F32)],
        [starts, terms, *grad_near[1:], *conv_near],
        scratch=[((rows, side), BF16), ((width, side), BF16), ((ext, LANES), F32)],
        smem=(0,),
        flops=2 * rows * width * side,
    )
    both_far = swap(both, "ch", top)
    d_in, sums_back = call(
        functools.partial(second_half_kernel, bin_count=bin_count),
        [((rows, width), F32), ((2, width), F32)],
        [starts, inputs, slope_in, vec_in, up_part, *grad_far, *conv_far],
        scratch=[((rows, side), BF16), ((width, side), BF16), ((ext, LANES), F32)],
        smem=(0,),
        flops=2 * rows * width * side,
    )
    parts = gather_parts(both, lower) + gather_parts(both_far, lower)
    (block_out,) = call(
        out_kernel,
        [((rows, width), BF16)],
        [inputs, *parts],
        scratch=[((rows, ch_size * LANES), BF16), ((width, ch_size * LANES), BF16)],
        after=[sums_back],
        flops=2 * rows * width * ch_size * LANES,
    )
    total_back = sums_back
    for k, reach in enumerate(sum_order):
        total_got = swap(total_back, "seq", reach)
        got = swap(sent, "seq", reach)
        if k < rounds - 1:
            half //= 2
            kept, sent = call(
                functools.partial(fold_kernel, reach=2 * reach),
                [((half, depth, 4 * slim), F32), ((half, depth, 4 * slim), BF16)],
                [kept, got],
                after=[total_back],
            )
            total_back = add(total_back, total_got, [sent] + [block_out] * (k == rounds - 2))
    input_grad, *in_new = call(
        functools.partial(final_kernel, bin_count=bin_count),
        [((rows, width), F32)] + [((2, width), F32)] * 3,
        [inputs, cotangent, d_in, vec_in, total_back, total_got, norm_in, first_in, second_in],
        flops=10 * rows * width,
    )
    news = call(
        weight_step_kernel,
        [(master_conv.shape, F32)] * 3 + [(master_point.shape, F32)] * 3 + [(norm_mid.shape, F32)] * 3,
        [kept, got, total_mid, master_conv, first_conv, second_conv]
        + [master_point, first_point, second_point, norm_mid, first_mid, second_mid],
    )
    return (block_out, input_grad, *news[:6], *in_new, *news[6:])


def solution(mesh):
    in_specs = (
        P("seq", None),
        P("seq", None),
        P(),
        P(None, "seq", "ch"),
        P(None, "seq", "ch"),
        P(None, "seq", "ch"),
        P("ch", "seq"),
        P("ch", "seq"),
        P("ch", "seq"),
        P(),
        P(),
        P(),
        P(None, "ch"),
        P(None, "ch"),
        P(None, "ch"),
    )
    out_specs = (
        P("seq", None),
        P("seq", None),
        P(None, "seq", "ch"),
        P(None, "seq", "ch"),
        P(None, "seq", "ch"),
        P("ch", "seq"),
        P("ch", "seq"),
        P("ch", "seq"),
        P(),
        P(),
        P(),
        P(None, "ch"),
        P(None, "ch"),
        P(None, "ch"),
    )
    return jax.shard_map(shards, mesh=mesh, in_specs=in_specs, out_specs=out_specs, check_vma=False)
```

time: 327 us -> 113 us (0.35)
  blocking collectives: 144 us -> 9.26 us
  waiting for transfers between devices: 115 us -> 41.3 us
  starting transfers between devices: 8.71 us -> 34.4 us
  Pallas kernels: 0 us -> 21.3 us
  other arithmetic: 19 us -> 0 us
  matrix products: 15.3 us -> 0 us
  between operations: 16 us -> 0.97 us
  local copies, waits for them, and re-layouts: 8.88 us -> 5.35 us
    unnamed x5 -> x0, waiting for transfers between devices: 85.5 us -> none
    psum x4 -> x0, blocking collectives: 82.2 us -> none  [the longest x2 43.4 us: normalize(): lax.psum((jnp.sum(values, axis=0), jnp.sum(values * values, axis=0)), 'seq')]
    all_gather x2 -> x0, blocking collectives: 62.2 us -> none  [the longest x1 31.6 us: shards(): lax.all_gather(master_conv.astype(jnp.bfloat16), 'seq', axis=1, tiled=True)]
    ppermute x4 -> x30, waiting for transfers between devices: 0.58 us -> 41.3 us  [the longest x28 40.2 us: swap(): return lax.ppermute(x, axis, flip(axis, reach))]
    psum x1 -> x0, waiting for transfers between devices: 28.4 us -> none  [shards(): branch = lax.psum(partial_value, 'ch')]
    ppermute x4 -> x30, starting transfers between devices: 8.59 us -> 34.4 us  [the longest x28 30.7 us: swap(): return lax.ppermute(x, axis, flip(axis, reach))]
    pallas_call x0 -> x22, Pallas kernels: none -> 21.3 us  [call(): pl.pallas_call(kernel, out_shape=[jax.ShapeDtypeStruct(s, t) for s, t in...]
    dot_general x11 -> x0, matrix products: 12.3 us -> none  [the longest x3 4.05 us: input_terms(): lax.dot_general(back_window, kernel[kernel_index], (((1,), (1,)), ((), ()...]
  transfers between devices with their start and end apart: 7 -> 30, of which waited for: 4 -> 12; matrix products, arithmetic and copies ran while one was open for 6% -> 1% of each run, Pallas kernels for 0% -> 16%
where the time goes in v3:
time: 113 us
  waiting for transfers between devices  41.3 us (37%)
  starting transfers between devices  34.4 us (30%)
  Pallas kernels  21.3 us (19%)
  blocking collectives  9.26 us (8%)
  local copies, waits for them, and re-layouts  5.35 us (5%)
    ppermute x28, waiting for transfers between devices, swap(): return lax.ppermute(x, axis, flip(axis, reach))  40.2 us
    ppermute x28, starting transfers between devices, swap(): return lax.ppermute(x, axis, flip(axis, reach))  30.7 us
    pallas_call x22, Pallas kernels, call(): pl.pallas_call(kernel, out_shape=[jax.ShapeDtypeStruct(s, t) for s, t in...  21.3 us
    all_to_all x1, blocking collectives, spread(): return lax.all_to_all(copies, axes, 0, 0, tiled=True)  9.26 us
    unnamed x38, local copies, waits for them, and re-layouts  4.6 us
    ppermute x1, starting transfers between devices, shards(): before = lax.ppermute(last, 'seq', up)  2.43 us
  transfers between devices with their start and end apart: 30, of which 12 were waited for; matrix products, arithmetic and copies ran while one was open for 1% of the time, Pallas kernels for 16%

profile of v3, /device:TPU:0, one launch (start us, length us, event | category | flops | bytes accessed | tf_op | source)
XLA Modules:
  0.0 112.6 jit_solution(2182005000085172977)
XLA Ops:
  1.6 4.1 %collective-permute-start = (bf16[1,96,384]{2,1,0:T(8,128)(2,1)S(1)}, bf16[1,96,384]{2,1,0:T(8,128)(2,1)S(1)}, u32[]{:S(2)}, u32[]{:S(2)}) collective-permute-start(bf16[1,96,384]{2,1,0:T(8,128)(2,1)S(1)} %bitcast.2), channel_id=1, source_target_pairs={{0,16},{4,20},{8,24},{12,28},{16,0},{20,4},{24,8},{28,12},{1,17},{... | collective-permute-start | bytes 221192 | tf_op jit(solution)/shard_map/ppermute | solution.py:446
  9.2 1.6 %collective-permute-start.1 = (bf16[1,96,128]{2,1,0:T(8,128)(2,1)S(1)}, bf16[1,96,128]{2,1,0:T(8,128)(2,1)S(1)}, u32[]{:S(2)}, u32[]{:S(2)}) collective-permute-start(bf16[1,96,128]{2,1,0:T(8,128)(2,1)S(1)} %bitcast.4), channel_id=1, source_target_pairs={{0,4},{4,0},{8,12},{12,8},{16,20},{20,16},{24,28},{28,24},{1,5},{5... | collective-permute-start | bytes 73736 | tf_op jit(solution)/shard_map/ppermute | solution.py:446
  11.2 3.1 %collective-permute-done.2.refs_5_ = f32[16,128]{1,0:T(8,128)S(1)} collective-permute-done((f32[16,128]{1,0:T(8,128)S(1)}, f32[16,128]{1,0:T(8,128)S(1)}, u32[]{:S(2)}, u32[]{:S(2)}) %collective-permute-start.2) | collective-permute-done | bytes 8224 | tf_op jit(solution)/shard_map/ppermute | solution.py:446
  14.4 1.6 %collective-permute-start.3 = (bf16[2,96,384]{2,1,0:T(8,128)(2,1)S(1)}, bf16[2,96,384]{2,1,0:T(8,128)(2,1)S(1)}, u32[]{:S(2)}, u32[]{:S(2)}) collective-permute-start(bf16[2,96,384]{2,1,0:T(8,128)(2,1)S(1)} %get-tuple-element.66.refs_0_), channel_id=1, source_target_pairs={{0,8},{4,12},{8,0},{12,4},{16,24},{20,28},{24,16},{28,20},{1,9},{5... | collective-permute-start | bytes 442376 | tf_op jit(solution)/shard_map/ppermute | solution.py:446
  16.0 2.4 %collective-permute-start.6 = (bf16[48,768]{1,0:T(8,128)(2,1)S(1)}, bf16[48,768]{1,0:T(8,128)(2,1)S(1)}, u32[]{:S(2)}, u32[]{:S(2)}) collective-permute-start(bf16[48,768]{1,0:T(8,128)(2,1)S(1)} %get-tuple-element.69), channel_id=1, source_target_pairs={{0,4},{4,8},{8,12},{12,16},{16,20},{20,24},{24,28},{1,5},{5,9},{9,... | collective-permute-start | bytes 221192 | tf_op jit(solution)/shard_map/ppermute | solution.py:498
  19.8 3.4 %collective-permute-start.4 = (bf16[2,96,128]{2,1,0:T(8,128)(2,1)S(1)}, bf16[2,96,128]{2,1,0:T(8,128)(2,1)S(1)}, u32[]{:S(2)}, u32[]{:S(2)}) collective-permute-start(bf16[2,96,128]{2,1,0:T(8,128)(2,1)S(1)} %get-tuple-element.67.refs_2_), channel_id=1, source_target_pairs={{0,16},{4,20},{8,24},{12,28},{16,0},{20,4},{24,8},{28,12},{1,17},{... | collective-permute-start | bytes 147464 | tf_op jit(solution)/shard_map/ppermute | solution.py:446
  24.7 2.1 %collective-permute-done.5.refs_5_ = f32[16,128]{1,0:T(8,128)S(1)} collective-permute-done((f32[16,128]{1,0:T(8,128)S(1)}, f32[16,128]{1,0:T(8,128)S(1)}, u32[]{:S(2)}, u32[]{:S(2)}) %collective-permute-start.5) | collective-permute-done | bytes 8224 | tf_op jit(solution)/shard_map/ppermute | solution.py:446
  28.0 1.5 %collective-permute-start.13 = (bf16[4,96,384]{2,1,0:T(8,128)(2,1)S(1)}, bf16[4,96,384]{2,1,0:T(8,128)(2,1)S(1)}, u32[]{:S(2)}, u32[]{:S(2)}) collective-permute-start(bf16[4,96,384]{2,1,0:T(8,128)(2,1)S(1)} %get-tuple-element.75.refs_2_), channel_id=1, source_target_pairs={{0,2},{1,3},{2,0},{3,1},{4,6},{5,7},{6,4},{7,5},{8,10},{9,11},{10,... | collective-permute-start | bytes 884744 | tf_op jit(solution)/shard_map/ppermute | solution.py:446
  29.5 4.1 %collective-permute-done.9.refs_3_ = bf16[4,96,384]{2,1,0:T(8,128)(2,1)S(1)} collective-permute-done((bf16[4,96,384]{2,1,0:T(8,128)(2,1)S(1)}, bf16[4,96,384]{2,1,0:T(8,128)(2,1)S(1)}, u32[]{:S(2)}, u32[]{:S(2)}) %collective-permute-start.9) | collective-permute-done | bytes 294944 | tf_op jit(solution)/shard_map/ppermute | solution.py:446
  33.7 1.5 %collective-permute-start.14 = (bf16[4,96,384]{2,1,0:T(8,128)(2,1)S(1)}, bf16[4,96,384]{2,1,0:T(8,128)(2,1)S(1)}, u32[]{:S(2)}, u32[]{:S(2)}) collective-permute-start(bf16[4,96,384]{2,1,0:T(8,128)(2,1)S(1)} %collective-permute-done.9.refs_3_), channel_id=1, source_target_pairs={{0,2},{1,3},{2,0},{3,1},{4,6},{5,7},{6,4},{7,5},{8,10},{9,11},{10,... | collective-permute-start | bytes 884744 | tf_op jit(solution)/shard_map/ppermute | solution.py:446
  35.2 1.4 %collective-permute-start.11 = (bf16[4,96,128]{2,1,0:T(8,128)(2,1)S(1)}, bf16[4,96,128]{2,1,0:T(8,128)(2,1)S(1)}, u32[]{:S(2)}, u32[]{:S(2)}) collective-permute-start(bf16[4,96,128]{2,1,0:T(8,128)(2,1)S(1)} %get-tuple-element.77.refs_3_), channel_id=1, source_target_pairs={{0,8},{4,12},{8,0},{12,4},{16,24},{20,28},{24,16},{28,20},{1,9},{5... | collective-permute-start | bytes 294920 | tf_op jit(solution)/shard_map/ppermute | solution.py:446
  36.6 1.6 %collective-permute-start.8 = (f32[16,128]{1,0:T(8,128)S(1)}, f32[16,128]{1,0:T(8,128)S(1)}, u32[]{:S(2)}, u32[]{:S(2)}) collective-permute-start(f32[16,128]{1,0:T(8,128)S(1)} %get-tuple-element.73.refs_3_), channel_id=1, source_target_pairs={{0,16},{4,20},{8,24},{12,28},{16,0},{20,4},{24,8},{28,12},{1,17},{... | collective-permute-start | bytes 24584 | tf_op jit(solution)/shard_map/ppermute | solution.py:446
  38.2 3.0 %collective-permute-done.8.refs_4_ = f32[16,128]{1,0:T(8,128)S(1)} collective-permute-done((f32[16,128]{1,0:T(8,128)S(1)}, f32[16,128]{1,0:T(8,128)S(1)}, u32[]{:S(2)}, u32[]{:S(2)}) %collective-permute-start.8) | collective-permute-done | bytes 8224 | tf_op jit(solution)/shard_map/ppermute | solution.py:446
  41.2 2.4 %act_kernel.1 = (bf16[1088,768]{1,0:T(8,128)(2,1)S(1)}, f32[1024,768]{1,0:T(8,128)S(1)}, f32[8,768]{1,0:T(8,128)S(1)}) custom-call(bf16[1024,768]{1,0:T(8,128)(2,1)S(1)} %copy-done.1, bf16[48,768]{1,0:T(8,128)(2,1)S(1)} %get-tuple-element.71.refs_1_, bf16[48,768]{1,0:T(8,128)(2,1)S(1)} %get-tuple-element.72.refs_2_, ...), custom_call_target="tpu_custom_call" | custom-call | flops 31457280 | bytes 1742848 | tf_op jit(solution)/shard_map/act_kernel/pallas_call | solution.py:42
  43.6 2.1 %conv_kernel.1 = (bf16[768,384]{1,0:T(8,128)(2,1)S(1)}, f32[1056,128]{1,0:T(8,128)S(1)}, f32[8,128]{1,0:T(8,128)S(1)}) custom-call(s32[8]{0:T(128)S(1)} %copy-done.13, bf16[1088,768]{1,0:T(8,128)(2,1)S(1)} %get-tuple-element.74.refs_1_.refs_2_, bf16[4,96,384]{2,1,0:T(8,128)(2,1)S(1)} %get-tuple-element.75.refs_2_, ...), custom_call_target="tpu_custom_call" | custom-call | flops 603979776 | bytes 2261024 | tf_op jit(solution)/shard_map/conv_kernel/pallas_call | solution.py:42
  47.1 3.6 %collective-permute-done.10.refs_1_ = f32[8,128]{1,0:T(8,128)S(1)} collective-permute-done((f32[8,128]{1,0:T(8,128)S(1)}, f32[8,128]{1,0:T(8,128)S(1)}, u32[]{:S(2)}, u32[]{:S(2)}) %collective-permute-start.10) | collective-permute-done | bytes 4128 | tf_op jit(solution)/shard_map/ppermute | solution.py:446
  51.4 3.0 %collective-permute-done.12.refs_1_ = f32[8,128]{1,0:T(8,128)S(1)} collective-permute-done((f32[8,128]{1,0:T(8,128)S(1)}, f32[8,128]{1,0:T(8,128)S(1)}, u32[]{:S(2)}, u32[]{:S(2)}) %collective-permute-start.12) | collective-permute-done | bytes 4128 | tf_op jit(solution)/shard_map/ppermute | solution.py:446
  54.3 1.6 %collective-permute-start.15 = (f32[8,128]{1,0:T(8,128)S(1)}, f32[8,128]{1,0:T(8,128)S(1)}, u32[]{:S(2)}, u32[]{:S(2)}) collective-permute-start(f32[8,128]{1,0:T(8,128)S(1)} %add_kernel.5.refs_0_), channel_id=1, source_target_pairs={{0,16},{4,20},{8,24},{12,28},{16,0},{20,4},{24,8},{28,12},{1,17},{... | collective-permute-start | bytes 12296 | tf_op jit(solution)/shard_map/ppermute | solution.py:446
  55.9 2.9 %collective-permute-done.15.refs_1_ = f32[8,128]{1,0:T(8,128)S(1)} collective-permute-done((f32[8,128]{1,0:T(8,128)S(1)}, f32[8,128]{1,0:T(8,128)S(1)}, u32[]{:S(2)}, u32[]{:S(2)}) %collective-permute-start.15) | collective-permute-done | bytes 4128 | tf_op jit(solution)/shard_map/ppermute | solution.py:446
  59.4 9.3 %all_to_all.5.refs_0_ = f32[8,2,128]{2,1,0:T(2,128)S(1)} all-to-all(f32[8,2,128]{2,1,0:T(2,128)S(1)} %get-tuple-element.81), channel_id=1, replica_groups=mesh['seq'=8,'ch'=4] {'seq'}, dimensions={0} | all-to-all | bytes 16384 | tf_op jit(solution)/shard_map/all_to_all | solution.py:457
  69.3 1.5 %collective-permute-start.22 = (bf16[1056,128]{1,0:T(8,128)(2,1)S(1)}, bf16[1056,128]{1,0:T(8,128)(2,1)S(1)}, u32[]{:S(2)}, u32[]{:S(2)}) collective-permute-start(bf16[1056,128]{1,0:T(8,128)(2,1)S(1)} %get-tuple-element.90.refs_1_), channel_id=1, source_target_pairs={{0,2},{1,3},{2,0},{3,1},{4,6},{5,7},{6,4},{7,5},{8,10},{9,11},{10,... | collective-permute-start | bytes 811016 | tf_op jit(solution)/shard_map/ppermute | solution.py:446
  70.9 11.4 %collective-permute-done.22.refs_5_ = bf16[1056,128]{1,0:T(8,128)(2,1)S(1)} collective-permute-done((bf16[1056,128]{1,0:T(8,128)(2,1)S(1)}, bf16[1056,128]{1,0:T(8,128)(2,1)S(1)}, u32[]{:S(2)}, u32[]{:S(2)}) %collective-permute-start.22) | collective-permute-done | bytes 270368 | tf_op jit(solution)/shard_map/ppermute | solution.py:446
  82.8 2.7 %weight_grad_kernel.1 = (bf16[1024,384]{1,0:T(8,128)(2,1)S(1)}, f32[4,96,384]{2,1,0:T(8,128)S(1)}, bf16[4,96,384]{2,1,0:T(8,128)(2,1)S(1)}) custom-call(s32[8]{0:T(128)S(1)} %copy-done.13, bf16[1056,128]{1,0:T(8,128)(2,1)S(1)} %get-tuple-element.90.refs_1_, bf16[1088,768]{1,0:T(8,128)(2,1)S(1)} %get-tuple-element.74.refs_1_.refs_2_, ...), custom_call_target="tpu_custom_call" | custom-call | flops 805306368 | bytes 3776544 | tf_op jit(solution)/shard_map/weight_grad_kernel/pallas_call | solution.py:42
  86.1 2.6 %first_half_kernel.1.refs_4_ = f32[1024,768]{1,0:T(8,128)S(1)} custom-call(s32[8]{0:T(128)S(1)} %copy-done.13, bf16[1024,384]{1,0:T(8,128)(2,1)S(1)} %get-tuple-element.91.refs_1_, bf16[1056,128]{1,0:T(8,128)(2,1)S(1)} %collective-permute-done.21.refs_2_, bf16[768,384]{1,0:T(8,128)(2,1)S(1)} %get-tuple-element.80.refs_3_, ...), custom_call_target="tpu_custom_call" | custom-call | flops 1207959552 | bytes 2236448 | tf_op jit(solution)/shard_map/first_half_kernel/pallas_call | solution.py:42
  88.7 3.4 %second_half_kernel.1 = (f32[1024,768]{1,0:T(8,128)S(1)}, f32[2,768]{1,0:T(2,128)S(1)}) custom-call(s32[8]{0:T(128)S(1)} %copy-done.13, bf16[1024,768]{1,0:T(8,128)(2,1)S(1)} %copy-done.1, f32[1024,768]{1,0:T(8,128)S(1)} %get-tuple-element.88.refs_2_, f32[8,768]{1,0:T(8,128)S(1)} %get-tuple-element.89.refs_3_, f32[1024,768]{1,0:T(8,128)S(1)} %first_half_kernel.1.refs_4_, ...), custom_call_target="tpu_custom_call" | custom-call | flops 1207959552 | bytes 9609248 | tf_op jit(solution)/shard_map/second_half_kernel/pallas_call | solution.py:42
  92.1 2.9 %collective-permute-done.25.refs_1_ = bf16[4,96,384]{2,1,0:T(8,128)(2,1)S(1)} collective-permute-done((bf16[4,96,384]{2,1,0:T(8,128)(2,1)S(1)}, bf16[4,96,384]{2,1,0:T(8,128)(2,1)S(1)}, u32[]{:S(2)}, u32[]{:S(2)}) %collective-permute-start.25) | collective-permute-done | bytes 294944 | tf_op jit(solution)/shard_map/ppermute | solution.py:446
  96.3 3.0 %collective-permute-done.24.refs_1_ = f32[2,768]{1,0:T(2,128)S(1)} collective-permute-done((f32[2,768]{1,0:T(2,128)S(1)}, f32[2,768]{1,0:T(2,128)S(1)}, u32[]{:S(2)}, u32[]{:S(2)}) %collective-permute-start.24) | collective-permute-done | bytes 6176 | tf_op jit(solution)/shard_map/ppermute | solution.py:446
  99.3 1.5 %collective-permute-start.26 = (f32[2,768]{1,0:T(2,128)S(1)}, f32[2,768]{1,0:T(2,128)S(1)}, u32[]{:S(2)}, u32[]{:S(2)}) collective-permute-start(f32[2,768]{1,0:T(2,128)S(1)} %add_kernel.6.refs_2_.refs_0_), channel_id=1, source_target_pairs={{0,8},{4,12},{8,0},{12,4},{16,24},{20,28},{24,16},{28,20},{1,9},{5... | collective-permute-start | bytes 18440 | tf_op jit(solution)/shard_map/ppermute | solution.py:446
  101.5 2.3 %out_kernel.1.refs_3_ = bf16[1024,768]{1,0:T(8,128)(2,1)} custom-call(bf16[1024,768]{1,0:T(8,128)(2,1)S(1)} %copy-done.1, bf16[1792,128]{1,0:T(8,128)(2,1)S(1)} %get-tuple-element.87.refs_1_, bf16[1792,128]{1,0:T(8,128)(2,1)S(1)} %collective-permute-done.18.refs_2_, bf16[1792,128]{1,0:T(8,128)(2,1)S(1)} %collective-permute-done.19.refs_3_, ...), custom_call_target="tpu_custom_call" | custom-call | flops 805306368 | bytes 3407872 | tf_op jit(solution)/shard_map/out_kernel/pallas_call | solution.py:42
  103.8 1.4 %copy-done.3 = bf16[1024,768]{1,0:T(8,128)(2,1)S(1)} copy-done((bf16[1024,768]{1,0:T(8,128)(2,1)S(1)}, bf16[1024,768]{1,0:T(8,128)(2,1)}, u32[]{:S(2)}) %copy-start.3) | copy-done | bytes 1572888
  105.3 2.4 %collective-permute-start.28 = (f32[2,768]{1,0:T(2,128)S(1)}, f32[2,768]{1,0:T(2,128)S(1)}, u32[]{:S(2)}, u32[]{:S(2)}) collective-permute-start(f32[2,768]{1,0:T(2,128)S(1)} %add_kernel.7.refs_4_), channel_id=1, source_target_pairs={{0,16},{4,20},{8,24},{12,28},{16,0},{20,4},{24,8},{28,12},{1,17},{... | collective-permute-start | bytes 18440 | tf_op jit(solution)/shard_map/ppermute | solution.py:446
  109.9 2.7 %final_kernel.1 = (f32[1024,768]{1,0:T(8,128)}, f32[2,768]{1,0:T(2,128)}, f32[2,768]{1,0:T(2,128)}, f32[2,768]{1,0:T(2,128)}) custom-call(bf16[1024,768]{1,0:T(8,128)(2,1)S(1)} %copy-done.1, bf16[1024,768]{1,0:T(8,128)(2,1)S(1)} %copy-done.2, f32[1024,768]{1,0:T(8,128)S(1)} %get-tuple-element.93.refs_2_, f32[8,768]{1,0:T(8,128)S(1)} %get-tuple-element.89.refs_3_, ...), custom_call_target="tpu_custom_call" | custom-call | flops 7864320 | bytes 6346752 | tf_op jit(solution)/shard_map/final_kernel/pallas_call | solution.py:42
  (90 shorter events, 17.4 us)
Async XLA Ops:
  1.6 39.6 %copy-start.12 = (f32[2,768]{1,0:T(2,128)S(1)}, f32[2,768]{1,0:T(2,128)}, u32[]{:S(2)}) copy-start(f32[2,768]{1,0:T(2,128)} %refs_6_.2) | copy-start | bytes 18436
  1.6 12.8 %collective-permute-start = (bf16[1,96,384]{2,1,0:T(8,128)(2,1)S(1)}, bf16[1,96,384]{2,1,0:T(8,128)(2,1)S(1)}, u32[]{:S(2)}, u32[]{:S(2)}) collective-permute-start(bf16[1,96,384]{2,1,0:T(8,128)(2,1)S(1)} %bitcast.2), channel_id=1, source_target_pairs={{0,16},{4,20},{8,24},{12,28},{16,0},{20,4},{24,8},{28,12},{1,17},{... | collective-permute-start | bytes 221192 | tf_op jit(solution)/shard_map/ppermute | solution.py:446
  9.1 34.4 %copy-start.13 = (s32[8]{0:T(128)S(1)}, s32[8]{0:T(128)}, u32[]{:S(2)}) copy-start(s32[8]{0:T(128)} %refs_0_.17) | copy-start | bytes 100
  9.2 5.2 %collective-permute-start.1 = (bf16[1,96,128]{2,1,0:T(8,128)(2,1)S(1)}, bf16[1,96,128]{2,1,0:T(8,128)(2,1)S(1)}, u32[]{:S(2)}, u32[]{:S(2)}) collective-permute-start(bf16[1,96,128]{2,1,0:T(8,128)(2,1)S(1)} %bitcast.4), channel_id=1, source_target_pairs={{0,4},{4,0},{8,12},{12,8},{16,20},{20,16},{24,28},{28,24},{1,5},{5... | collective-permute-start | bytes 73736 | tf_op jit(solution)/shard_map/ppermute | solution.py:446
  10.7 3.7 %collective-permute-start.2 = (f32[16,128]{1,0:T(8,128)S(1)}, f32[16,128]{1,0:T(8,128)S(1)}, u32[]{:S(2)}, u32[]{:S(2)}) collective-permute-start(f32[16,128]{1,0:T(8,128)S(1)} %get-tuple-element.65.refs_4_), channel_id=1, source_target_pairs={{0,4},{4,0},{8,12},{12,8},{16,20},{20,16},{24,28},{28,24},{1,5},{5... | collective-permute-start | bytes 24584 | tf_op jit(solution)/shard_map/ppermute | solution.py:446
  14.4 12.4 %collective-permute-start.3 = (bf16[2,96,384]{2,1,0:T(8,128)(2,1)S(1)}, bf16[2,96,384]{2,1,0:T(8,128)(2,1)S(1)}, u32[]{:S(2)}, u32[]{:S(2)}) collective-permute-start(bf16[2,96,384]{2,1,0:T(8,128)(2,1)S(1)} %get-tuple-element.66.refs_0_), channel_id=1, source_target_pairs={{0,8},{4,12},{8,0},{12,4},{16,24},{20,28},{24,16},{28,20},{1,9},{5... | collective-permute-start | bytes 442376 | tf_op jit(solution)/shard_map/ppermute | solution.py:446
  16.0 7.6 %collective-permute-start.6 = (bf16[48,768]{1,0:T(8,128)(2,1)S(1)}, bf16[48,768]{1,0:T(8,128)(2,1)S(1)}, u32[]{:S(2)}, u32[]{:S(2)}) collective-permute-start(bf16[48,768]{1,0:T(8,128)(2,1)S(1)} %get-tuple-element.69), channel_id=1, source_target_pairs={{0,4},{4,8},{8,12},{12,16},{16,20},{20,24},{24,28},{1,5},{5,9},{9,... | collective-permute-start | bytes 221192 | tf_op jit(solution)/shard_map/ppermute | solution.py:498
  18.5 6.2 %collective-permute-start.7 = (bf16[48,768]{1,0:T(8,128)(2,1)S(1)}, bf16[48,768]{1,0:T(8,128)(2,1)S(1)}, u32[]{:S(2)}, u32[]{:S(2)}) collective-permute-start(bf16[48,768]{1,0:T(8,128)(2,1)S(1)} %get-tuple-element.70), channel_id=1, source_target_pairs={{4,0},{8,4},{12,8},{16,12},{20,16},{24,20},{28,24},{5,1},{9,5},{13... | collective-permute-start | bytes 221192 | tf_op jit(solution)/shard_map/ppermute | solution.py:499
  19.8 7.1 %collective-permute-start.4 = (bf16[2,96,128]{2,1,0:T(8,128)(2,1)S(1)}, bf16[2,96,128]{2,1,0:T(8,128)(2,1)S(1)}, u32[]{:S(2)}, u32[]{:S(2)}) collective-permute-start(bf16[2,96,128]{2,1,0:T(8,128)(2,1)S(1)} %get-tuple-element.67.refs_2_), channel_id=1, source_target_pairs={{0,16},{4,20},{8,24},{12,28},{16,0},{20,4},{24,8},{28,12},{1,17},{... | collective-permute-start | bytes 147464 | tf_op jit(solution)/shard_map/ppermute | solution.py:446
  23.2 3.7 %collective-permute-start.5 = (f32[16,128]{1,0:T(8,128)S(1)}, f32[16,128]{1,0:T(8,128)S(1)}, u32[]{:S(2)}, u32[]{:S(2)}) collective-permute-start(f32[16,128]{1,0:T(8,128)S(1)} %get-tuple-element.68.refs_4_), channel_id=1, source_target_pairs={{0,8},{4,12},{8,0},{12,4},{16,24},{20,28},{24,16},{28,20},{1,9},{5... | collective-permute-start | bytes 24584 | tf_op jit(solution)/shard_map/ppermute | solution.py:446
  26.9 6.8 %collective-permute-start.9 = (bf16[4,96,384]{2,1,0:T(8,128)(2,1)S(1)}, bf16[4,96,384]{2,1,0:T(8,128)(2,1)S(1)}, u32[]{:S(2)}, u32[]{:S(2)}) collective-permute-start(bf16[4,96,384]{2,1,0:T(8,128)(2,1)S(1)} %get-tuple-element.75.refs_2_), channel_id=1, source_target_pairs={{0,4},{4,0},{8,12},{12,8},{16,20},{20,16},{24,28},{28,24},{1,5},{5... | collective-permute-start | bytes 884744 | tf_op jit(solution)/shard_map/ppermute | solution.py:446
  28.0 18.4 %collective-permute-start.13 = (bf16[4,96,384]{2,1,0:T(8,128)(2,1)S(1)}, bf16[4,96,384]{2,1,0:T(8,128)(2,1)S(1)}, u32[]{:S(2)}, u32[]{:S(2)}) collective-permute-start(bf16[4,96,384]{2,1,0:T(8,128)(2,1)S(1)} %get-tuple-element.75.refs_2_), channel_id=1, source_target_pairs={{0,2},{1,3},{2,0},{3,1},{4,6},{5,7},{6,4},{7,5},{8,10},{9,11},{10,... | collective-permute-start | bytes 884744 | tf_op jit(solution)/shard_map/ppermute | solution.py:446
  33.7 12.8 %collective-permute-start.14 = (bf16[4,96,384]{2,1,0:T(8,128)(2,1)S(1)}, bf16[4,96,384]{2,1,0:T(8,128)(2,1)S(1)}, u32[]{:S(2)}, u32[]{:S(2)}) collective-permute-start(bf16[4,96,384]{2,1,0:T(8,128)(2,1)S(1)} %collective-permute-done.9.refs_3_), channel_id=1, source_target_pairs={{0,2},{1,3},{2,0},{3,1},{4,6},{5,7},{6,4},{7,5},{8,10},{9,11},{10,... | collective-permute-start | bytes 884744 | tf_op jit(solution)/shard_map/ppermute | solution.py:446
  35.2 10.5 %collective-permute-start.11 = (bf16[4,96,128]{2,1,0:T(8,128)(2,1)S(1)}, bf16[4,96,128]{2,1,0:T(8,128)(2,1)S(1)}, u32[]{:S(2)}, u32[]{:S(2)}) collective-permute-start(bf16[4,96,128]{2,1,0:T(8,128)(2,1)S(1)} %get-tuple-element.77.refs_3_), channel_id=1, source_target_pairs={{0,8},{4,12},{8,0},{12,4},{16,24},{20,28},{24,16},{28,20},{1,9},{5... | collective-permute-start | bytes 294920 | tf_op jit(solution)/shard_map/ppermute | solution.py:446
  36.6 4.6 %collective-permute-start.8 = (f32[16,128]{1,0:T(8,128)S(1)}, f32[16,128]{1,0:T(8,128)S(1)}, u32[]{:S(2)}, u32[]{:S(2)}) collective-permute-start(f32[16,128]{1,0:T(8,128)S(1)} %get-tuple-element.73.refs_3_), channel_id=1, source_target_pairs={{0,16},{4,20},{8,24},{12,28},{16,0},{20,4},{24,8},{28,12},{1,17},{... | collective-permute-start | bytes 24584 | tf_op jit(solution)/shard_map/ppermute | solution.py:446
  45.7 13.2 %collective-permute-start.16 = (bf16[768,384]{1,0:T(8,128)(2,1)S(1)}, bf16[768,384]{1,0:T(8,128)(2,1)S(1)}, u32[]{:S(2)}, u32[]{:S(2)}) collective-permute-start(bf16[768,384]{1,0:T(8,128)(2,1)S(1)} %get-tuple-element.80.refs_3_), channel_id=1, source_target_pairs={{0,1},{1,0},{2,3},{3,2},{4,5},{5,4},{6,7},{7,6},{8,9},{9,8},{10,11... | collective-permute-start | bytes 1769480 | tf_op jit(solution)/shard_map/ppermute | solution.py:446
  46.6 12.3 %collective-permute-start.17 = (bf16[768,384]{1,0:T(8,128)(2,1)S(1)}, bf16[768,384]{1,0:T(8,128)(2,1)S(1)}, u32[]{:S(2)}, u32[]{:S(2)}) collective-permute-start(bf16[768,384]{1,0:T(8,128)(2,1)S(1)} %place_kernel.1.refs_2_.refs_7_), channel_id=1, source_target_pairs={{0,1},{1,0},{2,3},{3,2},{4,5},{5,4},{6,7},{7,6},{8,9},{9,8},{10,11... | collective-permute-start | bytes 1769480 | tf_op jit(solution)/shard_map/ppermute | solution.py:446
  47.1 3.6 %collective-permute-start.10 = (f32[8,128]{1,0:T(8,128)S(1)}, f32[8,128]{1,0:T(8,128)S(1)}, u32[]{:S(2)}, u32[]{:S(2)}) collective-permute-start(f32[8,128]{1,0:T(8,128)S(1)} %get-tuple-element.76.refs_5_.refs_0_), channel_id=1, source_target_pairs={{0,4},{4,0},{8,12},{12,8},{16,20},{20,16},{24,28},{28,24},{1,5},{5... | collective-permute-start | bytes 12296 | tf_op jit(solution)/shard_map/ppermute | solution.py:446
  50.7 3.6 %collective-permute-start.12 = (f32[8,128]{1,0:T(8,128)S(1)}, f32[8,128]{1,0:T(8,128)S(1)}, u32[]{:S(2)}, u32[]{:S(2)}) collective-permute-start(f32[8,128]{1,0:T(8,128)S(1)} %add_kernel.4.refs_0_), channel_id=1, source_target_pairs={{0,8},{4,12},{8,0},{12,4},{16,24},{20,28},{24,16},{28,20},{1,9},{5... | collective-permute-start | bytes 12296 | tf_op jit(solution)/shard_map/ppermute | solution.py:446
  54.3 4.5 %collective-permute-start.15 = (f32[8,128]{1,0:T(8,128)S(1)}, f32[8,128]{1,0:T(8,128)S(1)}, u32[]{:S(2)}, u32[]{:S(2)}) collective-permute-start(f32[8,128]{1,0:T(8,128)S(1)} %add_kernel.5.refs_0_), channel_id=1, source_target_pairs={{0,16},{4,20},{8,24},{12,28},{16,0},{20,4},{24,8},{28,12},{1,17},{... | collective-permute-start | bytes 12296 | tf_op jit(solution)/shard_map/ppermute | solution.py:446
  68.8 14.0 %collective-permute-start.19 = (bf16[1792,128]{1,0:T(8,128)(2,1)S(1)}, bf16[1792,128]{1,0:T(8,128)(2,1)S(1)}, u32[]{:S(2)}, u32[]{:S(2)}) collective-permute-start(bf16[1792,128]{1,0:T(8,128)(2,1)S(1)} %get-tuple-element.87.refs_1_), channel_id=1, source_target_pairs={{0,2},{1,3},{2,0},{3,1},{4,6},{5,7},{6,4},{7,5},{8,10},{9,11},{10,... | collective-permute-start | bytes 1376264 | tf_op jit(solution)/shard_map/ppermute | solution.py:446
  69.3 12.9 %collective-permute-start.22 = (bf16[1056,128]{1,0:T(8,128)(2,1)S(1)}, bf16[1056,128]{1,0:T(8,128)(2,1)S(1)}, u32[]{:S(2)}, u32[]{:S(2)}) collective-permute-start(bf16[1056,128]{1,0:T(8,128)(2,1)S(1)} %get-tuple-element.90.refs_1_), channel_id=1, source_target_pairs={{0,2},{1,3},{2,0},{3,1},{4,6},{5,7},{6,4},{7,5},{8,10},{9,11},{10,... | collective-permute-start | bytes 811016 | tf_op jit(solution)/shard_map/ppermute | solution.py:446
  70.9 15.3 %collective-permute-start.21 = (bf16[1056,128]{1,0:T(8,128)(2,1)S(1)}, bf16[1056,128]{1,0:T(8,128)(2,1)S(1)}, u32[]{:S(2)}, u32[]{:S(2)}) collective-permute-start(bf16[1056,128]{1,0:T(8,128)(2,1)S(1)} %get-tuple-element.90.refs_1_), channel_id=1, source_target_pairs={{0,1},{1,0},{2,3},{3,2},{4,5},{5,4},{6,7},{7,6},{8,9},{9,8},{10,11... | collective-permute-start | bytes 811016 | tf_op jit(solution)/shard_map/ppermute | solution.py:446
  82.3 6.5 %collective-permute-start.23 = (bf16[1056,128]{1,0:T(8,128)(2,1)S(1)}, bf16[1056,128]{1,0:T(8,128)(2,1)S(1)}, u32[]{:S(2)}, u32[]{:S(2)}) collective-permute-start(bf16[1056,128]{1,0:T(8,128)(2,1)S(1)} %collective-permute-done.22.refs_5_), channel_id=1, source_target_pairs={{0,1},{1,0},{2,3},{3,2},{4,5},{5,4},{6,7},{7,6},{8,9},{9,8},{10,11... | collective-permute-start | bytes 811016 | tf_op jit(solution)/shard_map/ppermute | solution.py:446
  82.3 19.2 %collective-permute-start.18 = (bf16[1792,128]{1,0:T(8,128)(2,1)S(1)}, bf16[1792,128]{1,0:T(8,128)(2,1)S(1)}, u32[]{:S(2)}, u32[]{:S(2)}) collective-permute-start(bf16[1792,128]{1,0:T(8,128)(2,1)S(1)} %get-tuple-element.87.refs_1_), channel_id=1, source_target_pairs={{0,1},{1,0},{2,3},{3,2},{4,5},{5,4},{6,7},{7,6},{8,9},{9,8},{10,11... | collective-permute-start | bytes 1376264 | tf_op jit(solution)/shard_map/ppermute | solution.py:446
  82.8 18.7 %collective-permute-start.20 = (bf16[1792,128]{1,0:T(8,128)(2,1)S(1)}, bf16[1792,128]{1,0:T(8,128)(2,1)S(1)}, u32[]{:S(2)}, u32[]{:S(2)}) collective-permute-start(bf16[1792,128]{1,0:T(8,128)(2,1)S(1)} %collective-permute-done.19.refs_3_), channel_id=1, source_target_pairs={{0,1},{1,0},{2,3},{3,2},{4,5},{5,4},{6,7},{7,6},{8,9},{9,8},{10,11... | collective-permute-start | bytes 1376264 | tf_op jit(solution)/shard_map/ppermute | solution.py:446
  85.5 9.5 %collective-permute-start.25 = (bf16[4,96,384]{2,1,0:T(8,128)(2,1)S(1)}, bf16[4,96,384]{2,1,0:T(8,128)(2,1)S(1)}, u32[]{:S(2)}, u32[]{:S(2)}) collective-permute-start(bf16[4,96,384]{2,1,0:T(8,128)(2,1)S(1)} %get-tuple-element.95), channel_id=1, source_target_pairs={{0,4},{4,0},{8,12},{12,8},{16,20},{20,16},{24,28},{28,24},{1,5},{5... | collective-permute-start | bytes 884744 | tf_op jit(solution)/shard_map/ppermute | solution.py:446
  95.1 5.7 %collective-permute-start.27 = (bf16[2,96,384]{2,1,0:T(8,128)(2,1)S(1)}, bf16[2,96,384]{2,1,0:T(8,128)(2,1)S(1)}, u32[]{:S(2)}, u32[]{:S(2)}) collective-permute-start(bf16[2,96,384]{2,1,0:T(8,128)(2,1)S(1)} %get-tuple-element.96.refs_2_), channel_id=1, source_target_pairs={{0,8},{4,12},{8,0},{12,4},{16,24},{20,28},{24,16},{28,20},{1,9},{5... | collective-permute-start | bytes 442376 | tf_op jit(solution)/shard_map/ppermute | solution.py:446
  95.7 3.6 %collective-permute-start.24 = (f32[2,768]{1,0:T(2,128)S(1)}, f32[2,768]{1,0:T(2,128)S(1)}, u32[]{:S(2)}, u32[]{:S(2)}) collective-permute-start(f32[2,768]{1,0:T(2,128)S(1)} %get-tuple-element.92.refs_5_.refs_2_.refs_0_), channel_id=1, source_target_pairs={{0,4},{4,0},{8,12},{12,8},{16,20},{20,16},{24,28},{28,24},{1,5},{5... | collective-permute-start | bytes 18440 | tf_op jit(solution)/shard_map/ppermute | solution.py:446
  99.3 4.5 %collective-permute-start.26 = (f32[2,768]{1,0:T(2,128)S(1)}, f32[2,768]{1,0:T(2,128)S(1)}, u32[]{:S(2)}, u32[]{:S(2)}) collective-permute-start(f32[2,768]{1,0:T(2,128)S(1)} %add_kernel.6.refs_2_.refs_0_), channel_id=1, source_target_pairs={{0,8},{4,12},{8,0},{12,4},{16,24},{20,28},{24,16},{28,20},{1,9},{5... | collective-permute-start | bytes 18440 | tf_op jit(solution)/shard_map/ppermute | solution.py:446
  100.9 6.9 %collective-permute-start.29 = (bf16[1,96,384]{2,1,0:T(8,128)(2,1)S(1)}, bf16[1,96,384]{2,1,0:T(8,128)(2,1)S(1)}, u32[]{:S(2)}, u32[]{:S(2)}) collective-permute-start(bf16[1,96,384]{2,1,0:T(8,128)(2,1)S(1)} %get-tuple-element.98.refs_2_), channel_id=1, source_target_pairs={{0,16},{4,20},{8,24},{12,28},{16,0},{20,4},{24,8},{28,12},{1,17},{... | collective-permute-start | bytes 221192 | tf_op jit(solution)/shard_map/ppermute | solution.py:446
  105.3 4.6 %collective-permute-start.28 = (f32[2,768]{1,0:T(2,128)S(1)}, f32[2,768]{1,0:T(2,128)S(1)}, u32[]{:S(2)}, u32[]{:S(2)}) collective-permute-start(f32[2,768]{1,0:T(2,128)S(1)} %add_kernel.7.refs_4_), channel_id=1, source_target_pairs={{0,16},{4,20},{8,24},{12,28},{16,0},{20,4},{24,8},{28,12},{1,17},{... | collective-permute-start | bytes 18440 | tf_op jit(solution)/shard_map/ppermute | solution.py:446
  (17 other events, 92.4 us)

commit v4 on v3

v4 whole, which is shorter than its diff:
```python
import functools

import jax
import jax.numpy as jnp
from jax import lax
from jax.experimental import pallas as pl
from jax.experimental.pallas import tpu as pltpu
from jax.sharding import PartitionSpec as P

KERNEL_WIDTH = 3
DILATION_BINS = 9
WIN = 1024
STEP = 10

NORM_EPS = 1e-05
ADAM_EPS = 1e-08
BETA_ONE = 0.9
BETA_TWO = 0.999
RATE_WEIGHT = 0.05
RATE_NORM = 0.5
DECAY_WEIGHT = 0.01

LANES = 128
EDGE = 16
RIM = 2 * EDGE
SUMS = 48
GELU_A = 0.7978845608028654
GELU_B = 0.044715
SHIFTS = [(j - KERNEL_WIDTH // 2) * DILATION_BINS for j in range(KERNEL_WIDTH)]
ROW_DIMS = (((0,), (0,)), ((), ()))
LANE_DIMS = (((1,), (1,)), ((), ()))
F32, BF16 = jnp.float32, jnp.bfloat16


def call(body, outs, args, scratch=(), smem=(), away=(), after=(), sems=0, away_outs=(), limit=16):
    spaces = [pltpu.SMEM if k in smem else pltpu.VMEM for k in range(len(args))]
    spaces = [pltpu.HBM if k in away else space for k, space in enumerate(spaces)]
    spaces += [pl.ANY] * len(after)

    args = [
        pltpu.with_memory_space_constraint(x, pltpu.HBM) if k in away else x
        for k, x in enumerate(args)
    ]

    def kernel(*refs):
        body(*refs[: len(args)], *refs[len(spaces) :])

    return pl.pallas_call(
        kernel,
        out_shape=[jax.ShapeDtypeStruct(s, t) for s, t in outs],
        in_specs=[pl.BlockSpec(memory_space=s) for s in spaces],
        out_specs=[
            pl.BlockSpec(memory_space=pltpu.HBM if k in away_outs else pltpu.VMEM)
            for k in range(len(outs))
        ],
        scratch_shapes=[pltpu.VMEM(s, t) for s, t in scratch]
        + [pltpu.SemaphoreType.DMA((sems,))] * (sems > 0),
        compiler_params=pltpu.CompilerParams(vmem_limit_bytes=limit * 2**20),
        cost_estimate=pl.CostEstimate(flops=1, bytes_accessed=1, transcendentals=0),
        name=getattr(body, "func", body).__name__,
    )(*args, *after)


def up_to(size, step):
    return -(-size // step) * step


def split_three(v):
    high = v.astype(BF16).astype(F32)
    rest = v - high
    middle = rest.astype(BF16).astype(F32)
    return high, middle, rest - middle


def gelu_and_slope(v):
    square = v * v
    t = jnp.tanh(v * (GELU_A + (GELU_A * GELU_B) * square))
    half = 0.5 * (1.0 + t)
    slope = half + (0.5 * v) * (1.0 - t * t) * (GELU_A + (3.0 * GELU_A * GELU_B) * square)
    return v * half, slope


def reach_of(first, count, shift, start, bin_count):
    here = first + lax.broadcasted_iota(jnp.int32, (count, LANES), 0)
    there = here + shift
    inside = (here >= 0) & (here < bin_count) & (there >= 0) & (there < bin_count)
    return inside & (((here - start) >> 10) == ((there - start) >> 10))


def folds(depth, slim):
    return 3 * (LANES - slim) == slim and depth % 32 == 0


def fold_rows(block):
    rows, slim = block.shape
    quarter, width = rows // 4, LANES - slim
    side = [block[3 * quarter :, p * width : (p + 1) * width] for p in range(3)]
    return jnp.concatenate([block[: 3 * quarter], jnp.concatenate(side, axis=0)], axis=1)


def unfold_rows(block, slim):
    quarter, width = block.shape[0] // 3, LANES - slim
    side = [block[p * quarter : (p + 1) * quarter, slim:] for p in range(3)]
    side.append(jnp.zeros((quarter, width), block.dtype))
    lane = lax.broadcasted_iota(jnp.int32, block.shape, 1)
    return jnp.concatenate([jnp.where(lane < slim, block, 0.0), jnp.concatenate(side, axis=1)], axis=0)


def first_kernel(
    x_hbm, cot_hbm, conv_hbm, point_hbm, x_ref, weight_ref, near_ref, rim_ref, edge_ref, conv_ref, point_ref, sum_ref, sems
):
    rows, width = x_ref.shape
    tiles = width // LANES
    depth, slim = conv_ref.shape[1:]
    chunks = sems.shape[0] - 4
    chunk = rows // chunks
    copies = [
        pltpu.make_async_copy(conv_hbm, conv_ref, sems.at[0]),
        pltpu.make_async_copy(point_hbm, point_ref, sems.at[1]),
        pltpu.make_async_copy(cot_hbm.at[pl.ds(0, EDGE)], edge_ref.at[0], sems.at[2]),
        pltpu.make_async_copy(cot_hbm.at[pl.ds(rows - EDGE, EDGE)], edge_ref.at[1], sems.at[3]),
    ]
    for k in range(chunks):
        part = pl.ds(k * chunk, chunk)
        copies.append(pltpu.make_async_copy(x_hbm.at[part], x_ref.at[part], sems.at[4 + k]))
    for copy in copies:
        copy.start()
    weight_ref[...] = jnp.zeros_like(weight_ref)
    near_ref[...] = jnp.zeros_like(near_ref)
    sum_ref[...] = jnp.zeros_like(sum_ref)
    copies[0].wait()
    for j in range(KERNEL_WIDTH):
        if folds(depth, slim):
            weight_ref[0, :, j * LANES : (j + 1) * LANES] = fold_rows(conv_ref[j]).astype(BF16)
        else:
            weight_ref[0, :, j * LANES : j * LANES + slim] = conv_ref[j].astype(BF16)
    copies[1].wait()
    near_ref[SUMS : SUMS + depth, :slim] = point_ref[...].T.astype(BF16)

    def step(k, carry):
        v = x_ref[pl.ds(pl.multiple_of(k * 32, 32), 32), :].astype(F32)
        v = v.reshape(4, 8, width)
        return carry[0] + v.sum(0), carry[1] + (v * v).sum(0)

    totals = (jnp.zeros((8, width), F32),) * 2
    for k in range(chunks):
        copies[4 + k].wait()
        totals = lax.fori_loop(
            k * chunk // 32, (k + 1) * chunk // 32, step, totals, unroll=chunk // 32
        )
    for stat, total in enumerate(totals):
        total = jnp.sum(total, 0, keepdims=True)
        for k in range(tiles):
            row = stat * tiles + k
            sum_ref[row : row + 1, :] = total[:, k * LANES : (k + 1) * LANES]
    put_sums(near_ref, sum_ref[...])
    copies[2].wait()
    copies[3].wait()
    for side in range(2):
        begin = (rows - RIM) * side
        rim_ref[side, :RIM, :] = x_ref[begin : begin + RIM, :]
        rim_ref[side, RIM:, :] = edge_ref[side]


def put_sums(ref, value):
    for p, part in enumerate(split_three(value)):
        ref[p * 16 : (p + 1) * 16, :] = part.astype(BF16)


def get_sums(ref):
    return sum(ref[p * 16 : (p + 1) * 16, :].astype(F32) for p in range(3))


def act_kernel(
    x_ref, cot_hbm, rim_ref, one_ref, two_ref, norm_ref, hid_ref, vec_ref, cot_ref, sems, *, bin_count
):
    copy = pltpu.make_async_copy(cot_hbm, cot_ref, sems.at[0])
    copy.start()
    rows, width = x_ref.shape
    tiles = width // LANES
    total = get_sums(one_ref) + get_sums(two_ref)
    for k in range(tiles):
        lanes = slice(k * LANES, (k + 1) * LANES)
        mean = total[k : k + 1, :] / bin_count
        square = total[tiles + k : tiles + k + 1, :] / bin_count
        root = lax.rsqrt(square - mean * mean + NORM_EPS)
        gain = root * norm_ref[0:1, lanes]
        vec_ref[0:1, lanes] = root
        vec_ref[1:2, lanes] = -mean * root
        vec_ref[2:3, lanes] = gain
        vec_ref[3:4, lanes] = norm_ref[1:2, lanes] - mean * gain

    gain, bias = vec_ref[2:3, :], vec_ref[3:4, :]
    for side, at in enumerate((0, RIM + rows)):
        for k in range(0, RIM, 16):
            hidden, _ = gelu_and_slope(rim_ref[side, k : k + 16, :].astype(F32) * gain + bias)
            hid_ref[at + k : at + k + 16, :] = hidden.astype(BF16)

    def step(k, carry):
        at = pl.multiple_of(k * 16, 16)
        v = x_ref[pl.ds(at, 16), :].astype(F32) * vec_ref[2:3, :] + vec_ref[3:4, :]
        hid_ref[pl.ds(pl.multiple_of(at + RIM, 16), 16), :] = gelu_and_slope(v)[0].astype(BF16)
        return carry

    lax.fori_loop(0, rows // 16, step, 0, unroll=2)
    copy.wait()


def place(pieces, relatives, stack, own, slim):
    depth = stack.shape[1]
    at = 0
    for piece in pieces:
        for k in range(piece.shape[0]):
            block = piece[k].astype(F32)
            for j in range(KERNEL_WIDTH):
                part = block[:, j * LANES : (j + 1) * LANES]
                if folds(depth, slim):
                    part = unfold_rows(part, slim)
                stack[own ^ relatives[at], :, j * LANES : (j + 1) * LANES] = part.astype(stack.dtype)
            at += 1
    return stack[...].reshape(-1, stack.shape[2]).astype(BF16)


def place_kernel(*refs, relatives, slim):
    pieces, (out_ref, stack) = refs[:-2], refs[-2:]
    out_ref[...] = place(pieces, relatives, stack, lax.axis_index("seq"), slim)


def mask_kernel(start_ref, ahead_ref, back_ref):
    rows = back_ref.shape[1]
    first = lax.axis_index("seq") * rows
    for j, shift in enumerate(SHIFTS):
        for begin in range(0, rows + RIM, 96):
            count = min(96, rows + RIM - begin)
            mask = reach_of(first + begin - EDGE, count, shift, start_ref[0], rows * lax.axis_size("seq"))
            ahead_ref[j, begin : begin + count, :] = jnp.where(mask, 1.0, 0.0)
        for begin in range(0, rows, 128):
            back_ref[j, begin : begin + 128, :] = ahead_ref[
                j, EDGE + begin - shift : EDGE + begin - shift + 128, :
            ]


def slope_kernel(x_ref, vec_ref, slope_ref):
    def step(k, carry):
        at = pl.ds(pl.multiple_of(k * 16, 16), 16)
        v = x_ref[at, :].astype(F32) * vec_ref[2:3, :] + vec_ref[3:4, :]
        slope_ref[at, :] = gelu_and_slope(v)[1]
        return carry

    lax.fori_loop(0, x_ref.shape[0] // 16, step, 0, unroll=2)


def conv_kernel(mask_ref, hid_ref, *refs, relatives, slim):
    pieces, (weight_ref, out_ref, sum_ref, all_ref, stack, prod) = refs[:-6], refs[-6:]
    size = all_ref.shape[0] // 2
    for k, piece in enumerate(pieces):
        all_ref[k * size : (k + 1) * size] = piece[...]
    rows = hid_ref.shape[0] - 2 * RIM
    weight_ref[...] = place(pieces, relatives, stack, lax.axis_index("seq"), slim)
    for at in range(0, weight_ref.shape[1], 256):
        part = slice(at, min(at + 256, weight_ref.shape[1]))
        prod[:, part] = jnp.dot(hid_ref[...], weight_ref[:, part], preferred_element_type=F32)

    def rows_of(begin, count):
        value = 0.0
        for j, shift in enumerate(SHIFTS):
            part = prod[begin + EDGE + shift : begin + EDGE + shift + count, j * LANES : (j + 1) * LANES]
            value = value + mask_ref[j, begin : begin + count, :] * part
        out_ref[begin : begin + count, :] = value
        return value

    rows_of(0, EDGE)
    rows_of(EDGE + rows, EDGE)
    one = two = jnp.zeros((8, LANES), F32)
    step = 128
    for k in range(rows // step):
        value = rows_of(EDGE + k * step, step).reshape(step // 8, 8, LANES)
        one = one + value.sum(0)
        two = two + (value * value).sum(0)
    sum_ref[...] = jnp.zeros_like(sum_ref)
    sum_ref[0:1, :] = jnp.sum(one, 0, keepdims=True)
    sum_ref[1:2, :] = jnp.sum(two, 0, keepdims=True)


def upstream_kernel(cot_ref, rim_ref, one_ref, two_ref, up_ref, point_ref, stack, *, relatives):
    rows = cot_ref.shape[0]
    depth = stack.shape[1]
    own = lax.axis_index("seq")
    count = len(relatives) // 2
    for k, relative in enumerate(relatives):
        piece = (one_ref, two_ref)[k // count]
        at = SUMS + (k % count) * up_to(depth, 16)
        stack[own ^ relative] = piece[at : at + depth, :].astype(stack.dtype)
    point_ref[...] = stack[...].reshape(point_ref.shape).astype(BF16)
    for side, at in enumerate((0, EDGE + rows)):
        up_ref[at : at + EDGE, :] = jnp.dot(
            rim_ref[side, RIM:, :], point_ref[...], preferred_element_type=F32
        )
    up_ref[EDGE : EDGE + rows, :] = jnp.dot(
        cot_ref[...], point_ref[...], preferred_element_type=F32
    )


def mid_kernel(
    total_ref, conv_ref, up_ref, norm_ref, hid_ref, d_ref, cen_ref, sent_ref, vec_ref, *, bin_count
):
    rows = hid_ref.shape[0]
    slim = norm_ref.shape[1]
    total = total_ref[...]
    mean = total[0:1] / bin_count
    root = lax.rsqrt(total[1:2] / bin_count - mean * mean + NORM_EPS)
    vec_ref[...] = jnp.zeros_like(vec_ref)
    vec_ref[0:1, :] = root
    vec_ref[1:3, :slim] = norm_ref[...]
    gain, bias = vec_ref[1:2, :], vec_ref[2:3, :]

    def rows_of(begin, count):
        centered = (conv_ref[pl.ds(begin, count), :] - mean) * root
        hidden, slope = gelu_and_slope(centered * gain + bias)
        d = up_ref[pl.ds(begin, count), :] * slope
        cen_ref[pl.ds(begin, count), :] = centered
        d_ref[pl.ds(begin, count), :] = d
        return centered, hidden, d

    rows_of(0, EDGE)
    rows_of(EDGE + rows, EDGE)
    step = 64

    def body(i, carry):
        begin = pl.multiple_of(EDGE + i * step, 16)
        centered, hidden, d = rows_of(begin, step)
        hid_ref[pl.ds(pl.multiple_of(i * step, 16), step), :] = hidden.astype(BF16)
        d = d.reshape(step // 8, 8, LANES)
        return carry[0] + (d * centered.reshape(d.shape)).sum(0), carry[1] + d.sum(0)

    zero = jnp.zeros((8, LANES), F32)
    gain_sum, bias_sum = lax.fori_loop(0, rows // step, body, (zero, zero), unroll=2)
    gain_sum = jnp.sum(gain_sum, 0, keepdims=True)
    bias_sum = jnp.sum(bias_sum, 0, keepdims=True)
    for d in range(sent_ref.shape[0]):
        sent_ref[d, 0:1, :] = gain_sum
        sent_ref[d, 1:2, :] = bias_sum


def conv_back_kernel(got_ref, vec_ref, d_ref, cen_ref, grad_ref, total_ref, grad, *, bin_count, slim):
    total = got_ref[0]
    for s in range(1, got_ref.shape[0]):
        total = total + got_ref[s]
    total_ref[...] = total
    scale = vec_ref[0:1, :] * vec_ref[1:2, :]
    pull, level = total[0:1] / bin_count, total[1:2] / bin_count
    count = d_ref.shape[0]
    for begin in range(0, count, 96):
        part = slice(begin, min(begin + 96, count))
        grad[part, :] = scale * (d_ref[part, :] - level - cen_ref[part, :] * pull)
    if folds(count, slim):
        grad_ref[...] = fold_rows(grad[:, :slim]).astype(BF16)
    else:
        grad_ref[...] = grad[...].astype(BF16)


def out_kernel(x_ref, *refs):
    parts, (out_ref, token_ref, hidden, point) = refs[:-4], refs[-4:]
    token_ref[...] = jnp.zeros_like(token_ref)
    rows = x_ref.shape[0]
    for r, part in enumerate(parts):
        hidden[:, r * LANES : (r + 1) * LANES] = part[:rows, :]
        point[:, r * LANES : (r + 1) * LANES] = part[rows:, :]
    for at in range(0, x_ref.shape[1], 256):
        part = slice(at, at + 256)
        branch = lax.dot_general(
            hidden[...], point[part, :], LANE_DIMS, preferred_element_type=F32
        )
        out_ref[:, part] = (x_ref[:, part].astype(F32) + branch).astype(BF16)


def halve(blocks, kept_ref, sent_ref, high):
    for k in range(kept_ref.shape[0]):
        kept_ref[k] = blocks(2 * k + high)
        sent_ref[k] = blocks(2 * k + 1 - high).astype(BF16)


def terms_of(part, grad, term_ref, at, mask_ref):
    rows = term_ref.shape[0]
    step = 64
    count = part.shape[0]
    grad[:count, :] = part[...].astype(F32)
    if count < grad.shape[0]:
        quarter = count // 3
        width = LANES // 4
        side = [grad[p * quarter : (p + 1) * quarter, 3 * width :] for p in range(3)]
        grad[count:, :] = jnp.concatenate(side + [jnp.zeros((quarter, width), F32)], axis=1)
    for j, shift in enumerate(SHIFTS):
        lanes = slice(at + j * LANES, at + (j + 1) * LANES)
        for begin in range(0, rows, step):
            value = grad[EDGE + begin - shift : EDGE + begin - shift + step, :]
            value = value * mask_ref[j, begin : begin + step, :]
            term_ref[begin : begin + step, lanes] = value.astype(BF16)


def weight_grad_kernel(
    mask_ref, part_ref, hid_ref, cot_ref, mid_ref, term_ref, kept_ref, sent_ref, grad, full, *, depth, slim
):
    rows = term_ref.shape[0]
    terms_of(part_ref, grad, term_ref, 0, mask_ref)
    taps = lax.dot_general(
        hid_ref[RIM : RIM + rows, :], term_ref[...], ROW_DIMS, preferred_element_type=F32
    )
    point = lax.dot_general(cot_ref[...], mid_ref[...], ROW_DIMS, preferred_element_type=F32)
    parts = [taps[:, j * LANES : j * LANES + slim] for j in range(KERNEL_WIDTH)] + [point[:, :slim]]
    full[...] = jnp.concatenate(parts, axis=1)
    high = lax.axis_index("seq") % 2
    halve(lambda k: full[pl.ds(pl.multiple_of(k * depth, 8), depth), :], kept_ref, sent_ref, high)


def fold_kernel(old_ref, got_ref, kept_ref, sent_ref, *, reach):
    high = (lax.axis_index("seq") // reach) % 2
    halve(lambda k: old_ref[k] + got_ref[k].astype(F32), kept_ref, sent_ref, high)


def adamw(weights_old, first_moment_state, second_mom, gradient, step_rate, decay_rate):
    first_next = BETA_ONE * first_moment_state + (1.0 - BETA_ONE) * gradient
    second_next = BETA_TWO * second_mom + (1.0 - BETA_TWO) * gradient * gradient
    corrected = (
        first_next
        / (1.0 - BETA_ONE**STEP)
        / (jnp.sqrt(second_next / (1.0 - BETA_TWO**STEP)) + ADAM_EPS)
    )
    weights_new = weights_old - step_rate * (corrected + decay_rate * weights_old)
    return (first_next, second_next, weights_new)


def weight_step_kernel(old_ref, got_ref, total_ref, *refs):
    conv, point, mid, outs = refs[:3], refs[3:6], refs[6:9], refs[9:]
    slim = conv[0].shape[2]
    both = old_ref[0] + got_ref[0].astype(F32)
    for j in range(KERNEL_WIDTH):
        grad = both[:, j * slim : (j + 1) * slim]
        new = adamw(*(ref[j] for ref in conv), grad, RATE_WEIGHT, DECAY_WEIGHT)
        for ref, value in zip(outs[:3], new):
            ref[j] = value
    grad = both[:, KERNEL_WIDTH * slim :].T
    new = adamw(*(ref[...] for ref in point), grad, RATE_WEIGHT, DECAY_WEIGHT)
    for ref, value in zip(outs[3:6], new):
        ref[...] = value
    new = adamw(*(ref[...] for ref in mid), total_ref[:, :slim], RATE_NORM, 0.0)
    for ref, value in zip(outs[6:], new):
        ref[...] = value


def first_half_kernel(mask_ref, own_ref, hid_ref, point_ref, *refs):
    up_ref, both_ref, term, weight, grad = refs[-5:]
    count = (len(refs) - 5 + 1) // 2
    grads, weights = refs[: count - 1], refs[count - 1 : -5]
    rows = up_ref.shape[0]
    both_ref[:rows, :] = hid_ref[...]
    both_ref[rows:, :] = point_ref[...]
    wide = KERNEL_WIDTH * LANES
    term[:, :wide] = own_ref[...]
    for r, part in enumerate(grads):
        terms_of(part, grad, term, (r + 1) * wide, mask_ref)
    for r, piece in enumerate(weights):
        weight[:, r * wide : (r + 1) * wide] = piece[...]
    for at in range(0, up_ref.shape[1], 256):
        part = slice(at, at + 256)
        up_ref[:, part] = lax.dot_general(
            term[...], weight[part, :], LANE_DIMS, preferred_element_type=F32
        )


def second_half_kernel(mask_ref, x_ref, slope_ref, vec_ref, part_ref, *refs):
    d_ref, sum_ref, term, weight, grad = refs[-5:]
    count = (len(refs) - 5) // 2
    grads, weights = refs[:count], refs[count:-5]
    rows, width = x_ref.shape
    wide = KERNEL_WIDTH * LANES
    for r, part in enumerate(grads):
        terms_of(part, grad, term, r * wide, mask_ref)
    for r, piece in enumerate(weights):
        weight[:, r * wide : (r + 1) * wide] = piece[...]
    for at in range(0, width, 256):
        part = slice(at, at + 256)
        up = lax.dot_general(term[...], weight[part, :], LANE_DIMS, preferred_element_type=F32)
        d = (up + part_ref[:, part]) * slope_ref[:, part]
        d_ref[:, part] = d
        centered = x_ref[:, part].astype(F32) * vec_ref[0:1, part] + vec_ref[1:2, part]
        sum_ref[0:1, part] = jnp.sum(d * centered, 0, keepdims=True)
        sum_ref[1:2, part] = jnp.sum(d, 0, keepdims=True)


def final_kernel(x_ref, cot_ref, d_ref, vec_ref, one_ref, two_ref, *refs, bin_count):
    norms, out_hbm, news, (out_ref, sems) = refs[:3], refs[3], refs[4:-2], refs[-2:]
    rows, width = x_ref.shape
    total = one_ref[...] + two_ref[...]
    root, offset, scale = vec_ref[0:1, :], vec_ref[1:2, :], vec_ref[2:3, :]
    pull = scale * total[0:1] / bin_count
    slant = pull * root
    level = scale * total[1:2] / bin_count + pull * offset
    step = 16
    chunk = rows // sems.shape[0]

    def body(i, carry):
        at = pl.ds(pl.multiple_of(i * step, 16), step)
        value = x_ref[at, :].astype(F32) * slant + level
        out_ref[at, :] = cot_ref[at, :].astype(F32) + (d_ref[at, :] * scale - value)
        return carry

    sends = []
    for k in range(sems.shape[0]):
        lax.fori_loop(k * chunk // step, (k + 1) * chunk // step, body, 0, unroll=4)
        part = pl.ds(k * chunk, chunk)
        sends.append(pltpu.make_async_copy(out_ref.at[part], out_hbm.at[part], sems.at[k]))
        sends[-1].start()
    new = adamw(*(ref[...] for ref in norms), total, RATE_NORM, 0.0)
    for ref, value in zip(news, new):
        ref[...] = value
    for send in sends:
        send.wait()


def flip(axis, reach):
    return [(i, i ^ reach) for i in range(lax.axis_size(axis))]


def relatives_of(order):
    found = [0]
    for reach in order:
        found = found + [r ^ reach for r in found]
    return found


def descending(size):
    return [size >> k for k in range(1, size.bit_length())]


def round_kernel(weight_one, weight_two, one_ref, two_ref, *refs, count=0):
    rims, (weight_ref, out_ref), outs = refs[:count], refs[count : count + 2], refs[count + 2 :]
    size = weight_one.shape[0]
    weight_ref[:size] = weight_one[...]
    weight_ref[size:] = weight_two[...]
    put_sums(out_ref, get_sums(one_ref) + get_sums(two_ref))
    size = (out_ref.shape[0] - SUMS) // 2
    out_ref[SUMS : SUMS + size, :] = one_ref[SUMS : SUMS + size, :]
    out_ref[SUMS + size :, :] = two_ref[SUMS : SUMS + size, :]
    odd = lax.axis_index("seq") % 2
    if len(rims) == 1:
        outs[0][...] = rims[0][1 - odd]
        outs[1][...] = rims[0][odd]
    elif rims:
        outs[0][1 - odd] = rims[0][...]
        outs[0][odd] = rims[1][...]


def copy_kernel(*refs):
    count = len(refs) // 2
    for src, out in zip(refs[:count], refs[count:]):
        out[...] = src[...]


def copies(arrays, after):
    return call(copy_kernel, [(x.shape, x.dtype) for x in arrays], arrays, after=after)


def add_kernel(one_ref, two_ref, out_ref):
    out_ref[...] = one_ref[...] + two_ref[...]


def add(one, two, after=()):
    return call(add_kernel, [(one.shape, one.dtype)], [one, two], after=after)[0]


def swap(x, axis, reach):
    return lax.ppermute(x, axis, flip(axis, reach))


def gather_parts(x, reaches):
    parts = [x]
    for reach in reaches:
        parts += [swap(part, "ch", reach) for part in parts]
    return parts


def spread(copies, axes):
    return lax.all_to_all(copies, axes, 0, 0, tiled=True)


def shards(
    inputs,
    cotangent,
    starts,
    master_conv,
    first_conv,
    second_conv,
    master_point,
    first_point,
    second_point,
    norm_in,
    first_in,
    second_in,
    norm_mid,
    first_mid,
    second_mid,
):
    rows, width = inputs.shape
    seq_size, ch_size = lax.axis_size("seq"), lax.axis_size("ch")
    bin_count = rows * seq_size
    depth, slim = master_conv.shape[1:]
    tiles = width // LANES
    wide = KERNEL_WIDTH * LANES
    weight_order = descending(seq_size)
    sum_order = weight_order[::-1]
    last_order = weight_order[:1] + sum_order[:-1]
    point_order = weight_order[:1] + [1] + weight_order[1:-1]
    ch_order = descending(ch_size)
    ext = rows + 2 * EDGE

    rounds = len(weight_order)
    top, lower = ch_order[0], ch_order[1:]
    chunks = 4
    rim = (RIM + EDGE, width)
    packed = 3 * depth // 4 if folds(depth, slim) else depth
    inputs, weight, near, rims = call(
        first_kernel,
        [
            (inputs.shape, BF16),
            ((1, packed, wide), BF16),
            ((SUMS + up_to(depth, 16), LANES), BF16),
            ((2, *rim), BF16),
        ],
        [inputs, cotangent, master_conv, master_point],
        scratch=[
            ((2, EDGE, width), BF16),
            (master_conv.shape, F32),
            (master_point.shape, F32),
            ((16, LANES), F32),
        ],
        away=(0, 1, 2, 3),
        sems=4 + chunks,
    )
    pairs = [(i, i + 1) for i in range(1, seq_size - 1, 2)]
    for k in range(rounds):
        weight_got = swap(weight, "seq", weight_order[k])
        near_got = swap(near, "seq", point_order[k])
        if k < rounds - 1:
            outs = [
                ((2 * weight.shape[0], packed, wide), BF16),
                ((SUMS + (2 << k) * up_to(depth, 16), LANES), BF16),
            ]
            args = [weight, weight_got, near, near_got]
            if k == 0:
                weight, near, *rims = call(
                    functools.partial(round_kernel, count=1), outs + [(rim, BF16)] * 2, args + [rims]
                )
                rims = [
                    swap(rims[0], "seq", 1),
                    lax.ppermute(rims[1], "seq", pairs + [(j, i) for i, j in pairs]),
                ]
                ahead, back = call(
                    mask_kernel,
                    [((KERNEL_WIDTH, ext, LANES), F32), ((KERNEL_WIDTH, rows, LANES), F32)],
                    [starts],
                    smem=(0,),
                    after=[near],
                )
            elif k == 1:
                weight, near, rims = call(
                    functools.partial(round_kernel, count=2),
                    outs + [((2, *rim), BF16)],
                    args + rims,
                    after=[back],
                )
            else:
                weight, near = call(round_kernel, outs, args)
    hidden_in, vec_in, cotangent = call(
        functools.partial(act_kernel, bin_count=bin_count),
        [((rows + 2 * RIM, width), BF16), ((8, width), F32), (cotangent.shape, BF16)],
        [inputs, cotangent, rims, near, near_got, norm_in],
        away=(1,),
        sems=1,
    )

    stack_type = BF16 if depth % 16 == 0 else F32
    conv_own, conv_out, sums_mid, weight = call(
        functools.partial(
            conv_kernel, relatives=relatives_of(weight_order), slim=slim
        ),
        [
            ((width, wide), BF16),
            ((ext, LANES), F32),
            ((8, LANES), F32),
            ((seq_size, packed, wide), BF16),
        ],
        [ahead, hidden_in, weight, weight_got],
        scratch=[((seq_size, depth, wide), stack_type), ((rows + 2 * RIM, wide), F32)],
    )
    weight = swap(weight, "ch", top)
    upstream, point_own = call(
        functools.partial(upstream_kernel, relatives=relatives_of(point_order)),
        [((ext, LANES), F32), ((width, LANES), BF16)],
        [cotangent, rims, near, near_got],
        scratch=[((seq_size, depth, LANES), stack_type)],
        after=[sums_mid],
    )
    conv_near = gather_parts(conv_own, lower)
    total = sums_mid
    for k, reach in enumerate(sum_order):
        total = add(total, swap(total, "seq", reach), [upstream])
    (conv_far,) = call(
        functools.partial(place_kernel, relatives=relatives_of(weight_order), slim=slim),
        [((width, wide), BF16)],
        [weight],
        scratch=[((seq_size, depth, wide), stack_type)],
        after=[total],
    )
    hidden_mid, d_mid, centered, sent_back, vec_mid = call(
        functools.partial(mid_kernel, bin_count=bin_count),
        [
            ((rows, LANES), BF16),
            ((ext, LANES), F32),
            ((ext, LANES), F32),
            ((seq_size, 2, LANES), F32),
            ((8, LANES), F32),
        ],
        [total, conv_out, upstream, norm_mid],
        after=[conv_far, *conv_near[1:]],
    )
    got_back = spread(sent_back, "seq")
    grad_own, total_mid = call(
        functools.partial(conv_back_kernel, bin_count=bin_count, slim=slim),
        [((3 * ext // 4 if folds(ext, slim) else ext, LANES), BF16), ((2, LANES), F32)],
        [got_back, vec_mid, d_mid, centered],
        scratch=[((ext, LANES), F32)],
    )
    grad_near = gather_parts(grad_own, lower)
    grad_far = swap(grad_own, "ch", top)
    conv_far = gather_parts(copies([conv_far], [grad_own])[0], lower)
    half = seq_size // 2
    terms, kept, sent = call(
        functools.partial(weight_grad_kernel, depth=depth, slim=slim),
        [
            ((rows, wide), BF16),
            ((half, depth, 4 * slim), F32),
            ((half, depth, 4 * slim), BF16),
        ],
        [back, grad_own, hidden_in, cotangent, hidden_mid],
        scratch=[((ext, LANES), F32), ((width, 4 * slim), F32)],
    )
    side = ch_size // 2 * wide
    up_part, both = call(
        first_half_kernel,
        [((rows, width), F32), ((rows + width, LANES), BF16)],
        [back, terms, hidden_mid, point_own, *grad_near[1:], *conv_near],
        scratch=[((rows, side), BF16), ((width, side), BF16), ((ext, LANES), F32)],
    )
    (slope_in,) = call(slope_kernel, [((rows, width), F32)], [inputs, vec_in], after=[up_part])
    grad_far = gather_parts(copies([grad_far], [slope_in])[0], lower)
    d_in, sums_back = call(
        second_half_kernel,
        [((rows, width), F32), ((2, width), F32)],
        [back, inputs, slope_in, vec_in, up_part, *grad_far, *conv_far],
        scratch=[((rows, side), BF16), ((width, side), BF16), ((ext, LANES), F32)],
    )
    both_parts = gather_parts(both, lower)
    both_far = swap(both, "ch", top)
    total_back = sums_back
    for k, reach in enumerate(sum_order):
        total_got = swap(total_back, "seq", last_order[k])
        got = swap(sent, "seq", reach)
        if k < rounds - 1:
            half //= 2
            kept, sent = call(
                functools.partial(fold_kernel, reach=2 * reach),
                [((half, depth, 4 * slim), F32), ((half, depth, 4 * slim), BF16)],
                [kept, got],
                after=[total_back],
            )
            total_back = add(total_back, total_got, [sent])
    both_parts += gather_parts(copies([both_far], [total_back])[0], lower)
    block_out, token = call(
        out_kernel,
        [((rows, width), BF16), ((8, LANES), F32)],
        [inputs, *both_parts],
        scratch=[((rows, ch_size * LANES), BF16), ((width, ch_size * LANES), BF16)],
        after=[total_back],
    )
    input_grad, *in_new = call(
        functools.partial(final_kernel, bin_count=bin_count),
        [((rows, width), F32)] + [((2, width), F32)] * 3,
        [inputs, cotangent, d_in, vec_in, total_back, total_got, norm_in, first_in, second_in],
        scratch=[((rows, width), F32)],
        after=[token],
        away_outs=(0,),
        sems=8,
    )
    news = call(
        weight_step_kernel,
        [(master_conv.shape, F32)] * 3 + [(master_point.shape, F32)] * 3 + [(norm_mid.shape, F32)] * 3,
        [kept, got, total_mid, master_conv, first_conv, second_conv]
        + [master_point, first_point, second_point, norm_mid, first_mid, second_mid],
        after=[token],
    )
    return (block_out, input_grad, *news[:6], *in_new, *news[6:])


def solution(mesh):
    in_specs = (
        P("seq", None),
        P("seq", None),
        P(),
        P(None, "seq", "ch"),
        P(None, "seq", "ch"),
        P(None, "seq", "ch"),
        P("ch", "seq"),
        P("ch", "seq"),
        P("ch", "seq"),
        P(),
        P(),
        P(),
        P(None, "ch"),
        P(None, "ch"),
        P(None, "ch"),
    )
    out_specs = (
        P("seq", None),
        P("seq", None),
        P(None, "seq", "ch"),
        P(None, "seq", "ch"),
        P(None, "seq", "ch"),
        P("ch", "seq"),
        P("ch", "seq"),
        P("ch", "seq"),
        P(),
        P(),
        P(),
        P(None, "ch"),
        P(None, "ch"),
        P(None, "ch"),
    )
    return jax.shard_map(shards, mesh=mesh, in_specs=in_specs, out_specs=out_specs, check_vma=False)
```

time: 113 us -> 88.7 us (0.78)
  waiting for transfers between devices: 41.3 us -> 26.3 us
  starting transfers between devices: 34.4 us -> 28.7 us
  local copies, waits for them, and re-layouts: 5.35 us -> 0.07 us
  blocking collectives: 9.26 us -> 10.5 us
    ppermute x28 -> x25, waiting for transfers between devices: 40.2 us -> 26.3 us  [swap(): return lax.ppermute(x, axis, flip(axis, reach))]
    unnamed x38 -> x26, local copies, waits for them, and re-layouts: 4.6 us -> 0.07 us
    ppermute x2 -> x1, starting transfers between devices: 3.72 us -> 0.65 us  [shards(): lax.ppermute(rims[1], 'seq', pairs + [(j, i) for i, j in pairs])]
    ppermute x28 -> x25, starting transfers between devices: 30.7 us -> 28.1 us  [swap(): return lax.ppermute(x, axis, flip(axis, reach))]
    all_to_all x1, blocking collectives: 9.26 us -> 10.5 us  [spread(): return lax.all_to_all(copies, axes, 0, 0, tiled=True)]
    pallas_call x22 -> x27, Pallas kernels: 21.3 us -> 21.8 us  [call(): pl.pallas_call(kernel, out_shape=[jax.ShapeDtypeStruct(s, t) for s, t in...]
  transfers between devices with their start and end apart: 30 -> 26, of which waited for: 12 -> 11; matrix products, arithmetic and copies ran while one was open for 1% -> 0% of each run, Pallas kernels for 16% -> 19%
where the time goes in v4:
time: 88.7 us; the launch traced here: 88.5 us
  starting transfers between devices  28.7 us (32%)
  waiting for transfers between devices  26.3 us (30%)
  Pallas kernels  21.8 us (25%)
  blocking collectives  10.5 us (12%)
  between operations  1.03 us (1%)
    ppermute x25, starting transfers between devices, swap(): return lax.ppermute(x, axis, flip(axis, reach))  28.1 us
    ppermute x25, waiting for transfers between devices, swap(): return lax.ppermute(x, axis, flip(axis, reach))  26.3 us
    pallas_call x27, Pallas kernels, call(): pl.pallas_call(kernel, out_shape=[jax.ShapeDtypeStruct(s, t) for s, t in...  21.8 us
    all_to_all x1, blocking collectives, spread(): return lax.all_to_all(copies, axes, 0, 0, tiled=True)  10.5 us
  transfers between devices with their start and end apart: 26, of which 11 were waited for; matrix products, arithmetic and copies ran while one was open for 0% of the time, Pallas kernels for 19%

profile of v4, /device:TPU:0, one launch (start us, length us, event | category | flops | bytes accessed | tf_op | source)
XLA Modules:
  0.0 88.5 jit_solution(3990671558665909422)
XLA Ops:
  0.7 1.7 %first_kernel.1 = (bf16[1024,768]{1,0:T(8,128)(2,1)S(1)}, bf16[1,72,384]{2,1,0:T(8,128)(2,1)S(1)}, bf16[144,128]{1,0:T(8,128)(2,1)S(1)}, bf16[2,48,768]{2,1,0:T(8,128)(2,1)S(1)}) custom-call(bf16[1024,768]{1,0:T(8,128)(2,1)} %refs_0_.2, bf16[1024,768]{1,0:T(8,128)(2,1)} %refs_1_.3, f32[3,96,96]{2,1,0:T(8,128)} %refs_3_.5, f32[96,96]{1,0:T(8,128)} %refs_6_.3), custom_call_target="tpu_custom_call" | custom-call | flops 1 | bytes 1 | tf_op jit(solution)/shard_map/first_kernel/pallas_call | solution.py:48
  2.4 4.1 %collective-permute-start = (bf16[1,72,384]{2,1,0:T(8,128)(2,1)S(1)}, bf16[1,72,384]{2,1,0:T(8,128)(2,1)S(1)}, u32[]{:S(2)}, u32[]{:S(2)}) collective-permute-start(bf16[1,72,384]{2,1,0:T(8,128)(2,1)S(1)} %get-tuple-element.70.refs_0_), channel_id=1, source_target_pairs={{0,16},{4,20},{8,24},{12,28},{16,0},{20,4},{24,8},{28,12},{1,17},{... | collective-permute-start | bytes 165896 | tf_op jit(solution)/shard_map/ppermute | solution.py:573
  6.6 4.8 %collective-permute-done.1.refs_3_ = bf16[144,128]{1,0:T(8,128)(2,1)S(1)} collective-permute-done((bf16[144,128]{1,0:T(8,128)(2,1)S(1)}, bf16[144,128]{1,0:T(8,128)(2,1)S(1)}, u32[]{:S(2)}, u32[]{:S(2)}) %collective-permute-start.1) | collective-permute-done | bytes 36896 | tf_op jit(solution)/shard_map/ppermute | solution.py:573
  11.4 1.6 %collective-permute-start.2 = (bf16[2,72,384]{2,1,0:T(8,128)(2,1)S(1)}, bf16[2,72,384]{2,1,0:T(8,128)(2,1)S(1)}, u32[]{:S(2)}, u32[]{:S(2)}) collective-permute-start(bf16[2,72,384]{2,1,0:T(8,128)(2,1)S(1)} %get-tuple-element.76.refs_0_), channel_id=1, source_target_pairs={{0,8},{4,12},{8,0},{12,4},{16,24},{20,28},{24,16},{28,20},{1,9},{5... | collective-permute-start | bytes 331784 | tf_op jit(solution)/shard_map/ppermute | solution.py:573
  13.0 1.5 %collective-permute-start.4 = (bf16[48,768]{1,0:T(8,128)(2,1)S(1)}, bf16[48,768]{1,0:T(8,128)(2,1)S(1)}, u32[]{:S(2)}, u32[]{:S(2)}) collective-permute-start(bf16[48,768]{1,0:T(8,128)(2,1)S(1)} %get-tuple-element.77), channel_id=1, source_target_pairs={{0,4},{4,0},{8,12},{12,8},{16,20},{20,16},{24,28},{28,24},{1,5},{5... | collective-permute-start | bytes 221192 | tf_op jit(solution)/shard_map/ppermute | solution.py:573
  15.2 3.2 %collective-permute-start.3 = (bf16[240,128]{1,0:T(8,128)(2,1)S(1)}, bf16[240,128]{1,0:T(8,128)(2,1)S(1)}, u32[]{:S(2)}, u32[]{:S(2)}) collective-permute-start(bf16[240,128]{1,0:T(8,128)(2,1)S(1)} %get-tuple-element.73.refs_1_.refs_2_), channel_id=1, source_target_pairs={{0,4},{4,0},{8,12},{12,8},{16,20},{20,16},{24,28},{28,24},{1,5},{5... | collective-permute-start | bytes 184328 | tf_op jit(solution)/shard_map/ppermute | solution.py:573
  18.4 1.4 %mask_kernel.1 = (f32[3,1056,128]{2,1,0:T(8,128)S(1)}, f32[3,1024,128]{2,1,0:T(8,128)S(1)}) custom-call(s32[8]{0:T(128)S(1)} %copy-done.12, bf16[240,128]{1,0:T(8,128)(2,1)S(1)} %get-tuple-element.73.refs_1_.refs_2_), custom_call_target="tpu_custom_call" | custom-call | flops 1 | bytes 1 | tf_op jit(solution)/shard_map/mask_kernel/pallas_call | solution.py:48
  20.7 2.3 %collective-permute-start.7 = (bf16[4,72,384]{2,1,0:T(8,128)(2,1)S(1)}, bf16[4,72,384]{2,1,0:T(8,128)(2,1)S(1)}, u32[]{:S(2)}, u32[]{:S(2)}) collective-permute-start(bf16[4,72,384]{2,1,0:T(8,128)(2,1)S(1)} %get-tuple-element.82.refs_2_), channel_id=1, source_target_pairs={{0,4},{4,0},{8,12},{12,8},{16,20},{20,16},{24,28},{28,24},{1,5},{5... | collective-permute-start | bytes 663560 | tf_op jit(solution)/shard_map/ppermute | solution.py:573
  23.0 2.2 %collective-permute-start.6 = (bf16[432,128]{1,0:T(8,128)(2,1)S(1)}, bf16[432,128]{1,0:T(8,128)(2,1)S(1)}, u32[]{:S(2)}, u32[]{:S(2)}) collective-permute-start(bf16[432,128]{1,0:T(8,128)(2,1)S(1)} %get-tuple-element.80.refs_3_.refs_2_), channel_id=1, source_target_pairs={{0,8},{4,12},{8,0},{12,4},{16,24},{20,28},{24,16},{28,20},{1,9},{5... | collective-permute-start | bytes 331784 | tf_op jit(solution)/shard_map/ppermute | solution.py:573
  25.2 2.7 %collective-permute-done.6.refs_4_.refs_3_ = bf16[432,128]{1,0:T(8,128)(2,1)S(1)} collective-permute-done((bf16[432,128]{1,0:T(8,128)(2,1)S(1)}, bf16[432,128]{1,0:T(8,128)(2,1)S(1)}, u32[]{:S(2)}, u32[]{:S(2)}) %collective-permute-start.6) | collective-permute-done | bytes 110624 | tf_op jit(solution)/shard_map/ppermute | solution.py:573
  27.9 1.6 %act_kernel.1 = (bf16[1088,768]{1,0:T(8,128)(2,1)S(1)}, f32[8,768]{1,0:T(8,128)S(1)}, bf16[1024,768]{1,0:T(8,128)(2,1)S(1)}) custom-call(bf16[1024,768]{1,0:T(8,128)(2,1)S(1)} %get-tuple-element.69.refs_0_.refs_1_, bf16[1024,768]{1,0:T(8,128)(2,1)} %refs_1_.3, bf16[2,48,768]{2,1,0:T(8,128)(2,1)S(1)} %get-tuple-element.79.refs_2_.refs_1_, ...), custom_call_target="tpu_custom_call" | custom-call | flops 1 | bytes 1 | tf_op jit(solution)/shard_map/act_kernel/pallas_call | solution.py:48
  29.5 1.3 %conv_kernel.1 = (bf16[768,384]{1,0:T(8,128)(2,1)S(1)}, f32[1056,128]{1,0:T(8,128)S(1)}, f32[8,128]{1,0:T(8,128)S(1)}, bf16[8,72,384]{2,1,0:T(8,128)(2,1)S(1)}) custom-call(f32[3,1056,128]{2,1,0:T(8,128)S(1)} %get-tuple-element.75.refs_0_, bf16[1088,768]{1,0:T(8,128)(2,1)S(1)} %get-tuple-element.81.refs_1_.refs_2_, ...), custom_call_target="tpu_custom_call" | custom-call | flops 1 | bytes 1 | tf_op jit(solution)/shard_map/conv_kernel/pallas_call | solution.py:48
  30.9 1.6 %collective-permute-start.11 = (bf16[8,72,384]{2,1,0:T(8,128)(2,1)S(1)}, bf16[8,72,384]{2,1,0:T(8,128)(2,1)S(1)}, u32[]{:S(2)}, u32[]{:S(2)}) collective-permute-start(bf16[8,72,384]{2,1,0:T(8,128)(2,1)S(1)} %get-tuple-element.87), channel_id=1, source_target_pairs={{0,2},{1,3},{2,0},{3,1},{4,6},{5,7},{6,4},{7,5},{8,10},{9,11},{10,... | collective-permute-start | bytes 1327112 | tf_op jit(solution)/shard_map/ppermute | solution.py:573
  33.3 2.8 %collective-permute-done.8.refs_1_ = f32[8,128]{1,0:T(8,128)S(1)} collective-permute-done((f32[8,128]{1,0:T(8,128)S(1)}, f32[8,128]{1,0:T(8,128)S(1)}, u32[]{:S(2)}, u32[]{:S(2)}) %collective-permute-start.8) | collective-permute-done | bytes 4128 | tf_op jit(solution)/shard_map/ppermute | solution.py:573
  36.1 2.0 %collective-permute-start.9 = (f32[8,128]{1,0:T(8,128)S(1)}, f32[8,128]{1,0:T(8,128)S(1)}, u32[]{:S(2)}, u32[]{:S(2)}) collective-permute-start(f32[8,128]{1,0:T(8,128)S(1)} %add_kernel.5.refs_0_), channel_id=1, source_target_pairs={{0,8},{4,12},{8,0},{12,4},{16,24},{20,28},{24,16},{28,20},{1,9},{5... | collective-permute-start | bytes 12296 | tf_op jit(solution)/shard_map/ppermute | solution.py:573
  38.1 1.6 %collective-permute-done.9.refs_1_ = f32[8,128]{1,0:T(8,128)S(1)} collective-permute-done((f32[8,128]{1,0:T(8,128)S(1)}, f32[8,128]{1,0:T(8,128)S(1)}, u32[]{:S(2)}, u32[]{:S(2)}) %collective-permute-start.9) | collective-permute-done | bytes 4128 | tf_op jit(solution)/shard_map/ppermute | solution.py:573
  39.7 2.1 %collective-permute-start.10 = (f32[8,128]{1,0:T(8,128)S(1)}, f32[8,128]{1,0:T(8,128)S(1)}, u32[]{:S(2)}, u32[]{:S(2)}) collective-permute-start(f32[8,128]{1,0:T(8,128)S(1)} %add_kernel.6.refs_0_), channel_id=1, source_target_pairs={{0,16},{4,20},{8,24},{12,28},{16,0},{20,4},{24,8},{28,12},{1,17},{... | collective-permute-start | bytes 12296 | tf_op jit(solution)/shard_map/ppermute | solution.py:573
  41.8 2.4 %collective-permute-done.10.refs_1_ = f32[8,128]{1,0:T(8,128)S(1)} collective-permute-done((f32[8,128]{1,0:T(8,128)S(1)}, f32[8,128]{1,0:T(8,128)S(1)}, u32[]{:S(2)}, u32[]{:S(2)}) %collective-permute-start.10) | collective-permute-done | bytes 4128 | tf_op jit(solution)/shard_map/ppermute | solution.py:573
  45.1 10.5 %all_to_all.5.refs_0_ = f32[8,2,128]{2,1,0:T(2,128)S(1)} all-to-all(f32[8,2,128]{2,1,0:T(2,128)S(1)} %get-tuple-element.89), channel_id=1, replica_groups=mesh['seq'=8,'ch'=4] {'seq'}, dimensions={0} | all-to-all | bytes 16384 | tf_op jit(solution)/shard_map/all_to_all | solution.py:584
  57.2 2.0 %weight_grad_kernel.1 = (bf16[1024,384]{1,0:T(8,128)(2,1)S(1)}, f32[4,96,384]{2,1,0:T(8,128)S(1)}, bf16[4,96,384]{2,1,0:T(8,128)(2,1)S(1)}) custom-call(f32[3,1024,128]{2,1,0:T(8,128)S(1)} %get-tuple-element.74.refs_6_.refs_0_, bf16[792,128]{1,0:T(8,128)(2,1)S(1)} %get-tuple-element.93.refs_1_, bf16[1088,768]{1,0:T(8,128)(2,1)S(1)} %get-tuple-element.81.refs_1_.refs_2_, ...), custom_call_target="tpu_custom_call" | custom-call | flops 1 | bytes 1 | tf_op jit(solution)/shard_map/weight_grad_kernel/pallas_call | solution.py:48
  59.2 1.6 %first_half_kernel.1 = (f32[1024,768]{1,0:T(8,128)S(1)}, bf16[1792,128]{1,0:T(8,128)(2,1)S(1)}) custom-call(f32[3,1024,128]{2,1,0:T(8,128)S(1)} %get-tuple-element.74.refs_6_.refs_0_, bf16[1024,384]{1,0:T(8,128)(2,1)S(1)} %get-tuple-element.95.refs_1_, bf16[1024,128]{1,0:T(8,128)(2,1)S(1)} %get-tuple-element.94.refs_4_.refs_2_, ...), custom_call_target="tpu_custom_call" | custom-call | flops 1 | bytes 1 | tf_op jit(solution)/shard_map/first_half_kernel/pallas_call | solution.py:48
  60.8 1.3 %collective-permute-start.15 = (bf16[1792,128]{1,0:T(8,128)(2,1)S(1)}, bf16[1792,128]{1,0:T(8,128)(2,1)S(1)}, u32[]{:S(2)}, u32[]{:S(2)}) collective-permute-start(bf16[1792,128]{1,0:T(8,128)(2,1)S(1)} %get-tuple-element.97.refs_1_), channel_id=1, source_target_pairs={{0,2},{1,3},{2,0},{3,1},{4,6},{5,7},{6,4},{7,5},{8,10},{9,11},{10,... | collective-permute-start | bytes 1376264 | tf_op jit(solution)/shard_map/ppermute | solution.py:573
  62.7 2.3 %slope_kernel.1.refs_1_.refs_2_ = f32[1024,768]{1,0:T(8,128)S(1)} custom-call(bf16[1024,768]{1,0:T(8,128)(2,1)S(1)} %get-tuple-element.69.refs_0_.refs_1_, f32[8,768]{1,0:T(8,128)S(1)} %get-tuple-element.98.refs_1_.refs_3_, f32[1024,768]{1,0:T(8,128)S(1)} %get-tuple-element.99.refs_2_.refs_4_), custom_call_target="tpu_custom_call" | custom-call | flops 1 | bytes 1 | tf_op jit(solution)/shard_map/slope_kernel/pallas_call | solution.py:48
  65.1 1.4 %collective-permute-done.17.refs_6_ = bf16[792,128]{1,0:T(8,128)(2,1)S(1)} collective-permute-done((bf16[792,128]{1,0:T(8,128)(2,1)S(1)}, bf16[792,128]{1,0:T(8,128)(2,1)S(1)}, u32[]{:S(2)}, u32[]{:S(2)}) %collective-permute-start.17) | collective-permute-done | bytes 202784 | tf_op jit(solution)/shard_map/ppermute | solution.py:573
  66.5 2.2 %second_half_kernel.1 = (f32[1024,768]{1,0:T(8,128)S(1)}, f32[2,768]{1,0:T(2,128)S(1)}) custom-call(f32[3,1024,128]{2,1,0:T(8,128)S(1)} %get-tuple-element.74.refs_6_.refs_0_, bf16[1024,768]{1,0:T(8,128)(2,1)S(1)} %get-tuple-element.69.refs_0_.refs_1_, f32[1024,768]{1,0:T(8,128)S(1)} %slope_kernel.1.refs_1_.refs_2_, ...), custom_call_target="tpu_custom_call" | custom-call | flops 1 | bytes 1 | tf_op jit(solution)/shard_map/second_half_kernel/pallas_call | solution.py:48
  68.7 1.9 %collective-permute-done.20.refs_1_ = bf16[4,96,384]{2,1,0:T(8,128)(2,1)S(1)} collective-permute-done((bf16[4,96,384]{2,1,0:T(8,128)(2,1)S(1)}, bf16[4,96,384]{2,1,0:T(8,128)(2,1)S(1)}, u32[]{:S(2)}, u32[]{:S(2)}) %collective-permute-start.20) | collective-permute-done | bytes 294944 | tf_op jit(solution)/shard_map/ppermute | solution.py:573
  71.8 4.0 %collective-permute-done.19.refs_1_ = f32[2,768]{1,0:T(2,128)S(1)} collective-permute-done((f32[2,768]{1,0:T(2,128)S(1)}, f32[2,768]{1,0:T(2,128)S(1)}, u32[]{:S(2)}, u32[]{:S(2)}) %collective-permute-start.19) | collective-permute-done | bytes 6176 | tf_op jit(solution)/shard_map/ppermute | solution.py:573
  76.5 3.0 %collective-permute-done.21.refs_1_ = f32[2,768]{1,0:T(2,128)S(1)} collective-permute-done((f32[2,768]{1,0:T(2,128)S(1)}, f32[2,768]{1,0:T(2,128)S(1)}, u32[]{:S(2)}, u32[]{:S(2)}) %collective-permute-start.21) | collective-permute-done | bytes 6176 | tf_op jit(solution)/shard_map/ppermute | solution.py:573
  79.6 1.5 %collective-permute-start.25 = (bf16[1,96,384]{2,1,0:T(8,128)(2,1)S(1)}, bf16[1,96,384]{2,1,0:T(8,128)(2,1)S(1)}, u32[]{:S(2)}, u32[]{:S(2)}) collective-permute-start(bf16[1,96,384]{2,1,0:T(8,128)(2,1)S(1)} %get-tuple-element.105.refs_2_), channel_id=1, source_target_pairs={{0,16},{4,20},{8,24},{12,28},{16,0},{20,4},{24,8},{28,12},{1,17},{... | collective-permute-start | bytes 221192 | tf_op jit(solution)/shard_map/ppermute | solution.py:573
  81.7 2.3 %out_kernel.1 = (bf16[1024,768]{1,0:T(8,128)(2,1)}, f32[8,128]{1,0:T(8,128)S(1)}) custom-call(bf16[1024,768]{1,0:T(8,128)(2,1)S(1)} %get-tuple-element.69.refs_0_.refs_1_, bf16[1792,128]{1,0:T(8,128)(2,1)S(1)} %get-tuple-element.97.refs_1_, bf16[1792,128]{1,0:T(8,128)(2,1)S(1)} %collective-permute-done.14.refs_2_, bf16[1792,128]{1,0:T(8,128)(2,1)S(1)} %copy_kernel.5.refs_3_, ...), custom_call_target="tpu_custom_call" | custom-call | flops 1 | bytes 1 | tf_op jit(solution)/shard_map/out_kernel/pallas_call | solution.py:48
  84.9 2.5 %final_kernel.1 = (f32[1024,768]{1,0:T(8,128)}, f32[2,768]{1,0:T(2,128)}, f32[2,768]{1,0:T(2,128)}, f32[2,768]{1,0:T(2,128)}) custom-call(bf16[1024,768]{1,0:T(8,128)(2,1)S(1)} %get-tuple-element.69.refs_0_.refs_1_, bf16[1024,768]{1,0:T(8,128)(2,1)S(1)} %get-tuple-element.84.refs_0_.refs_3_.refs_1_, f32[1024,768]{1,0:T(8,128)S(1)} %get-tuple-element.107.refs_2_, ...), custom_call_target="tpu_custom_call" | custom-call | flops 1 | bytes 1 | tf_op jit(solution)/shard_map/final_kernel/pallas_call | solution.py:48
  87.4 1.0 %weight_step_kernel.1 = (f32[3,96,96]{2,1,0:T(8,128)}, f32[3,96,96]{2,1,0:T(8,128)}, f32[3,96,96]{2,1,0:T(8,128)}, f32[96,96]{1,0:T(8,128)}, f32[96,96]{1,0:T(8,...) custom-call(f32[1,96,384]{2,1,0:T(8,128)S(1)} %get-tuple-element.110.refs_0_, ...), custom_call_target="tpu_custom_call" | custom-call | flops 1 | bytes 1 | tf_op jit(solution)/shard_map/weight_step_kernel/pallas_call | solution.py:48
  (74 shorter events, 8.9 us)
Async XLA Ops:
  0.6 17.8 %copy-start.12 = (s32[8]{0:T(128)S(1)}, s32[8]{0:T(128)}, u32[]{:S(2)}) copy-start(s32[8]{0:T(128)} %refs_0_.3) | copy-start | bytes 100
  2.4 25.5 %copy-start.6 = (f32[2,768]{1,0:T(2,128)S(1)}, f32[2,768]{1,0:T(2,128)}, u32[]{:S(2)}) copy-start(f32[2,768]{1,0:T(2,128)} %refs_6_.2) | copy-start | bytes 18436
  2.4 9.0 %collective-permute-start = (bf16[1,72,384]{2,1,0:T(8,128)(2,1)S(1)}, bf16[1,72,384]{2,1,0:T(8,128)(2,1)S(1)}, u32[]{:S(2)}, u32[]{:S(2)}) collective-permute-start(bf16[1,72,384]{2,1,0:T(8,128)(2,1)S(1)} %get-tuple-element.70.refs_0_), channel_id=1, source_target_pairs={{0,16},{4,20},{8,24},{12,28},{16,0},{20,4},{24,8},{28,12},{1,17},{... | collective-permute-start | bytes 165896 | tf_op jit(solution)/shard_map/ppermute | solution.py:573
  6.5 4.9 %collective-permute-start.1 = (bf16[144,128]{1,0:T(8,128)(2,1)S(1)}, bf16[144,128]{1,0:T(8,128)(2,1)S(1)}, u32[]{:S(2)}, u32[]{:S(2)}) collective-permute-start(bf16[144,128]{1,0:T(8,128)(2,1)S(1)} %get-tuple-element.71.refs_2_), channel_id=1, source_target_pairs={{0,16},{4,20},{8,24},{12,28},{16,0},{20,4},{24,8},{28,12},{1,17},{... | collective-permute-start | bytes 110600 | tf_op jit(solution)/shard_map/ppermute | solution.py:573
  11.4 9.2 %collective-permute-start.2 = (bf16[2,72,384]{2,1,0:T(8,128)(2,1)S(1)}, bf16[2,72,384]{2,1,0:T(8,128)(2,1)S(1)}, u32[]{:S(2)}, u32[]{:S(2)}) collective-permute-start(bf16[2,72,384]{2,1,0:T(8,128)(2,1)S(1)} %get-tuple-element.76.refs_0_), channel_id=1, source_target_pairs={{0,8},{4,12},{8,0},{12,4},{16,24},{20,28},{24,16},{28,20},{1,9},{5... | collective-permute-start | bytes 331784 | tf_op jit(solution)/shard_map/ppermute | solution.py:573
  13.0 7.6 %collective-permute-start.4 = (bf16[48,768]{1,0:T(8,128)(2,1)S(1)}, bf16[48,768]{1,0:T(8,128)(2,1)S(1)}, u32[]{:S(2)}, u32[]{:S(2)}) collective-permute-start(bf16[48,768]{1,0:T(8,128)(2,1)S(1)} %get-tuple-element.77), channel_id=1, source_target_pairs={{0,4},{4,0},{8,12},{12,8},{16,20},{20,16},{24,28},{28,24},{1,5},{5... | collective-permute-start | bytes 221192 | tf_op jit(solution)/shard_map/ppermute | solution.py:573
  14.5 6.1 %collective-permute-start.5 = (bf16[48,768]{1,0:T(8,128)(2,1)S(1)}, bf16[48,768]{1,0:T(8,128)(2,1)S(1)}, u32[]{:S(2)}, u32[]{:S(2)}) collective-permute-start(bf16[48,768]{1,0:T(8,128)(2,1)S(1)} %get-tuple-element.78), channel_id=1, source_target_pairs={{4,8},{12,16},{20,24},{8,4},{16,12},{24,20},{5,9},{13,17},{21,25},... | collective-permute-start | bytes 221192 | tf_op jit(solution)/shard_map/ppermute | solution.py:656
  15.2 5.4 %collective-permute-start.3 = (bf16[240,128]{1,0:T(8,128)(2,1)S(1)}, bf16[240,128]{1,0:T(8,128)(2,1)S(1)}, u32[]{:S(2)}, u32[]{:S(2)}) collective-permute-start(bf16[240,128]{1,0:T(8,128)(2,1)S(1)} %get-tuple-element.73.refs_1_.refs_2_), channel_id=1, source_target_pairs={{0,4},{4,0},{8,12},{12,8},{16,20},{20,16},{24,28},{28,24},{1,5},{5... | collective-permute-start | bytes 184328 | tf_op jit(solution)/shard_map/ppermute | solution.py:573
  20.7 8.8 %collective-permute-start.7 = (bf16[4,72,384]{2,1,0:T(8,128)(2,1)S(1)}, bf16[4,72,384]{2,1,0:T(8,128)(2,1)S(1)}, u32[]{:S(2)}, u32[]{:S(2)}) collective-permute-start(bf16[4,72,384]{2,1,0:T(8,128)(2,1)S(1)} %get-tuple-element.82.refs_2_), channel_id=1, source_target_pairs={{0,4},{4,0},{8,12},{12,8},{16,20},{20,16},{24,28},{28,24},{1,5},{5... | collective-permute-start | bytes 663560 | tf_op jit(solution)/shard_map/ppermute | solution.py:573
  23.0 4.9 %collective-permute-start.6 = (bf16[432,128]{1,0:T(8,128)(2,1)S(1)}, bf16[432,128]{1,0:T(8,128)(2,1)S(1)}, u32[]{:S(2)}, u32[]{:S(2)}) collective-permute-start(bf16[432,128]{1,0:T(8,128)(2,1)S(1)} %get-tuple-element.80.refs_3_.refs_2_), channel_id=1, source_target_pairs={{0,8},{4,12},{8,0},{12,4},{16,24},{20,28},{24,16},{28,20},{1,9},{5... | collective-permute-start | bytes 331784 | tf_op jit(solution)/shard_map/ppermute | solution.py:573
  30.8 13.7 %collective-permute-start.12 = (bf16[768,384]{1,0:T(8,128)(2,1)S(1)}, bf16[768,384]{1,0:T(8,128)(2,1)S(1)}, u32[]{:S(2)}, u32[]{:S(2)}) collective-permute-start(bf16[768,384]{1,0:T(8,128)(2,1)S(1)} %get-tuple-element.88.refs_5_), channel_id=1, source_target_pairs={{0,1},{1,0},{2,3},{3,2},{4,5},{5,4},{6,7},{7,6},{8,9},{9,8},{10,11... | collective-permute-start | bytes 1769480 | tf_op jit(solution)/shard_map/ppermute | solution.py:573
  30.9 13.3 %collective-permute-start.11 = (bf16[8,72,384]{2,1,0:T(8,128)(2,1)S(1)}, bf16[8,72,384]{2,1,0:T(8,128)(2,1)S(1)}, u32[]{:S(2)}, u32[]{:S(2)}) collective-permute-start(bf16[8,72,384]{2,1,0:T(8,128)(2,1)S(1)} %get-tuple-element.87), channel_id=1, source_target_pairs={{0,2},{1,3},{2,0},{3,1},{4,6},{5,7},{6,4},{7,5},{8,10},{9,11},{10,... | collective-permute-start | bytes 1327112 | tf_op jit(solution)/shard_map/ppermute | solution.py:573
  32.5 3.6 %collective-permute-start.8 = (f32[8,128]{1,0:T(8,128)S(1)}, f32[8,128]{1,0:T(8,128)S(1)}, u32[]{:S(2)}, u32[]{:S(2)}) collective-permute-start(f32[8,128]{1,0:T(8,128)S(1)} %get-tuple-element.83.refs_4_.refs_0_), channel_id=1, source_target_pairs={{0,4},{4,0},{8,12},{12,8},{16,20},{20,16},{24,28},{28,24},{1,5},{5... | collective-permute-start | bytes 12296 | tf_op jit(solution)/shard_map/ppermute | solution.py:573
  33.2 11.3 %copy-start.9 = (f32[2,96]{1,0:T(2,128)S(1)}, f32[2,96]{1,0:T(2,128)}, u32[]{:S(2)}) copy-start(f32[2,96]{1,0:T(2,128)} %refs_9_.1) | copy-start | bytes 2308
  36.1 3.6 %collective-permute-start.9 = (f32[8,128]{1,0:T(8,128)S(1)}, f32[8,128]{1,0:T(8,128)S(1)}, u32[]{:S(2)}, u32[]{:S(2)}) collective-permute-start(f32[8,128]{1,0:T(8,128)S(1)} %add_kernel.5.refs_0_), channel_id=1, source_target_pairs={{0,8},{4,12},{8,0},{12,4},{16,24},{20,28},{24,16},{28,20},{1,9},{5... | collective-permute-start | bytes 12296 | tf_op jit(solution)/shard_map/ppermute | solution.py:573
  39.7 4.5 %collective-permute-start.10 = (f32[8,128]{1,0:T(8,128)S(1)}, f32[8,128]{1,0:T(8,128)S(1)}, u32[]{:S(2)}, u32[]{:S(2)}) collective-permute-start(f32[8,128]{1,0:T(8,128)S(1)} %add_kernel.6.refs_0_), channel_id=1, source_target_pairs={{0,16},{4,20},{8,24},{12,28},{16,0},{20,4},{24,8},{28,12},{1,17},{... | collective-permute-start | bytes 12296 | tf_op jit(solution)/shard_map/ppermute | solution.py:573
  55.9 10.6 %collective-permute-start.18 = (bf16[768,384]{1,0:T(8,128)(2,1)S(1)}, bf16[768,384]{1,0:T(8,128)(2,1)S(1)}, u32[]{:S(2)}, u32[]{:S(2)}) collective-permute-start(bf16[768,384]{1,0:T(8,128)(2,1)S(1)} %copy_kernel.4.refs_7_), channel_id=1, source_target_pairs={{0,1},{1,0},{2,3},{3,2},{4,5},{5,4},{6,7},{7,6},{8,9},{9,8},{10,11... | collective-permute-start | bytes 1769480 | tf_op jit(solution)/shard_map/ppermute | solution.py:573
  55.9 3.2 %collective-permute-start.13 = (bf16[792,128]{1,0:T(8,128)(2,1)S(1)}, bf16[792,128]{1,0:T(8,128)(2,1)S(1)}, u32[]{:S(2)}, u32[]{:S(2)}) collective-permute-start(bf16[792,128]{1,0:T(8,128)(2,1)S(1)} %get-tuple-element.93.refs_1_), channel_id=1, source_target_pairs={{0,1},{1,0},{2,3},{3,2},{4,5},{5,4},{6,7},{7,6},{8,9},{9,8},{10,11... | collective-permute-start | bytes 608264 | tf_op jit(solution)/shard_map/ppermute | solution.py:573
  56.4 8.5 %collective-permute-start.16 = (bf16[792,128]{1,0:T(8,128)(2,1)S(1)}, bf16[792,128]{1,0:T(8,128)(2,1)S(1)}, u32[]{:S(2)}, u32[]{:S(2)}) collective-permute-start(bf16[792,128]{1,0:T(8,128)(2,1)S(1)} %get-tuple-element.93.refs_1_), channel_id=1, source_target_pairs={{0,2},{1,3},{2,0},{3,1},{4,6},{5,7},{6,4},{7,5},{8,10},{9,11},{10,... | collective-permute-start | bytes 608264 | tf_op jit(solution)/shard_map/ppermute | solution.py:573
  60.8 18.7 %collective-permute-start.15 = (bf16[1792,128]{1,0:T(8,128)(2,1)S(1)}, bf16[1792,128]{1,0:T(8,128)(2,1)S(1)}, u32[]{:S(2)}, u32[]{:S(2)}) collective-permute-start(bf16[1792,128]{1,0:T(8,128)(2,1)S(1)} %get-tuple-element.97.refs_1_), channel_id=1, source_target_pairs={{0,2},{1,3},{2,0},{3,1},{4,6},{5,7},{6,4},{7,5},{8,10},{9,11},{10,... | collective-permute-start | bytes 1376264 | tf_op jit(solution)/shard_map/ppermute | solution.py:573
  62.1 8.4 %collective-permute-start.20 = (bf16[4,96,384]{2,1,0:T(8,128)(2,1)S(1)}, bf16[4,96,384]{2,1,0:T(8,128)(2,1)S(1)}, u32[]{:S(2)}, u32[]{:S(2)}) collective-permute-start(bf16[4,96,384]{2,1,0:T(8,128)(2,1)S(1)} %get-tuple-element.102), channel_id=1, source_target_pairs={{0,4},{4,0},{8,12},{12,8},{16,20},{20,16},{24,28},{28,24},{1,5},{5... | collective-permute-start | bytes 884744 | tf_op jit(solution)/shard_map/ppermute | solution.py:573
  65.0 1.5 %collective-permute-start.17 = (bf16[792,128]{1,0:T(8,128)(2,1)S(1)}, bf16[792,128]{1,0:T(8,128)(2,1)S(1)}, u32[]{:S(2)}, u32[]{:S(2)}) collective-permute-start(bf16[792,128]{1,0:T(8,128)(2,1)S(1)} %copy_kernel.3.refs_5_), channel_id=1, source_target_pairs={{0,1},{1,0},{2,3},{3,2},{4,5},{5,4},{6,7},{7,6},{8,9},{9,8},{10,11... | collective-permute-start | bytes 608264 | tf_op jit(solution)/shard_map/ppermute | solution.py:573
  70.6 5.8 %collective-permute-start.22 = (bf16[2,96,384]{2,1,0:T(8,128)(2,1)S(1)}, bf16[2,96,384]{2,1,0:T(8,128)(2,1)S(1)}, u32[]{:S(2)}, u32[]{:S(2)}) collective-permute-start(bf16[2,96,384]{2,1,0:T(8,128)(2,1)S(1)} %get-tuple-element.103.refs_2_), channel_id=1, source_target_pairs={{0,8},{4,12},{8,0},{12,4},{16,24},{20,28},{24,16},{28,20},{1,9},{5... | collective-permute-start | bytes 442376 | tf_op jit(solution)/shard_map/ppermute | solution.py:573
  71.2 4.6 %collective-permute-start.19 = (f32[2,768]{1,0:T(2,128)S(1)}, f32[2,768]{1,0:T(2,128)S(1)}, u32[]{:S(2)}, u32[]{:S(2)}) collective-permute-start(f32[2,768]{1,0:T(2,128)S(1)} %get-tuple-element.100.refs_2_.refs_0_), channel_id=1, source_target_pairs={{0,16},{4,20},{8,24},{12,28},{16,0},{20,4},{24,8},{28,12},{1,17},{... | collective-permute-start | bytes 18440 | tf_op jit(solution)/shard_map/ppermute | solution.py:573
  75.9 3.6 %collective-permute-start.21 = (f32[2,768]{1,0:T(2,128)S(1)}, f32[2,768]{1,0:T(2,128)S(1)}, u32[]{:S(2)}, u32[]{:S(2)}) collective-permute-start(f32[2,768]{1,0:T(2,128)S(1)} %add_kernel.8.refs_2_.refs_0_), channel_id=1, source_target_pairs={{0,4},{4,0},{8,12},{12,8},{16,20},{20,16},{24,28},{28,24},{1,5},{5... | collective-permute-start | bytes 18440 | tf_op jit(solution)/shard_map/ppermute | solution.py:573
  76.5 5.2 %collective-permute-start.14 = (bf16[1792,128]{1,0:T(8,128)(2,1)S(1)}, bf16[1792,128]{1,0:T(8,128)(2,1)S(1)}, u32[]{:S(2)}, u32[]{:S(2)}) collective-permute-start(bf16[1792,128]{1,0:T(8,128)(2,1)S(1)} %get-tuple-element.97.refs_1_), channel_id=1, source_target_pairs={{0,1},{1,0},{2,3},{3,2},{4,5},{5,4},{6,7},{7,6},{8,9},{9,8},{10,11... | collective-permute-start | bytes 1376264 | tf_op jit(solution)/shard_map/ppermute | solution.py:573
  79.5 5.3 %copy-start.7 = (f32[2,768]{1,0:T(2,128)S(1)}, f32[2,768]{1,0:T(2,128)}, u32[]{:S(2)}) copy-start(f32[2,768]{1,0:T(2,128)} %refs_7_.2) | copy-start | bytes 18436
  79.5 5.3 %copy-start.8 = (f32[2,768]{1,0:T(2,128)S(1)}, f32[2,768]{1,0:T(2,128)}, u32[]{:S(2)}) copy-start(f32[2,768]{1,0:T(2,128)} %refs_8_.2) | copy-start | bytes 18436
  79.5 2.1 %collective-permute-start.23 = (bf16[1792,128]{1,0:T(8,128)(2,1)S(1)}, bf16[1792,128]{1,0:T(8,128)(2,1)S(1)}, u32[]{:S(2)}, u32[]{:S(2)}) collective-permute-start(bf16[1792,128]{1,0:T(8,128)(2,1)S(1)} %copy_kernel.5.refs_3_), channel_id=1, source_target_pairs={{0,1},{1,0},{2,3},{3,2},{4,5},{5,4},{6,7},{7,6},{8,9},{9,8},{10,11... | collective-permute-start | bytes 1376264 | tf_op jit(solution)/shard_map/ppermute | solution.py:573
  79.6 7.7 %collective-permute-start.25 = (bf16[1,96,384]{2,1,0:T(8,128)(2,1)S(1)}, bf16[1,96,384]{2,1,0:T(8,128)(2,1)S(1)}, u32[]{:S(2)}, u32[]{:S(2)}) collective-permute-start(bf16[1,96,384]{2,1,0:T(8,128)(2,1)S(1)} %get-tuple-element.105.refs_2_), channel_id=1, source_target_pairs={{0,16},{4,20},{8,24},{12,28},{16,0},{20,4},{24,8},{28,12},{1,17},{... | collective-permute-start | bytes 221192 | tf_op jit(solution)/shard_map/ppermute | solution.py:573
  81.2 3.6 %collective-permute-start.24 = (f32[2,768]{1,0:T(2,128)S(1)}, f32[2,768]{1,0:T(2,128)S(1)}, u32[]{:S(2)}, u32[]{:S(2)}) collective-permute-start(f32[2,768]{1,0:T(2,128)S(1)} %add_kernel.9.refs_1_.refs_5_.refs_4_), channel_id=1, source_target_pairs={{0,8},{4,12},{8,0},{12,4},{16,24},{20,28},{24,16},{28,20},{1,9},{5... | collective-permute-start | bytes 18440 | tf_op jit(solution)/shard_map/ppermute | solution.py:573
  84.8 2.6 %copy-start.2 = (f32[3,96,96]{2,1,0:T(8,128)S(1)}, f32[3,96,96]{2,1,0:T(8,128)}, u32[]{:S(2)}) copy-start(f32[3,96,96]{2,1,0:T(8,128)} %refs_4_.1) | copy-start | bytes 331780
  (7 other events, 18.0 us)

commit v5 on v4

--- a/solution.py
+++ b/solution.py
@@ -172,7 +172,7 @@
 
 
 def act_kernel(
-    x_ref, cot_hbm, rim_ref, one_ref, two_ref, norm_ref, hid_ref, vec_ref, cot_ref, sems, *, bin_count
+    x_ref, cot_hbm, one_ref, two_ref, norm_ref, hid_ref, vec_ref, cot_ref, sems, *, bin_count
 ):
     copy = pltpu.make_async_copy(cot_hbm, cot_ref, sems.at[0])
     copy.start()
@@ -190,16 +190,10 @@
         vec_ref[2:3, lanes] = gain
         vec_ref[3:4, lanes] = norm_ref[1:2, lanes] - mean * gain
 
-    gain, bias = vec_ref[2:3, :], vec_ref[3:4, :]
-    for side, at in enumerate((0, RIM + rows)):
-        for k in range(0, RIM, 16):
-            hidden, _ = gelu_and_slope(rim_ref[side, k : k + 16, :].astype(F32) * gain + bias)
-            hid_ref[at + k : at + k + 16, :] = hidden.astype(BF16)
-
     def step(k, carry):
         at = pl.multiple_of(k * 16, 16)
         v = x_ref[pl.ds(at, 16), :].astype(F32) * vec_ref[2:3, :] + vec_ref[3:4, :]
-        hid_ref[pl.ds(pl.multiple_of(at + RIM, 16), 16), :] = gelu_and_slope(v)[0].astype(BF16)
+        hid_ref[pl.ds(at, 16), :] = gelu_and_slope(v)[0].astype(BF16)
         return carry
 
     lax.fori_loop(0, rows // 16, step, 0, unroll=2)
@@ -226,7 +220,10 @@
     out_ref[...] = place(pieces, relatives, stack, lax.axis_index("seq"), slim)
 
 
-def mask_kernel(start_ref, ahead_ref, back_ref):
+def mask_kernel(start_ref, rim_ref, ahead_ref, back_ref, near_ref, far_ref):
+    odd = lax.axis_index("seq") % 2
+    near_ref[...] = rim_ref[1 - odd]
+    far_ref[...] = rim_ref[odd]
     rows = back_ref.shape[1]
     first = lax.axis_index("seq") * rows
     for j, shift in enumerate(SHIFTS):
@@ -240,26 +237,39 @@
             ]
 
 
-def slope_kernel(x_ref, vec_ref, slope_ref):
+def slope_kernel(x_ref, vec_ref, slope_ref, *, first):
     def step(k, carry):
-        at = pl.ds(pl.multiple_of(k * 16, 16), 16)
-        v = x_ref[at, :].astype(F32) * vec_ref[2:3, :] + vec_ref[3:4, :]
-        slope_ref[at, :] = gelu_and_slope(v)[1]
+        at = pl.multiple_of(k * 16, 16)
+        v = x_ref[pl.ds(first + at, 16), :].astype(F32) * vec_ref[2:3, :] + vec_ref[3:4, :]
+        slope_ref[pl.ds(at, 16), :] = gelu_and_slope(v)[1]
         return carry
 
-    lax.fori_loop(0, x_ref.shape[0] // 16, step, 0, unroll=2)
-
-
-def conv_kernel(mask_ref, hid_ref, *refs, relatives, slim):
-    pieces, (weight_ref, out_ref, sum_ref, all_ref, stack, prod) = refs[:-6], refs[-6:]
+    lax.fori_loop(0, slope_ref.shape[0] // 16, step, 0, unroll=2)
+
+
+def conv_kernel(mask_ref, hid_ref, near_ref, far_ref, vec_ref, *refs, relatives, slim):
+    pieces, refs = refs[:2], refs[2:]
+    weight_ref, out_ref, sum_ref, rim_ref, all_ref, stack, prod, edge = refs
     size = all_ref.shape[0] // 2
     for k, piece in enumerate(pieces):
         all_ref[k * size : (k + 1) * size] = piece[...]
-    rows = hid_ref.shape[0] - 2 * RIM
+    odd = lax.axis_index("seq") % 2
+    rim_ref[1 - odd] = near_ref[...]
+    rim_ref[odd] = far_ref[...]
+    for side in range(2):
+        for k in range(0, RIM, 16):
+            v = rim_ref[side, k : k + 16, :].astype(F32) * vec_ref[2:3, :] + vec_ref[3:4, :]
+            edge[side * RIM + k : side * RIM + k + 16, :] = gelu_and_slope(v)[0].astype(BF16)
+    rows = hid_ref.shape[0]
     weight_ref[...] = place(pieces, relatives, stack, lax.axis_index("seq"), slim)
     for at in range(0, weight_ref.shape[1], 256):
         part = slice(at, min(at + 256, weight_ref.shape[1]))
-        prod[:, part] = jnp.dot(hid_ref[...], weight_ref[:, part], preferred_element_type=F32)
+        prod[RIM : RIM + rows, part] = jnp.dot(
+            hid_ref[...], weight_ref[:, part], preferred_element_type=F32
+        )
+        sides = jnp.dot(edge[...], weight_ref[:, part], preferred_element_type=F32)
+        prod[:RIM, part] = sides[:RIM]
+        prod[RIM + rows :, part] = sides[RIM:]
 
     def rows_of(begin, count):
         value = 0.0
@@ -364,6 +374,9 @@
     token_ref[...] = jnp.zeros_like(token_ref)
     rows = x_ref.shape[0]
     for r, part in enumerate(parts):
+        part = part[...]
+        if part.shape[0] < rows + point.shape[0]:
+            part = unfold_rows(part.astype(F32), 3 * LANES // 4).astype(BF16)
         hidden[:, r * LANES : (r + 1) * LANES] = part[:rows, :]
         point[:, r * LANES : (r + 1) * LANES] = part[rows:, :]
     for at in range(0, x_ref.shape[1], 256):
@@ -378,6 +391,10 @@
     for k in range(kept_ref.shape[0]):
         kept_ref[k] = blocks(2 * k + high)
         sent_ref[k] = blocks(2 * k + 1 - high).astype(BF16)
+
+
+def bit_of(reach):
+    return (lax.axis_index("seq") // reach) % 2
 
 
 def terms_of(part, grad, term_ref, at, mask_ref):
@@ -404,18 +421,18 @@
     rows = term_ref.shape[0]
     terms_of(part_ref, grad, term_ref, 0, mask_ref)
     taps = lax.dot_general(
-        hid_ref[RIM : RIM + rows, :], term_ref[...], ROW_DIMS, preferred_element_type=F32
+        hid_ref[...], term_ref[...], ROW_DIMS, preferred_element_type=F32
     )
     point = lax.dot_general(cot_ref[...], mid_ref[...], ROW_DIMS, preferred_element_type=F32)
     parts = [taps[:, j * LANES : j * LANES + slim] for j in range(KERNEL_WIDTH)] + [point[:, :slim]]
     full[...] = jnp.concatenate(parts, axis=1)
-    high = lax.axis_index("seq") % 2
-    halve(lambda k: full[pl.ds(pl.multiple_of(k * depth, 8), depth), :], kept_ref, sent_ref, high)
+    halve(
+        lambda k: full[pl.ds(pl.multiple_of(k * depth, 8), depth), :], kept_ref, sent_ref, bit_of(1)
+    )
 
 
 def fold_kernel(old_ref, got_ref, kept_ref, sent_ref, *, reach):
-    high = (lax.axis_index("seq") // reach) % 2
-    halve(lambda k: old_ref[k] + got_ref[k].astype(F32), kept_ref, sent_ref, high)
+    halve(lambda k: old_ref[k] + got_ref[k].astype(F32), kept_ref, sent_ref, bit_of(reach))
 
 
 def adamw(weights_old, first_moment_state, second_mom, gradient, step_rate, decay_rate):
@@ -428,6 +445,82 @@
     )
     weights_new = weights_old - step_rate * (corrected + decay_rate * weights_old)
     return (first_next, second_next, weights_new)
+
+
+def first_half_kernel(mask_ref, own_ref, hid_ref, point_ref, *refs):
+    up_ref, both_ref, term, weight, grad = refs[-5:]
+    count = (len(refs) - 5 + 1) // 2
+    grads, weights = refs[: count - 1], refs[count - 1 : -5]
+    rows = up_ref.shape[0]
+    if both_ref.shape[0] < rows + point_ref.shape[0]:
+        both = jnp.concatenate([hid_ref[...].astype(F32), point_ref[...].astype(F32)], axis=0)
+        both_ref[...] = fold_rows(both[:, : 3 * LANES // 4]).astype(BF16)
+    else:
+        both_ref[:rows, :] = hid_ref[...]
+        both_ref[rows:, :] = point_ref[...]
+    wide = KERNEL_WIDTH * LANES
+    term[:, :wide] = own_ref[...]
+    for r, part in enumerate(grads):
+        terms_of(part, grad, term, (r + 1) * wide, mask_ref)
+    for r, piece in enumerate(weights):
+        weight[:, r * wide : (r + 1) * wide] = piece[...]
+    for at in range(0, up_ref.shape[1], 256):
+        part = slice(at, at + 256)
+        up_ref[:, part] = lax.dot_general(
+            term[...], weight[part, :], LANE_DIMS, preferred_element_type=F32
+        )
+
+
+def second_half_kernel(mask_ref, x_ref, slope_one, slope_two, vec_ref, part_ref, *refs):
+    d_ref, sum_ref, term, weight, grad = refs[-5:]
+    count = (len(refs) - 5) // 2
+    grads, weights = refs[:count], refs[count:-5]
+    rows, width = x_ref.shape
+    wide = KERNEL_WIDTH * LANES
+    for r in range(count):
+        terms_of(grads[r], grad, term, r * wide, mask_ref)
+    for r, piece in enumerate(weights):
+        weight[:, r * wide : (r + 1) * wide] = piece[...]
+    for at in range(0, width, 256):
+        part = slice(at, at + 256)
+        up = lax.dot_general(term[...], weight[part, :], LANE_DIMS, preferred_element_type=F32)
+        slope = jnp.concatenate([slope_one[:, part], slope_two[:, part]], axis=0)
+        d = (up + part_ref[:, part]) * slope
+        d_ref[:, part] = d
+        centered = x_ref[:, part].astype(F32) * vec_ref[0:1, part] + vec_ref[1:2, part]
+        sum_ref[0:1, part] = jnp.sum(d * centered, 0, keepdims=True)
+        sum_ref[1:2, part] = jnp.sum(d, 0, keepdims=True)
+
+
+def final_kernel(x_ref, cot_ref, d_ref, vec_ref, one_ref, two_ref, *refs, bin_count):
+    states, late_ref, outs, (out_ref, sems) = refs[:3], refs[3], refs[4:8], refs[8:]
+    late_ref[...] = jnp.zeros_like(late_ref)
+    rows, width = x_ref.shape
+    total = one_ref[...] + two_ref[...]
+    root, offset, scale = vec_ref[0:1, :], vec_ref[1:2, :], vec_ref[2:3, :]
+    pull = scale * total[0:1] / bin_count
+    slant = pull * root
+    level = scale * total[1:2] / bin_count + pull * offset
+    step = 16
+    chunk = rows // sems.shape[0]
+
+    def body(i, carry):
+        at = pl.ds(pl.multiple_of(i * step, 16), step)
+        value = x_ref[at, :].astype(F32) * slant + level
+        out_ref[at, :] = cot_ref[at, :].astype(F32) + (d_ref[at, :] * scale - value)
+        return carry
+
+    sends = []
+    for k in range(sems.shape[0]):
+        lax.fori_loop(k * chunk // step, (k + 1) * chunk // step, body, 0, unroll=4)
+        part = pl.ds(k * chunk, chunk)
+        sends.append(pltpu.make_async_copy(out_ref.at[part], outs[0].at[part], sems.at[k]))
+        sends[-1].start()
+    new = adamw(*(ref[...] for ref in states), total, RATE_NORM, 0.0)
+    for ref, value in zip(outs[1:], new):
+        ref[...] = value
+    for send in sends:
+        send.wait()
 
 
 def weight_step_kernel(old_ref, got_ref, total_ref, *refs):
@@ -448,76 +541,6 @@
         ref[...] = value
 
 
-def first_half_kernel(mask_ref, own_ref, hid_ref, point_ref, *refs):
-    up_ref, both_ref, term, weight, grad = refs[-5:]
-    count = (len(refs) - 5 + 1) // 2
-    grads, weights = refs[: count - 1], refs[count - 1 : -5]
-    rows = up_ref.shape[0]
-    both_ref[:rows, :] = hid_ref[...]
-    both_ref[rows:, :] = point_ref[...]
-    wide = KERNEL_WIDTH * LANES
-    term[:, :wide] = own_ref[...]
-    for r, part in enumerate(grads):
-        terms_of(part, grad, term, (r + 1) * wide, mask_ref)
-    for r, piece in enumerate(weights):
-        weight[:, r * wide : (r + 1) * wide] = piece[...]
-    for at in range(0, up_ref.shape[1], 256):
-        part = slice(at, at + 256)
-        up_ref[:, part] = lax.dot_general(
-            term[...], weight[part, :], LANE_DIMS, preferred_element_type=F32
-        )
-
-
-def second_half_kernel(mask_ref, x_ref, slope_ref, vec_ref, part_ref, *refs):
-    d_ref, sum_ref, term, weight, grad = refs[-5:]
-    count = (len(refs) - 5) // 2
-    grads, weights = refs[:count], refs[count:-5]
-    rows, width = x_ref.shape
-    wide = KERNEL_WIDTH * LANES
-    for r, part in enumerate(grads):
-        terms_of(part, grad, term, r * wide, mask_ref)
-    for r, piece in enumerate(weights):
-        weight[:, r * wide : (r + 1) * wide] = piece[...]
-    for at in range(0, width, 256):
-        part = slice(at, at + 256)
-        up = lax.dot_general(term[...], weight[part, :], LANE_DIMS, preferred_element_type=F32)
-        d = (up + part_ref[:, part]) * slope_ref[:, part]
-        d_ref[:, part] = d
-        centered = x_ref[:, part].astype(F32) * vec_ref[0:1, part] + vec_ref[1:2, part]
-        sum_ref[0:1, part] = jnp.sum(d * centered, 0, keepdims=True)
-        sum_ref[1:2, part] = jnp.sum(d, 0, keepdims=True)
-
-
-def final_kernel(x_ref, cot_ref, d_ref, vec_ref, one_ref, two_ref, *refs, bin_count):
-    norms, out_hbm, news, (out_ref, sems) = refs[:3], refs[3], refs[4:-2], refs[-2:]
-    rows, width = x_ref.shape
-    total = one_ref[...] + two_ref[...]
-    root, offset, scale = vec_ref[0:1, :], vec_ref[1:2, :], vec_ref[2:3, :]
-    pull = scale * total[0:1] / bin_count
-    slant = pull * root
-    level = scale * total[1:2] / bin_count + pull * offset
-    step = 16
-    chunk = rows // sems.shape[0]
-
-    def body(i, carry):
-        at = pl.ds(pl.multiple_of(i * step, 16), step)
-        value = x_ref[at, :].astype(F32) * slant + level
-        out_ref[at, :] = cot_ref[at, :].astype(F32) + (d_ref[at, :] * scale - value)
-        return carry
-
-    sends = []
-    for k in range(sems.shape[0]):
-        lax.fori_loop(k * chunk // step, (k + 1) * chunk // step, body, 0, unroll=4)
-        part = pl.ds(k * chunk, chunk)
-        sends.append(pltpu.make_async_copy(out_ref.at[part], out_hbm.at[part], sems.at[k]))
-        sends[-1].start()
-    new = adamw(*(ref[...] for ref in norms), total, RATE_NORM, 0.0)
-    for ref, value in zip(news, new):
-        ref[...] = value
-    for send in sends:
-        send.wait()
-
-
 def flip(axis, reach):
     return [(i, i ^ reach) for i in range(lax.axis_size(axis))]
 
@@ -533,8 +556,7 @@
     return [size >> k for k in range(1, size.bit_length())]
 
 
-def round_kernel(weight_one, weight_two, one_ref, two_ref, *refs, count=0):
-    rims, (weight_ref, out_ref), outs = refs[:count], refs[count : count + 2], refs[count + 2 :]
+def round_kernel(weight_one, weight_two, one_ref, two_ref, weight_ref, out_ref):
     size = weight_one.shape[0]
     weight_ref[:size] = weight_one[...]
     weight_ref[size:] = weight_two[...]
@@ -542,13 +564,6 @@
     size = (out_ref.shape[0] - SUMS) // 2
     out_ref[SUMS : SUMS + size, :] = one_ref[SUMS : SUMS + size, :]
     out_ref[SUMS + size :, :] = two_ref[SUMS : SUMS + size, :]
-    odd = lax.axis_index("seq") % 2
-    if len(rims) == 1:
-        outs[0][...] = rims[0][1 - odd]
-        outs[1][...] = rims[0][odd]
-    elif rims:
-        outs[0][1 - odd] = rims[0][...]
-        outs[0][odd] = rims[1][...]
 
 
 def copy_kernel(*refs):
@@ -647,40 +662,30 @@
                 ((SUMS + (2 << k) * up_to(depth, 16), LANES), BF16),
             ]
             args = [weight, weight_got, near, near_got]
+            weight, near = call(round_kernel, outs, args, after=[back] if k == 1 else [])
             if k == 0:
-                weight, near, *rims = call(
-                    functools.partial(round_kernel, count=1), outs + [(rim, BF16)] * 2, args + [rims]
+                ahead, back, *rims = call(
+                    mask_kernel,
+                    [((KERNEL_WIDTH, ext, LANES), F32), ((KERNEL_WIDTH, rows, LANES), F32)]
+                    + [(rim, BF16)] * 2,
+                    [starts, rims],
+                    smem=(0,),
+                    after=[near],
                 )
                 rims = [
                     swap(rims[0], "seq", 1),
                     lax.ppermute(rims[1], "seq", pairs + [(j, i) for i, j in pairs]),
                 ]
-                ahead, back = call(
-                    mask_kernel,
-                    [((KERNEL_WIDTH, ext, LANES), F32), ((KERNEL_WIDTH, rows, LANES), F32)],
-                    [starts],
-                    smem=(0,),
-                    after=[near],
-                )
-            elif k == 1:
-                weight, near, rims = call(
-                    functools.partial(round_kernel, count=2),
-                    outs + [((2, *rim), BF16)],
-                    args + rims,
-                    after=[back],
-                )
-            else:
-                weight, near = call(round_kernel, outs, args)
     hidden_in, vec_in, cotangent = call(
         functools.partial(act_kernel, bin_count=bin_count),
-        [((rows + 2 * RIM, width), BF16), ((8, width), F32), (cotangent.shape, BF16)],
-        [inputs, cotangent, rims, near, near_got, norm_in],
+        [((rows, width), BF16), ((8, width), F32), (cotangent.shape, BF16)],
+        [inputs, cotangent, near, near_got, norm_in],
         away=(1,),
         sems=1,
     )
 
     stack_type = BF16 if depth % 16 == 0 else F32
-    conv_own, conv_out, sums_mid, weight = call(
+    conv_own, conv_out, sums_mid, rims, weight = call(
         functools.partial(
             conv_kernel, relatives=relatives_of(weight_order), slim=slim
         ),
@@ -688,10 +693,15 @@
             ((width, wide), BF16),
             ((ext, LANES), F32),
             ((8, LANES), F32),
+            ((2, *rim), BF16),
             ((seq_size, packed, wide), BF16),
         ],
-        [ahead, hidden_in, weight, weight_got],
-        scratch=[((seq_size, depth, wide), stack_type), ((rows + 2 * RIM, wide), F32)],
+        [ahead, hidden_in, *rims, vec_in, weight, weight_got],
+        scratch=[
+            ((seq_size, depth, wide), stack_type),
+            ((rows + 2 * RIM, wide), F32),
+            ((2 * RIM, width), BF16),
+        ],
     )
     weight = swap(weight, "ch", top)
     upstream, point_own = call(
@@ -702,9 +712,17 @@
         after=[sums_mid],
     )
     conv_near = gather_parts(conv_own, lower)
-    total = sums_mid
+    total, others, slopes = sums_mid, [upstream], []
     for k, reach in enumerate(sum_order):
-        total = add(total, swap(total, "seq", reach), [upstream])
+        total = add(total, swap(total, "seq", reach), others)
+        if k < 2:
+            others = call(
+                functools.partial(slope_kernel, first=k * rows // 2),
+                [((rows // 2, width), F32)],
+                [inputs, vec_in],
+                after=[total],
+            )
+            slopes += others
     (conv_far,) = call(
         functools.partial(place_kernel, relatives=relatives_of(weight_order), slim=slim),
         [((width, wide), BF16)],
@@ -748,16 +766,15 @@
     side = ch_size // 2 * wide
     up_part, both = call(
         first_half_kernel,
-        [((rows, width), F32), ((rows + width, LANES), BF16)],
+        [((rows, width), F32), ((3 * (rows + width) // 4 if folds(rows + width, slim) else rows + width, LANES), BF16)],
         [back, terms, hidden_mid, point_own, *grad_near[1:], *conv_near],
         scratch=[((rows, side), BF16), ((width, side), BF16), ((ext, LANES), F32)],
     )
-    (slope_in,) = call(slope_kernel, [((rows, width), F32)], [inputs, vec_in], after=[up_part])
-    grad_far = gather_parts(copies([grad_far], [slope_in])[0], lower)
+    grad_far = gather_parts(copies([grad_far], [up_part])[0], lower)
     d_in, sums_back = call(
         second_half_kernel,
         [((rows, width), F32), ((2, width), F32)],
-        [back, inputs, slope_in, vec_in, up_part, *grad_far, *conv_far],
+        [back, inputs, *slopes, vec_in, up_part, *grad_far, *conv_far],
         scratch=[((rows, side), BF16), ((width, side), BF16), ((ext, LANES), F32)],
     )
     both_parts = gather_parts(both, lower)
@@ -783,21 +800,22 @@
         scratch=[((rows, ch_size * LANES), BF16), ((width, ch_size * LANES), BF16)],
         after=[total_back],
     )
-    input_grad, *in_new = call(
+    late, input_grad, *in_new = call(
         functools.partial(final_kernel, bin_count=bin_count),
-        [((rows, width), F32)] + [((2, width), F32)] * 3,
+        [((8, LANES), F32), ((rows, width), F32)] + [((2, width), F32)] * 3,
         [inputs, cotangent, d_in, vec_in, total_back, total_got, norm_in, first_in, second_in],
         scratch=[((rows, width), F32)],
+        away_outs=(1,),
+        sems=8,
         after=[token],
-        away_outs=(0,),
-        sems=8,
-    )
+    )
+    states = [master_conv, first_conv, second_conv, master_point, first_point, second_point]
+    states += [norm_mid, first_mid, second_mid]
     news = call(
         weight_step_kernel,
-        [(master_conv.shape, F32)] * 3 + [(master_point.shape, F32)] * 3 + [(norm_mid.shape, F32)] * 3,
-        [kept, got, total_mid, master_conv, first_conv, second_conv]
-        + [master_point, first_point, second_point, norm_mid, first_mid, second_mid],
-        after=[token],
+        [(x.shape, F32) for x in states],
+        [kept, got, total_mid] + states,
+        after=[late],
     )
     return (block_out, input_grad, *news[:6], *in_new, *news[6:])
 

time: 88.7 us -> 84.2 us (0.949)
  waiting for transfers between devices: 26.3 us -> 22.7 us
  starting transfers between devices: 28.7 us -> 26.8 us
  blocking collectives: 10.5 us -> 11.4 us
    ppermute x25, waiting for transfers between devices: 26.3 us -> 22.7 us  [swap(): return lax.ppermute(x, axis, flip(axis, reach))]
    ppermute x25, starting transfers between devices: 28.1 us -> 26.2 us  [swap(): return lax.ppermute(x, axis, flip(axis, reach))]
    all_to_all x1, blocking collectives: 10.5 us -> 11.4 us  [spread(): return lax.all_to_all(copies, axes, 0, 0, tiled=True)]
    pallas_call x27 -> x28, Pallas kernels: 21.8 us -> 21.9 us  [call(): pl.pallas_call(kernel, out_shape=[jax.ShapeDtypeStruct(s, t) for s, t in...]
  transfers between devices with their start and end apart: 26 -> 26, of which waited for: 11 -> 12; matrix products, arithmetic and copies ran while one was open for 0% -> 0% of each run, Pallas kernels for 19% -> 20%
where the time goes in v5:
time: 84.2 us; the launch traced here: 84 us
  starting transfers between devices  26.8 us (32%)
  waiting for transfers between devices  22.7 us (27%)
  Pallas kernels  21.9 us (26%)
  blocking collectives  11.4 us (14%)
  between operations  1.02 us (1%)
    ppermute x25, starting transfers between devices, swap(): return lax.ppermute(x, axis, flip(axis, reach))  26.2 us
    ppermute x25, waiting for transfers between devices, swap(): return lax.ppermute(x, axis, flip(axis, reach))  22.7 us
    pallas_call x28, Pallas kernels, call(): pl.pallas_call(kernel, out_shape=[jax.ShapeDtypeStruct(s, t) for s, t in...  21.9 us
    all_to_all x1, blocking collectives, spread(): return lax.all_to_all(copies, axes, 0, 0, tiled=True)  11.4 us
  transfers between devices with their start and end apart: 26, of which 12 were waited for; matrix products, arithmetic and copies ran while one was open for 0% of the time, Pallas kernels for 20%

profile of v5, /device:TPU:0, one launch (start us, length us, event | category | flops | bytes accessed | tf_op | source)
XLA Modules:
  0.0 84.0 jit_solution(5648486444931544523)
XLA Ops:
  0.7 1.7 %first_kernel.1 = (bf16[1024,768]{1,0:T(8,128)(2,1)S(1)}, bf16[1,72,384]{2,1,0:T(8,128)(2,1)S(1)}, bf16[144,128]{1,0:T(8,128)(2,1)S(1)}, bf16[2,48,768]{2,1,0:T(8,128)(2,1)S(1)}) custom-call(bf16[1024,768]{1,0:T(8,128)(2,1)} %refs_0_.2, bf16[1024,768]{1,0:T(8,128)(2,1)} %refs_1_.3, f32[3,96,96]{2,1,0:T(8,128)} %refs_3_.5, f32[96,96]{1,0:T(8,128)} %refs_6_.3), custom_call_target="tpu_custom_call" | custom-call | flops 1 | bytes 1 | tf_op jit(solution)/shard_map/first_kernel/pallas_call | solution.py:48
  2.4 4.1 %collective-permute-start = (bf16[1,72,384]{2,1,0:T(8,128)(2,1)S(1)}, bf16[1,72,384]{2,1,0:T(8,128)(2,1)S(1)}, u32[]{:S(2)}, u32[]{:S(2)}) collective-permute-start(bf16[1,72,384]{2,1,0:T(8,128)(2,1)S(1)} %get-tuple-element.72.refs_0_), channel_id=1, source_target_pairs={{0,16},{4,20},{8,24},{12,28},{16,0},{20,4},{24,8},{28,12},{1,17},{... | collective-permute-start | bytes 165896 | tf_op jit(solution)/shard_map/ppermute | solution.py:588
  6.6 4.8 %collective-permute-done.1.refs_3_ = bf16[144,128]{1,0:T(8,128)(2,1)S(1)} collective-permute-done((bf16[144,128]{1,0:T(8,128)(2,1)S(1)}, bf16[144,128]{1,0:T(8,128)(2,1)S(1)}, u32[]{:S(2)}, u32[]{:S(2)}) %collective-permute-start.1) | collective-permute-done | bytes 36896 | tf_op jit(solution)/shard_map/ppermute | solution.py:588
  11.4 1.6 %collective-permute-start.2 = (bf16[2,72,384]{2,1,0:T(8,128)(2,1)S(1)}, bf16[2,72,384]{2,1,0:T(8,128)(2,1)S(1)}, u32[]{:S(2)}, u32[]{:S(2)}) collective-permute-start(bf16[2,72,384]{2,1,0:T(8,128)(2,1)S(1)} %get-tuple-element.77.refs_0_), channel_id=1, source_target_pairs={{0,8},{4,12},{8,0},{12,4},{16,24},{20,28},{24,16},{28,20},{1,9},{5... | collective-permute-start | bytes 331784 | tf_op jit(solution)/shard_map/ppermute | solution.py:588
  13.0 1.5 %collective-permute-start.3 = (bf16[240,128]{1,0:T(8,128)(2,1)S(1)}, bf16[240,128]{1,0:T(8,128)(2,1)S(1)}, u32[]{:S(2)}, u32[]{:S(2)}) collective-permute-start(bf16[240,128]{1,0:T(8,128)(2,1)S(1)} %get-tuple-element.74.refs_2_), channel_id=1, source_target_pairs={{0,4},{4,0},{8,12},{12,8},{16,20},{20,16},{24,28},{28,24},{1,5},{5... | collective-permute-start | bytes 184328 | tf_op jit(solution)/shard_map/ppermute | solution.py:588
  14.5 1.4 %mask_kernel.1 = (f32[3,1056,128]{2,1,0:T(8,128)S(1)}, f32[3,1024,128]{2,1,0:T(8,128)S(1)}, bf16[48,768]{1,0:T(8,128)(2,1)S(1)}, bf16[48,768]{1,0:T(8,128)(2,1)S(1)}) custom-call(s32[8]{0:T(128)S(1)} %copy-done.12, bf16[2,48,768]{2,1,0:T(8,128)(2,1)S(1)} %get-tuple-element.71.refs_1_, bf16[240,128]{1,0:T(8,128)(2,1)S(1)} %get-tuple-element.74.refs_2_), custom_call_target="tpu_custom_call" | custom-call | flops 1 | bytes 1 | tf_op jit(solution)/shard_map/mask_kernel/pallas_call | solution.py:48
  15.9 1.3 %collective-permute-done.3.refs_3_ = bf16[240,128]{1,0:T(8,128)(2,1)S(1)} collective-permute-done((bf16[240,128]{1,0:T(8,128)(2,1)S(1)}, bf16[240,128]{1,0:T(8,128)(2,1)S(1)}, u32[]{:S(2)}, u32[]{:S(2)}) %collective-permute-start.3) | collective-permute-done | bytes 61472 | tf_op jit(solution)/shard_map/ppermute | solution.py:588
  17.3 1.6 %collective-permute-start.7 = (bf16[4,72,384]{2,1,0:T(8,128)(2,1)S(1)}, bf16[4,72,384]{2,1,0:T(8,128)(2,1)S(1)}, u32[]{:S(2)}, u32[]{:S(2)}) collective-permute-start(bf16[4,72,384]{2,1,0:T(8,128)(2,1)S(1)} %get-tuple-element.83.refs_5_), channel_id=1, source_target_pairs={{0,4},{4,0},{8,12},{12,8},{16,20},{20,16},{24,28},{28,24},{1,5},{5... | collective-permute-start | bytes 663560 | tf_op jit(solution)/shard_map/ppermute | solution.py:588
  20.5 3.6 %collective-permute-done.4.refs_3_ = bf16[432,128]{1,0:T(8,128)(2,1)S(1)} collective-permute-done((bf16[432,128]{1,0:T(8,128)(2,1)S(1)}, bf16[432,128]{1,0:T(8,128)(2,1)S(1)}, u32[]{:S(2)}, u32[]{:S(2)}) %collective-permute-start.4) | collective-permute-done | bytes 110624 | tf_op jit(solution)/shard_map/ppermute | solution.py:588
  24.2 1.5 %act_kernel.1 = (bf16[1024,768]{1,0:T(8,128)(2,1)S(1)}, f32[8,768]{1,0:T(8,128)S(1)}, bf16[1024,768]{1,0:T(8,128)(2,1)S(1)}) custom-call(bf16[1024,768]{1,0:T(8,128)(2,1)S(1)} %get-tuple-element.70.refs_0_.refs_1_, bf16[1024,768]{1,0:T(8,128)(2,1)} %refs_1_.3, bf16[432,128]{1,0:T(8,128)(2,1)S(1)} %get-tuple-element.78.refs_2_, ...), custom_call_target="tpu_custom_call" | custom-call | flops 1 | bytes 1 | tf_op jit(solution)/shard_map/act_kernel/pallas_call | solution.py:48
  25.7 1.4 %conv_kernel.1 = (bf16[768,384]{1,0:T(8,128)(2,1)S(1)}, f32[1056,128]{1,0:T(8,128)S(1)}, f32[8,128]{1,0:T(8,128)S(1)}, bf16[2,48,768]{2,1,0:T(8,128)(2,1)S(1)}, bf16[8,72,384]{2,1,0:T(8,128)(2,1)S(1)}) custom-call(f32[3,1056,128]{2,1,0:T(8,128)S(1)} %get-tuple-element.76.refs_0_, bf16[1024,768]{1,0:T(8,128)(2,1)S(1)} %get-tuple-element.79.refs_1_.refs_2_, ...), custom_call_target="tpu_custom_call" | custom-call | flops 1 | bytes 1 | tf_op jit(solution)/shard_map/conv_kernel/pallas_call | solution.py:48
  27.2 1.6 %collective-permute-start.11 = (bf16[8,72,384]{2,1,0:T(8,128)(2,1)S(1)}, bf16[8,72,384]{2,1,0:T(8,128)(2,1)S(1)}, u32[]{:S(2)}, u32[]{:S(2)}) collective-permute-start(bf16[8,72,384]{2,1,0:T(8,128)(2,1)S(1)} %get-tuple-element.89), channel_id=1, source_target_pairs={{0,2},{1,3},{2,0},{3,1},{4,6},{5,7},{6,4},{7,5},{8,10},{9,11},{10,... | collective-permute-start | bytes 1327112 | tf_op jit(solution)/shard_map/ppermute | solution.py:588
  28.8 2.8 %collective-permute-start.8 = (f32[8,128]{1,0:T(8,128)S(1)}, f32[8,128]{1,0:T(8,128)S(1)}, u32[]{:S(2)}, u32[]{:S(2)}) collective-permute-start(f32[8,128]{1,0:T(8,128)S(1)} %get-tuple-element.84.refs_4_.refs_0_), channel_id=1, source_target_pairs={{0,4},{4,0},{8,12},{12,8},{16,20},{20,16},{24,28},{28,24},{1,5},{5... | collective-permute-start | bytes 12296 | tf_op jit(solution)/shard_map/ppermute | solution.py:588
  32.3 0.9 %collective-permute-done.8.refs_1_ = f32[8,128]{1,0:T(8,128)S(1)} collective-permute-done((f32[8,128]{1,0:T(8,128)S(1)}, f32[8,128]{1,0:T(8,128)S(1)}, u32[]{:S(2)}, u32[]{:S(2)}) %collective-permute-start.8) | collective-permute-done | bytes 4128 | tf_op jit(solution)/shard_map/ppermute | solution.py:588
  33.2 2.0 %collective-permute-start.9 = (f32[8,128]{1,0:T(8,128)S(1)}, f32[8,128]{1,0:T(8,128)S(1)}, u32[]{:S(2)}, u32[]{:S(2)}) collective-permute-start(f32[8,128]{1,0:T(8,128)S(1)} %add_kernel.5.refs_2_.refs_0_), channel_id=1, source_target_pairs={{0,8},{4,12},{8,0},{12,4},{16,24},{20,28},{24,16},{28,20},{1,9},{5... | collective-permute-start | bytes 12296 | tf_op jit(solution)/shard_map/ppermute | solution.py:588
  35.2 1.1 %slope_kernel.2.refs_2_ = f32[512,768]{1,0:T(8,128)S(1)} custom-call(bf16[1024,768]{1,0:T(8,128)(2,1)S(1)} %get-tuple-element.70.refs_0_.refs_1_, f32[8,768]{1,0:T(8,128)S(1)} %get-tuple-element.82.refs_4_.refs_1_.refs_3_, f32[8,128]{1,0:T(8,128)S(1)} %add_kernel.5.refs_2_.refs_0_), custom_call_target="tpu_custom_call" | custom-call | flops 1 | bytes 1 | tf_op jit(solution)/shard_map/slope_kernel/pallas_call | solution.py:48
  36.8 3.0 %collective-permute-start.10 = (f32[8,128]{1,0:T(8,128)S(1)}, f32[8,128]{1,0:T(8,128)S(1)}, u32[]{:S(2)}, u32[]{:S(2)}) collective-permute-start(f32[8,128]{1,0:T(8,128)S(1)} %add_kernel.6.refs_2_.refs_0_), channel_id=1, source_target_pairs={{0,16},{4,20},{8,24},{12,28},{16,0},{20,4},{24,8},{28,12},{1,17},{... | collective-permute-start | bytes 12296 | tf_op jit(solution)/shard_map/ppermute | solution.py:588
  39.8 1.1 %slope_kernel.3.refs_2_.refs_3_ = f32[512,768]{1,0:T(8,128)S(1)} custom-call(bf16[1024,768]{1,0:T(8,128)(2,1)S(1)} %get-tuple-element.70.refs_0_.refs_1_, f32[8,768]{1,0:T(8,128)S(1)} %get-tuple-element.82.refs_4_.refs_1_.refs_3_, f32[8,128]{1,0:T(8,128)S(1)} %add_kernel.6.refs_2_.refs_0_), custom_call_target="tpu_custom_call" | custom-call | flops 1 | bytes 1 | tf_op jit(solution)/shard_map/slope_kernel/pallas_call | solution.py:48
  42.2 11.4 %all_to_all.5.refs_0_ = f32[8,2,128]{2,1,0:T(2,128)S(1)} all-to-all(f32[8,2,128]{2,1,0:T(2,128)S(1)} %get-tuple-element.91), channel_id=1, replica_groups=mesh['seq'=8,'ch'=4] {'seq'}, dimensions={0} | all-to-all | bytes 16384 | tf_op jit(solution)/shard_map/all_to_all | solution.py:599
  54.6 0.8 collective-permute-start.16
  55.4 1.9 %weight_grad_kernel.1 = (bf16[1024,384]{1,0:T(8,128)(2,1)S(1)}, f32[4,96,384]{2,1,0:T(8,128)S(1)}, bf16[4,96,384]{2,1,0:T(8,128)(2,1)S(1)}) custom-call(f32[3,1024,128]{2,1,0:T(8,128)S(1)} %get-tuple-element.75.refs_4_.refs_0_, bf16[792,128]{1,0:T(8,128)(2,1)S(1)} %get-tuple-element.95.refs_1_, bf16[1024,768]{1,0:T(8,128)(2,1)S(1)} %get-tuple-element.79.refs_1_.refs_2_, ...), custom_call_target="tpu_custom_call" | custom-call | flops 1 | bytes 1 | tf_op jit(solution)/shard_map/weight_grad_kernel/pallas_call | solution.py:48
  57.9 1.5 %first_half_kernel.1 = (f32[1024,768]{1,0:T(8,128)S(1)}, bf16[1344,128]{1,0:T(8,128)(2,1)S(1)}) custom-call(f32[3,1024,128]{2,1,0:T(8,128)S(1)} %get-tuple-element.75.refs_4_.refs_0_, bf16[1024,384]{1,0:T(8,128)(2,1)S(1)} %get-tuple-element.97.refs_1_, bf16[1024,128]{1,0:T(8,128)(2,1)S(1)} %get-tuple-element.96.refs_4_.refs_2_, ...), custom_call_target="tpu_custom_call" | custom-call | flops 1 | bytes 1 | tf_op jit(solution)/shard_map/first_half_kernel/pallas_call | solution.py:48
  59.5 2.1 %collective-permute-done.16.refs_0_ = bf16[792,128]{1,0:T(8,128)(2,1)S(1)} collective-permute-done((bf16[792,128]{1,0:T(8,128)(2,1)S(1)}, bf16[792,128]{1,0:T(8,128)(2,1)S(1)}, u32[]{:S(2)}, u32[]{:S(2)}) %collective-permute-start.16) | collective-permute-done | bytes 202784 | tf_op jit(solution)/shard_map/ppermute | solution.py:588
  61.7 0.8 %collective-permute-start.15 = (bf16[1344,128]{1,0:T(8,128)(2,1)S(1)}, bf16[1344,128]{1,0:T(8,128)(2,1)S(1)}, u32[]{:S(2)}, u32[]{:S(2)}) collective-permute-start(bf16[1344,128]{1,0:T(8,128)(2,1)S(1)} %get-tuple-element.99.refs_1_), channel_id=1, source_target_pairs={{0,2},{1,3},{2,0},{3,1},{4,6},{5,7},{6,4},{7,5},{8,10},{9,11},{10,... | collective-permute-start | bytes 1032200 | tf_op jit(solution)/shard_map/ppermute | solution.py:588
  63.1 2.1 %second_half_kernel.1 = (f32[1024,768]{1,0:T(8,128)S(1)}, f32[2,768]{1,0:T(2,128)S(1)}) custom-call(f32[3,1024,128]{2,1,0:T(8,128)S(1)} %get-tuple-element.75.refs_4_.refs_0_, bf16[1024,768]{1,0:T(8,128)(2,1)S(1)} %get-tuple-element.70.refs_0_.refs_1_, f32[512,768]{1,0:T(8,128)S(1)} %slope_kernel.2.refs_2_, f32[512,768]{1,0:T(8,128)S(1)} %slope_kernel.3.refs_2_.refs_3_, ...), custom_call_target="tpu_custom_call" | custom-call | flops 1 | bytes 1 | tf_op jit(solution)/shard_map/second_half_kernel/pallas_call | solution.py:48
  65.3 0.8 collective-permute-done.20.refs_1_
  67.3 4.0 %collective-permute-done.19.refs_1_ = f32[2,768]{1,0:T(2,128)S(1)} collective-permute-done((f32[2,768]{1,0:T(2,128)S(1)}, f32[2,768]{1,0:T(2,128)S(1)}, u32[]{:S(2)}, u32[]{:S(2)}) %collective-permute-start.19) | collective-permute-done | bytes 6176 | tf_op jit(solution)/shard_map/ppermute | solution.py:588
  72.0 3.0 %collective-permute-done.21.refs_1_ = f32[2,768]{1,0:T(2,128)S(1)} collective-permute-done((f32[2,768]{1,0:T(2,128)S(1)}, f32[2,768]{1,0:T(2,128)S(1)}, u32[]{:S(2)}, u32[]{:S(2)}) %collective-permute-start.21) | collective-permute-done | bytes 6176 | tf_op jit(solution)/shard_map/ppermute | solution.py:588
  75.1 1.6 %collective-permute-start.25 = (bf16[1,96,384]{2,1,0:T(8,128)(2,1)S(1)}, bf16[1,96,384]{2,1,0:T(8,128)(2,1)S(1)}, u32[]{:S(2)}, u32[]{:S(2)}) collective-permute-start(bf16[1,96,384]{2,1,0:T(8,128)(2,1)S(1)} %get-tuple-element.106.refs_2_), channel_id=1, source_target_pairs={{0,16},{4,20},{8,24},{12,28},{16,0},{20,4},{24,8},{28,12},{1,17},{... | collective-permute-start | bytes 221192 | tf_op jit(solution)/shard_map/ppermute | solution.py:588
  77.1 2.5 %out_kernel.1 = (bf16[1024,768]{1,0:T(8,128)(2,1)}, f32[8,128]{1,0:T(8,128)S(1)}) custom-call(bf16[1024,768]{1,0:T(8,128)(2,1)S(1)} %get-tuple-element.70.refs_0_.refs_1_, bf16[1344,128]{1,0:T(8,128)(2,1)S(1)} %get-tuple-element.99.refs_1_, bf16[1344,128]{1,0:T(8,128)(2,1)S(1)} %collective-permute-done.14.refs_2_, bf16[1344,128]{1,0:T(8,128)(2,1)S(1)} %copy_kernel.5.refs_3_, ...), custom_call_target="tpu_custom_call" | custom-call | flops 1 | bytes 1 | tf_op jit(solution)/shard_map/out_kernel/pallas_call | solution.py:48
  80.4 2.5 %final_kernel.1 = (f32[8,128]{1,0:T(8,128)S(1)}, f32[1024,768]{1,0:T(8,128)}, f32[2,768]{1,0:T(2,128)}, f32[2,768]{1,0:T(2,128)}, f32[2,768]{1,0:T(2,128)}) custom-call(bf16[1024,768]{1,0:T(8,128)(2,1)S(1)} %get-tuple-element.70.refs_0_.refs_1_, bf16[1024,768]{1,0:T(8,128)(2,1)S(1)} %get-tuple-element.85.refs_0_.refs_3_.refs_1_, ...), custom_call_target="tpu_custom_call" | custom-call | flops 1 | bytes 1 | tf_op jit(solution)/shard_map/final_kernel/pallas_call | solution.py:48
  83.0 1.0 %weight_step_kernel.1 = (f32[3,96,96]{2,1,0:T(8,128)}, f32[3,96,96]{2,1,0:T(8,128)}, f32[3,96,96]{2,1,0:T(8,128)}, f32[96,96]{1,0:T(8,128)}, f32[96,96]{1,0:T(8,...) custom-call(f32[1,96,384]{2,1,0:T(8,128)S(1)} %get-tuple-element.111.refs_0_, ...), custom_call_target="tpu_custom_call" | custom-call | flops 1 | bytes 1 | tf_op jit(solution)/shard_map/weight_step_kernel/pallas_call | solution.py:48
  (75 shorter events, 9.7 us)
Async XLA Ops:
  0.6 13.9 %copy-start.12 = (s32[8]{0:T(128)S(1)}, s32[8]{0:T(128)}, u32[]{:S(2)}) copy-start(s32[8]{0:T(128)} %refs_0_.3) | copy-start | bytes 100
  2.4 21.8 %copy-start.6 = (f32[2,768]{1,0:T(2,128)S(1)}, f32[2,768]{1,0:T(2,128)}, u32[]{:S(2)}) copy-start(f32[2,768]{1,0:T(2,128)} %refs_6_.2) | copy-start | bytes 18436
  2.4 9.0 %collective-permute-start = (bf16[1,72,384]{2,1,0:T(8,128)(2,1)S(1)}, bf16[1,72,384]{2,1,0:T(8,128)(2,1)S(1)}, u32[]{:S(2)}, u32[]{:S(2)}) collective-permute-start(bf16[1,72,384]{2,1,0:T(8,128)(2,1)S(1)} %get-tuple-element.72.refs_0_), channel_id=1, source_target_pairs={{0,16},{4,20},{8,24},{12,28},{16,0},{20,4},{24,8},{28,12},{1,17},{... | collective-permute-start | bytes 165896 | tf_op jit(solution)/shard_map/ppermute | solution.py:588
  6.5 4.9 %collective-permute-start.1 = (bf16[144,128]{1,0:T(8,128)(2,1)S(1)}, bf16[144,128]{1,0:T(8,128)(2,1)S(1)}, u32[]{:S(2)}, u32[]{:S(2)}) collective-permute-start(bf16[144,128]{1,0:T(8,128)(2,1)S(1)} %get-tuple-element.73.refs_2_), channel_id=1, source_target_pairs={{0,16},{4,20},{8,24},{12,28},{16,0},{20,4},{24,8},{28,12},{1,17},{... | collective-permute-start | bytes 110600 | tf_op jit(solution)/shard_map/ppermute | solution.py:588
  11.4 5.9 %collective-permute-start.2 = (bf16[2,72,384]{2,1,0:T(8,128)(2,1)S(1)}, bf16[2,72,384]{2,1,0:T(8,128)(2,1)S(1)}, u32[]{:S(2)}, u32[]{:S(2)}) collective-permute-start(bf16[2,72,384]{2,1,0:T(8,128)(2,1)S(1)} %get-tuple-element.77.refs_0_), channel_id=1, source_target_pairs={{0,8},{4,12},{8,0},{12,4},{16,24},{20,28},{24,16},{28,20},{1,9},{5... | collective-permute-start | bytes 331784 | tf_op jit(solution)/shard_map/ppermute | solution.py:588
  13.0 4.2 %collective-permute-start.3 = (bf16[240,128]{1,0:T(8,128)(2,1)S(1)}, bf16[240,128]{1,0:T(8,128)(2,1)S(1)}, u32[]{:S(2)}, u32[]{:S(2)}) collective-permute-start(bf16[240,128]{1,0:T(8,128)(2,1)S(1)} %get-tuple-element.74.refs_2_), channel_id=1, source_target_pairs={{0,4},{4,0},{8,12},{12,8},{16,20},{20,16},{24,28},{28,24},{1,5},{5... | collective-permute-start | bytes 184328 | tf_op jit(solution)/shard_map/ppermute | solution.py:588
  17.3 8.5 %collective-permute-start.7 = (bf16[4,72,384]{2,1,0:T(8,128)(2,1)S(1)}, bf16[4,72,384]{2,1,0:T(8,128)(2,1)S(1)}, u32[]{:S(2)}, u32[]{:S(2)}) collective-permute-start(bf16[4,72,384]{2,1,0:T(8,128)(2,1)S(1)} %get-tuple-element.83.refs_5_), channel_id=1, source_target_pairs={{0,4},{4,0},{8,12},{12,8},{16,20},{20,16},{24,28},{28,24},{1,5},{5... | collective-permute-start | bytes 663560 | tf_op jit(solution)/shard_map/ppermute | solution.py:588
  18.8 5.3 %collective-permute-start.4 = (bf16[432,128]{1,0:T(8,128)(2,1)S(1)}, bf16[432,128]{1,0:T(8,128)(2,1)S(1)}, u32[]{:S(2)}, u32[]{:S(2)}) collective-permute-start(bf16[432,128]{1,0:T(8,128)(2,1)S(1)} %get-tuple-element.78.refs_2_), channel_id=1, source_target_pairs={{0,8},{4,12},{8,0},{12,4},{16,24},{20,28},{24,16},{28,20},{1,9},{5... | collective-permute-start | bytes 331784 | tf_op jit(solution)/shard_map/ppermute | solution.py:588
  19.3 6.4 %collective-permute-start.5 = (bf16[48,768]{1,0:T(8,128)(2,1)S(1)}, bf16[48,768]{1,0:T(8,128)(2,1)S(1)}, u32[]{:S(2)}, u32[]{:S(2)}) collective-permute-start(bf16[48,768]{1,0:T(8,128)(2,1)S(1)} %get-tuple-element.80), channel_id=1, source_target_pairs={{0,4},{4,0},{8,12},{12,8},{16,20},{20,16},{24,28},{28,24},{1,5},{5... | collective-permute-start | bytes 221192 | tf_op jit(solution)/shard_map/ppermute | solution.py:588
  19.9 5.8 %collective-permute-start.6 = (bf16[48,768]{1,0:T(8,128)(2,1)S(1)}, bf16[48,768]{1,0:T(8,128)(2,1)S(1)}, u32[]{:S(2)}, u32[]{:S(2)}) collective-permute-start(bf16[48,768]{1,0:T(8,128)(2,1)S(1)} %get-tuple-element.81), channel_id=1, source_target_pairs={{4,8},{12,16},{20,24},{8,4},{16,12},{24,20},{5,9},{13,17},{21,25},... | collective-permute-start | bytes 221192 | tf_op jit(solution)/shard_map/ppermute | solution.py:677
  27.2 14.5 %collective-permute-start.12 = (bf16[768,384]{1,0:T(8,128)(2,1)S(1)}, bf16[768,384]{1,0:T(8,128)(2,1)S(1)}, u32[]{:S(2)}, u32[]{:S(2)}) collective-permute-start(bf16[768,384]{1,0:T(8,128)(2,1)S(1)} %get-tuple-element.90.refs_5_), channel_id=1, source_target_pairs={{0,1},{1,0},{2,3},{3,2},{4,5},{5,4},{6,7},{7,6},{8,9},{9,8},{10,11... | collective-permute-start | bytes 1769480 | tf_op jit(solution)/shard_map/ppermute | solution.py:588
  27.2 14.2 %collective-permute-start.11 = (bf16[8,72,384]{2,1,0:T(8,128)(2,1)S(1)}, bf16[8,72,384]{2,1,0:T(8,128)(2,1)S(1)}, u32[]{:S(2)}, u32[]{:S(2)}) collective-permute-start(bf16[8,72,384]{2,1,0:T(8,128)(2,1)S(1)} %get-tuple-element.89), channel_id=1, source_target_pairs={{0,2},{1,3},{2,0},{3,1},{4,6},{5,7},{6,4},{7,5},{8,10},{9,11},{10,... | collective-permute-start | bytes 1327112 | tf_op jit(solution)/shard_map/ppermute | solution.py:588
  28.8 4.4 %collective-permute-start.8 = (f32[8,128]{1,0:T(8,128)S(1)}, f32[8,128]{1,0:T(8,128)S(1)}, u32[]{:S(2)}, u32[]{:S(2)}) collective-permute-start(f32[8,128]{1,0:T(8,128)S(1)} %get-tuple-element.84.refs_4_.refs_0_), channel_id=1, source_target_pairs={{0,4},{4,0},{8,12},{12,8},{16,20},{20,16},{24,28},{28,24},{1,5},{5... | collective-permute-start | bytes 12296 | tf_op jit(solution)/shard_map/ppermute | solution.py:588
  33.2 3.6 %collective-permute-start.9 = (f32[8,128]{1,0:T(8,128)S(1)}, f32[8,128]{1,0:T(8,128)S(1)}, u32[]{:S(2)}, u32[]{:S(2)}) collective-permute-start(f32[8,128]{1,0:T(8,128)S(1)} %add_kernel.5.refs_2_.refs_0_), channel_id=1, source_target_pairs={{0,8},{4,12},{8,0},{12,4},{16,24},{20,28},{24,16},{28,20},{1,9},{5... | collective-permute-start | bytes 12296 | tf_op jit(solution)/shard_map/ppermute | solution.py:588
  36.8 4.6 %collective-permute-start.10 = (f32[8,128]{1,0:T(8,128)S(1)}, f32[8,128]{1,0:T(8,128)S(1)}, u32[]{:S(2)}, u32[]{:S(2)}) collective-permute-start(f32[8,128]{1,0:T(8,128)S(1)} %add_kernel.6.refs_2_.refs_0_), channel_id=1, source_target_pairs={{0,16},{4,20},{8,24},{12,28},{16,0},{20,4},{24,8},{28,12},{1,17},{... | collective-permute-start | bytes 12296 | tf_op jit(solution)/shard_map/ppermute | solution.py:588
  54.0 9.1 %collective-permute-start.18 = (bf16[768,384]{1,0:T(8,128)(2,1)S(1)}, bf16[768,384]{1,0:T(8,128)(2,1)S(1)}, u32[]{:S(2)}, u32[]{:S(2)}) collective-permute-start(bf16[768,384]{1,0:T(8,128)(2,1)S(1)} %copy_kernel.4.refs_8_), channel_id=1, source_target_pairs={{0,1},{1,0},{2,3},{3,2},{4,5},{5,4},{6,7},{7,6},{8,9},{9,8},{10,11... | collective-permute-start | bytes 1769480 | tf_op jit(solution)/shard_map/ppermute | solution.py:588
  54.1 3.8 %collective-permute-start.13 = (bf16[792,128]{1,0:T(8,128)(2,1)S(1)}, bf16[792,128]{1,0:T(8,128)(2,1)S(1)}, u32[]{:S(2)}, u32[]{:S(2)}) collective-permute-start(bf16[792,128]{1,0:T(8,128)(2,1)S(1)} %get-tuple-element.95.refs_1_), channel_id=1, source_target_pairs={{0,1},{1,0},{2,3},{3,2},{4,5},{5,4},{6,7},{7,6},{8,9},{9,8},{10,11... | collective-permute-start | bytes 608264 | tf_op jit(solution)/shard_map/ppermute | solution.py:588
  54.6 7.0 %collective-permute-start.16 = (bf16[792,128]{1,0:T(8,128)(2,1)S(1)}, bf16[792,128]{1,0:T(8,128)(2,1)S(1)}, u32[]{:S(2)}, u32[]{:S(2)}) collective-permute-start(bf16[792,128]{1,0:T(8,128)(2,1)S(1)} %get-tuple-element.95.refs_1_), channel_id=1, source_target_pairs={{0,2},{1,3},{2,0},{3,1},{4,6},{5,7},{6,4},{7,5},{8,10},{9,11},{10,... | collective-permute-start | bytes 608264 | tf_op jit(solution)/shard_map/ppermute | solution.py:588
  57.3 8.8 %collective-permute-start.20 = (bf16[4,96,384]{2,1,0:T(8,128)(2,1)S(1)}, bf16[4,96,384]{2,1,0:T(8,128)(2,1)S(1)}, u32[]{:S(2)}, u32[]{:S(2)}) collective-permute-start(bf16[4,96,384]{2,1,0:T(8,128)(2,1)S(1)} %get-tuple-element.103), channel_id=1, source_target_pairs={{0,4},{4,0},{8,12},{12,8},{16,20},{20,16},{24,28},{28,24},{1,5},{5... | collective-permute-start | bytes 884744 | tf_op jit(solution)/shard_map/ppermute | solution.py:588
  61.6 1.5 %collective-permute-start.17 = (bf16[792,128]{1,0:T(8,128)(2,1)S(1)}, bf16[792,128]{1,0:T(8,128)(2,1)S(1)}, u32[]{:S(2)}, u32[]{:S(2)}) collective-permute-start(bf16[792,128]{1,0:T(8,128)(2,1)S(1)} %copy_kernel.3.refs_6_), channel_id=1, source_target_pairs={{0,1},{1,0},{2,3},{3,2},{4,5},{5,4},{6,7},{7,6},{8,9},{9,8},{10,11... | collective-permute-start | bytes 608264 | tf_op jit(solution)/shard_map/ppermute | solution.py:588
  61.7 13.3 %collective-permute-start.15 = (bf16[1344,128]{1,0:T(8,128)(2,1)S(1)}, bf16[1344,128]{1,0:T(8,128)(2,1)S(1)}, u32[]{:S(2)}, u32[]{:S(2)}) collective-permute-start(bf16[1344,128]{1,0:T(8,128)(2,1)S(1)} %get-tuple-element.99.refs_1_), channel_id=1, source_target_pairs={{0,2},{1,3},{2,0},{3,1},{4,6},{5,7},{6,4},{7,5},{8,10},{9,11},{10,... | collective-permute-start | bytes 1032200 | tf_op jit(solution)/shard_map/ppermute | solution.py:588
  66.1 5.9 %collective-permute-start.22 = (bf16[2,96,384]{2,1,0:T(8,128)(2,1)S(1)}, bf16[2,96,384]{2,1,0:T(8,128)(2,1)S(1)}, u32[]{:S(2)}, u32[]{:S(2)}) collective-permute-start(bf16[2,96,384]{2,1,0:T(8,128)(2,1)S(1)} %get-tuple-element.104.refs_2_), channel_id=1, source_target_pairs={{0,8},{4,12},{8,0},{12,4},{16,24},{20,28},{24,16},{28,20},{1,9},{5... | collective-permute-start | bytes 442376 | tf_op jit(solution)/shard_map/ppermute | solution.py:588
  66.7 4.6 %collective-permute-start.19 = (f32[2,768]{1,0:T(2,128)S(1)}, f32[2,768]{1,0:T(2,128)S(1)}, u32[]{:S(2)}, u32[]{:S(2)}) collective-permute-start(f32[2,768]{1,0:T(2,128)S(1)} %get-tuple-element.101.refs_2_.refs_0_), channel_id=1, source_target_pairs={{0,16},{4,20},{8,24},{12,28},{16,0},{20,4},{24,8},{28,12},{1,17},{... | collective-permute-start | bytes 18440 | tf_op jit(solution)/shard_map/ppermute | solution.py:588
  71.4 3.6 %collective-permute-start.21 = (f32[2,768]{1,0:T(2,128)S(1)}, f32[2,768]{1,0:T(2,128)S(1)}, u32[]{:S(2)}, u32[]{:S(2)}) collective-permute-start(f32[2,768]{1,0:T(2,128)S(1)} %add_kernel.8.refs_2_.refs_0_), channel_id=1, source_target_pairs={{0,4},{4,0},{8,12},{12,8},{16,20},{20,16},{24,28},{28,24},{1,5},{5... | collective-permute-start | bytes 18440 | tf_op jit(solution)/shard_map/ppermute | solution.py:588
  72.0 5.2 %collective-permute-start.14 = (bf16[1344,128]{1,0:T(8,128)(2,1)S(1)}, bf16[1344,128]{1,0:T(8,128)(2,1)S(1)}, u32[]{:S(2)}, u32[]{:S(2)}) collective-permute-start(bf16[1344,128]{1,0:T(8,128)(2,1)S(1)} %get-tuple-element.99.refs_1_), channel_id=1, source_target_pairs={{0,1},{1,0},{2,3},{3,2},{4,5},{5,4},{6,7},{7,6},{8,9},{9,8},{10,11... | collective-permute-start | bytes 1032200 | tf_op jit(solution)/shard_map/ppermute | solution.py:588
  75.0 5.3 %copy-start.7 = (f32[2,768]{1,0:T(2,128)S(1)}, f32[2,768]{1,0:T(2,128)}, u32[]{:S(2)}) copy-start(f32[2,768]{1,0:T(2,128)} %refs_7_.2) | copy-start | bytes 18436
  75.0 5.3 %copy-start.8 = (f32[2,768]{1,0:T(2,128)S(1)}, f32[2,768]{1,0:T(2,128)}, u32[]{:S(2)}) copy-start(f32[2,768]{1,0:T(2,128)} %refs_8_.2) | copy-start | bytes 18436
  75.1 2.1 %collective-permute-start.23 = (bf16[1344,128]{1,0:T(8,128)(2,1)S(1)}, bf16[1344,128]{1,0:T(8,128)(2,1)S(1)}, u32[]{:S(2)}, u32[]{:S(2)}) collective-permute-start(bf16[1344,128]{1,0:T(8,128)(2,1)S(1)} %copy_kernel.5.refs_3_), channel_id=1, source_target_pairs={{0,1},{1,0},{2,3},{3,2},{4,5},{5,4},{6,7},{7,6},{8,9},{9,8},{10,11... | collective-permute-start | bytes 1032200 | tf_op jit(solution)/shard_map/ppermute | solution.py:588
  75.1 7.8 %collective-permute-start.25 = (bf16[1,96,384]{2,1,0:T(8,128)(2,1)S(1)}, bf16[1,96,384]{2,1,0:T(8,128)(2,1)S(1)}, u32[]{:S(2)}, u32[]{:S(2)}) collective-permute-start(bf16[1,96,384]{2,1,0:T(8,128)(2,1)S(1)} %get-tuple-element.106.refs_2_), channel_id=1, source_target_pairs={{0,16},{4,20},{8,24},{12,28},{16,0},{20,4},{24,8},{28,12},{1,17},{... | collective-permute-start | bytes 221192 | tf_op jit(solution)/shard_map/ppermute | solution.py:588
  76.7 3.6 %collective-permute-start.24 = (f32[2,768]{1,0:T(2,128)S(1)}, f32[2,768]{1,0:T(2,128)S(1)}, u32[]{:S(2)}, u32[]{:S(2)}) collective-permute-start(f32[2,768]{1,0:T(2,128)S(1)} %add_kernel.9.refs_1_.refs_5_.refs_4_), channel_id=1, source_target_pairs={{0,8},{4,12},{8,0},{12,4},{16,24},{20,28},{24,16},{28,20},{1,9},{5... | collective-permute-start | bytes 18440 | tf_op jit(solution)/shard_map/ppermute | solution.py:588
  80.4 2.6 %copy-start.2 = (f32[3,96,96]{2,1,0:T(8,128)S(1)}, f32[3,96,96]{2,1,0:T(8,128)}, u32[]{:S(2)}) copy-start(f32[3,96,96]{2,1,0:T(8,128)} %refs_4_.3) | copy-start | bytes 331780
  80.4 2.6 %copy-start.3 = (f32[3,96,96]{2,1,0:T(8,128)S(1)}, f32[3,96,96]{2,1,0:T(8,128)}, u32[]{:S(2)}) copy-start(f32[3,96,96]{2,1,0:T(8,128)} %refs_5_.1) | copy-start | bytes 331780
  (7 other events, 16.2 us)

commit v6 on v5

--- a/solution.py
+++ b/solution.py
@@ -107,7 +107,7 @@
 
 
 def first_kernel(
-    x_hbm, cot_hbm, conv_hbm, point_hbm, x_ref, weight_ref, near_ref, rim_ref, edge_ref, conv_ref, point_ref, sum_ref, sems
+    x_hbm, cot_hbm, conv_hbm, point_hbm, x_ref, weight_ref, near_ref, near_rim, far_rim, edge_ref, conv_ref, point_ref, sum_ref, sems
 ):
     rows, width = x_ref.shape
     tiles = width // LANES
@@ -156,10 +156,10 @@
     put_sums(near_ref, sum_ref[...])
     copies[2].wait()
     copies[3].wait()
-    for side in range(2):
-        begin = (rows - RIM) * side
-        rim_ref[side, :RIM, :] = x_ref[begin : begin + RIM, :]
-        rim_ref[side, RIM:, :] = edge_ref[side]
+    odd = lax.axis_index("seq") % 2
+    for ref, side in ((near_rim, 1 - odd), (far_rim, odd)):
+        ref[:RIM, :] = x_ref[pl.ds(pl.multiple_of(side * (rows - RIM), RIM), RIM), :]
+        ref[RIM:, :] = edge_ref[side]
 
 
 def put_sums(ref, value):
@@ -220,10 +220,8 @@
     out_ref[...] = place(pieces, relatives, stack, lax.axis_index("seq"), slim)
 
 
-def mask_kernel(start_ref, rim_ref, ahead_ref, back_ref, near_ref, far_ref):
-    odd = lax.axis_index("seq") % 2
-    near_ref[...] = rim_ref[1 - odd]
-    far_ref[...] = rim_ref[odd]
+def mask_kernel(start_ref, rim_ref, ahead_ref, back_ref, far_ref):
+    far_ref[...] = rim_ref[...]
     rows = back_ref.shape[1]
     first = lax.axis_index("seq") * rows
     for j, shift in enumerate(SHIFTS):
@@ -254,8 +252,12 @@
     for k, piece in enumerate(pieces):
         all_ref[k * size : (k + 1) * size] = piece[...]
     odd = lax.axis_index("seq") % 2
-    rim_ref[1 - odd] = near_ref[...]
+    height, width = far_ref.shape
     rim_ref[odd] = far_ref[...]
+    base = near_ref.shape[0] - width // LANES * height
+    for k in range(width // LANES):
+        at = base + k * height
+        rim_ref[1 - odd, :, k * LANES : (k + 1) * LANES] = near_ref[at : at + height, :]
     for side in range(2):
         for k in range(0, RIM, 16):
             v = rim_ref[side, k : k + 16, :].astype(F32) * vec_ref[2:3, :] + vec_ref[3:4, :]
@@ -492,9 +494,16 @@
         sum_ref[1:2, part] = jnp.sum(d, 0, keepdims=True)
 
 
-def final_kernel(x_ref, cot_ref, d_ref, vec_ref, one_ref, two_ref, *refs, bin_count):
-    states, late_ref, outs, (out_ref, sems) = refs[:3], refs[3], refs[4:8], refs[8:]
-    late_ref[...] = jnp.zeros_like(late_ref)
+def final_kernel(
+    x_ref, cot_ref, d_ref, vec_ref, one_ref, two_ref, old_ref, got_ref, mid_ref, *refs, bin_count, chunks
+):
+    states, outs, refs = refs[:12], refs[12:25], refs[25:]
+    held, news, out_ref, sems = refs[:12], refs[12:24], refs[24], refs[25]
+    fetches = [
+        pltpu.make_async_copy(src, dst, sems.at[k]) for k, (src, dst) in enumerate(zip(states, held))
+    ]
+    for fetch in fetches:
+        fetch.start()
     rows, width = x_ref.shape
     total = one_ref[...] + two_ref[...]
     root, offset, scale = vec_ref[0:1, :], vec_ref[1:2, :], vec_ref[2:3, :]
@@ -502,7 +511,7 @@
     slant = pull * root
     level = scale * total[1:2] / bin_count + pull * offset
     step = 16
-    chunk = rows // sems.shape[0]
+    chunk = rows // chunks
 
     def body(i, carry):
         at = pl.ds(pl.multiple_of(i * step, 16), step)
@@ -511,34 +520,31 @@
         return carry
 
     sends = []
-    for k in range(sems.shape[0]):
+    for k in range(chunks):
         lax.fori_loop(k * chunk // step, (k + 1) * chunk // step, body, 0, unroll=4)
         part = pl.ds(k * chunk, chunk)
-        sends.append(pltpu.make_async_copy(out_ref.at[part], outs[0].at[part], sems.at[k]))
+        sends.append(pltpu.make_async_copy(out_ref.at[part], outs[0].at[part], sems.at[24 + k]))
         sends[-1].start()
-    new = adamw(*(ref[...] for ref in states), total, RATE_NORM, 0.0)
-    for ref, value in zip(outs[1:], new):
-        ref[...] = value
+    for fetch in fetches:
+        fetch.wait()
+
+    def step_of(first, at, grad, rate, decay):
+        new = adamw(*(ref[at] for ref in held[first : first + 3]), grad, rate, decay)
+        for ref, value in zip(news[first : first + 3], new):
+            ref[at] = value
+
+    slim = held[3].shape[2]
+    both = old_ref[0] + got_ref[0].astype(F32)
+    step_of(0, ..., total, RATE_NORM, 0.0)
+    for j in range(KERNEL_WIDTH):
+        step_of(3, j, both[:, j * slim : (j + 1) * slim], RATE_WEIGHT, DECAY_WEIGHT)
+    step_of(6, ..., both[:, KERNEL_WIDTH * slim :].T, RATE_WEIGHT, DECAY_WEIGHT)
+    step_of(9, ..., mid_ref[:, :slim], RATE_NORM, 0.0)
+    for k in range(12):
+        sends.append(pltpu.make_async_copy(news[k], outs[1 + k], sems.at[12 + k]))
+        sends[-1].start()
     for send in sends:
         send.wait()
-
-
-def weight_step_kernel(old_ref, got_ref, total_ref, *refs):
-    conv, point, mid, outs = refs[:3], refs[3:6], refs[6:9], refs[9:]
-    slim = conv[0].shape[2]
-    both = old_ref[0] + got_ref[0].astype(F32)
-    for j in range(KERNEL_WIDTH):
-        grad = both[:, j * slim : (j + 1) * slim]
-        new = adamw(*(ref[j] for ref in conv), grad, RATE_WEIGHT, DECAY_WEIGHT)
-        for ref, value in zip(outs[:3], new):
-            ref[j] = value
-    grad = both[:, KERNEL_WIDTH * slim :].T
-    new = adamw(*(ref[...] for ref in point), grad, RATE_WEIGHT, DECAY_WEIGHT)
-    for ref, value in zip(outs[3:6], new):
-        ref[...] = value
-    new = adamw(*(ref[...] for ref in mid), total_ref[:, :slim], RATE_NORM, 0.0)
-    for ref, value in zip(outs[6:], new):
-        ref[...] = value
 
 
 def flip(axis, reach):
@@ -556,14 +562,21 @@
     return [size >> k for k in range(1, size.bit_length())]
 
 
-def round_kernel(weight_one, weight_two, one_ref, two_ref, weight_ref, out_ref):
+def round_kernel(weight_one, weight_two, one_ref, two_ref, *refs):
+    weight_ref, out_ref = refs[-2:]
     size = weight_one.shape[0]
     weight_ref[:size] = weight_one[...]
     weight_ref[size:] = weight_two[...]
     put_sums(out_ref, get_sums(one_ref) + get_sums(two_ref))
-    size = (out_ref.shape[0] - SUMS) // 2
+    rim = out_ref.shape[0] - one_ref.shape[0] * 2 + SUMS if len(refs) > 2 else 0
+    size = (out_ref.shape[0] - SUMS - rim) // 2
     out_ref[SUMS : SUMS + size, :] = one_ref[SUMS : SUMS + size, :]
-    out_ref[SUMS + size :, :] = two_ref[SUMS : SUMS + size, :]
+    out_ref[SUMS + size : SUMS + 2 * size, :] = two_ref[SUMS : SUMS + size, :]
+    if rim:
+        height, width = refs[0].shape
+        for k in range(width // LANES):
+            at = SUMS + 2 * size + k * height
+            out_ref[at : at + height, :] = refs[0][:, k * LANES : (k + 1) * LANES]
 
 
 def copy_kernel(*refs):
@@ -634,13 +647,14 @@
     chunks = 4
     rim = (RIM + EDGE, width)
     packed = 3 * depth // 4 if folds(depth, slim) else depth
-    inputs, weight, near, rims = call(
+    inputs, weight, near, *rims = call(
         first_kernel,
         [
             (inputs.shape, BF16),
             ((1, packed, wide), BF16),
             ((SUMS + up_to(depth, 16), LANES), BF16),
-            ((2, *rim), BF16),
+            (rim, BF16),
+            (rim, BF16),
         ],
         [inputs, cotangent, master_conv, master_point],
         scratch=[
@@ -659,23 +673,23 @@
         if k < rounds - 1:
             outs = [
                 ((2 * weight.shape[0], packed, wide), BF16),
-                ((SUMS + (2 << k) * up_to(depth, 16), LANES), BF16),
+                ((SUMS + (2 << k) * up_to(depth, 16) + (tiles * rim[0] if k == 0 else 0), LANES), BF16),
             ]
             args = [weight, weight_got, near, near_got]
-            weight, near = call(round_kernel, outs, args, after=[back] if k == 1 else [])
             if k == 0:
-                ahead, back, *rims = call(
+                weight, near = call(round_kernel, outs, args + [rims[0]])
+                ahead, back, far = call(
                     mask_kernel,
-                    [((KERNEL_WIDTH, ext, LANES), F32), ((KERNEL_WIDTH, rows, LANES), F32)]
-                    + [(rim, BF16)] * 2,
-                    [starts, rims],
+                    [((KERNEL_WIDTH, ext, LANES), F32), ((KERNEL_WIDTH, rows, LANES), F32), (rim, BF16)],
+                    [starts, rims[1]],
                     smem=(0,),
                     after=[near],
                 )
-                rims = [
-                    swap(rims[0], "seq", 1),
-                    lax.ppermute(rims[1], "seq", pairs + [(j, i) for i, j in pairs]),
-                ]
+                far = lax.ppermute(far, "seq", pairs + [(j, i) for i, j in pairs])
+            else:
+                if k == 1:
+                    near_rim = near_got
+                weight, near = call(round_kernel, outs, args, after=[back] if k == 1 else [])
     hidden_in, vec_in, cotangent = call(
         functools.partial(act_kernel, bin_count=bin_count),
         [((rows, width), BF16), ((8, width), F32), (cotangent.shape, BF16)],
@@ -696,7 +710,7 @@
             ((2, *rim), BF16),
             ((seq_size, packed, wide), BF16),
         ],
-        [ahead, hidden_in, *rims, vec_in, weight, weight_got],
+        [ahead, hidden_in, near_rim, far, vec_in, weight, weight_got],
         scratch=[
             ((seq_size, depth, wide), stack_type),
             ((rows + 2 * RIM, wide), F32),
@@ -723,13 +737,7 @@
                 after=[total],
             )
             slopes += others
-    (conv_far,) = call(
-        functools.partial(place_kernel, relatives=relatives_of(weight_order), slim=slim),
-        [((width, wide), BF16)],
-        [weight],
-        scratch=[((seq_size, depth, wide), stack_type)],
-        after=[total],
-    )
+    (weight,) = copies([weight], [total])
     hidden_mid, d_mid, centered, sent_back, vec_mid = call(
         functools.partial(mid_kernel, bin_count=bin_count),
         [
@@ -740,7 +748,7 @@
             ((8, LANES), F32),
         ],
         [total, conv_out, upstream, norm_mid],
-        after=[conv_far, *conv_near[1:]],
+        after=[weight, *conv_near[1:]],
     )
     got_back = spread(sent_back, "seq")
     grad_own, total_mid = call(
@@ -751,7 +759,16 @@
     )
     grad_near = gather_parts(grad_own, lower)
     grad_far = swap(grad_own, "ch", top)
-    conv_far = gather_parts(copies([conv_far], [grad_own])[0], lower)
+    (weight,) = copies([weight], [grad_own])
+    conv_far = [
+        call(
+            functools.partial(place_kernel, relatives=relatives_of(weight_order), slim=slim),
+            [((width, wide), BF16)],
+            [part],
+            scratch=[((seq_size, depth, wide), stack_type)],
+        )[0]
+        for part in gather_parts(weight, lower)
+    ]
     half = seq_size // 2
     terms, kept, sent = call(
         functools.partial(weight_grad_kernel, depth=depth, slim=slim),
@@ -779,20 +796,26 @@
     )
     both_parts = gather_parts(both, lower)
     both_far = swap(both, "ch", top)
-    total_back = sums_back
-    for k, reach in enumerate(sum_order):
-        total_got = swap(total_back, "seq", last_order[k])
-        got = swap(sent, "seq", reach)
-        if k < rounds - 1:
-            half //= 2
-            kept, sent = call(
+    folds_done = [(kept, sent)]
+    for reach in sum_order[:-1]:
+        half //= 2
+        folds_done.append(
+            call(
                 functools.partial(fold_kernel, reach=2 * reach),
                 [((half, depth, 4 * slim), F32), ((half, depth, 4 * slim), BF16)],
-                [kept, got],
-                after=[total_back],
+                [folds_done[-1][0], swap(folds_done[-1][1], "seq", reach)],
+                after=[sums_back],
             )
-            total_back = add(total_back, total_got, [sent])
-    both_parts += gather_parts(copies([both_far], [total_back])[0], lower)
+        )
+    kept, got = folds_done[-1][0], swap(folds_done[-1][1], "seq", sum_order[-1])
+    total_back = sums_back
+    for k in range(rounds):
+        total_got = swap(total_back, "seq", last_order[k])
+        if k < rounds - 1:
+            follows = [folds_done[-1][1]] if k == 0 else []
+            total_back = add(total_back, total_got, follows)
+        if k == 0:
+            both_parts += gather_parts(copies([both_far], [total_back])[0], lower)
     block_out, token = call(
         out_kernel,
         [((rows, width), BF16), ((8, LANES), F32)],
@@ -800,24 +823,21 @@
         scratch=[((rows, ch_size * LANES), BF16), ((width, ch_size * LANES), BF16)],
         after=[total_back],
     )
-    late, input_grad, *in_new = call(
-        functools.partial(final_kernel, bin_count=bin_count),
-        [((8, LANES), F32), ((rows, width), F32)] + [((2, width), F32)] * 3,
-        [inputs, cotangent, d_in, vec_in, total_back, total_got, norm_in, first_in, second_in],
-        scratch=[((rows, width), F32)],
-        away_outs=(1,),
-        sems=8,
+    states = [norm_in, first_in, second_in, master_conv, first_conv, second_conv]
+    states += [master_point, first_point, second_point, norm_mid, first_mid, second_mid]
+    arrays = [inputs, cotangent, d_in, vec_in, total_back, total_got, kept, got, total_mid]
+    small = [(x.shape, F32) for x in states]
+    input_grad, *news = call(
+        functools.partial(final_kernel, bin_count=bin_count, chunks=8),
+        [((rows, width), F32)] + small,
+        arrays + states,
+        scratch=small + small + [((rows, width), F32)],
+        away=range(len(arrays), len(arrays) + 12),
+        away_outs=range(13),
+        sems=24 + 8,
         after=[token],
     )
-    states = [master_conv, first_conv, second_conv, master_point, first_point, second_point]
-    states += [norm_mid, first_mid, second_mid]
-    news = call(
-        weight_step_kernel,
-        [(x.shape, F32) for x in states],
-        [kept, got, total_mid] + states,
-        after=[late],
-    )
-    return (block_out, input_grad, *news[:6], *in_new, *news[6:])
+    return (block_out, input_grad, *news[3:9], *news[:3], *news[9:])
 
 
 def solution(mesh):

time: 84.2 us -> 83.1 us (0.987)
  starting transfers between devices: 26.8 us -> 25.1 us
  waiting for transfers between devices: 22.7 us -> 23.9 us
    ppermute x25 -> x24, starting transfers between devices: 26.2 us -> 24.4 us  [swap(): return lax.ppermute(x, axis, flip(axis, reach))]
    ppermute x25 -> x24, waiting for transfers between devices: 22.7 us -> 23.9 us  [swap(): return lax.ppermute(x, axis, flip(axis, reach))]
    pallas_call x28 -> x29, Pallas kernels: 21.9 us -> 21.6 us  [call(): pl.pallas_call(kernel, out_shape=[jax.ShapeDtypeStruct(s, t) for s, t in...]
  transfers between devices with their start and end apart: 26 -> 25, of which waited for: 12 -> 12; matrix products, arithmetic and copies ran while one was open for 0% -> 0% of each run, Pallas kernels for 20% -> 18%
where the time goes in v6:
time: 83.1 us; the launch traced here: 82.9 us
  starting transfers between devices  25.1 us (30%)
  waiting for transfers between devices  23.9 us (29%)
  Pallas kernels  21.6 us (26%)
  blocking collectives  11.1 us (13%)
  between operations  1.05 us (1%)
    ppermute x24, starting transfers between devices, swap(): return lax.ppermute(x, axis, flip(axis, reach))  24.4 us
    ppermute x24, waiting for transfers between devices, swap(): return lax.ppermute(x, axis, flip(axis, reach))  23.9 us
    pallas_call x29, Pallas kernels, call(): pl.pallas_call(kernel, out_shape=[jax.ShapeDtypeStruct(s, t) for s, t in...  21.6 us
    all_to_all x1, blocking collectives, spread(): return lax.all_to_all(copies, axes, 0, 0, tiled=True)  11.1 us
  transfers between devices with their start and end apart: 25, of which 12 were waited for; matrix products, arithmetic and copies ran while one was open for 0% of the time, Pallas kernels for 18%

profile of v6, /device:TPU:0, one launch (start us, length us, event | category | flops | bytes accessed | tf_op | source)
XLA Modules:
  0.0 82.9 jit_solution(5480853434446555750)
XLA Ops:
  0.7 1.7 %first_kernel.1 = (bf16[1024,768]{1,0:T(8,128)(2,1)S(1)}, bf16[1,72,384]{2,1,0:T(8,128)(2,1)S(1)}, bf16[144,128]{1,0:T(8,128)(2,1)S(1)}, bf16[48,768]{1,0:T(8,128)(2,1)S(1)}, bf16[48,768]{1,0:T(8,128)(2,1)S(1)}) custom-call(bf16[1024,768]{1,0:T(8,128)(2,1)} %refs_0_.2, bf16[1024,768]{1,0:T(8,128)(2,1)} %refs_1_.3, f32[3,96,96]{2,1,0:T(8,128)} %refs_12_.1, ...), custom_call_target="tpu_custom_call" | custom-call | flops 1 | bytes 1 | tf_op jit(solution)/shard_map/first_kernel/pallas_call | solution.py:48
  2.4 4.1 %collective-permute-start = (bf16[1,72,384]{2,1,0:T(8,128)(2,1)S(1)}, bf16[1,72,384]{2,1,0:T(8,128)(2,1)S(1)}, u32[]{:S(2)}, u32[]{:S(2)}) collective-permute-start(bf16[1,72,384]{2,1,0:T(8,128)(2,1)S(1)} %get-tuple-element.71.refs_0_), channel_id=1, source_target_pairs={{0,16},{4,20},{8,24},{12,28},{16,0},{20,4},{24,8},{28,12},{1,17},{... | collective-permute-start | bytes 165896 | tf_op jit(solution)/shard_map/ppermute | solution.py:601
  6.6 4.8 %collective-permute-done.1.refs_3_ = bf16[144,128]{1,0:T(8,128)(2,1)S(1)} collective-permute-done((bf16[144,128]{1,0:T(8,128)(2,1)S(1)}, bf16[144,128]{1,0:T(8,128)(2,1)S(1)}, u32[]{:S(2)}, u32[]{:S(2)}) %collective-permute-start.1) | collective-permute-done | bytes 36896 | tf_op jit(solution)/shard_map/ppermute | solution.py:601
  11.4 1.6 %collective-permute-start.3 = (bf16[528,128]{1,0:T(8,128)(2,1)S(1)}, bf16[528,128]{1,0:T(8,128)(2,1)S(1)}, u32[]{:S(2)}, u32[]{:S(2)}) collective-permute-start(bf16[528,128]{1,0:T(8,128)(2,1)S(1)} %get-tuple-element.74.refs_2_), channel_id=1, source_target_pairs={{0,4},{4,0},{8,12},{12,8},{16,20},{20,16},{24,28},{28,24},{1,5},{5... | collective-permute-start | bytes 405512 | tf_op jit(solution)/shard_map/ppermute | solution.py:601
  12.9 1.6 %collective-permute-start.2 = (bf16[2,72,384]{2,1,0:T(8,128)(2,1)S(1)}, bf16[2,72,384]{2,1,0:T(8,128)(2,1)S(1)}, u32[]{:S(2)}, u32[]{:S(2)}) collective-permute-start(bf16[2,72,384]{2,1,0:T(8,128)(2,1)S(1)} %get-tuple-element.77.refs_0_), channel_id=1, source_target_pairs={{0,8},{4,12},{8,0},{12,4},{16,24},{20,28},{24,16},{28,20},{1,9},{5... | collective-permute-start | bytes 331784 | tf_op jit(solution)/shard_map/ppermute | solution.py:601
  14.5 1.4 %mask_kernel.1 = (f32[3,1056,128]{2,1,0:T(8,128)S(1)}, f32[3,1024,128]{2,1,0:T(8,128)S(1)}, bf16[48,768]{1,0:T(8,128)(2,1)S(1)}) custom-call(s32[8]{0:T(128)S(1)} %copy-done.2, bf16[48,768]{1,0:T(8,128)(2,1)S(1)} %get-tuple-element.70.refs_1_, bf16[528,128]{1,0:T(8,128)(2,1)S(1)} %get-tuple-element.74.refs_2_), custom_call_target="tpu_custom_call" | custom-call | flops 1 | bytes 1 | tf_op jit(solution)/shard_map/mask_kernel/pallas_call | solution.py:48
  15.9 1.7 %collective-permute-done.2.refs_1_ = bf16[2,72,384]{2,1,0:T(8,128)(2,1)S(1)} collective-permute-done((bf16[2,72,384]{2,1,0:T(8,128)(2,1)S(1)}, bf16[2,72,384]{2,1,0:T(8,128)(2,1)S(1)}, u32[]{:S(2)}, u32[]{:S(2)}) %collective-permute-start.2) | collective-permute-done | bytes 110624 | tf_op jit(solution)/shard_map/ppermute | solution.py:601
  18.3 1.6 %collective-permute-start.4 = (bf16[432,128]{1,0:T(8,128)(2,1)S(1)}, bf16[432,128]{1,0:T(8,128)(2,1)S(1)}, u32[]{:S(2)}, u32[]{:S(2)}) collective-permute-start(bf16[432,128]{1,0:T(8,128)(2,1)S(1)} %get-tuple-element.78.refs_2_), channel_id=1, source_target_pairs={{0,8},{4,12},{8,0},{12,4},{16,24},{20,28},{24,16},{28,20},{1,9},{5... | collective-permute-start | bytes 331784 | tf_op jit(solution)/shard_map/ppermute | solution.py:601
  20.6 3.1 %collective-permute-done.4.refs_3_ = bf16[432,128]{1,0:T(8,128)(2,1)S(1)} collective-permute-done((bf16[432,128]{1,0:T(8,128)(2,1)S(1)}, bf16[432,128]{1,0:T(8,128)(2,1)S(1)}, u32[]{:S(2)}, u32[]{:S(2)}) %collective-permute-start.4) | collective-permute-done | bytes 110624 | tf_op jit(solution)/shard_map/ppermute | solution.py:601
  23.7 1.5 %act_kernel.1 = (bf16[1024,768]{1,0:T(8,128)(2,1)S(1)}, f32[8,768]{1,0:T(8,128)S(1)}, bf16[1024,768]{1,0:T(8,128)(2,1)S(1)}) custom-call(bf16[1024,768]{1,0:T(8,128)(2,1)S(1)} %get-tuple-element.69.refs_0_.refs_1_, bf16[1024,768]{1,0:T(8,128)(2,1)} %refs_1_.3, bf16[432,128]{1,0:T(8,128)(2,1)S(1)} %get-tuple-element.78.refs_2_, ...), custom_call_target="tpu_custom_call" | custom-call | flops 1 | bytes 1 | tf_op jit(solution)/shard_map/act_kernel/pallas_call | solution.py:48
  25.3 1.4 %conv_kernel.1 = (bf16[768,384]{1,0:T(8,128)(2,1)S(1)}, f32[1056,128]{1,0:T(8,128)S(1)}, f32[8,128]{1,0:T(8,128)S(1)}, bf16[2,48,768]{2,1,0:T(8,128)(2,1)S(1)}, bf16[8,72,384]{2,1,0:T(8,128)(2,1)S(1)}) custom-call(f32[3,1056,128]{2,1,0:T(8,128)S(1)} %get-tuple-element.76.refs_0_, bf16[1024,768]{1,0:T(8,128)(2,1)S(1)} %get-tuple-element.79.refs_1_.refs_2_, ...), custom_call_target="tpu_custom_call" | custom-call | flops 1 | bytes 1 | tf_op jit(solution)/shard_map/conv_kernel/pallas_call | solution.py:48
  26.8 1.6 %collective-permute-start.10 = (bf16[8,72,384]{2,1,0:T(8,128)(2,1)S(1)}, bf16[8,72,384]{2,1,0:T(8,128)(2,1)S(1)}, u32[]{:S(2)}, u32[]{:S(2)}) collective-permute-start(bf16[8,72,384]{2,1,0:T(8,128)(2,1)S(1)} %get-tuple-element.88), channel_id=1, source_target_pairs={{0,2},{1,3},{2,0},{3,1},{4,6},{5,7},{6,4},{7,5},{8,10},{9,11},{10,... | collective-permute-start | bytes 1327112 | tf_op jit(solution)/shard_map/ppermute | solution.py:601
  28.3 3.3 %collective-permute-start.7 = (f32[8,128]{1,0:T(8,128)S(1)}, f32[8,128]{1,0:T(8,128)S(1)}, u32[]{:S(2)}, u32[]{:S(2)}) collective-permute-start(f32[8,128]{1,0:T(8,128)S(1)} %get-tuple-element.83.refs_4_.refs_0_), channel_id=1, source_target_pairs={{0,4},{4,0},{8,12},{12,8},{16,20},{20,16},{24,28},{28,24},{1,5},{5... | collective-permute-start | bytes 12296 | tf_op jit(solution)/shard_map/ppermute | solution.py:601
  32.3 0.9 %collective-permute-done.7.refs_1_ = f32[8,128]{1,0:T(8,128)S(1)} collective-permute-done((f32[8,128]{1,0:T(8,128)S(1)}, f32[8,128]{1,0:T(8,128)S(1)}, u32[]{:S(2)}, u32[]{:S(2)}) %collective-permute-start.7) | collective-permute-done | bytes 4128 | tf_op jit(solution)/shard_map/ppermute | solution.py:601
  33.2 1.0 %collective-permute-start.8 = (f32[8,128]{1,0:T(8,128)S(1)}, f32[8,128]{1,0:T(8,128)S(1)}, u32[]{:S(2)}, u32[]{:S(2)}) collective-permute-start(f32[8,128]{1,0:T(8,128)S(1)} %add_kernel.5.refs_2_.refs_0_), channel_id=1, source_target_pairs={{0,8},{4,12},{8,0},{12,4},{16,24},{20,28},{24,16},{28,20},{1,9},{5... | collective-permute-start | bytes 12296 | tf_op jit(solution)/shard_map/ppermute | solution.py:601
  34.2 1.1 %slope_kernel.2.refs_2_ = f32[512,768]{1,0:T(8,128)S(1)} custom-call(bf16[1024,768]{1,0:T(8,128)(2,1)S(1)} %get-tuple-element.69.refs_0_.refs_1_, f32[8,768]{1,0:T(8,128)S(1)} %get-tuple-element.81.refs_4_.refs_1_.refs_3_, f32[8,128]{1,0:T(8,128)S(1)} %add_kernel.5.refs_2_.refs_0_), custom_call_target="tpu_custom_call" | custom-call | flops 1 | bytes 1 | tf_op jit(solution)/shard_map/slope_kernel/pallas_call | solution.py:48
  35.3 1.5 %collective-permute-done.8.refs_1_ = f32[8,128]{1,0:T(8,128)S(1)} collective-permute-done((f32[8,128]{1,0:T(8,128)S(1)}, f32[8,128]{1,0:T(8,128)S(1)}, u32[]{:S(2)}, u32[]{:S(2)}) %collective-permute-start.8) | collective-permute-done | bytes 4128 | tf_op jit(solution)/shard_map/ppermute | solution.py:601
  36.8 3.0 %collective-permute-start.9 = (f32[8,128]{1,0:T(8,128)S(1)}, f32[8,128]{1,0:T(8,128)S(1)}, u32[]{:S(2)}, u32[]{:S(2)}) collective-permute-start(f32[8,128]{1,0:T(8,128)S(1)} %add_kernel.6.refs_2_.refs_0_), channel_id=1, source_target_pairs={{0,16},{4,20},{8,24},{12,28},{16,0},{20,4},{24,8},{28,12},{1,17},{... | collective-permute-start | bytes 12296 | tf_op jit(solution)/shard_map/ppermute | solution.py:601
  39.8 1.1 %slope_kernel.3.refs_2_.refs_3_ = f32[512,768]{1,0:T(8,128)S(1)} custom-call(bf16[1024,768]{1,0:T(8,128)(2,1)S(1)} %get-tuple-element.69.refs_0_.refs_1_, f32[8,768]{1,0:T(8,128)S(1)} %get-tuple-element.81.refs_4_.refs_1_.refs_3_, f32[8,128]{1,0:T(8,128)S(1)} %add_kernel.6.refs_2_.refs_0_), custom_call_target="tpu_custom_call" | custom-call | flops 1 | bytes 1 | tf_op jit(solution)/shard_map/slope_kernel/pallas_call | solution.py:48
  42.2 11.1 %all_to_all.5.refs_0_ = f32[8,2,128]{2,1,0:T(2,128)S(1)} all-to-all(f32[8,2,128]{2,1,0:T(2,128)S(1)} %get-tuple-element.90), channel_id=1, replica_groups=mesh['seq'=8,'ch'=4] {'seq'}, dimensions={0} | all-to-all | bytes 16384 | tf_op jit(solution)/shard_map/all_to_all | solution.py:612
  54.2 0.8 collective-permute-start.15
  54.9 2.0 %weight_grad_kernel.1 = (bf16[1024,384]{1,0:T(8,128)(2,1)S(1)}, f32[4,96,384]{2,1,0:T(8,128)S(1)}, bf16[4,96,384]{2,1,0:T(8,128)(2,1)S(1)}) custom-call(f32[3,1024,128]{2,1,0:T(8,128)S(1)} %get-tuple-element.75.refs_4_.refs_0_, bf16[792,128]{1,0:T(8,128)(2,1)S(1)} %get-tuple-element.94.refs_1_, bf16[1024,768]{1,0:T(8,128)(2,1)S(1)} %get-tuple-element.79.refs_1_.refs_2_, ...), custom_call_target="tpu_custom_call" | custom-call | flops 1 | bytes 1 | tf_op jit(solution)/shard_map/weight_grad_kernel/pallas_call | solution.py:48
  57.5 1.6 %first_half_kernel.1 = (f32[1024,768]{1,0:T(8,128)S(1)}, bf16[1344,128]{1,0:T(8,128)(2,1)S(1)}) custom-call(f32[3,1024,128]{2,1,0:T(8,128)S(1)} %get-tuple-element.75.refs_4_.refs_0_, bf16[1024,384]{1,0:T(8,128)(2,1)S(1)} %get-tuple-element.96.refs_1_, bf16[1024,128]{1,0:T(8,128)(2,1)S(1)} %get-tuple-element.95.refs_4_.refs_2_, ...), custom_call_target="tpu_custom_call" | custom-call | flops 1 | bytes 1 | tf_op jit(solution)/shard_map/first_half_kernel/pallas_call | solution.py:48
  59.1 2.1 %collective-permute-done.15.refs_0_ = bf16[792,128]{1,0:T(8,128)(2,1)S(1)} collective-permute-done((bf16[792,128]{1,0:T(8,128)(2,1)S(1)}, bf16[792,128]{1,0:T(8,128)(2,1)S(1)}, u32[]{:S(2)}, u32[]{:S(2)}) %collective-permute-start.15) | collective-permute-done | bytes 202784 | tf_op jit(solution)/shard_map/ppermute | solution.py:601
  61.3 0.8 %collective-permute-start.14 = (bf16[1344,128]{1,0:T(8,128)(2,1)S(1)}, bf16[1344,128]{1,0:T(8,128)(2,1)S(1)}, u32[]{:S(2)}, u32[]{:S(2)}) collective-permute-start(bf16[1344,128]{1,0:T(8,128)(2,1)S(1)} %get-tuple-element.98.refs_1_), channel_id=1, source_target_pairs={{0,2},{1,3},{2,0},{3,1},{4,6},{5,7},{6,4},{7,5},{8,10},{9,11},{10,... | collective-permute-start | bytes 1032200 | tf_op jit(solution)/shard_map/ppermute | solution.py:601
  62.7 2.1 %second_half_kernel.1 = (f32[1024,768]{1,0:T(8,128)S(1)}, f32[2,768]{1,0:T(2,128)S(1)}) custom-call(f32[3,1024,128]{2,1,0:T(8,128)S(1)} %get-tuple-element.75.refs_4_.refs_0_, bf16[1024,768]{1,0:T(8,128)(2,1)S(1)} %get-tuple-element.69.refs_0_.refs_1_, f32[512,768]{1,0:T(8,128)S(1)} %slope_kernel.2.refs_2_, f32[512,768]{1,0:T(8,128)S(1)} %slope_kernel.3.refs_2_.refs_3_, ...), custom_call_target="tpu_custom_call" | custom-call | flops 1 | bytes 1 | tf_op jit(solution)/shard_map/second_half_kernel/pallas_call | solution.py:48
  64.8 0.9 %collective-permute-done.19.refs_1_ = bf16[4,96,384]{2,1,0:T(8,128)(2,1)S(1)} collective-permute-done((bf16[4,96,384]{2,1,0:T(8,128)(2,1)S(1)}, bf16[4,96,384]{2,1,0:T(8,128)(2,1)S(1)}, u32[]{:S(2)}, u32[]{:S(2)}) %collective-permute-start.19) | collective-permute-done | bytes 294944 | tf_op jit(solution)/shard_map/ppermute | solution.py:601
  66.9 4.1 %collective-permute-done.20.refs_1_ = bf16[2,96,384]{2,1,0:T(8,128)(2,1)S(1)} collective-permute-done((bf16[2,96,384]{2,1,0:T(8,128)(2,1)S(1)}, bf16[2,96,384]{2,1,0:T(8,128)(2,1)S(1)}, u32[]{:S(2)}, u32[]{:S(2)}) %collective-permute-start.20) | collective-permute-done | bytes 147488 | tf_op jit(solution)/shard_map/ppermute | solution.py:601
  71.9 0.8 collective-permute-start.24
  73.2 3.0 %collective-permute-done.22.refs_1_ = f32[2,768]{1,0:T(2,128)S(1)} collective-permute-done((f32[2,768]{1,0:T(2,128)S(1)}, f32[2,768]{1,0:T(2,128)S(1)}, u32[]{:S(2)}, u32[]{:S(2)}) %collective-permute-start.22) | collective-permute-done | bytes 6176 | tf_op jit(solution)/shard_map/ppermute | solution.py:601
  76.7 2.5 %out_kernel.1 = (bf16[1024,768]{1,0:T(8,128)(2,1)}, f32[8,128]{1,0:T(8,128)S(1)}) custom-call(bf16[1024,768]{1,0:T(8,128)(2,1)S(1)} %get-tuple-element.69.refs_0_.refs_1_, bf16[1344,128]{1,0:T(8,128)(2,1)S(1)} %get-tuple-element.98.refs_1_, bf16[1344,128]{1,0:T(8,128)(2,1)S(1)} %collective-permute-done.13.refs_2_, bf16[1344,128]{1,0:T(8,128)(2,1)S(1)} %copy_kernel.7.refs_3_, ...), custom_call_target="tpu_custom_call" | custom-call | flops 1 | bytes 1 | tf_op jit(solution)/shard_map/out_kernel/pallas_call | solution.py:48
  79.9 2.8 %final_kernel.1 = (f32[1024,768]{1,0:T(8,128)}, f32[2,768]{1,0:T(2,128)}, f32[2,768]{1,0:T(2,128)}, f32[2,768]{1,0:T(2,128)}, f32[3,96,96]{2,1,0:T(8,128)}, /*in...) custom-call(bf16[1024,768]{1,0:T(8,128)(2,1)S(1)} %get-tuple-element, ...), custom_call_target="tpu_custom_call" | custom-call | flops 1 | bytes 1 | tf_op jit(solution)/shard_map/final_kernel/pallas_call | solution.py:48
  (54 shorter events, 9.2 us)
Async XLA Ops:
  0.6 13.9 %copy-start.2 = (s32[8]{0:T(128)S(1)}, s32[8]{0:T(128)}, u32[]{:S(2)}) copy-start(s32[8]{0:T(128)} %refs_0_.3) | copy-start | bytes 100
  2.4 21.3 %copy-start = (f32[2,768]{1,0:T(2,128)S(1)}, f32[2,768]{1,0:T(2,128)}, u32[]{:S(2)}) copy-start(f32[2,768]{1,0:T(2,128)} %refs_9_.1) | copy-start | bytes 18436
  2.4 9.0 %collective-permute-start = (bf16[1,72,384]{2,1,0:T(8,128)(2,1)S(1)}, bf16[1,72,384]{2,1,0:T(8,128)(2,1)S(1)}, u32[]{:S(2)}, u32[]{:S(2)}) collective-permute-start(bf16[1,72,384]{2,1,0:T(8,128)(2,1)S(1)} %get-tuple-element.71.refs_0_), channel_id=1, source_target_pairs={{0,16},{4,20},{8,24},{12,28},{16,0},{20,4},{24,8},{28,12},{1,17},{... | collective-permute-start | bytes 165896 | tf_op jit(solution)/shard_map/ppermute | solution.py:601
  6.5 4.9 %collective-permute-start.1 = (bf16[144,128]{1,0:T(8,128)(2,1)S(1)}, bf16[144,128]{1,0:T(8,128)(2,1)S(1)}, u32[]{:S(2)}, u32[]{:S(2)}) collective-permute-start(bf16[144,128]{1,0:T(8,128)(2,1)S(1)} %get-tuple-element.72.refs_2_), channel_id=1, source_target_pairs={{0,16},{4,20},{8,24},{12,28},{16,0},{20,4},{24,8},{28,12},{1,17},{... | collective-permute-start | bytes 110600 | tf_op jit(solution)/shard_map/ppermute | solution.py:601
  11.4 6.3 %collective-permute-start.3 = (bf16[528,128]{1,0:T(8,128)(2,1)S(1)}, bf16[528,128]{1,0:T(8,128)(2,1)S(1)}, u32[]{:S(2)}, u32[]{:S(2)}) collective-permute-start(bf16[528,128]{1,0:T(8,128)(2,1)S(1)} %get-tuple-element.74.refs_2_), channel_id=1, source_target_pairs={{0,4},{4,0},{8,12},{12,8},{16,20},{20,16},{24,28},{28,24},{1,5},{5... | collective-permute-start | bytes 405512 | tf_op jit(solution)/shard_map/ppermute | solution.py:601
  12.9 4.7 %collective-permute-start.2 = (bf16[2,72,384]{2,1,0:T(8,128)(2,1)S(1)}, bf16[2,72,384]{2,1,0:T(8,128)(2,1)S(1)}, u32[]{:S(2)}, u32[]{:S(2)}) collective-permute-start(bf16[2,72,384]{2,1,0:T(8,128)(2,1)S(1)} %get-tuple-element.77.refs_0_), channel_id=1, source_target_pairs={{0,8},{4,12},{8,0},{12,4},{16,24},{20,28},{24,16},{28,20},{1,9},{5... | collective-permute-start | bytes 331784 | tf_op jit(solution)/shard_map/ppermute | solution.py:601
  17.7 7.5 %collective-permute-start.6 = (bf16[4,72,384]{2,1,0:T(8,128)(2,1)S(1)}, bf16[4,72,384]{2,1,0:T(8,128)(2,1)S(1)}, u32[]{:S(2)}, u32[]{:S(2)}) collective-permute-start(bf16[4,72,384]{2,1,0:T(8,128)(2,1)S(1)} %get-tuple-element.82.refs_5_), channel_id=1, source_target_pairs={{0,4},{4,0},{8,12},{12,8},{16,20},{20,16},{24,28},{28,24},{1,5},{5... | collective-permute-start | bytes 663560 | tf_op jit(solution)/shard_map/ppermute | solution.py:601
  18.3 5.4 %collective-permute-start.4 = (bf16[432,128]{1,0:T(8,128)(2,1)S(1)}, bf16[432,128]{1,0:T(8,128)(2,1)S(1)}, u32[]{:S(2)}, u32[]{:S(2)}) collective-permute-start(bf16[432,128]{1,0:T(8,128)(2,1)S(1)} %get-tuple-element.78.refs_2_), channel_id=1, source_target_pairs={{0,8},{4,12},{8,0},{12,4},{16,24},{20,28},{24,16},{28,20},{1,9},{5... | collective-permute-start | bytes 331784 | tf_op jit(solution)/shard_map/ppermute | solution.py:601
  19.9 5.3 %collective-permute-start.5 = (bf16[48,768]{1,0:T(8,128)(2,1)S(1)}, bf16[48,768]{1,0:T(8,128)(2,1)S(1)}, u32[]{:S(2)}, u32[]{:S(2)}) collective-permute-start(bf16[48,768]{1,0:T(8,128)(2,1)S(1)} %get-tuple-element.80), channel_id=1, source_target_pairs={{4,8},{12,16},{20,24},{8,4},{16,12},{24,20},{5,9},{13,17},{21,25},... | collective-permute-start | bytes 221192 | tf_op jit(solution)/shard_map/ppermute | solution.py:688
  26.7 14.8 %collective-permute-start.11 = (bf16[768,384]{1,0:T(8,128)(2,1)S(1)}, bf16[768,384]{1,0:T(8,128)(2,1)S(1)}, u32[]{:S(2)}, u32[]{:S(2)}) collective-permute-start(bf16[768,384]{1,0:T(8,128)(2,1)S(1)} %get-tuple-element.89.refs_5_), channel_id=1, source_target_pairs={{0,1},{1,0},{2,3},{3,2},{4,5},{5,4},{6,7},{7,6},{8,9},{9,8},{10,11... | collective-permute-start | bytes 1769480 | tf_op jit(solution)/shard_map/ppermute | solution.py:601
  26.8 14.7 %collective-permute-start.10 = (bf16[8,72,384]{2,1,0:T(8,128)(2,1)S(1)}, bf16[8,72,384]{2,1,0:T(8,128)(2,1)S(1)}, u32[]{:S(2)}, u32[]{:S(2)}) collective-permute-start(bf16[8,72,384]{2,1,0:T(8,128)(2,1)S(1)} %get-tuple-element.88), channel_id=1, source_target_pairs={{0,2},{1,3},{2,0},{3,1},{4,6},{5,7},{6,4},{7,5},{8,10},{9,11},{10,... | collective-permute-start | bytes 1327112 | tf_op jit(solution)/shard_map/ppermute | solution.py:601
  28.3 4.9 %collective-permute-start.7 = (f32[8,128]{1,0:T(8,128)S(1)}, f32[8,128]{1,0:T(8,128)S(1)}, u32[]{:S(2)}, u32[]{:S(2)}) collective-permute-start(f32[8,128]{1,0:T(8,128)S(1)} %get-tuple-element.83.refs_4_.refs_0_), channel_id=1, source_target_pairs={{0,4},{4,0},{8,12},{12,8},{16,20},{20,16},{24,28},{28,24},{1,5},{5... | collective-permute-start | bytes 12296 | tf_op jit(solution)/shard_map/ppermute | solution.py:601
  33.2 3.6 %collective-permute-start.8 = (f32[8,128]{1,0:T(8,128)S(1)}, f32[8,128]{1,0:T(8,128)S(1)}, u32[]{:S(2)}, u32[]{:S(2)}) collective-permute-start(f32[8,128]{1,0:T(8,128)S(1)} %add_kernel.5.refs_2_.refs_0_), channel_id=1, source_target_pairs={{0,8},{4,12},{8,0},{12,4},{16,24},{20,28},{24,16},{28,20},{1,9},{5... | collective-permute-start | bytes 12296 | tf_op jit(solution)/shard_map/ppermute | solution.py:601
  36.8 4.6 %collective-permute-start.9 = (f32[8,128]{1,0:T(8,128)S(1)}, f32[8,128]{1,0:T(8,128)S(1)}, u32[]{:S(2)}, u32[]{:S(2)}) collective-permute-start(f32[8,128]{1,0:T(8,128)S(1)} %add_kernel.6.refs_2_.refs_0_), channel_id=1, source_target_pairs={{0,16},{4,20},{8,24},{12,28},{16,0},{20,4},{24,8},{28,12},{1,17},{... | collective-permute-start | bytes 12296 | tf_op jit(solution)/shard_map/ppermute | solution.py:601
  41.0 0.7 copy-start.1
  53.6 8.8 %collective-permute-start.17 = (bf16[8,72,384]{2,1,0:T(8,128)(2,1)S(1)}, bf16[8,72,384]{2,1,0:T(8,128)(2,1)S(1)}, u32[]{:S(2)}, u32[]{:S(2)}) collective-permute-start(bf16[8,72,384]{2,1,0:T(8,128)(2,1)S(1)} %copy_kernel.6.refs_0_), channel_id=1, source_target_pairs={{0,1},{1,0},{2,3},{3,2},{4,5},{5,4},{6,7},{7,6},{8,9},{9,8},{10,11... | collective-permute-start | bytes 1327112 | tf_op jit(solution)/shard_map/ppermute | solution.py:601
  53.7 3.9 %collective-permute-start.12 = (bf16[792,128]{1,0:T(8,128)(2,1)S(1)}, bf16[792,128]{1,0:T(8,128)(2,1)S(1)}, u32[]{:S(2)}, u32[]{:S(2)}) collective-permute-start(bf16[792,128]{1,0:T(8,128)(2,1)S(1)} %get-tuple-element.94.refs_1_), channel_id=1, source_target_pairs={{0,1},{1,0},{2,3},{3,2},{4,5},{5,4},{6,7},{7,6},{8,9},{9,8},{10,11... | collective-permute-start | bytes 608264 | tf_op jit(solution)/shard_map/ppermute | solution.py:601
  54.2 7.0 %collective-permute-start.15 = (bf16[792,128]{1,0:T(8,128)(2,1)S(1)}, bf16[792,128]{1,0:T(8,128)(2,1)S(1)}, u32[]{:S(2)}, u32[]{:S(2)}) collective-permute-start(bf16[792,128]{1,0:T(8,128)(2,1)S(1)} %get-tuple-element.94.refs_1_), channel_id=1, source_target_pairs={{0,2},{1,3},{2,0},{3,1},{4,6},{5,7},{6,4},{7,5},{8,10},{9,11},{10,... | collective-permute-start | bytes 608264 | tf_op jit(solution)/shard_map/ppermute | solution.py:601
  56.9 8.8 %collective-permute-start.19 = (bf16[4,96,384]{2,1,0:T(8,128)(2,1)S(1)}, bf16[4,96,384]{2,1,0:T(8,128)(2,1)S(1)}, u32[]{:S(2)}, u32[]{:S(2)}) collective-permute-start(bf16[4,96,384]{2,1,0:T(8,128)(2,1)S(1)} %get-tuple-element.102), channel_id=1, source_target_pairs={{0,4},{4,0},{8,12},{12,8},{16,20},{20,16},{24,28},{28,24},{1,5},{5... | collective-permute-start | bytes 884744 | tf_op jit(solution)/shard_map/ppermute | solution.py:601
  61.2 1.5 %collective-permute-start.16 = (bf16[792,128]{1,0:T(8,128)(2,1)S(1)}, bf16[792,128]{1,0:T(8,128)(2,1)S(1)}, u32[]{:S(2)}, u32[]{:S(2)}) collective-permute-start(bf16[792,128]{1,0:T(8,128)(2,1)S(1)} %copy_kernel.5.refs_6_), channel_id=1, source_target_pairs={{0,1},{1,0},{2,3},{3,2},{4,5},{5,4},{6,7},{7,6},{8,9},{9,8},{10,11... | collective-permute-start | bytes 608264 | tf_op jit(solution)/shard_map/ppermute | solution.py:601
  61.3 10.5 %collective-permute-start.14 = (bf16[1344,128]{1,0:T(8,128)(2,1)S(1)}, bf16[1344,128]{1,0:T(8,128)(2,1)S(1)}, u32[]{:S(2)}, u32[]{:S(2)}) collective-permute-start(bf16[1344,128]{1,0:T(8,128)(2,1)S(1)} %get-tuple-element.98.refs_1_), channel_id=1, source_target_pairs={{0,2},{1,3},{2,0},{3,1},{4,6},{5,7},{6,4},{7,5},{8,10},{9,11},{10,... | collective-permute-start | bytes 1032200 | tf_op jit(solution)/shard_map/ppermute | solution.py:601
  65.7 5.3 %collective-permute-start.20 = (bf16[2,96,384]{2,1,0:T(8,128)(2,1)S(1)}, bf16[2,96,384]{2,1,0:T(8,128)(2,1)S(1)}, u32[]{:S(2)}, u32[]{:S(2)}) collective-permute-start(bf16[2,96,384]{2,1,0:T(8,128)(2,1)S(1)} %get-tuple-element.104), channel_id=1, source_target_pairs={{0,8},{4,12},{8,0},{12,4},{16,24},{20,28},{24,16},{28,20},{1,9},{5... | collective-permute-start | bytes 442376 | tf_op jit(solution)/shard_map/ppermute | solution.py:601
  66.3 4.7 %collective-permute-start.18 = (f32[2,768]{1,0:T(2,128)S(1)}, f32[2,768]{1,0:T(2,128)S(1)}, u32[]{:S(2)}, u32[]{:S(2)}) collective-permute-start(f32[2,768]{1,0:T(2,128)S(1)} %get-tuple-element.100.refs_2_.refs_0_), channel_id=1, source_target_pairs={{0,16},{4,20},{8,24},{12,28},{16,0},{20,4},{24,8},{28,12},{1,17},{... | collective-permute-start | bytes 18440 | tf_op jit(solution)/shard_map/ppermute | solution.py:601
  66.9 9.8 %collective-permute-start.13 = (bf16[1344,128]{1,0:T(8,128)(2,1)S(1)}, bf16[1344,128]{1,0:T(8,128)(2,1)S(1)}, u32[]{:S(2)}, u32[]{:S(2)}) collective-permute-start(bf16[1344,128]{1,0:T(8,128)(2,1)S(1)} %get-tuple-element.98.refs_1_), channel_id=1, source_target_pairs={{0,1},{1,0},{2,3},{3,2},{4,5},{5,4},{6,7},{7,6},{8,9},{9,8},{10,11... | collective-permute-start | bytes 1032200 | tf_op jit(solution)/shard_map/ppermute | solution.py:601
  71.8 4.9 %collective-permute-start.21 = (bf16[1344,128]{1,0:T(8,128)(2,1)S(1)}, bf16[1344,128]{1,0:T(8,128)(2,1)S(1)}, u32[]{:S(2)}, u32[]{:S(2)}) collective-permute-start(bf16[1344,128]{1,0:T(8,128)(2,1)S(1)} %copy_kernel.7.refs_3_), channel_id=1, source_target_pairs={{0,1},{1,0},{2,3},{3,2},{4,5},{5,4},{6,7},{7,6},{8,9},{9,8},{10,11... | collective-permute-start | bytes 1032200 | tf_op jit(solution)/shard_map/ppermute | solution.py:601
  71.9 8.0 %collective-permute-start.24 = (bf16[1,96,384]{2,1,0:T(8,128)(2,1)S(1)}, bf16[1,96,384]{2,1,0:T(8,128)(2,1)S(1)}, u32[]{:S(2)}, u32[]{:S(2)}) collective-permute-start(bf16[1,96,384]{2,1,0:T(8,128)(2,1)S(1)} %get-tuple-element.105.refs_2_), channel_id=1, source_target_pairs={{0,16},{4,20},{8,24},{12,28},{16,0},{20,4},{24,8},{28,12},{1,17},{... | collective-permute-start | bytes 221192 | tf_op jit(solution)/shard_map/ppermute | solution.py:601
  72.6 3.6 %collective-permute-start.22 = (f32[2,768]{1,0:T(2,128)S(1)}, f32[2,768]{1,0:T(2,128)S(1)}, u32[]{:S(2)}, u32[]{:S(2)}) collective-permute-start(f32[2,768]{1,0:T(2,128)S(1)} %add_kernel.8.refs_1_.refs_0_), channel_id=1, source_target_pairs={{0,4},{4,0},{8,12},{12,8},{16,20},{20,16},{24,28},{28,24},{1,5},{5... | collective-permute-start | bytes 18440 | tf_op jit(solution)/shard_map/ppermute | solution.py:601
  76.3 3.6 %collective-permute-start.23 = (f32[2,768]{1,0:T(2,128)S(1)}, f32[2,768]{1,0:T(2,128)S(1)}, u32[]{:S(2)}, u32[]{:S(2)}) collective-permute-start(f32[2,768]{1,0:T(2,128)S(1)} %add_kernel.9.refs_5_.refs_4_), channel_id=1, source_target_pairs={{0,8},{4,12},{8,0},{12,4},{16,24},{20,28},{24,16},{28,20},{1,9},{5... | collective-permute-start | bytes 18440 | tf_op jit(solution)/shard_map/ppermute | solution.py:601

commit v7 on v6

--- a/solution.py
+++ b/solution.py
@@ -289,9 +289,10 @@
         value = rows_of(EDGE + k * step, step).reshape(step // 8, 8, LANES)
         one = one + value.sum(0)
         two = two + (value * value).sum(0)
-    sum_ref[...] = jnp.zeros_like(sum_ref)
-    sum_ref[0:1, :] = jnp.sum(one, 0, keepdims=True)
-    sum_ref[1:2, :] = jnp.sum(two, 0, keepdims=True)
+    one, two = jnp.sum(one, 0, keepdims=True), jnp.sum(two, 0, keepdims=True)
+    for d in range(sum_ref.shape[0]):
+        sum_ref[d, 0:1, :] = one
+        sum_ref[d, 1:2, :] = two
 
 
 def upstream_kernel(cot_ref, rim_ref, one_ref, two_ref, up_ref, point_ref, stack, *, relatives):
@@ -314,11 +315,13 @@
 
 
 def mid_kernel(
-    total_ref, conv_ref, up_ref, norm_ref, hid_ref, d_ref, cen_ref, sent_ref, vec_ref, *, bin_count
+    got_ref, conv_ref, up_ref, norm_ref, point_ref, hid_ref, d_ref, cen_ref, sent_ref, vec_ref, both_ref, *, bin_count
 ):
     rows = hid_ref.shape[0]
     slim = norm_ref.shape[1]
-    total = total_ref[...]
+    total = got_ref[0]
+    for s in range(1, got_ref.shape[0]):
+        total = total + got_ref[s]
     mean = total[0:1] / bin_count
     root = lax.rsqrt(total[1:2] / bin_count - mean * mean + NORM_EPS)
     vec_ref[...] = jnp.zeros_like(vec_ref)
@@ -352,6 +355,12 @@
     for d in range(sent_ref.shape[0]):
         sent_ref[d, 0:1, :] = gain_sum
         sent_ref[d, 1:2, :] = bias_sum
+    if both_ref.shape[0] < rows + point_ref.shape[0]:
+        both = jnp.concatenate([hid_ref[...].astype(F32), point_ref[...].astype(F32)], axis=0)
+        both_ref[...] = fold_rows(both[:, : 3 * LANES // 4]).astype(BF16)
+    else:
+        both_ref[:rows, :] = hid_ref[...]
+        both_ref[rows:, :] = point_ref[...]
 
 
 def conv_back_kernel(got_ref, vec_ref, d_ref, cen_ref, grad_ref, total_ref, grad, *, bin_count, slim):
@@ -375,8 +384,13 @@
     parts, (out_ref, token_ref, hidden, point) = refs[:-4], refs[-4:]
     token_ref[...] = jnp.zeros_like(token_ref)
     rows = x_ref.shape[0]
-    for r, part in enumerate(parts):
-        part = part[...]
+    side = hidden.shape[1] // LANES // 2
+    for r in range(2 * side):
+        if r < side:
+            part = parts[r][...]
+        else:
+            at = side + 3 * (r - side)
+            part = jnp.concatenate([piece[...] for piece in parts[at : at + 3]], axis=0)
         if part.shape[0] < rows + point.shape[0]:
             part = unfold_rows(part.astype(F32), 3 * LANES // 4).astype(BF16)
         hidden[:, r * LANES : (r + 1) * LANES] = part[:rows, :]
@@ -449,17 +463,10 @@
     return (first_next, second_next, weights_new)
 
 
-def first_half_kernel(mask_ref, own_ref, hid_ref, point_ref, *refs):
-    up_ref, both_ref, term, weight, grad = refs[-5:]
-    count = (len(refs) - 5 + 1) // 2
-    grads, weights = refs[: count - 1], refs[count - 1 : -5]
-    rows = up_ref.shape[0]
-    if both_ref.shape[0] < rows + point_ref.shape[0]:
-        both = jnp.concatenate([hid_ref[...].astype(F32), point_ref[...].astype(F32)], axis=0)
-        both_ref[...] = fold_rows(both[:, : 3 * LANES // 4]).astype(BF16)
-    else:
-        both_ref[:rows, :] = hid_ref[...]
-        both_ref[rows:, :] = point_ref[...]
+def first_half_kernel(mask_ref, own_ref, *refs):
+    up_ref, term, weight, grad = refs[-4:]
+    count = (len(refs) - 4 + 1) // 2
+    grads, weights = refs[: count - 1], refs[count - 1 : -4]
     wide = KERNEL_WIDTH * LANES
     term[:, :wide] = own_ref[...]
     for r, part in enumerate(grads):
@@ -583,6 +590,10 @@
     count = len(refs) // 2
     for src, out in zip(refs[:count], refs[count:]):
         out[...] = src[...]
+
+
+def slice_kernel(src_ref, out_ref, *, first):
+    out_ref[...] = src_ref[first : first + out_ref.shape[0], :]
 
 
 def copies(arrays, after):
@@ -697,6 +708,12 @@
         away=(1,),
         sems=1,
     )
+    slopes = call(
+        functools.partial(slope_kernel, first=0),
+        [((rows // 2, width), F32)],
+        [inputs, vec_in],
+        after=[hidden_in],
+    )
 
     stack_type = BF16 if depth % 16 == 0 else F32
     conv_own, conv_out, sums_mid, rims, weight = call(
@@ -706,7 +723,7 @@
         [
             ((width, wide), BF16),
             ((ext, LANES), F32),
-            ((8, LANES), F32),
+            ((seq_size, 2, LANES), F32),
             ((2, *rim), BF16),
             ((seq_size, packed, wide), BF16),
         ],
@@ -716,29 +733,19 @@
             ((rows + 2 * RIM, wide), F32),
             ((2 * RIM, width), BF16),
         ],
+        after=slopes,
     )
     weight = swap(weight, "ch", top)
+    got_mid = spread(sums_mid, "seq")
     upstream, point_own = call(
         functools.partial(upstream_kernel, relatives=relatives_of(point_order)),
         [((ext, LANES), F32), ((width, LANES), BF16)],
         [cotangent, rims, near, near_got],
         scratch=[((seq_size, depth, LANES), stack_type)],
-        after=[sums_mid],
+        after=[got_mid],
     )
     conv_near = gather_parts(conv_own, lower)
-    total, others, slopes = sums_mid, [upstream], []
-    for k, reach in enumerate(sum_order):
-        total = add(total, swap(total, "seq", reach), others)
-        if k < 2:
-            others = call(
-                functools.partial(slope_kernel, first=k * rows // 2),
-                [((rows // 2, width), F32)],
-                [inputs, vec_in],
-                after=[total],
-            )
-            slopes += others
-    (weight,) = copies([weight], [total])
-    hidden_mid, d_mid, centered, sent_back, vec_mid = call(
+    hidden_mid, d_mid, centered, sent_back, vec_mid, both = call(
         functools.partial(mid_kernel, bin_count=bin_count),
         [
             ((rows, LANES), BF16),
@@ -746,9 +753,10 @@
             ((ext, LANES), F32),
             ((seq_size, 2, LANES), F32),
             ((8, LANES), F32),
+            ((3 * (rows + width) // 4 if folds(rows + width, slim) else rows + width, LANES), BF16),
         ],
-        [total, conv_out, upstream, norm_mid],
-        after=[weight, *conv_near[1:]],
+        [got_mid, conv_out, upstream, norm_mid, point_own],
+        after=conv_near[1:],
     )
     got_back = spread(sent_back, "seq")
     grad_own, total_mid = call(
@@ -759,7 +767,8 @@
     )
     grad_near = gather_parts(grad_own, lower)
     grad_far = swap(grad_own, "ch", top)
-    (weight,) = copies([weight], [grad_own])
+    both_parts = gather_parts(both, lower)
+    weight, both_far = copies([weight, swap(both, "ch", top)], [grad_own])
     conv_far = [
         call(
             functools.partial(place_kernel, relatives=relatives_of(weight_order), slim=slim),
@@ -781,41 +790,50 @@
         scratch=[((ext, LANES), F32), ((width, 4 * slim), F32)],
     )
     side = ch_size // 2 * wide
-    up_part, both = call(
+    (up_part,) = call(
         first_half_kernel,
-        [((rows, width), F32), ((3 * (rows + width) // 4 if folds(rows + width, slim) else rows + width, LANES), BF16)],
-        [back, terms, hidden_mid, point_own, *grad_near[1:], *conv_near],
+        [((rows, width), F32)],
+        [back, terms, *grad_near[1:], *conv_near],
         scratch=[((rows, side), BF16), ((width, side), BF16), ((ext, LANES), F32)],
     )
-    grad_far = gather_parts(copies([grad_far], [up_part])[0], lower)
+    slopes += call(
+        functools.partial(slope_kernel, first=rows // 2),
+        [((rows // 2, width), F32)],
+        [inputs, vec_in],
+        after=[up_part],
+    )
+    grad_far = gather_parts(copies([grad_far], slopes[1:])[0], lower)
     d_in, sums_back = call(
         second_half_kernel,
         [((rows, width), F32), ((2, width), F32)],
         [back, inputs, *slopes, vec_in, up_part, *grad_far, *conv_far],
         scratch=[((rows, side), BF16), ((width, side), BF16), ((ext, LANES), F32)],
     )
-    both_parts = gather_parts(both, lower)
-    both_far = swap(both, "ch", top)
-    folds_done = [(kept, sent)]
-    for reach in sum_order[:-1]:
-        half //= 2
-        folds_done.append(
-            call(
+    total_back = sums_back
+    size = both_far.shape[0]
+    cuts = [0, up_to(63 * size // 100, 16), up_to(79 * size // 100, 16), size]
+    for k, reach in enumerate(sum_order):
+        total_got = swap(total_back, "seq", last_order[k])
+        got = swap(sent, "seq", reach)
+        if k < rounds - 1:
+            half //= 2
+            kept, sent = call(
                 functools.partial(fold_kernel, reach=2 * reach),
                 [((half, depth, 4 * slim), F32), ((half, depth, 4 * slim), BF16)],
-                [folds_done[-1][0], swap(folds_done[-1][1], "seq", reach)],
-                after=[sums_back],
+                [kept, got],
+                after=[total_back] if k else [],
             )
-        )
-    kept, got = folds_done[-1][0], swap(folds_done[-1][1], "seq", sum_order[-1])
-    total_back = sums_back
-    for k in range(rounds):
-        total_got = swap(total_back, "seq", last_order[k])
-        if k < rounds - 1:
-            follows = [folds_done[-1][1]] if k == 0 else []
-            total_back = add(total_back, total_got, follows)
-        if k == 0:
-            both_parts += gather_parts(copies([both_far], [total_back])[0], lower)
+            total_back = add(total_back, total_got)
+        for part in {rounds - 3: [0, 1], rounds - 2: [2]}.get(k, []):
+            begin, end = cuts[part : part + 2]
+            (far_part,) = call(
+                functools.partial(slice_kernel, first=begin),
+                [((end - begin, LANES), BF16)],
+                [both_far],
+                after=[total_back],
+            )
+            both_parts.append(gather_parts(far_part, lower))
+    both_parts = both_parts[:-3] + [part for group in zip(*both_parts[-3:]) for part in group]
     block_out, token = call(
         out_kernel,
         [((rows, width), BF16), ((8, LANES), F32)],

time: 83.1 us -> 80.2 us (0.965)
  blocking collectives: 11.1 us -> 20.7 us
  waiting for transfers between devices: 23.9 us -> 15 us
  starting transfers between devices: 25.1 us -> 21.3 us
    all_to_all x1 -> x2, blocking collectives: 11.1 us -> 20.7 us  [spread(): return lax.all_to_all(copies, axes, 0, 0, tiled=True)]
    ppermute x24 -> x23, waiting for transfers between devices: 23.9 us -> 15 us  [swap(): return lax.ppermute(x, axis, flip(axis, reach))]
    ppermute x24 -> x23, starting transfers between devices: 24.4 us -> 20.7 us  [swap(): return lax.ppermute(x, axis, flip(axis, reach))]
    pallas_call x29 -> x27, Pallas kernels: 21.6 us -> 21.7 us  [call(): pl.pallas_call(kernel, out_shape=[jax.ShapeDtypeStruct(s, t) for s, t in...]
  transfers between devices with their start and end apart: 25 -> 24, of which waited for: 12 -> 10; matrix products, arithmetic and copies ran while one was open for 0% -> 0% of each run, Pallas kernels for 18% -> 20%
where the time goes in v7:
time: 80.2 us; the launch traced here: 79.9 us
  Pallas kernels  21.7 us (27%)
  starting transfers between devices  21.3 us (27%)
  blocking collectives  20.7 us (26%)
  waiting for transfers between devices  15 us (19%)
  between operations  1.08 us (1%)
    pallas_call x27, Pallas kernels, call(): pl.pallas_call(kernel, out_shape=[jax.ShapeDtypeStruct(s, t) for s, t in...  21.7 us
    all_to_all x2, blocking collectives, spread(): return lax.all_to_all(copies, axes, 0, 0, tiled=True)  20.7 us
    ppermute x23, starting transfers between devices, swap(): return lax.ppermute(x, axis, flip(axis, reach))  20.7 us
    ppermute x23, waiting for transfers between devices, swap(): return lax.ppermute(x, axis, flip(axis, reach))  15 us
  transfers between devices with their start and end apart: 24, of which 10 were waited for; matrix products, arithmetic and copies ran while one was open for 0% of the time, Pallas kernels for 20%

profile of v7, /device:TPU:0, one launch (start us, length us, event | category | flops | bytes accessed | tf_op | source)
XLA Modules:
  0.0 79.9 jit_solution(17739318209857091764)
XLA Ops:
  0.7 1.7 %first_kernel.1 = (bf16[1024,768]{1,0:T(8,128)(2,1)S(1)}, bf16[1,72,384]{2,1,0:T(8,128)(2,1)S(1)}, bf16[144,128]{1,0:T(8,128)(2,1)S(1)}, bf16[48,768]{1,0:T(8,128)(2,1)S(1)}, bf16[48,768]{1,0:T(8,128)(2,1)S(1)}) custom-call(bf16[1024,768]{1,0:T(8,128)(2,1)} %refs_0_.2, bf16[1024,768]{1,0:T(8,128)(2,1)} %refs_1_.3, f32[3,96,96]{2,1,0:T(8,128)} %refs_12_.1, ...), custom_call_target="tpu_custom_call" | custom-call | flops 1 | bytes 1 | tf_op jit(solution)/shard_map/first_kernel/pallas_call | solution.py:48
  2.4 4.1 %collective-permute-start = (bf16[1,72,384]{2,1,0:T(8,128)(2,1)S(1)}, bf16[1,72,384]{2,1,0:T(8,128)(2,1)S(1)}, u32[]{:S(2)}, u32[]{:S(2)}) collective-permute-start(bf16[1,72,384]{2,1,0:T(8,128)(2,1)S(1)} %get-tuple-element.72.refs_0_), channel_id=1, source_target_pairs={{0,16},{4,20},{8,24},{12,28},{16,0},{20,4},{24,8},{28,12},{1,17},{... | collective-permute-start | bytes 165896 | tf_op jit(solution)/shard_map/ppermute | solution.py:612
  6.6 4.8 %collective-permute-done.1.refs_3_ = bf16[144,128]{1,0:T(8,128)(2,1)S(1)} collective-permute-done((bf16[144,128]{1,0:T(8,128)(2,1)S(1)}, bf16[144,128]{1,0:T(8,128)(2,1)S(1)}, u32[]{:S(2)}, u32[]{:S(2)}) %collective-permute-start.1) | collective-permute-done | bytes 36896 | tf_op jit(solution)/shard_map/ppermute | solution.py:612
  11.4 1.6 %collective-permute-start.3 = (bf16[528,128]{1,0:T(8,128)(2,1)S(1)}, bf16[528,128]{1,0:T(8,128)(2,1)S(1)}, u32[]{:S(2)}, u32[]{:S(2)}) collective-permute-start(bf16[528,128]{1,0:T(8,128)(2,1)S(1)} %get-tuple-element.75.refs_2_), channel_id=1, source_target_pairs={{0,4},{4,0},{8,12},{12,8},{16,20},{20,16},{24,28},{28,24},{1,5},{5... | collective-permute-start | bytes 405512 | tf_op jit(solution)/shard_map/ppermute | solution.py:612
  12.9 1.6 %collective-permute-start.2 = (bf16[2,72,384]{2,1,0:T(8,128)(2,1)S(1)}, bf16[2,72,384]{2,1,0:T(8,128)(2,1)S(1)}, u32[]{:S(2)}, u32[]{:S(2)}) collective-permute-start(bf16[2,72,384]{2,1,0:T(8,128)(2,1)S(1)} %get-tuple-element.77.refs_0_), channel_id=1, source_target_pairs={{0,8},{4,12},{8,0},{12,4},{16,24},{20,28},{24,16},{28,20},{1,9},{5... | collective-permute-start | bytes 331784 | tf_op jit(solution)/shard_map/ppermute | solution.py:612
  14.5 1.4 %mask_kernel.1 = (f32[3,1056,128]{2,1,0:T(8,128)S(1)}, f32[3,1024,128]{2,1,0:T(8,128)S(1)}, bf16[48,768]{1,0:T(8,128)(2,1)S(1)}) custom-call(s32[8]{0:T(128)S(1)} %copy-done.2, bf16[48,768]{1,0:T(8,128)(2,1)S(1)} %get-tuple-element.71.refs_1_, bf16[528,128]{1,0:T(8,128)(2,1)S(1)} %get-tuple-element.75.refs_2_), custom_call_target="tpu_custom_call" | custom-call | flops 1 | bytes 1 | tf_op jit(solution)/shard_map/mask_kernel/pallas_call | solution.py:48
  15.9 1.7 %collective-permute-done.2.refs_1_ = bf16[2,72,384]{2,1,0:T(8,128)(2,1)S(1)} collective-permute-done((bf16[2,72,384]{2,1,0:T(8,128)(2,1)S(1)}, bf16[2,72,384]{2,1,0:T(8,128)(2,1)S(1)}, u32[]{:S(2)}, u32[]{:S(2)}) %collective-permute-start.2) | collective-permute-done | bytes 110624 | tf_op jit(solution)/shard_map/ppermute | solution.py:612
  18.3 1.6 %collective-permute-start.4 = (bf16[432,128]{1,0:T(8,128)(2,1)S(1)}, bf16[432,128]{1,0:T(8,128)(2,1)S(1)}, u32[]{:S(2)}, u32[]{:S(2)}) collective-permute-start(bf16[432,128]{1,0:T(8,128)(2,1)S(1)} %get-tuple-element.79.refs_2_), channel_id=1, source_target_pairs={{0,8},{4,12},{8,0},{12,4},{16,24},{20,28},{24,16},{28,20},{1,9},{5... | collective-permute-start | bytes 331784 | tf_op jit(solution)/shard_map/ppermute | solution.py:612
  19.9 0.7 collective-permute-start.5
  20.6 3.1 %collective-permute-done.4.refs_3_ = bf16[432,128]{1,0:T(8,128)(2,1)S(1)} collective-permute-done((bf16[432,128]{1,0:T(8,128)(2,1)S(1)}, bf16[432,128]{1,0:T(8,128)(2,1)S(1)}, u32[]{:S(2)}, u32[]{:S(2)}) %collective-permute-start.4) | collective-permute-done | bytes 110624 | tf_op jit(solution)/shard_map/ppermute | solution.py:612
  23.7 1.5 %act_kernel.1 = (bf16[1024,768]{1,0:T(8,128)(2,1)S(1)}, f32[8,768]{1,0:T(8,128)S(1)}, bf16[1024,768]{1,0:T(8,128)(2,1)S(1)}) custom-call(bf16[1024,768]{1,0:T(8,128)(2,1)S(1)} %get-tuple-element.70.refs_0_.refs_1_, bf16[1024,768]{1,0:T(8,128)(2,1)} %refs_1_.3, bf16[432,128]{1,0:T(8,128)(2,1)S(1)} %get-tuple-element.79.refs_2_, ...), custom_call_target="tpu_custom_call" | custom-call | flops 1 | bytes 1 | tf_op jit(solution)/shard_map/act_kernel/pallas_call | solution.py:48
  25.2 1.1 %slope_kernel.2.refs_7_.refs_2_ = f32[512,768]{1,0:T(8,128)S(1)} custom-call(bf16[1024,768]{1,0:T(8,128)(2,1)S(1)} %get-tuple-element.70.refs_0_.refs_1_, f32[8,768]{1,0:T(8,128)S(1)} %get-tuple-element.82.refs_1_.refs_4_.refs_3_, bf16[1024,768]{1,0:T(8,128)(2,1)S(1)} %get-tuple-element.80.refs_2_.refs_1_), custom_call_target="tpu_custom_call" | custom-call | flops 1 | bytes 1 | tf_op jit(solution)/shard_map/slope_kernel/pallas_call | solution.py:48
  26.4 1.4 %conv_kernel.1 = (bf16[768,384]{1,0:T(8,128)(2,1)S(1)}, f32[1056,128]{1,0:T(8,128)S(1)}, f32[8,2,128]{2,1,0:T(2,128)S(1)}, bf16[2,48,768]{2,1,0:T(8,128)(2,1)S(1)}, bf16[8,72,384]{2,1,0:T(8,128)(2,1)S(1)}) custom-call(f32[3,1056,128]{2,1,0:T(8,128)S(1)} %get-tuple-element.76.refs_0_, bf16[1024,768]{1,0:T(8,128)(2,1)S(1)} %get-tuple-element.80.refs_2_.refs_1_, ...), custom_call_target="tpu_custom_call" | custom-call | flops 1 | bytes 1 | tf_op jit(solution)/shard_map/conv_kernel/pallas_call | solution.py:48
  27.9 1.6 %collective-permute-start.9 = (bf16[8,72,384]{2,1,0:T(8,128)(2,1)S(1)}, bf16[8,72,384]{2,1,0:T(8,128)(2,1)S(1)}, u32[]{:S(2)}, u32[]{:S(2)}) collective-permute-start(bf16[8,72,384]{2,1,0:T(8,128)(2,1)S(1)} %get-tuple-element.92), channel_id=1, source_target_pairs={{0,2},{1,3},{2,0},{3,1},{4,6},{5,7},{6,4},{7,5},{8,10},{9,11},{10,... | collective-permute-start | bytes 1327112 | tf_op jit(solution)/shard_map/ppermute | solution.py:612
  29.5 11.9 %all_to_all.10.refs_4_.refs_0_ = f32[8,2,128]{2,1,0:T(2,128)S(1)} all-to-all(f32[8,2,128]{2,1,0:T(2,128)S(1)} %get-tuple-element.84), channel_id=1, replica_groups=mesh['seq'=8,'ch'=4] {'seq'}, dimensions={0} | all-to-all | bytes 16384 | tf_op jit(solution)/shard_map/all_to_all | solution.py:623
  41.4 0.7 upstream_kernel.1
  42.0 0.7 mid_kernel.1
  43.4 8.9 %all_to_all.11.refs_0_ = f32[8,2,128]{2,1,0:T(2,128)S(1)} all-to-all(f32[8,2,128]{2,1,0:T(2,128)S(1)} %get-tuple-element.93), channel_id=1, replica_groups=mesh['seq'=8,'ch'=4] {'seq'}, dimensions={0} | all-to-all | bytes 16384 | tf_op jit(solution)/shard_map/all_to_all | solution.py:623
  53.2 1.5 %collective-permute-start.12 = (bf16[792,128]{1,0:T(8,128)(2,1)S(1)}, bf16[792,128]{1,0:T(8,128)(2,1)S(1)}, u32[]{:S(2)}, u32[]{:S(2)}) collective-permute-start(bf16[792,128]{1,0:T(8,128)(2,1)S(1)} %get-tuple-element.97.refs_2_.refs_1_), channel_id=1, source_target_pairs={{0,2},{1,3},{2,0},{3,1},{4,6},{5,7},{6,4},{7,5},{8,10},{9,11},{10,... | collective-permute-start | bytes 608264 | tf_op jit(solution)/shard_map/ppermute | solution.py:612
  54.7 1.9 %weight_grad_kernel.1 = (bf16[1024,384]{1,0:T(8,128)(2,1)S(1)}, f32[4,96,384]{2,1,0:T(8,128)S(1)}, bf16[4,96,384]{2,1,0:T(8,128)(2,1)S(1)}) custom-call(f32[3,1024,128]{2,1,0:T(8,128)S(1)} %get-tuple-element.78.refs_4_.refs_0_, bf16[792,128]{1,0:T(8,128)(2,1)S(1)} %get-tuple-element.97.refs_2_.refs_1_, ...), custom_call_target="tpu_custom_call" | custom-call | flops 1 | bytes 1 | tf_op jit(solution)/shard_map/weight_grad_kernel/pallas_call | solution.py:48
  56.6 0.6 collective-permute-start.21
  57.2 1.6 %first_half_kernel.1.refs_2_.refs_5_ = f32[1024,768]{1,0:T(8,128)S(1)} custom-call(f32[3,1024,128]{2,1,0:T(8,128)S(1)} %get-tuple-element.78.refs_4_.refs_0_, bf16[1024,384]{1,0:T(8,128)(2,1)S(1)} %get-tuple-element.100.refs_1_, bf16[792,128]{1,0:T(8,128)(2,1)S(1)} %collective-permute-done.11.refs_2_, bf16[768,384]{1,0:T(8,128)(2,1)S(1)} %get-tuple-element.90.refs_3_, ...), custom_call_target="tpu_custom_call" | custom-call | flops 1 | bytes 1 | tf_op jit(solution)/shard_map/first_half_kernel/pallas_call | solution.py:48
  58.8 1.1 %slope_kernel.3.refs_1_.refs_3_ = f32[512,768]{1,0:T(8,128)S(1)} custom-call(bf16[1024,768]{1,0:T(8,128)(2,1)S(1)} %get-tuple-element.70.refs_0_.refs_1_, f32[8,768]{1,0:T(8,128)S(1)} %get-tuple-element.82.refs_1_.refs_4_.refs_3_, f32[1024,768]{1,0:T(8,128)S(1)} %first_half_kernel.1.refs_2_.refs_5_), custom_call_target="tpu_custom_call" | custom-call | flops 1 | bytes 1 | tf_op jit(solution)/shard_map/slope_kernel/pallas_call | solution.py:48
  61.7 2.2 %second_half_kernel.1 = (f32[1024,768]{1,0:T(8,128)S(1)}, f32[2,768]{1,0:T(2,128)S(1)}) custom-call(f32[3,1024,128]{2,1,0:T(8,128)S(1)} %get-tuple-element.78.refs_4_.refs_0_, bf16[1024,768]{1,0:T(8,128)(2,1)S(1)} %get-tuple-element.70.refs_0_.refs_1_, f32[512,768]{1,0:T(8,128)S(1)} %slope_kernel.2.refs_7_.refs_2_, ...), custom_call_target="tpu_custom_call" | custom-call | flops 1 | bytes 1 | tf_op jit(solution)/shard_map/second_half_kernel/pallas_call | solution.py:48
  63.9 0.6 collective-permute-start.15
  64.5 0.9 %collective-permute-done.21.refs_1_ = bf16[4,96,384]{2,1,0:T(8,128)(2,1)S(1)} collective-permute-done((bf16[4,96,384]{2,1,0:T(8,128)(2,1)S(1)}, bf16[4,96,384]{2,1,0:T(8,128)(2,1)S(1)}, u32[]{:S(2)}, u32[]{:S(2)}) %collective-permute-start.21) | collective-permute-done | bytes 294944 | tf_op jit(solution)/shard_map/ppermute | solution.py:612
  66.0 2.6 %collective-permute-done.15.refs_1_ = f32[2,768]{1,0:T(2,128)S(1)} collective-permute-done((f32[2,768]{1,0:T(2,128)S(1)}, f32[2,768]{1,0:T(2,128)S(1)}, u32[]{:S(2)}, u32[]{:S(2)}) %collective-permute-start.15) | collective-permute-done | bytes 6176 | tf_op jit(solution)/shard_map/ppermute | solution.py:612
  68.7 1.3 %collective-permute-start.16 = (f32[2,768]{1,0:T(2,128)S(1)}, f32[2,768]{1,0:T(2,128)S(1)}, u32[]{:S(2)}, u32[]{:S(2)}) collective-permute-start(f32[2,768]{1,0:T(2,128)S(1)} %add_kernel.2.refs_1_.refs_0_.refs_2_), channel_id=1, source_target_pairs={{0,4},{4,0},{8,12},{12,8},{16,20},{20,16},{24,28},{28,24},{1,5},{5... | collective-permute-start | bytes 18440 | tf_op jit(solution)/shard_map/ppermute | solution.py:612
  70.0 0.7 collective-permute-done.22.refs_1_
  70.7 2.0 %collective-permute-start.23 = (bf16[1,96,384]{2,1,0:T(8,128)(2,1)S(1)}, bf16[1,96,384]{2,1,0:T(8,128)(2,1)S(1)}, u32[]{:S(2)}, u32[]{:S(2)}) collective-permute-start(bf16[1,96,384]{2,1,0:T(8,128)(2,1)S(1)} %get-tuple-element.110), channel_id=1, source_target_pairs={{0,16},{4,20},{8,24},{12,28},{16,0},{20,4},{24,8},{28,12},{1,17},{... | collective-permute-start | bytes 221192 | tf_op jit(solution)/shard_map/ppermute | solution.py:612
  74.2 2.5 %out_kernel.1 = (bf16[1024,768]{1,0:T(8,128)(2,1)}, f32[8,128]{1,0:T(8,128)S(1)}) custom-call(bf16[1024,768]{1,0:T(8,128)(2,1)S(1)} %get-tuple-element.70.refs_0_.refs_1_, bf16[1344,128]{1,0:T(8,128)(2,1)S(1)} %get-tuple-element.91.refs_1_, bf16[1344,128]{1,0:T(8,128)(2,1)S(1)} %collective-permute-done.8.refs_2_, bf16[848,128]{1,0:T(8,128)(2,1)S(1)} %slice_kernel.3.refs_3_, ...), custom_call_target="tpu_custom_call" | custom-call | flops 1 | bytes 1 | tf_op jit(solution)/shard_map/out_kernel/pallas_call | solution.py:48
  76.9 2.8 %final_kernel.1 = (f32[1024,768]{1,0:T(8,128)}, f32[2,768]{1,0:T(2,128)}, f32[2,768]{1,0:T(2,128)}, f32[2,768]{1,0:T(2,128)}, f32[3,96,96]{2,1,0:T(8,128)}, /*in...) custom-call(bf16[1024,768]{1,0:T(8,128)(2,1)S(1)} %get-tuple-element, ...), custom_call_target="tpu_custom_call" | custom-call | flops 1 | bytes 1 | tf_op jit(solution)/shard_map/final_kernel/pallas_call | solution.py:48
  (51 shorter events, 6.5 us)
Async XLA Ops:
  0.6 13.9 %copy-start.2 = (s32[8]{0:T(128)S(1)}, s32[8]{0:T(128)}, u32[]{:S(2)}) copy-start(s32[8]{0:T(128)} %refs_0_.3) | copy-start | bytes 100
  2.4 21.3 %copy-start = (f32[2,768]{1,0:T(2,128)S(1)}, f32[2,768]{1,0:T(2,128)}, u32[]{:S(2)}) copy-start(f32[2,768]{1,0:T(2,128)} %refs_9_.1) | copy-start | bytes 18436
  2.4 9.0 %collective-permute-start = (bf16[1,72,384]{2,1,0:T(8,128)(2,1)S(1)}, bf16[1,72,384]{2,1,0:T(8,128)(2,1)S(1)}, u32[]{:S(2)}, u32[]{:S(2)}) collective-permute-start(bf16[1,72,384]{2,1,0:T(8,128)(2,1)S(1)} %get-tuple-element.72.refs_0_), channel_id=1, source_target_pairs={{0,16},{4,20},{8,24},{12,28},{16,0},{20,4},{24,8},{28,12},{1,17},{... | collective-permute-start | bytes 165896 | tf_op jit(solution)/shard_map/ppermute | solution.py:612
  6.5 4.9 %collective-permute-start.1 = (bf16[144,128]{1,0:T(8,128)(2,1)S(1)}, bf16[144,128]{1,0:T(8,128)(2,1)S(1)}, u32[]{:S(2)}, u32[]{:S(2)}) collective-permute-start(bf16[144,128]{1,0:T(8,128)(2,1)S(1)} %get-tuple-element.73.refs_2_), channel_id=1, source_target_pairs={{0,16},{4,20},{8,24},{12,28},{16,0},{20,4},{24,8},{28,12},{1,17},{... | collective-permute-start | bytes 110600 | tf_op jit(solution)/shard_map/ppermute | solution.py:612
  11.4 6.3 %collective-permute-start.3 = (bf16[528,128]{1,0:T(8,128)(2,1)S(1)}, bf16[528,128]{1,0:T(8,128)(2,1)S(1)}, u32[]{:S(2)}, u32[]{:S(2)}) collective-permute-start(bf16[528,128]{1,0:T(8,128)(2,1)S(1)} %get-tuple-element.75.refs_2_), channel_id=1, source_target_pairs={{0,4},{4,0},{8,12},{12,8},{16,20},{20,16},{24,28},{28,24},{1,5},{5... | collective-permute-start | bytes 405512 | tf_op jit(solution)/shard_map/ppermute | solution.py:612
  12.9 4.7 %collective-permute-start.2 = (bf16[2,72,384]{2,1,0:T(8,128)(2,1)S(1)}, bf16[2,72,384]{2,1,0:T(8,128)(2,1)S(1)}, u32[]{:S(2)}, u32[]{:S(2)}) collective-permute-start(bf16[2,72,384]{2,1,0:T(8,128)(2,1)S(1)} %get-tuple-element.77.refs_0_), channel_id=1, source_target_pairs={{0,8},{4,12},{8,0},{12,4},{16,24},{20,28},{24,16},{28,20},{1,9},{5... | collective-permute-start | bytes 331784 | tf_op jit(solution)/shard_map/ppermute | solution.py:612
  17.7 8.7 %collective-permute-start.6 = (bf16[4,72,384]{2,1,0:T(8,128)(2,1)S(1)}, bf16[4,72,384]{2,1,0:T(8,128)(2,1)S(1)}, u32[]{:S(2)}, u32[]{:S(2)}) collective-permute-start(bf16[4,72,384]{2,1,0:T(8,128)(2,1)S(1)} %get-tuple-element.83.refs_5_), channel_id=1, source_target_pairs={{0,4},{4,0},{8,12},{12,8},{16,20},{20,16},{24,28},{28,24},{1,5},{5... | collective-permute-start | bytes 663560 | tf_op jit(solution)/shard_map/ppermute | solution.py:612
  18.3 5.4 %collective-permute-start.4 = (bf16[432,128]{1,0:T(8,128)(2,1)S(1)}, bf16[432,128]{1,0:T(8,128)(2,1)S(1)}, u32[]{:S(2)}, u32[]{:S(2)}) collective-permute-start(bf16[432,128]{1,0:T(8,128)(2,1)S(1)} %get-tuple-element.79.refs_2_), channel_id=1, source_target_pairs={{0,8},{4,12},{8,0},{12,4},{16,24},{20,28},{24,16},{28,20},{1,9},{5... | collective-permute-start | bytes 331784 | tf_op jit(solution)/shard_map/ppermute | solution.py:612
  19.9 6.5 %collective-permute-start.5 = (bf16[48,768]{1,0:T(8,128)(2,1)S(1)}, bf16[48,768]{1,0:T(8,128)(2,1)S(1)}, u32[]{:S(2)}, u32[]{:S(2)}) collective-permute-start(bf16[48,768]{1,0:T(8,128)(2,1)S(1)} %get-tuple-element.81), channel_id=1, source_target_pairs={{4,8},{12,16},{20,24},{8,4},{16,12},{24,20},{5,9},{13,17},{21,25},... | collective-permute-start | bytes 221192 | tf_op jit(solution)/shard_map/ppermute | solution.py:699
  27.8 14.2 %copy-start.1 = (f32[2,96]{1,0:T(2,128)S(1)}, f32[2,96]{1,0:T(2,128)}, u32[]{:S(2)}) copy-start(f32[2,96]{1,0:T(2,128)} %refs_18_.1) | copy-start | bytes 2308
  27.8 14.2 %collective-permute-start.7 = (bf16[768,384]{1,0:T(8,128)(2,1)S(1)}, bf16[768,384]{1,0:T(8,128)(2,1)S(1)}, u32[]{:S(2)}, u32[]{:S(2)}) collective-permute-start(bf16[768,384]{1,0:T(8,128)(2,1)S(1)} %get-tuple-element.90.refs_3_), channel_id=1, source_target_pairs={{0,1},{1,0},{2,3},{3,2},{4,5},{5,4},{6,7},{7,6},{8,9},{9,8},{10,11... | collective-permute-start | bytes 1769480 | tf_op jit(solution)/shard_map/ppermute | solution.py:612
  27.9 24.6 %collective-permute-start.9 = (bf16[8,72,384]{2,1,0:T(8,128)(2,1)S(1)}, bf16[8,72,384]{2,1,0:T(8,128)(2,1)S(1)}, u32[]{:S(2)}, u32[]{:S(2)}) collective-permute-start(bf16[8,72,384]{2,1,0:T(8,128)(2,1)S(1)} %get-tuple-element.92), channel_id=1, source_target_pairs={{0,2},{1,3},{2,0},{3,1},{4,6},{5,7},{6,4},{7,5},{8,10},{9,11},{10,... | collective-permute-start | bytes 1327112 | tf_op jit(solution)/shard_map/ppermute | solution.py:612
  42.8 9.7 %collective-permute-start.10 = (bf16[1344,128]{1,0:T(8,128)(2,1)S(1)}, bf16[1344,128]{1,0:T(8,128)(2,1)S(1)}, u32[]{:S(2)}, u32[]{:S(2)}) collective-permute-start(bf16[1344,128]{1,0:T(8,128)(2,1)S(1)} %get-tuple-element.91.refs_1_), channel_id=1, source_target_pairs={{0,2},{1,3},{2,0},{3,1},{4,6},{5,7},{6,4},{7,5},{8,10},{9,11},{10,... | collective-permute-start | bytes 1032200 | tf_op jit(solution)/shard_map/ppermute | solution.py:612
  52.6 8.5 %collective-permute-start.14 = (bf16[8,72,384]{2,1,0:T(8,128)(2,1)S(1)}, bf16[8,72,384]{2,1,0:T(8,128)(2,1)S(1)}, u32[]{:S(2)}, u32[]{:S(2)}) collective-permute-start(bf16[8,72,384]{2,1,0:T(8,128)(2,1)S(1)} %get-tuple-element.101.refs_0_), channel_id=1, source_target_pairs={{0,1},{1,0},{2,3},{3,2},{4,5},{5,4},{6,7},{7,6},{8,9},{9,8},{10,11... | collective-permute-start | bytes 1327112 | tf_op jit(solution)/shard_map/ppermute | solution.py:612
  52.7 4.5 %collective-permute-start.11 = (bf16[792,128]{1,0:T(8,128)(2,1)S(1)}, bf16[792,128]{1,0:T(8,128)(2,1)S(1)}, u32[]{:S(2)}, u32[]{:S(2)}) collective-permute-start(bf16[792,128]{1,0:T(8,128)(2,1)S(1)} %get-tuple-element.97.refs_2_.refs_1_), channel_id=1, source_target_pairs={{0,1},{1,0},{2,3},{3,2},{4,5},{5,4},{6,7},{7,6},{8,9},{9,8},{10,11... | collective-permute-start | bytes 608264 | tf_op jit(solution)/shard_map/ppermute | solution.py:612
  53.2 7.0 %collective-permute-start.12 = (bf16[792,128]{1,0:T(8,128)(2,1)S(1)}, bf16[792,128]{1,0:T(8,128)(2,1)S(1)}, u32[]{:S(2)}, u32[]{:S(2)}) collective-permute-start(bf16[792,128]{1,0:T(8,128)(2,1)S(1)} %get-tuple-element.97.refs_2_.refs_1_), channel_id=1, source_target_pairs={{0,2},{1,3},{2,0},{3,1},{4,6},{5,7},{6,4},{7,5},{8,10},{9,11},{10,... | collective-permute-start | bytes 608264 | tf_op jit(solution)/shard_map/ppermute | solution.py:612
  56.6 8.8 %collective-permute-start.21 = (bf16[4,96,384]{2,1,0:T(8,128)(2,1)S(1)}, bf16[4,96,384]{2,1,0:T(8,128)(2,1)S(1)}, u32[]{:S(2)}, u32[]{:S(2)}) collective-permute-start(bf16[4,96,384]{2,1,0:T(8,128)(2,1)S(1)} %get-tuple-element.106), channel_id=1, source_target_pairs={{0,4},{4,0},{8,12},{12,8},{16,20},{20,16},{24,28},{28,24},{1,5},{5... | collective-permute-start | bytes 884744 | tf_op jit(solution)/shard_map/ppermute | solution.py:612
  60.2 1.5 %collective-permute-start.13 = (bf16[792,128]{1,0:T(8,128)(2,1)S(1)}, bf16[792,128]{1,0:T(8,128)(2,1)S(1)}, u32[]{:S(2)}, u32[]{:S(2)}) collective-permute-start(bf16[792,128]{1,0:T(8,128)(2,1)S(1)} %copy_kernel.3.refs_6_), channel_id=1, source_target_pairs={{0,1},{1,0},{2,3},{3,2},{4,5},{5,4},{6,7},{7,6},{8,9},{9,8},{10,11... | collective-permute-start | bytes 608264 | tf_op jit(solution)/shard_map/ppermute | solution.py:612
  60.3 13.0 %collective-permute-start.8 = (bf16[1344,128]{1,0:T(8,128)(2,1)S(1)}, bf16[1344,128]{1,0:T(8,128)(2,1)S(1)}, u32[]{:S(2)}, u32[]{:S(2)}) collective-permute-start(bf16[1344,128]{1,0:T(8,128)(2,1)S(1)} %get-tuple-element.91.refs_1_), channel_id=1, source_target_pairs={{0,1},{1,0},{2,3},{3,2},{4,5},{5,4},{6,7},{7,6},{8,9},{9,8},{10,11... | collective-permute-start | bytes 1032200 | tf_op jit(solution)/shard_map/ppermute | solution.py:612
  63.9 4.7 %collective-permute-start.15 = (f32[2,768]{1,0:T(2,128)S(1)}, f32[2,768]{1,0:T(2,128)S(1)}, u32[]{:S(2)}, u32[]{:S(2)}) collective-permute-start(f32[2,768]{1,0:T(2,128)S(1)} %get-tuple-element.102.refs_0_), channel_id=1, source_target_pairs={{0,16},{4,20},{8,24},{12,28},{16,0},{20,4},{24,8},{28,12},{1,17},{... | collective-permute-start | bytes 18440 | tf_op jit(solution)/shard_map/ppermute | solution.py:612
  65.4 5.2 %collective-permute-start.22 = (bf16[2,96,384]{2,1,0:T(8,128)(2,1)S(1)}, bf16[2,96,384]{2,1,0:T(8,128)(2,1)S(1)}, u32[]{:S(2)}, u32[]{:S(2)}) collective-permute-start(bf16[2,96,384]{2,1,0:T(8,128)(2,1)S(1)} %get-tuple-element.108), channel_id=1, source_target_pairs={{0,8},{4,12},{8,0},{12,4},{16,24},{20,28},{24,16},{28,20},{1,9},{5... | collective-permute-start | bytes 442376 | tf_op jit(solution)/shard_map/ppermute | solution.py:612
  68.6 5.6 %collective-permute-start.17 = (bf16[848,128]{1,0:T(8,128)(2,1)S(1)}, bf16[848,128]{1,0:T(8,128)(2,1)S(1)}, u32[]{:S(2)}, u32[]{:S(2)}) collective-permute-start(bf16[848,128]{1,0:T(8,128)(2,1)S(1)} %slice_kernel.3.refs_3_), channel_id=1, source_target_pairs={{0,1},{1,0},{2,3},{3,2},{4,5},{5,4},{6,7},{7,6},{8,9},{9,8},{10,11... | collective-permute-start | bytes 651272 | tf_op jit(solution)/shard_map/ppermute | solution.py:612
  68.7 4.0 %collective-permute-start.16 = (f32[2,768]{1,0:T(2,128)S(1)}, f32[2,768]{1,0:T(2,128)S(1)}, u32[]{:S(2)}, u32[]{:S(2)}) collective-permute-start(f32[2,768]{1,0:T(2,128)S(1)} %add_kernel.2.refs_1_.refs_0_.refs_2_), channel_id=1, source_target_pairs={{0,4},{4,0},{8,12},{12,8},{16,20},{20,16},{24,28},{28,24},{1,5},{5... | collective-permute-start | bytes 18440 | tf_op jit(solution)/shard_map/ppermute | solution.py:612
  70.7 6.3 %collective-permute-start.23 = (bf16[1,96,384]{2,1,0:T(8,128)(2,1)S(1)}, bf16[1,96,384]{2,1,0:T(8,128)(2,1)S(1)}, u32[]{:S(2)}, u32[]{:S(2)}) collective-permute-start(bf16[1,96,384]{2,1,0:T(8,128)(2,1)S(1)} %get-tuple-element.110), channel_id=1, source_target_pairs={{0,16},{4,20},{8,24},{12,28},{16,0},{20,4},{24,8},{28,12},{1,17},{... | collective-permute-start | bytes 221192 | tf_op jit(solution)/shard_map/ppermute | solution.py:612
  72.7 1.5 %collective-permute-start.19 = (bf16[272,128]{1,0:T(8,128)(2,1)S(1)}, bf16[272,128]{1,0:T(8,128)(2,1)S(1)}, u32[]{:S(2)}, u32[]{:S(2)}) collective-permute-start(bf16[272,128]{1,0:T(8,128)(2,1)S(1)} %slice_kernel.5.refs_5_), channel_id=1, source_target_pairs={{0,1},{1,0},{2,3},{3,2},{4,5},{5,4},{6,7},{7,6},{8,9},{9,8},{10,11... | collective-permute-start | bytes 208904 | tf_op jit(solution)/shard_map/ppermute | solution.py:612
  72.8 1.4 %collective-permute-start.18 = (bf16[224,128]{1,0:T(8,128)(2,1)S(1)}, bf16[224,128]{1,0:T(8,128)(2,1)S(1)}, u32[]{:S(2)}, u32[]{:S(2)}) collective-permute-start(bf16[224,128]{1,0:T(8,128)(2,1)S(1)} %slice_kernel.4.refs_4_), channel_id=1, source_target_pairs={{0,1},{1,0},{2,3},{3,2},{4,5},{5,4},{6,7},{7,6},{8,9},{9,8},{10,11... | collective-permute-start | bytes 172040 | tf_op jit(solution)/shard_map/ppermute | solution.py:612
  73.3 3.6 %collective-permute-start.20 = (f32[2,768]{1,0:T(2,128)S(1)}, f32[2,768]{1,0:T(2,128)S(1)}, u32[]{:S(2)}, u32[]{:S(2)}) collective-permute-start(f32[2,768]{1,0:T(2,128)S(1)} %add_kernel.3.refs_1_.refs_9_.refs_4_), channel_id=1, source_target_pairs={{0,8},{4,12},{8,0},{12,4},{16,24},{20,28},{24,16},{28,20},{1,9},{5... | collective-permute-start | bytes 18440 | tf_op jit(solution)/shard_map/ppermute | solution.py:612

commit v8 on v7

--- a/solution.py
+++ b/solution.py
@@ -104,6 +104,22 @@
     side.append(jnp.zeros((quarter, width), block.dtype))
     lane = lax.broadcasted_iota(jnp.int32, block.shape, 1)
     return jnp.concatenate([jnp.where(lane < slim, block, 0.0), jnp.concatenate(side, axis=1)], axis=0)
+
+
+def folded_rows(rows, slim):
+    return 3 * rows // 4 if folds(rows, slim) else rows
+
+
+def put_folded(block, out_ref):
+    if out_ref.shape[0] < block.shape[0]:
+        block = fold_rows(block[:, : 3 * LANES // 4].astype(F32)).astype(BF16)
+    out_ref[...] = block
+
+
+def get_folded(block, rows):
+    if block.shape[0] < rows:
+        block = unfold_rows(block.astype(F32), 3 * LANES // 4).astype(BF16)
+    return block
 
 
 def first_kernel(
@@ -245,12 +261,16 @@
     lax.fori_loop(0, slope_ref.shape[0] // 16, step, 0, unroll=2)
 
 
-def conv_kernel(mask_ref, hid_ref, near_ref, far_ref, vec_ref, *refs, relatives, slim):
+def conv_kernel(mask_ref, hid_ref, near_ref, far_ref, vec_ref, pack_ref, *refs, relatives, slim):
     pieces, refs = refs[:2], refs[2:]
     weight_ref, out_ref, sum_ref, rim_ref, all_ref, stack, prod, edge = refs
-    size = all_ref.shape[0] // 2
-    for k, piece in enumerate(pieces):
-        all_ref[k * size : (k + 1) * size] = piece[...]
+    at, packed = 0, pieces[0].shape[1]
+    for piece in pieces:
+        all_ref[at : at + piece.shape[0]] = piece[...]
+        at += piece.shape[0]
+    for k in range(pack_ref.shape[0] // packed):
+        lanes = slice(k % KERNEL_WIDTH * LANES, (k % KERNEL_WIDTH + 1) * LANES)
+        all_ref[at + k // KERNEL_WIDTH, :, lanes] = pack_ref[k * packed : (k + 1) * packed, :]
     odd = lax.axis_index("seq") % 2
     height, width = far_ref.shape
     rim_ref[odd] = far_ref[...]
@@ -295,7 +315,7 @@
         sum_ref[d, 1:2, :] = two
 
 
-def upstream_kernel(cot_ref, rim_ref, one_ref, two_ref, up_ref, point_ref, stack, *, relatives):
+def upstream_kernel(cot_ref, one_ref, two_ref, up_ref, point_ref, pack_ref, stack, *, relatives):
     rows = cot_ref.shape[0]
     depth = stack.shape[1]
     own = lax.axis_index("seq")
@@ -305,17 +325,12 @@
         at = SUMS + (k % count) * up_to(depth, 16)
         stack[own ^ relative] = piece[at : at + depth, :].astype(stack.dtype)
     point_ref[...] = stack[...].reshape(point_ref.shape).astype(BF16)
-    for side, at in enumerate((0, EDGE + rows)):
-        up_ref[at : at + EDGE, :] = jnp.dot(
-            rim_ref[side, RIM:, :], point_ref[...], preferred_element_type=F32
-        )
-    up_ref[EDGE : EDGE + rows, :] = jnp.dot(
-        cot_ref[...], point_ref[...], preferred_element_type=F32
-    )
+    put_folded(point_ref[...], pack_ref)
+    up_ref[...] = jnp.dot(cot_ref[...], point_ref[...], preferred_element_type=F32)
 
 
 def mid_kernel(
-    got_ref, conv_ref, up_ref, norm_ref, point_ref, hid_ref, d_ref, cen_ref, sent_ref, vec_ref, both_ref, *, bin_count
+    got_ref, conv_ref, up_ref, rim_ref, norm_ref, point_ref, hid_ref, d_ref, cen_ref, sent_ref, vec_ref, *, bin_count
 ):
     rows = hid_ref.shape[0]
     slim = norm_ref.shape[1]
@@ -329,21 +344,23 @@
     vec_ref[1:3, :slim] = norm_ref[...]
     gain, bias = vec_ref[1:2, :], vec_ref[2:3, :]
 
-    def rows_of(begin, count):
+    def rows_of(begin, count, up):
         centered = (conv_ref[pl.ds(begin, count), :] - mean) * root
         hidden, slope = gelu_and_slope(centered * gain + bias)
-        d = up_ref[pl.ds(begin, count), :] * slope
+        d = up * slope
         cen_ref[pl.ds(begin, count), :] = centered
         d_ref[pl.ds(begin, count), :] = d
         return centered, hidden, d
 
-    rows_of(0, EDGE)
-    rows_of(EDGE + rows, EDGE)
+    for side, begin in enumerate((0, EDGE + rows)):
+        up = jnp.dot(rim_ref[side, RIM:, :], point_ref[...], preferred_element_type=F32)
+        rows_of(begin, EDGE, up)
     step = 64
 
     def body(i, carry):
         begin = pl.multiple_of(EDGE + i * step, 16)
-        centered, hidden, d = rows_of(begin, step)
+        up = up_ref[pl.ds(pl.multiple_of(i * step, 16), step), :]
+        centered, hidden, d = rows_of(begin, step, up)
         hid_ref[pl.ds(pl.multiple_of(i * step, 16), step), :] = hidden.astype(BF16)
         d = d.reshape(step // 8, 8, LANES)
         return carry[0] + (d * centered.reshape(d.shape)).sum(0), carry[1] + d.sum(0)
@@ -355,12 +372,6 @@
     for d in range(sent_ref.shape[0]):
         sent_ref[d, 0:1, :] = gain_sum
         sent_ref[d, 1:2, :] = bias_sum
-    if both_ref.shape[0] < rows + point_ref.shape[0]:
-        both = jnp.concatenate([hid_ref[...].astype(F32), point_ref[...].astype(F32)], axis=0)
-        both_ref[...] = fold_rows(both[:, : 3 * LANES // 4]).astype(BF16)
-    else:
-        both_ref[:rows, :] = hid_ref[...]
-        both_ref[rows:, :] = point_ref[...]
 
 
 def conv_back_kernel(got_ref, vec_ref, d_ref, cen_ref, grad_ref, total_ref, grad, *, bin_count, slim):
@@ -391,10 +402,10 @@
         else:
             at = side + 3 * (r - side)
             part = jnp.concatenate([piece[...] for piece in parts[at : at + 3]], axis=0)
-        if part.shape[0] < rows + point.shape[0]:
-            part = unfold_rows(part.astype(F32), 3 * LANES // 4).astype(BF16)
-        hidden[:, r * LANES : (r + 1) * LANES] = part[:rows, :]
-        point[:, r * LANES : (r + 1) * LANES] = part[rows:, :]
+        width = point.shape[0]
+        count = part.shape[0] * rows // (rows + width)
+        hidden[:, r * LANES : (r + 1) * LANES] = get_folded(part[:count, :], rows)
+        point[:, r * LANES : (r + 1) * LANES] = get_folded(part[count:, :], width)
     for at in range(0, x_ref.shape[1], 256):
         part = slice(at, at + 256)
         branch = lax.dot_general(
@@ -432,8 +443,12 @@
 
 
 def weight_grad_kernel(
-    mask_ref, part_ref, hid_ref, cot_ref, mid_ref, term_ref, kept_ref, sent_ref, grad, full, *, depth, slim
+    mask_ref, part_ref, hid_ref, cot_ref, mid_ref, point_ref, term_ref, kept_ref, sent_ref, pack_ref, both_ref, grad, full, *, depth, slim
 ):
+    put_folded(mid_ref[...], pack_ref)
+    both_ref[: pack_ref.shape[0], :] = pack_ref[...]
+    both_ref[pack_ref.shape[0] :, :] = point_ref[...]
+
     rows = term_ref.shape[0]
     terms_of(part_ref, grad, term_ref, 0, mask_ref)
     taps = lax.dot_general(
@@ -592,8 +607,32 @@
         out[...] = src[...]
 
 
-def slice_kernel(src_ref, out_ref, *, first):
-    out_ref[...] = src_ref[first : first + out_ref.shape[0], :]
+def packs(wanted, after):
+    arrays, places = [], []
+    for pieces in wanted:
+        places.append([])
+        for piece in pieces:
+            array, begin, end = piece if isinstance(piece, tuple) else (piece, 0, piece.shape[0])
+            places[-1].append((len(arrays), begin, end))
+            arrays.append(array)
+
+    def pack_kernel(*refs):
+        for out, group in zip(refs[len(arrays) :], places):
+            at = 0
+            for index, begin, end in group:
+                out[at : at + end - begin, :] = refs[index][begin:end, :]
+                at += end - begin
+
+    sizes = [sum(end - begin for _, begin, end in group) for group in places]
+    return call(pack_kernel, [((size, LANES), BF16) for size in sizes], arrays, after=after)
+
+
+def take_kernel(src_ref, weight_ref, pack_ref):
+    count, packed = weight_ref.shape[:2]
+    weight_ref[...] = src_ref[:count]
+    for k in range(pack_ref.shape[0] // packed):
+        lanes = slice(k % KERNEL_WIDTH * LANES, (k % KERNEL_WIDTH + 1) * LANES)
+        pack_ref[k * packed : (k + 1) * packed, :] = src_ref[count + k // KERNEL_WIDTH, :, lanes]
 
 
 def copies(arrays, after):
@@ -714,8 +753,15 @@
         [inputs, vec_in],
         after=[hidden_in],
     )
-
     stack_type = BF16 if depth % 16 == 0 else F32
+    upstream, point_own, point_pack = call(
+        functools.partial(upstream_kernel, relatives=relatives_of(point_order)),
+        [((rows, LANES), F32), ((width, LANES), BF16), ((folded_rows(width, slim), LANES), BF16)],
+        [cotangent, near, near_got],
+        scratch=[((seq_size, depth, LANES), stack_type)],
+        after=slopes,
+    )
+    blocks = -(-point_pack.shape[0] // (packed * KERNEL_WIDTH))
     conv_own, conv_out, sums_mid, rims, weight = call(
         functools.partial(
             conv_kernel, relatives=relatives_of(weight_order), slim=slim
@@ -725,27 +771,20 @@
             ((ext, LANES), F32),
             ((seq_size, 2, LANES), F32),
             ((2, *rim), BF16),
-            ((seq_size, packed, wide), BF16),
+            ((seq_size + blocks, packed, wide), BF16),
         ],
-        [ahead, hidden_in, near_rim, far, vec_in, weight, weight_got],
+        [ahead, hidden_in, near_rim, far, vec_in, point_pack, weight, weight_got],
         scratch=[
             ((seq_size, depth, wide), stack_type),
             ((rows + 2 * RIM, wide), F32),
             ((2 * RIM, width), BF16),
         ],
-        after=slopes,
+        after=[upstream],
     )
     weight = swap(weight, "ch", top)
     got_mid = spread(sums_mid, "seq")
-    upstream, point_own = call(
-        functools.partial(upstream_kernel, relatives=relatives_of(point_order)),
-        [((ext, LANES), F32), ((width, LANES), BF16)],
-        [cotangent, rims, near, near_got],
-        scratch=[((seq_size, depth, LANES), stack_type)],
-        after=[got_mid],
-    )
     conv_near = gather_parts(conv_own, lower)
-    hidden_mid, d_mid, centered, sent_back, vec_mid, both = call(
+    hidden_mid, d_mid, centered, sent_back, vec_mid = call(
         functools.partial(mid_kernel, bin_count=bin_count),
         [
             ((rows, LANES), BF16),
@@ -753,9 +792,8 @@
             ((ext, LANES), F32),
             ((seq_size, 2, LANES), F32),
             ((8, LANES), F32),
-            ((3 * (rows + width) // 4 if folds(rows + width, slim) else rows + width, LANES), BF16),
         ],
-        [got_mid, conv_out, upstream, norm_mid, point_own],
+        [got_mid, conv_out, upstream, rims, norm_mid, point_own],
         after=conv_near[1:],
     )
     got_back = spread(sent_back, "seq")
@@ -767,8 +805,12 @@
     )
     grad_near = gather_parts(grad_own, lower)
     grad_far = swap(grad_own, "ch", top)
-    both_parts = gather_parts(both, lower)
-    weight, both_far = copies([weight, swap(both, "ch", top)], [grad_own])
+    weight, point_far = call(
+        take_kernel,
+        [((seq_size, packed, wide), BF16), (point_pack.shape, BF16)],
+        [weight],
+        after=[grad_own],
+    )
     conv_far = [
         call(
             functools.partial(place_kernel, relatives=relatives_of(weight_order), slim=slim),
@@ -779,14 +821,17 @@
         for part in gather_parts(weight, lower)
     ]
     half = seq_size // 2
-    terms, kept, sent = call(
+    hidden_rows = folded_rows(rows, slim)
+    terms, kept, sent, hidden_pack, both = call(
         functools.partial(weight_grad_kernel, depth=depth, slim=slim),
         [
             ((rows, wide), BF16),
             ((half, depth, 4 * slim), F32),
             ((half, depth, 4 * slim), BF16),
+            ((hidden_rows, LANES), BF16),
+            ((hidden_rows + point_pack.shape[0], LANES), BF16),
         ],
-        [back, grad_own, hidden_in, cotangent, hidden_mid],
+        [back, grad_own, hidden_in, cotangent, hidden_mid, point_pack],
         scratch=[((ext, LANES), F32), ((width, 4 * slim), F32)],
     )
     side = ch_size // 2 * wide
@@ -803,15 +848,18 @@
         after=[up_part],
     )
     grad_far = gather_parts(copies([grad_far], slopes[1:])[0], lower)
+    both_parts = gather_parts(both, lower)
     d_in, sums_back = call(
         second_half_kernel,
         [((rows, width), F32), ((2, width), F32)],
         [back, inputs, *slopes, vec_in, up_part, *grad_far, *conv_far],
         scratch=[((rows, side), BF16), ((width, side), BF16), ((ext, LANES), F32)],
+        after=both_parts[1:],
     )
     total_back = sums_back
-    size = both_far.shape[0]
-    cuts = [0, up_to(63 * size // 100, 16), up_to(79 * size // 100, 16), size]
+    hidden_far = swap(hidden_pack, "ch", top)
+    count = point_far.shape[0]
+    cuts = [0, up_to(13 * count // 100, 16), up_to(52 * count // 100, 16), count]
     for k, reach in enumerate(sum_order):
         total_got = swap(total_back, "seq", last_order[k])
         got = swap(sent, "seq", reach)
@@ -824,16 +872,13 @@
                 after=[total_back] if k else [],
             )
             total_back = add(total_back, total_got)
-        for part in {rounds - 3: [0, 1], rounds - 2: [2]}.get(k, []):
-            begin, end = cuts[part : part + 2]
-            (far_part,) = call(
-                functools.partial(slice_kernel, first=begin),
-                [((end - begin, LANES), BF16)],
-                [both_far],
-                after=[total_back],
-            )
-            both_parts.append(gather_parts(far_part, lower))
-    both_parts = both_parts[:-3] + [part for group in zip(*both_parts[-3:]) for part in group]
+        if k == rounds - 3:
+            wanted = [[hidden_far, (point_far, *cuts[:2])], [(point_far, *cuts[1:3])]]
+            far_parts = [gather_parts(x, lower) for x in packs(wanted, [total_back])]
+        if k == rounds - 2:
+            (last,) = packs([[(point_far, *cuts[2:])]], [total_back])
+            far_parts.append(gather_parts(last, lower))
+    both_parts += [part for group in zip(*far_parts) for part in group]
     block_out, token = call(
         out_kernel,
         [((rows, width), BF16), ((8, LANES), F32)],

time: 80.2 us -> 79.4 us (0.990)
  starting transfers between devices: 21.3 us -> 19.6 us
  waiting for transfers between devices: 15 us -> 16 us
    ppermute x23, starting transfers between devices: 20.7 us -> 18.9 us  [swap(): return lax.ppermute(x, axis, flip(axis, reach))]
    ppermute x23, waiting for transfers between devices: 15 us -> 16 us  [swap(): return lax.ppermute(x, axis, flip(axis, reach))]
    pallas_call x27 -> x26, Pallas kernels: 21.7 us -> 21.7 us  [call(): pl.pallas_call(kernel, out_shape=[jax.ShapeDtypeStruct(s, t) for s, t in...]
where the time goes in v8:
time: 79.4 us; the launch traced here: 79.1 us
  Pallas kernels  21.7 us (27%)
  blocking collectives  20.8 us (26%)
  starting transfers between devices  19.6 us (25%)
  waiting for transfers between devices  16 us (20%)
  between operations  1.05 us (1%)
    pallas_call x26, Pallas kernels, call(): pl.pallas_call(kernel, out_shape=[jax.ShapeDtypeStruct(s, t) for s, t in...  21.7 us
    all_to_all x2, blocking collectives, spread(): return lax.all_to_all(copies, axes, 0, 0, tiled=True)  20.8 us
    ppermute x23, starting transfers between devices, swap(): return lax.ppermute(x, axis, flip(axis, reach))  18.9 us
    ppermute x23, waiting for transfers between devices, swap(): return lax.ppermute(x, axis, flip(axis, reach))  16 us
  transfers between devices with their start and end apart: 24, of which 10 were waited for; matrix products, arithmetic and copies ran while one was open for 0% of the time, Pallas kernels for 20%

profile of v8, /device:TPU:0, one launch (start us, length us, event | category | flops | bytes accessed | tf_op | source)
XLA Modules:
  0.0 79.1 jit_solution(17820397672442756702)
XLA Ops:
  0.7 1.7 %first_kernel.1 = (bf16[1024,768]{1,0:T(8,128)(2,1)S(1)}, bf16[1,72,384]{2,1,0:T(8,128)(2,1)S(1)}, bf16[144,128]{1,0:T(8,128)(2,1)S(1)}, bf16[48,768]{1,0:T(8,128)(2,1)S(1)}, bf16[48,768]{1,0:T(8,128)(2,1)S(1)}) custom-call(bf16[1024,768]{1,0:T(8,128)(2,1)} %refs_0_.2, bf16[1024,768]{1,0:T(8,128)(2,1)} %refs_1_.3, f32[3,96,96]{2,1,0:T(8,128)} %refs_12_.1, ...), custom_call_target="tpu_custom_call" | custom-call | flops 1 | bytes 1 | tf_op jit(solution)/shard_map/first_kernel/pallas_call | solution.py:48
  2.4 4.1 %collective-permute-start = (bf16[1,72,384]{2,1,0:T(8,128)(2,1)S(1)}, bf16[1,72,384]{2,1,0:T(8,128)(2,1)S(1)}, u32[]{:S(2)}, u32[]{:S(2)}) collective-permute-start(bf16[1,72,384]{2,1,0:T(8,128)(2,1)S(1)} %get-tuple-element.76.refs_0_), channel_id=1, source_target_pairs={{0,16},{4,20},{8,24},{12,28},{16,0},{20,4},{24,8},{28,12},{1,17},{... | collective-permute-start | bytes 165896 | tf_op jit(solution)/shard_map/ppermute | solution.py:651
  6.6 4.8 %collective-permute-done.1.refs_3_ = bf16[144,128]{1,0:T(8,128)(2,1)S(1)} collective-permute-done((bf16[144,128]{1,0:T(8,128)(2,1)S(1)}, bf16[144,128]{1,0:T(8,128)(2,1)S(1)}, u32[]{:S(2)}, u32[]{:S(2)}) %collective-permute-start.1) | collective-permute-done | bytes 36896 | tf_op jit(solution)/shard_map/ppermute | solution.py:651
  11.4 1.6 %collective-permute-start.3 = (bf16[528,128]{1,0:T(8,128)(2,1)S(1)}, bf16[528,128]{1,0:T(8,128)(2,1)S(1)}, u32[]{:S(2)}, u32[]{:S(2)}) collective-permute-start(bf16[528,128]{1,0:T(8,128)(2,1)S(1)} %get-tuple-element.79.refs_2_), channel_id=1, source_target_pairs={{0,4},{4,0},{8,12},{12,8},{16,20},{20,16},{24,28},{28,24},{1,5},{5... | collective-permute-start | bytes 405512 | tf_op jit(solution)/shard_map/ppermute | solution.py:651
  12.9 1.6 %collective-permute-start.2 = (bf16[2,72,384]{2,1,0:T(8,128)(2,1)S(1)}, bf16[2,72,384]{2,1,0:T(8,128)(2,1)S(1)}, u32[]{:S(2)}, u32[]{:S(2)}) collective-permute-start(bf16[2,72,384]{2,1,0:T(8,128)(2,1)S(1)} %get-tuple-element.82.refs_0_), channel_id=1, source_target_pairs={{0,8},{4,12},{8,0},{12,4},{16,24},{20,28},{24,16},{28,20},{1,9},{5... | collective-permute-start | bytes 331784 | tf_op jit(solution)/shard_map/ppermute | solution.py:651
  14.5 1.4 %mask_kernel.1 = (f32[3,1056,128]{2,1,0:T(8,128)S(1)}, f32[3,1024,128]{2,1,0:T(8,128)S(1)}, bf16[48,768]{1,0:T(8,128)(2,1)S(1)}) custom-call(s32[8]{0:T(128)S(1)} %copy-done.2, bf16[48,768]{1,0:T(8,128)(2,1)S(1)} %get-tuple-element.75.refs_1_, bf16[528,128]{1,0:T(8,128)(2,1)S(1)} %get-tuple-element.79.refs_2_), custom_call_target="tpu_custom_call" | custom-call | flops 1 | bytes 1 | tf_op jit(solution)/shard_map/mask_kernel/pallas_call | solution.py:48
  15.9 1.7 %collective-permute-done.2.refs_1_ = bf16[2,72,384]{2,1,0:T(8,128)(2,1)S(1)} collective-permute-done((bf16[2,72,384]{2,1,0:T(8,128)(2,1)S(1)}, bf16[2,72,384]{2,1,0:T(8,128)(2,1)S(1)}, u32[]{:S(2)}, u32[]{:S(2)}) %collective-permute-start.2) | collective-permute-done | bytes 110624 | tf_op jit(solution)/shard_map/ppermute | solution.py:651
  18.3 1.6 %collective-permute-start.4 = (bf16[432,128]{1,0:T(8,128)(2,1)S(1)}, bf16[432,128]{1,0:T(8,128)(2,1)S(1)}, u32[]{:S(2)}, u32[]{:S(2)}) collective-permute-start(bf16[432,128]{1,0:T(8,128)(2,1)S(1)} %get-tuple-element.83.refs_2_.refs_1_), channel_id=1, source_target_pairs={{0,8},{4,12},{8,0},{12,4},{16,24},{20,28},{24,16},{28,20},{1,9},{5... | collective-permute-start | bytes 331784 | tf_op jit(solution)/shard_map/ppermute | solution.py:651
  19.9 0.7 collective-permute-start.5
  20.6 3.1 %collective-permute-done.4.refs_3_.refs_2_ = bf16[432,128]{1,0:T(8,128)(2,1)S(1)} collective-permute-done((bf16[432,128]{1,0:T(8,128)(2,1)S(1)}, bf16[432,128]{1,0:T(8,128)(2,1)S(1)}, u32[]{:S(2)}, u32[]{:S(2)}) %collective-permute-start.4) | collective-permute-done | bytes 110624 | tf_op jit(solution)/shard_map/ppermute | solution.py:651
  23.7 1.5 %act_kernel.1 = (bf16[1024,768]{1,0:T(8,128)(2,1)S(1)}, f32[8,768]{1,0:T(8,128)S(1)}, bf16[1024,768]{1,0:T(8,128)(2,1)S(1)}) custom-call(bf16[1024,768]{1,0:T(8,128)(2,1)S(1)} %get-tuple-element.74.refs_0_.refs_1_, bf16[1024,768]{1,0:T(8,128)(2,1)} %refs_1_.3, bf16[432,128]{1,0:T(8,128)(2,1)S(1)} %get-tuple-element.83.refs_2_.refs_1_, ...), custom_call_target="tpu_custom_call" | custom-call | flops 1 | bytes 1 | tf_op jit(solution)/shard_map/act_kernel/pallas_call | solution.py:48
  25.2 1.1 %slope_kernel.2.refs_3_.refs_2_ = f32[512,768]{1,0:T(8,128)S(1)} custom-call(bf16[1024,768]{1,0:T(8,128)(2,1)S(1)} %get-tuple-element.74.refs_0_.refs_1_, f32[8,768]{1,0:T(8,128)S(1)} %get-tuple-element.86.refs_1_.refs_4_.refs_3_, bf16[1024,768]{1,0:T(8,128)(2,1)S(1)} %get-tuple-element.84.refs_2_.refs_1_), custom_call_target="tpu_custom_call" | custom-call | flops 1 | bytes 1 | tf_op jit(solution)/shard_map/slope_kernel/pallas_call | solution.py:48
  26.4 0.6 upstream_kernel.1
  27.0 1.4 %conv_kernel.1 = (bf16[768,384]{1,0:T(8,128)(2,1)S(1)}, f32[1056,128]{1,0:T(8,128)S(1)}, f32[8,2,128]{2,1,0:T(2,128)S(1)}, bf16[2,48,768]{2,1,0:T(8,128)(2,1)S(1)}, bf16[11,72,384]{2,1,0:T(8,128)(2,1)S(1)}) custom-call(f32[3,1056,128]{2,1,0:T(8,128)S(1)} %get-tuple-element.81.refs_0_, bf16[1024,768]{1,0:T(8,128)(2,1)S(1)} %get-tuple-element.84.refs_2_.refs_1_, ...), custom_call_target="tpu_custom_call" | custom-call | flops 1 | bytes 1 | tf_op jit(solution)/shard_map/conv_kernel/pallas_call | solution.py:48
  28.4 1.6 %collective-permute-start.10 = (bf16[11,72,384]{2,1,0:T(8,128)(2,1)S(1)}, bf16[11,72,384]{2,1,0:T(8,128)(2,1)S(1)}, u32[]{:S(2)}, u32[]{:S(2)}) collective-permute-start(bf16[11,72,384]{2,1,0:T(8,128)(2,1)S(1)} %get-tuple-element.104), channel_id=1, source_target_pairs={{0,2},{1,3},{2,0},{3,1},{4,6},{5,7},{6,4},{7,5},{8,10},{9,11},{10,... | collective-permute-start | bytes 1824776 | tf_op jit(solution)/shard_map/ppermute | solution.py:651
  30.0 11.9 %all_to_all.10.refs_0_ = f32[8,2,128]{2,1,0:T(2,128)S(1)} all-to-all(f32[8,2,128]{2,1,0:T(2,128)S(1)} %get-tuple-element.91), channel_id=1, replica_groups=mesh['seq'=8,'ch'=4] {'seq'}, dimensions={0} | all-to-all | bytes 16384 | tf_op jit(solution)/shard_map/all_to_all | solution.py:662
  41.9 0.7 mid_kernel.1
  42.6 8.9 %all_to_all.11.refs_0_ = f32[8,2,128]{2,1,0:T(2,128)S(1)} all-to-all(f32[8,2,128]{2,1,0:T(2,128)S(1)} %get-tuple-element.96), channel_id=1, replica_groups=mesh['seq'=8,'ch'=4] {'seq'}, dimensions={0} | all-to-all | bytes 16384 | tf_op jit(solution)/shard_map/all_to_all | solution.py:662
  52.9 2.0 %weight_grad_kernel.1 = (bf16[1024,384]{1,0:T(8,128)(2,1)S(1)}, f32[4,96,384]{2,1,0:T(8,128)S(1)}, bf16[4,96,384]{2,1,0:T(8,128)(2,1)S(1)}, bf16[768,128]{1,0:T(8,128)(2,1)S(1)}, bf16[1344,128]{1,0:T(8,128)(2,1)S(1)}) custom-call(f32[3,1024,128]{2,1,0:T(8,128)S(1)} %get-tuple-element.80.refs_4_.refs_0_, bf16[792,128]{1,0:T(8,128)(2,1)S(1)} %get-tuple-element.100.refs_1_, ...), custom_call_target="tpu_custom_call" | custom-call | flops 1 | bytes 1 | tf_op jit(solution)/shard_map/weight_grad_kernel/pallas_call | solution.py:48
  55.0 0.6 collective-permute-start.21
  55.6 1.5 %first_half_kernel.1.refs_2_.refs_5_ = f32[1024,768]{1,0:T(8,128)S(1)} custom-call(f32[3,1024,128]{2,1,0:T(8,128)S(1)} %get-tuple-element.80.refs_4_.refs_0_, bf16[1024,384]{1,0:T(8,128)(2,1)S(1)} %get-tuple-element.106.refs_1_, bf16[792,128]{1,0:T(8,128)(2,1)S(1)} %collective-permute-done.11.refs_2_, bf16[768,384]{1,0:T(8,128)(2,1)S(1)} %get-tuple-element.95.refs_3_, ...), custom_call_target="tpu_custom_call" | custom-call | flops 1 | bytes 1 | tf_op jit(solution)/shard_map/first_half_kernel/pallas_call | solution.py:48
  57.2 1.1 %slope_kernel.3.refs_1_.refs_3_ = f32[512,768]{1,0:T(8,128)S(1)} custom-call(bf16[1024,768]{1,0:T(8,128)(2,1)S(1)} %get-tuple-element.74.refs_0_.refs_1_, f32[8,768]{1,0:T(8,128)S(1)} %get-tuple-element.86.refs_1_.refs_4_.refs_3_, f32[1024,768]{1,0:T(8,128)S(1)} %first_half_kernel.1.refs_2_.refs_5_), custom_call_target="tpu_custom_call" | custom-call | flops 1 | bytes 1 | tf_op jit(solution)/shard_map/slope_kernel/pallas_call | solution.py:48
  58.3 1.1 %collective-permute-done.12.refs_0_ = bf16[792,128]{1,0:T(8,128)(2,1)S(1)} collective-permute-done((bf16[792,128]{1,0:T(8,128)(2,1)S(1)}, bf16[792,128]{1,0:T(8,128)(2,1)S(1)}, u32[]{:S(2)}, u32[]{:S(2)}) %collective-permute-start.12) | collective-permute-done | bytes 202784 | tf_op jit(solution)/shard_map/ppermute | solution.py:651
  60.9 2.1 %second_half_kernel.1 = (f32[1024,768]{1,0:T(8,128)S(1)}, f32[2,768]{1,0:T(2,128)S(1)}) custom-call(f32[3,1024,128]{2,1,0:T(8,128)S(1)} %get-tuple-element.80.refs_4_.refs_0_, bf16[1024,768]{1,0:T(8,128)(2,1)S(1)} %get-tuple-element.74.refs_0_.refs_1_, f32[512,768]{1,0:T(8,128)S(1)} %slope_kernel.2.refs_3_.refs_2_, ...), custom_call_target="tpu_custom_call" | custom-call | flops 1 | bytes 1 | tf_op jit(solution)/shard_map/second_half_kernel/pallas_call | solution.py:48
  63.1 0.6 collective-permute-start.15
  63.7 0.7 collective-permute-done.21.refs_1_
  65.1 2.7 %collective-permute-done.15.refs_1_ = f32[2,768]{1,0:T(2,128)S(1)} collective-permute-done((f32[2,768]{1,0:T(2,128)S(1)}, f32[2,768]{1,0:T(2,128)S(1)}, u32[]{:S(2)}, u32[]{:S(2)}) %collective-permute-start.15) | collective-permute-done | bytes 6176 | tf_op jit(solution)/shard_map/ppermute | solution.py:651
  67.9 1.3 %collective-permute-start.16 = (f32[2,768]{1,0:T(2,128)S(1)}, f32[2,768]{1,0:T(2,128)S(1)}, u32[]{:S(2)}, u32[]{:S(2)}) collective-permute-start(f32[2,768]{1,0:T(2,128)S(1)} %add_kernel.2.refs_3_.refs_0_.refs_2_), channel_id=1, source_target_pairs={{0,4},{4,0},{8,12},{12,8},{16,20},{20,16},{24,28},{28,24},{1,5},{5... | collective-permute-start | bytes 18440 | tf_op jit(solution)/shard_map/ppermute | solution.py:651
  69.2 0.9 %collective-permute-done.22.refs_1_ = bf16[2,96,384]{2,1,0:T(8,128)(2,1)S(1)} collective-permute-done((bf16[2,96,384]{2,1,0:T(8,128)(2,1)S(1)}, bf16[2,96,384]{2,1,0:T(8,128)(2,1)S(1)}, u32[]{:S(2)}, u32[]{:S(2)}) %collective-permute-start.22) | collective-permute-done | bytes 147488 | tf_op jit(solution)/shard_map/ppermute | solution.py:651
  70.1 1.8 %collective-permute-start.23 = (bf16[1,96,384]{2,1,0:T(8,128)(2,1)S(1)}, bf16[1,96,384]{2,1,0:T(8,128)(2,1)S(1)}, u32[]{:S(2)}, u32[]{:S(2)}) collective-permute-start(bf16[1,96,384]{2,1,0:T(8,128)(2,1)S(1)} %get-tuple-element.118), channel_id=1, source_target_pairs={{0,16},{4,20},{8,24},{12,28},{16,0},{20,4},{24,8},{28,12},{1,17},{... | collective-permute-start | bytes 221192 | tf_op jit(solution)/shard_map/ppermute | solution.py:651
  73.4 2.5 %out_kernel.1 = (bf16[1024,768]{1,0:T(8,128)(2,1)}, f32[8,128]{1,0:T(8,128)S(1)}) custom-call(bf16[1024,768]{1,0:T(8,128)(2,1)S(1)} %get-tuple-element.74.refs_0_.refs_1_, bf16[1344,128]{1,0:T(8,128)(2,1)S(1)} %get-tuple-element.102.refs_1_, bf16[1344,128]{1,0:T(8,128)(2,1)S(1)} %collective-permute-done.8.refs_10_.refs_2_, ...), custom_call_target="tpu_custom_call" | custom-call | flops 1 | bytes 1 | tf_op jit(solution)/shard_map/out_kernel/pallas_call | solution.py:48
  76.1 2.8 %final_kernel.1 = (f32[1024,768]{1,0:T(8,128)}, f32[2,768]{1,0:T(2,128)}, f32[2,768]{1,0:T(2,128)}, f32[2,768]{1,0:T(2,128)}, f32[3,96,96]{2,1,0:T(8,128)}, /*in...) custom-call(bf16[1024,768]{1,0:T(8,128)(2,1)S(1)} %get-tuple-element, ...), custom_call_target="tpu_custom_call" | custom-call | flops 1 | bytes 1 | tf_op jit(solution)/shard_map/final_kernel/pallas_call | solution.py:48
  (50 shorter events, 6.2 us)
Async XLA Ops:
  0.6 13.9 %copy-start.2 = (s32[8]{0:T(128)S(1)}, s32[8]{0:T(128)}, u32[]{:S(2)}) copy-start(s32[8]{0:T(128)} %refs_0_.3) | copy-start | bytes 100
  2.4 21.3 %copy-start = (f32[2,768]{1,0:T(2,128)S(1)}, f32[2,768]{1,0:T(2,128)}, u32[]{:S(2)}) copy-start(f32[2,768]{1,0:T(2,128)} %refs_9_.1) | copy-start | bytes 18436
  2.4 9.0 %collective-permute-start = (bf16[1,72,384]{2,1,0:T(8,128)(2,1)S(1)}, bf16[1,72,384]{2,1,0:T(8,128)(2,1)S(1)}, u32[]{:S(2)}, u32[]{:S(2)}) collective-permute-start(bf16[1,72,384]{2,1,0:T(8,128)(2,1)S(1)} %get-tuple-element.76.refs_0_), channel_id=1, source_target_pairs={{0,16},{4,20},{8,24},{12,28},{16,0},{20,4},{24,8},{28,12},{1,17},{... | collective-permute-start | bytes 165896 | tf_op jit(solution)/shard_map/ppermute | solution.py:651
  6.5 4.9 %collective-permute-start.1 = (bf16[144,128]{1,0:T(8,128)(2,1)S(1)}, bf16[144,128]{1,0:T(8,128)(2,1)S(1)}, u32[]{:S(2)}, u32[]{:S(2)}) collective-permute-start(bf16[144,128]{1,0:T(8,128)(2,1)S(1)} %get-tuple-element.77.refs_2_), channel_id=1, source_target_pairs={{0,16},{4,20},{8,24},{12,28},{16,0},{20,4},{24,8},{28,12},{1,17},{... | collective-permute-start | bytes 110600 | tf_op jit(solution)/shard_map/ppermute | solution.py:651
  11.4 6.3 %collective-permute-start.3 = (bf16[528,128]{1,0:T(8,128)(2,1)S(1)}, bf16[528,128]{1,0:T(8,128)(2,1)S(1)}, u32[]{:S(2)}, u32[]{:S(2)}) collective-permute-start(bf16[528,128]{1,0:T(8,128)(2,1)S(1)} %get-tuple-element.79.refs_2_), channel_id=1, source_target_pairs={{0,4},{4,0},{8,12},{12,8},{16,20},{20,16},{24,28},{28,24},{1,5},{5... | collective-permute-start | bytes 405512 | tf_op jit(solution)/shard_map/ppermute | solution.py:651
  12.9 4.7 %collective-permute-start.2 = (bf16[2,72,384]{2,1,0:T(8,128)(2,1)S(1)}, bf16[2,72,384]{2,1,0:T(8,128)(2,1)S(1)}, u32[]{:S(2)}, u32[]{:S(2)}) collective-permute-start(bf16[2,72,384]{2,1,0:T(8,128)(2,1)S(1)} %get-tuple-element.82.refs_0_), channel_id=1, source_target_pairs={{0,8},{4,12},{8,0},{12,4},{16,24},{20,28},{24,16},{28,20},{1,9},{5... | collective-permute-start | bytes 331784 | tf_op jit(solution)/shard_map/ppermute | solution.py:651
  17.7 9.3 %collective-permute-start.6 = (bf16[4,72,384]{2,1,0:T(8,128)(2,1)S(1)}, bf16[4,72,384]{2,1,0:T(8,128)(2,1)S(1)}, u32[]{:S(2)}, u32[]{:S(2)}) collective-permute-start(bf16[4,72,384]{2,1,0:T(8,128)(2,1)S(1)} %get-tuple-element.89.refs_6_), channel_id=1, source_target_pairs={{0,4},{4,0},{8,12},{12,8},{16,20},{20,16},{24,28},{28,24},{1,5},{5... | collective-permute-start | bytes 663560 | tf_op jit(solution)/shard_map/ppermute | solution.py:651
  18.3 5.4 %collective-permute-start.4 = (bf16[432,128]{1,0:T(8,128)(2,1)S(1)}, bf16[432,128]{1,0:T(8,128)(2,1)S(1)}, u32[]{:S(2)}, u32[]{:S(2)}) collective-permute-start(bf16[432,128]{1,0:T(8,128)(2,1)S(1)} %get-tuple-element.83.refs_2_.refs_1_), channel_id=1, source_target_pairs={{0,8},{4,12},{8,0},{12,4},{16,24},{20,28},{24,16},{28,20},{1,9},{5... | collective-permute-start | bytes 331784 | tf_op jit(solution)/shard_map/ppermute | solution.py:651
  19.9 7.1 %collective-permute-start.5 = (bf16[48,768]{1,0:T(8,128)(2,1)S(1)}, bf16[48,768]{1,0:T(8,128)(2,1)S(1)}, u32[]{:S(2)}, u32[]{:S(2)}) collective-permute-start(bf16[48,768]{1,0:T(8,128)(2,1)S(1)} %get-tuple-element.85), channel_id=1, source_target_pairs={{4,8},{12,16},{20,24},{8,4},{16,12},{24,20},{5,9},{13,17},{21,25},... | collective-permute-start | bytes 221192 | tf_op jit(solution)/shard_map/ppermute | solution.py:738
  27.0 14.9 %copy-start.1 = (f32[2,96]{1,0:T(2,128)S(1)}, f32[2,96]{1,0:T(2,128)}, u32[]{:S(2)}) copy-start(f32[2,96]{1,0:T(2,128)} %refs_18_.1) | copy-start | bytes 2308
  28.4 23.3 %collective-permute-start.10 = (bf16[11,72,384]{2,1,0:T(8,128)(2,1)S(1)}, bf16[11,72,384]{2,1,0:T(8,128)(2,1)S(1)}, u32[]{:S(2)}, u32[]{:S(2)}) collective-permute-start(bf16[11,72,384]{2,1,0:T(8,128)(2,1)S(1)} %get-tuple-element.104), channel_id=1, source_target_pairs={{0,2},{1,3},{2,0},{3,1},{4,6},{5,7},{6,4},{7,5},{8,10},{9,11},{10,... | collective-permute-start | bytes 1824776 | tf_op jit(solution)/shard_map/ppermute | solution.py:651
  30.0 11.9 %collective-permute-start.7 = (bf16[768,384]{1,0:T(8,128)(2,1)S(1)}, bf16[768,384]{1,0:T(8,128)(2,1)S(1)}, u32[]{:S(2)}, u32[]{:S(2)}) collective-permute-start(bf16[768,384]{1,0:T(8,128)(2,1)S(1)} %get-tuple-element.95.refs_3_), channel_id=1, source_target_pairs={{0,1},{1,0},{2,3},{3,2},{4,5},{5,4},{6,7},{7,6},{8,9},{9,8},{10,11... | collective-permute-start | bytes 1769480 | tf_op jit(solution)/shard_map/ppermute | solution.py:651
  51.8 8.6 %collective-permute-start.14 = (bf16[8,72,384]{2,1,0:T(8,128)(2,1)S(1)}, bf16[8,72,384]{2,1,0:T(8,128)(2,1)S(1)}, u32[]{:S(2)}, u32[]{:S(2)}) collective-permute-start(bf16[8,72,384]{2,1,0:T(8,128)(2,1)S(1)} %get-tuple-element.107.refs_0_), channel_id=1, source_target_pairs={{0,1},{1,0},{2,3},{3,2},{4,5},{5,4},{6,7},{7,6},{8,9},{9,8},{10,11... | collective-permute-start | bytes 1327112 | tf_op jit(solution)/shard_map/ppermute | solution.py:651
  51.9 3.7 %collective-permute-start.11 = (bf16[792,128]{1,0:T(8,128)(2,1)S(1)}, bf16[792,128]{1,0:T(8,128)(2,1)S(1)}, u32[]{:S(2)}, u32[]{:S(2)}) collective-permute-start(bf16[792,128]{1,0:T(8,128)(2,1)S(1)} %get-tuple-element.100.refs_1_), channel_id=1, source_target_pairs={{0,1},{1,0},{2,3},{3,2},{4,5},{5,4},{6,7},{7,6},{8,9},{9,8},{10,11... | collective-permute-start | bytes 608264 | tf_op jit(solution)/shard_map/ppermute | solution.py:651
  52.4 7.0 %collective-permute-start.12 = (bf16[792,128]{1,0:T(8,128)(2,1)S(1)}, bf16[792,128]{1,0:T(8,128)(2,1)S(1)}, u32[]{:S(2)}, u32[]{:S(2)}) collective-permute-start(bf16[792,128]{1,0:T(8,128)(2,1)S(1)} %get-tuple-element.100.refs_1_), channel_id=1, source_target_pairs={{0,2},{1,3},{2,0},{3,1},{4,6},{5,7},{6,4},{7,5},{8,10},{9,11},{10,... | collective-permute-start | bytes 608264 | tf_op jit(solution)/shard_map/ppermute | solution.py:651
  54.9 5.7 %collective-permute-start.8 = (bf16[1344,128]{1,0:T(8,128)(2,1)S(1)}, bf16[1344,128]{1,0:T(8,128)(2,1)S(1)}, u32[]{:S(2)}, u32[]{:S(2)}) collective-permute-start(bf16[1344,128]{1,0:T(8,128)(2,1)S(1)} %get-tuple-element.102.refs_1_), channel_id=1, source_target_pairs={{0,1},{1,0},{2,3},{3,2},{4,5},{5,4},{6,7},{7,6},{8,9},{9,8},{10,11... | collective-permute-start | bytes 1032200 | tf_op jit(solution)/shard_map/ppermute | solution.py:651
  55.0 9.4 %collective-permute-start.21 = (bf16[4,96,384]{2,1,0:T(8,128)(2,1)S(1)}, bf16[4,96,384]{2,1,0:T(8,128)(2,1)S(1)}, u32[]{:S(2)}, u32[]{:S(2)}) collective-permute-start(bf16[4,96,384]{2,1,0:T(8,128)(2,1)S(1)} %get-tuple-element.114), channel_id=1, source_target_pairs={{0,4},{4,0},{8,12},{12,8},{16,20},{20,16},{24,28},{28,24},{1,5},{5... | collective-permute-start | bytes 884744 | tf_op jit(solution)/shard_map/ppermute | solution.py:651
  59.4 1.5 %collective-permute-start.13 = (bf16[792,128]{1,0:T(8,128)(2,1)S(1)}, bf16[792,128]{1,0:T(8,128)(2,1)S(1)}, u32[]{:S(2)}, u32[]{:S(2)}) collective-permute-start(bf16[792,128]{1,0:T(8,128)(2,1)S(1)} %copy_kernel.1.refs_6_), channel_id=1, source_target_pairs={{0,1},{1,0},{2,3},{3,2},{4,5},{5,4},{6,7},{7,6},{8,9},{9,8},{10,11... | collective-permute-start | bytes 608264 | tf_op jit(solution)/shard_map/ppermute | solution.py:651
  59.5 8.3 %collective-permute-start.9 = (bf16[768,128]{1,0:T(8,128)(2,1)S(1)}, bf16[768,128]{1,0:T(8,128)(2,1)S(1)}, u32[]{:S(2)}, u32[]{:S(2)}) collective-permute-start(bf16[768,128]{1,0:T(8,128)(2,1)S(1)} %get-tuple-element.103), channel_id=1, source_target_pairs={{0,2},{1,3},{2,0},{3,1},{4,6},{5,7},{6,4},{7,5},{8,10},{9,11},{10,... | collective-permute-start | bytes 589832 | tf_op jit(solution)/shard_map/ppermute | solution.py:651
  63.1 4.7 %collective-permute-start.15 = (f32[2,768]{1,0:T(2,128)S(1)}, f32[2,768]{1,0:T(2,128)S(1)}, u32[]{:S(2)}, u32[]{:S(2)}) collective-permute-start(f32[2,768]{1,0:T(2,128)S(1)} %get-tuple-element.108.refs_0_), channel_id=1, source_target_pairs={{0,16},{4,20},{8,24},{12,28},{16,0},{20,4},{24,8},{28,12},{1,17},{... | collective-permute-start | bytes 18440 | tf_op jit(solution)/shard_map/ppermute | solution.py:651
  64.5 5.6 %collective-permute-start.22 = (bf16[2,96,384]{2,1,0:T(8,128)(2,1)S(1)}, bf16[2,96,384]{2,1,0:T(8,128)(2,1)S(1)}, u32[]{:S(2)}, u32[]{:S(2)}) collective-permute-start(bf16[2,96,384]{2,1,0:T(8,128)(2,1)S(1)} %get-tuple-element.116), channel_id=1, source_target_pairs={{0,8},{4,12},{8,0},{12,4},{16,24},{20,28},{24,16},{28,20},{1,9},{5... | collective-permute-start | bytes 442376 | tf_op jit(solution)/shard_map/ppermute | solution.py:651
  67.8 5.6 %collective-permute-start.17 = (bf16[848,128]{1,0:T(8,128)(2,1)S(1)}, bf16[848,128]{1,0:T(8,128)(2,1)S(1)}, u32[]{:S(2)}, u32[]{:S(2)}) collective-permute-start(bf16[848,128]{1,0:T(8,128)(2,1)S(1)} %get-tuple-element.109.refs_3_), channel_id=1, source_target_pairs={{0,1},{1,0},{2,3},{3,2},{4,5},{5,4},{6,7},{7,6},{8,9},{9,8},{10,11... | collective-permute-start | bytes 651272 | tf_op jit(solution)/shard_map/ppermute | solution.py:651
  67.9 4.0 %collective-permute-start.16 = (f32[2,768]{1,0:T(2,128)S(1)}, f32[2,768]{1,0:T(2,128)S(1)}, u32[]{:S(2)}, u32[]{:S(2)}) collective-permute-start(f32[2,768]{1,0:T(2,128)S(1)} %add_kernel.2.refs_3_.refs_0_.refs_2_), channel_id=1, source_target_pairs={{0,4},{4,0},{8,12},{12,8},{16,20},{20,16},{24,28},{28,24},{1,5},{5... | collective-permute-start | bytes 18440 | tf_op jit(solution)/shard_map/ppermute | solution.py:651
  70.1 6.0 %collective-permute-start.23 = (bf16[1,96,384]{2,1,0:T(8,128)(2,1)S(1)}, bf16[1,96,384]{2,1,0:T(8,128)(2,1)S(1)}, u32[]{:S(2)}, u32[]{:S(2)}) collective-permute-start(bf16[1,96,384]{2,1,0:T(8,128)(2,1)S(1)} %get-tuple-element.118), channel_id=1, source_target_pairs={{0,16},{4,20},{8,24},{12,28},{16,0},{20,4},{24,8},{28,12},{1,17},{... | collective-permute-start | bytes 221192 | tf_op jit(solution)/shard_map/ppermute | solution.py:651
  71.9 1.5 %collective-permute-start.19 = (bf16[272,128]{1,0:T(8,128)(2,1)S(1)}, bf16[272,128]{1,0:T(8,128)(2,1)S(1)}, u32[]{:S(2)}, u32[]{:S(2)}) collective-permute-start(bf16[272,128]{1,0:T(8,128)(2,1)S(1)} %pack_kernel.3.refs_5_), channel_id=1, source_target_pairs={{0,1},{1,0},{2,3},{3,2},{4,5},{5,4},{6,7},{7,6},{8,9},{9,8},{10,11... | collective-permute-start | bytes 208904 | tf_op jit(solution)/shard_map/ppermute | solution.py:651
  72.0 1.4 %collective-permute-start.18 = (bf16[224,128]{1,0:T(8,128)(2,1)S(1)}, bf16[224,128]{1,0:T(8,128)(2,1)S(1)}, u32[]{:S(2)}, u32[]{:S(2)}) collective-permute-start(bf16[224,128]{1,0:T(8,128)(2,1)S(1)} %get-tuple-element.110.refs_4_), channel_id=1, source_target_pairs={{0,1},{1,0},{2,3},{3,2},{4,5},{5,4},{6,7},{7,6},{8,9},{9,8},{10,11... | collective-permute-start | bytes 172040 | tf_op jit(solution)/shard_map/ppermute | solution.py:651
  72.5 3.6 %collective-permute-start.20 = (f32[2,768]{1,0:T(2,128)S(1)}, f32[2,768]{1,0:T(2,128)S(1)}, u32[]{:S(2)}, u32[]{:S(2)}) collective-permute-start(f32[2,768]{1,0:T(2,128)S(1)} %add_kernel.3.refs_1_.refs_9_.refs_4_), channel_id=1, source_target_pairs={{0,8},{4,12},{8,0},{12,4},{16,24},{20,28},{24,16},{28,20},{1,9},{5... | collective-permute-start | bytes 18440 | tf_op jit(solution)/shard_map/ppermute | solution.py:651

commit v9 on v8

--- a/solution.py
+++ b/solution.py
@@ -173,9 +173,14 @@
     copies[2].wait()
     copies[3].wait()
     odd = lax.axis_index("seq") % 2
+    lanes = half_of(width, lax.axis_index("ch") % 2)
     for ref, side in ((near_rim, 1 - odd), (far_rim, odd)):
-        ref[:RIM, :] = x_ref[pl.ds(pl.multiple_of(side * (rows - RIM), RIM), RIM), :]
-        ref[RIM:, :] = edge_ref[side]
+        ref[:RIM, :] = x_ref[pl.ds(pl.multiple_of(side * (rows - RIM), RIM), RIM), lanes]
+        ref[RIM:, :] = edge_ref[side, :, lanes]
+
+
+def half_of(width, core):
+    return pl.ds(pl.multiple_of(core * (width // 2), LANES), width // 2)
 
 
 def put_sums(ref, value):
@@ -188,7 +193,7 @@
 
 
 def act_kernel(
-    x_ref, cot_hbm, one_ref, two_ref, norm_ref, hid_ref, vec_ref, cot_ref, sems, *, bin_count
+    x_ref, cot_hbm, one_ref, two_ref, norm_ref, hid_ref, slope_ref, vec_ref, cot_ref, sems, *, bin_count
 ):
     copy = pltpu.make_async_copy(cot_hbm, cot_ref, sems.at[0])
     copy.start()
@@ -209,7 +214,9 @@
     def step(k, carry):
         at = pl.multiple_of(k * 16, 16)
         v = x_ref[pl.ds(at, 16), :].astype(F32) * vec_ref[2:3, :] + vec_ref[3:4, :]
-        hid_ref[pl.ds(at, 16), :] = gelu_and_slope(v)[0].astype(BF16)
+        hidden, slope = gelu_and_slope(v)
+        hid_ref[pl.ds(at, 16), :] = hidden.astype(BF16)
+        slope_ref[pl.ds(at, 16), :] = slope
         return carry
 
     lax.fori_loop(0, rows // 16, step, 0, unroll=2)
@@ -233,7 +240,20 @@
 
 def place_kernel(*refs, relatives, slim):
     pieces, (out_ref, stack) = refs[:-2], refs[-2:]
-    out_ref[...] = place(pieces, relatives, stack, lax.axis_index("seq"), slim)
+    wide = stack.shape[2]
+    for r, piece in enumerate(pieces):
+        block = place([piece], relatives, stack, lax.axis_index("seq"), slim)
+        out_ref[:, r * wide : (r + 1) * wide] = block
+
+
+def rim_kernel(near_ref, far_ref, out_ref):
+    height, width = far_ref.shape
+    base = near_ref.shape[0] - width // LANES * height
+    for k in range(width // LANES):
+        at = base + k * height
+        out_ref[:height, k * LANES : (k + 1) * LANES] = near_ref[at : at + height, :]
+    out_ref[height : 2 * height, :] = far_ref[...]
+    out_ref[2 * height :, :] = jnp.zeros_like(out_ref[2 * height :, :])
 
 
 def mask_kernel(start_ref, rim_ref, ahead_ref, back_ref, far_ref):
@@ -251,18 +271,8 @@
             ]
 
 
-def slope_kernel(x_ref, vec_ref, slope_ref, *, first):
-    def step(k, carry):
-        at = pl.multiple_of(k * 16, 16)
-        v = x_ref[pl.ds(first + at, 16), :].astype(F32) * vec_ref[2:3, :] + vec_ref[3:4, :]
-        slope_ref[pl.ds(at, 16), :] = gelu_and_slope(v)[1]
-        return carry
-
-    lax.fori_loop(0, slope_ref.shape[0] // 16, step, 0, unroll=2)
-
-
-def conv_kernel(mask_ref, hid_ref, near_ref, far_ref, vec_ref, pack_ref, *refs, relatives, slim):
-    pieces, refs = refs[:2], refs[2:]
+def conv_kernel(mask_ref, hid_ref, own_rims, other_rims, vec_ref, pack_ref, *refs, relatives, slim):
+    pieces, refs = refs[:-8], refs[-8:]
     weight_ref, out_ref, sum_ref, rim_ref, all_ref, stack, prod, edge = refs
     at, packed = 0, pieces[0].shape[1]
     for piece in pieces:
@@ -271,13 +281,11 @@
     for k in range(pack_ref.shape[0] // packed):
         lanes = slice(k % KERNEL_WIDTH * LANES, (k % KERNEL_WIDTH + 1) * LANES)
         all_ref[at + k // KERNEL_WIDTH, :, lanes] = pack_ref[k * packed : (k + 1) * packed, :]
-    odd = lax.axis_index("seq") % 2
-    height, width = far_ref.shape
-    rim_ref[odd] = far_ref[...]
-    base = near_ref.shape[0] - width // LANES * height
-    for k in range(width // LANES):
-        at = base + k * height
-        rim_ref[1 - odd, :, k * LANES : (k + 1) * LANES] = near_ref[at : at + height, :]
+    odd, core = lax.axis_index("seq") % 2, lax.axis_index("ch") % 2
+    height, width = rim_ref.shape[1:]
+    for half, owner in ((own_rims, core), (other_rims, 1 - core)):
+        rim_ref[1 - odd, :, half_of(width, owner)] = half[:height, :]
+        rim_ref[odd, :, half_of(width, owner)] = half[height : 2 * height, :]
     for side in range(2):
         for k in range(0, RIM, 16):
             v = rim_ref[side, k : k + 16, :].astype(F32) * vec_ref[2:3, :] + vec_ref[3:4, :]
@@ -495,21 +503,16 @@
         )
 
 
-def second_half_kernel(mask_ref, x_ref, slope_one, slope_two, vec_ref, part_ref, *refs):
-    d_ref, sum_ref, term, weight, grad = refs[-5:]
-    count = (len(refs) - 5) // 2
-    grads, weights = refs[:count], refs[count:-5]
+def second_half_kernel(mask_ref, x_ref, slope_ref, vec_ref, part_ref, weight_ref, *refs):
+    grads, (d_ref, sum_ref, term, grad) = refs[:-4], refs[-4:]
     rows, width = x_ref.shape
     wide = KERNEL_WIDTH * LANES
-    for r in range(count):
-        terms_of(grads[r], grad, term, r * wide, mask_ref)
-    for r, piece in enumerate(weights):
-        weight[:, r * wide : (r + 1) * wide] = piece[...]
+    for r, part in enumerate(grads):
+        terms_of(part, grad, term, r * wide, mask_ref)
     for at in range(0, width, 256):
         part = slice(at, at + 256)
-        up = lax.dot_general(term[...], weight[part, :], LANE_DIMS, preferred_element_type=F32)
-        slope = jnp.concatenate([slope_one[:, part], slope_two[:, part]], axis=0)
-        d = (up + part_ref[:, part]) * slope
+        up = lax.dot_general(term[...], weight_ref[part, :], LANE_DIMS, preferred_element_type=F32)
+        d = (up + part_ref[:, part]) * slope_ref[:, part]
         d_ref[:, part] = d
         centered = x_ref[:, part].astype(F32) * vec_ref[0:1, part] + vec_ref[1:2, part]
         sum_ref[0:1, part] = jnp.sum(d * centered, 0, keepdims=True)
@@ -584,21 +587,21 @@
     return [size >> k for k in range(1, size.bit_length())]
 
 
-def round_kernel(weight_one, weight_two, one_ref, two_ref, *refs):
-    weight_ref, out_ref = refs[-2:]
-    size = weight_one.shape[0]
-    weight_ref[:size] = weight_one[...]
-    weight_ref[size:] = weight_two[...]
+def round_kernel(weight_one, weight_two, one_ref, two_ref, *refs, size, sides):
+    rims, (weight_ref, out_ref), halves = refs[: len(refs) - 2 - sides], refs[-2 - sides :][:2], refs[len(refs) - sides :]
+    count = weight_one.shape[0]
+    weight_ref[:count] = weight_one[...]
+    weight_ref[count:] = weight_two[...]
+    for half, src in zip(halves, (weight_one, weight_two)):
+        half[...] = src[...]
     put_sums(out_ref, get_sums(one_ref) + get_sums(two_ref))
-    rim = out_ref.shape[0] - one_ref.shape[0] * 2 + SUMS if len(refs) > 2 else 0
-    size = (out_ref.shape[0] - SUMS - rim) // 2
     out_ref[SUMS : SUMS + size, :] = one_ref[SUMS : SUMS + size, :]
     out_ref[SUMS + size : SUMS + 2 * size, :] = two_ref[SUMS : SUMS + size, :]
-    if rim:
-        height, width = refs[0].shape
+    for rim in rims:
+        height, width = rim.shape
         for k in range(width // LANES):
             at = SUMS + 2 * size + k * height
-            out_ref[at : at + height, :] = refs[0][:, k * LANES : (k + 1) * LANES]
+            out_ref[at : at + height, :] = rim[:, k * LANES : (k + 1) * LANES]
 
 
 def copy_kernel(*refs):
@@ -695,7 +698,7 @@
     rounds = len(weight_order)
     top, lower = ch_order[0], ch_order[1:]
     chunks = 4
-    rim = (RIM + EDGE, width)
+    rim = (RIM + EDGE, width // 2)
     packed = 3 * depth // 4 if folds(depth, slim) else depth
     inputs, weight, near, *rims = call(
         first_kernel,
@@ -717,17 +720,20 @@
         sems=4 + chunks,
     )
     pairs = [(i, i + 1) for i in range(1, seq_size - 1, 2)]
+    parts = [weight]
     for k in range(rounds):
-        weight_got = swap(weight, "seq", weight_order[k])
+        weight_got = [swap(part, "seq", weight_order[k]) for part in parts]
         near_got = swap(near, "seq", point_order[k])
         if k < rounds - 1:
-            outs = [
-                ((2 * weight.shape[0], packed, wide), BF16),
-                ((SUMS + (2 << k) * up_to(depth, 16) + (tiles * rim[0] if k == 0 else 0), LANES), BF16),
-            ]
-            args = [weight, weight_got, near, near_got]
+            size = up_to(depth, 16) << k
+            spare = {0: tiles // 2 * rim[0], rounds - 2: 16}.get(k, 0)
+            outs = [((2 * weight.shape[0], packed, wide), BF16), ((SUMS + 2 * size + spare, LANES), BF16)]
+            sides = 2 if k == rounds - 2 else 0
+            outs += [(weight.shape, BF16)] * sides
+            join = functools.partial(round_kernel, size=size, sides=sides)
+            args = [weight, weight_got[0], near, near_got]
             if k == 0:
-                weight, near = call(round_kernel, outs, args + [rims[0]])
+                weight, near = call(join, outs, args + [rims[0]])
                 ahead, back, far = call(
                     mask_kernel,
                     [((KERNEL_WIDTH, ext, LANES), F32), ((KERNEL_WIDTH, rows, LANES), F32), (rim, BF16)],
@@ -736,22 +742,21 @@
                     after=[near],
                 )
                 far = lax.ppermute(far, "seq", pairs + [(j, i) for i, j in pairs])
+                parts = [weight]
             else:
                 if k == 1:
-                    near_rim = near_got
-                weight, near = call(round_kernel, outs, args, after=[back] if k == 1 else [])
-    hidden_in, vec_in, cotangent = call(
+                    (rims,) = call(
+                        rim_kernel, [((2 * rim[0] + 16, rim[1]), BF16)], [near_got, far], after=[back]
+                    )
+                    other_rims = swap(rims, "ch", 1)
+                weight, near, *parts = call(join, outs, args, after=[back] if k == 1 else [])
+                parts = parts or [weight]
+    hidden_in, slope_in, vec_in, cotangent = call(
         functools.partial(act_kernel, bin_count=bin_count),
-        [((rows, width), BF16), ((8, width), F32), (cotangent.shape, BF16)],
+        [((rows, width), BF16), ((rows, width), F32), ((8, width), F32), (cotangent.shape, BF16)],
         [inputs, cotangent, near, near_got, norm_in],
         away=(1,),
         sems=1,
-    )
-    slopes = call(
-        functools.partial(slope_kernel, first=0),
-        [((rows // 2, width), F32)],
-        [inputs, vec_in],
-        after=[hidden_in],
     )
     stack_type = BF16 if depth % 16 == 0 else F32
     upstream, point_own, point_pack = call(
@@ -759,7 +764,6 @@
         [((rows, LANES), F32), ((width, LANES), BF16), ((folded_rows(width, slim), LANES), BF16)],
         [cotangent, near, near_got],
         scratch=[((seq_size, depth, LANES), stack_type)],
-        after=slopes,
     )
     blocks = -(-point_pack.shape[0] // (packed * KERNEL_WIDTH))
     conv_own, conv_out, sums_mid, rims, weight = call(
@@ -770,10 +774,10 @@
             ((width, wide), BF16),
             ((ext, LANES), F32),
             ((seq_size, 2, LANES), F32),
-            ((2, *rim), BF16),
+            ((2, RIM + EDGE, width), BF16),
             ((seq_size + blocks, packed, wide), BF16),
         ],
-        [ahead, hidden_in, near_rim, far, vec_in, point_pack, weight, weight_got],
+        [ahead, hidden_in, rims, other_rims, vec_in, point_pack, weight, *weight_got],
         scratch=[
             ((seq_size, depth, wide), stack_type),
             ((rows + 2 * RIM, wide), F32),
@@ -811,15 +815,13 @@
         [weight],
         after=[grad_own],
     )
-    conv_far = [
-        call(
-            functools.partial(place_kernel, relatives=relatives_of(weight_order), slim=slim),
-            [((width, wide), BF16)],
-            [part],
-            scratch=[((seq_size, depth, wide), stack_type)],
-        )[0]
-        for part in gather_parts(weight, lower)
-    ]
+    side = ch_size // 2 * wide
+    (conv_far,) = call(
+        functools.partial(place_kernel, relatives=relatives_of(weight_order), slim=slim),
+        [((width, side), BF16)],
+        gather_parts(weight, lower),
+        scratch=[((seq_size, depth, wide), stack_type)],
+    )
     half = seq_size // 2
     hidden_rows = folded_rows(rows, slim)
     terms, kept, sent, hidden_pack, both = call(
@@ -834,26 +836,19 @@
         [back, grad_own, hidden_in, cotangent, hidden_mid, point_pack],
         scratch=[((ext, LANES), F32), ((width, 4 * slim), F32)],
     )
-    side = ch_size // 2 * wide
     (up_part,) = call(
         first_half_kernel,
         [((rows, width), F32)],
         [back, terms, *grad_near[1:], *conv_near],
         scratch=[((rows, side), BF16), ((width, side), BF16), ((ext, LANES), F32)],
     )
-    slopes += call(
-        functools.partial(slope_kernel, first=rows // 2),
-        [((rows // 2, width), F32)],
-        [inputs, vec_in],
-        after=[up_part],
-    )
-    grad_far = gather_parts(copies([grad_far], slopes[1:])[0], lower)
+    grad_far = gather_parts(copies([grad_far], [up_part, conv_far])[0], lower)
     both_parts = gather_parts(both, lower)
     d_in, sums_back = call(
         second_half_kernel,
         [((rows, width), F32), ((2, width), F32)],
-        [back, inputs, *slopes, vec_in, up_part, *grad_far, *conv_far],
-        scratch=[((rows, side), BF16), ((width, side), BF16), ((ext, LANES), F32)],
+        [back, inputs, slope_in, vec_in, up_part, conv_far, *grad_far],
+        scratch=[((rows, side), BF16), ((ext, LANES), F32)],
         after=both_parts[1:],
     )
     total_back = sums_back

time: 79.4 us -> 77.6 us (0.977)
  blocking collectives: 20.8 us -> 18.9 us
  starting transfers between devices: 19.6 us -> 21.4 us
  Pallas kernels: 21.7 us -> 20.2 us
    all_to_all x2, blocking collectives: 20.8 us -> 18.9 us  [spread(): return lax.all_to_all(copies, axes, 0, 0, tiled=True)]
    ppermute x23 -> x25, starting transfers between devices: 18.9 us -> 20.7 us  [swap(): return lax.ppermute(x, axis, flip(axis, reach))]
    pallas_call x26 -> x24, Pallas kernels: 21.7 us -> 20.2 us  [call(): pl.pallas_call(kernel, out_shape=[jax.ShapeDtypeStruct(s, t) for s, t in...]
    ppermute x23 -> x25, waiting for transfers between devices: 16 us -> 15.8 us  [swap(): return lax.ppermute(x, axis, flip(axis, reach))]
  transfers between devices with their start and end apart: 24 -> 26, of which waited for: 10 -> 11; matrix products, arithmetic and copies ran while one was open for 0% -> 0% of each run, Pallas kernels for 20% -> 18%
where the time goes in v9:
time: 77.6 us; the launch traced here: 77.4 us
  starting transfers between devices  21.4 us (28%)
  Pallas kernels  20.2 us (26%)
  blocking collectives  18.9 us (24%)
  waiting for transfers between devices  15.8 us (20%)
  between operations  1.03 us (1%)
    ppermute x25, starting transfers between devices, swap(): return lax.ppermute(x, axis, flip(axis, reach))  20.7 us
    pallas_call x24, Pallas kernels, call(): pl.pallas_call(kernel, out_shape=[jax.ShapeDtypeStruct(s, t) for s, t in...  20.2 us
    all_to_all x2, blocking collectives, spread(): return lax.all_to_all(copies, axes, 0, 0, tiled=True)  18.9 us
    ppermute x25, waiting for transfers between devices, swap(): return lax.ppermute(x, axis, flip(axis, reach))  15.8 us
  transfers between devices with their start and end apart: 26, of which 11 were waited for; matrix products, arithmetic and copies ran while one was open for 0% of the time, Pallas kernels for 18%

profile of v9, /device:TPU:0, one launch (start us, length us, event | category | flops | bytes accessed | tf_op | source)
XLA Modules:
  0.0 77.4 jit_solution(15268256969519586947)
XLA Ops:
  0.7 1.7 %first_kernel.1 = (bf16[1024,768]{1,0:T(8,128)(2,1)S(1)}, bf16[1,72,384]{2,1,0:T(8,128)(2,1)S(1)}, bf16[144,128]{1,0:T(8,128)(2,1)S(1)}, bf16[48,384]{1,0:T(8,128)(2,1)S(1)}, bf16[48,384]{1,0:T(8,128)(2,1)S(1)}) custom-call(bf16[1024,768]{1,0:T(8,128)(2,1)} %refs_0_.2, bf16[1024,768]{1,0:T(8,128)(2,1)} %refs_1_.3, f32[3,96,96]{2,1,0:T(8,128)} %refs_12_.1, ...), custom_call_target="tpu_custom_call" | custom-call | flops 1 | bytes 1 | tf_op jit(solution)/shard_map/first_kernel/pallas_call | solution.py:48
  2.4 4.1 %collective-permute-start = (bf16[1,72,384]{2,1,0:T(8,128)(2,1)S(1)}, bf16[1,72,384]{2,1,0:T(8,128)(2,1)S(1)}, u32[]{:S(2)}, u32[]{:S(2)}) collective-permute-start(bf16[1,72,384]{2,1,0:T(8,128)(2,1)S(1)} %get-tuple-element.79.refs_0_), channel_id=1, source_target_pairs={{0,16},{4,20},{8,24},{12,28},{16,0},{20,4},{24,8},{28,12},{1,17},{... | collective-permute-start | bytes 165896 | tf_op jit(solution)/shard_map/ppermute | solution.py:654
  6.5 4.8 %collective-permute-done.1.refs_3_ = bf16[144,128]{1,0:T(8,128)(2,1)S(1)} collective-permute-done((bf16[144,128]{1,0:T(8,128)(2,1)S(1)}, bf16[144,128]{1,0:T(8,128)(2,1)S(1)}, u32[]{:S(2)}, u32[]{:S(2)}) %collective-permute-start.1) | collective-permute-done | bytes 36896 | tf_op jit(solution)/shard_map/ppermute | solution.py:654
  11.4 1.6 %collective-permute-start.2 = (bf16[2,72,384]{2,1,0:T(8,128)(2,1)S(1)}, bf16[2,72,384]{2,1,0:T(8,128)(2,1)S(1)}, u32[]{:S(2)}, u32[]{:S(2)}) collective-permute-start(bf16[2,72,384]{2,1,0:T(8,128)(2,1)S(1)} %get-tuple-element.85.refs_0_), channel_id=1, source_target_pairs={{0,8},{4,12},{8,0},{12,4},{16,24},{20,28},{24,16},{28,20},{1,9},{5... | collective-permute-start | bytes 331784 | tf_op jit(solution)/shard_map/ppermute | solution.py:654
  13.0 1.5 %collective-permute-start.3 = (bf16[384,128]{1,0:T(8,128)(2,1)S(1)}, bf16[384,128]{1,0:T(8,128)(2,1)S(1)}, u32[]{:S(2)}, u32[]{:S(2)}) collective-permute-start(bf16[384,128]{1,0:T(8,128)(2,1)S(1)} %get-tuple-element.82.refs_2_), channel_id=1, source_target_pairs={{0,4},{4,0},{8,12},{12,8},{16,20},{20,16},{24,28},{28,24},{1,5},{5... | collective-permute-start | bytes 294920 | tf_op jit(solution)/shard_map/ppermute | solution.py:654
  14.5 1.4 %mask_kernel.1 = (f32[3,1056,128]{2,1,0:T(8,128)S(1)}, f32[3,1024,128]{2,1,0:T(8,128)S(1)}, bf16[48,384]{1,0:T(8,128)(2,1)S(1)}) custom-call(s32[8]{0:T(128)S(1)} %copy-done.2, bf16[48,384]{1,0:T(8,128)(2,1)S(1)} %get-tuple-element.78.refs_1_, bf16[384,128]{1,0:T(8,128)(2,1)S(1)} %get-tuple-element.82.refs_2_), custom_call_target="tpu_custom_call" | custom-call | flops 1 | bytes 1 | tf_op jit(solution)/shard_map/mask_kernel/pallas_call | solution.py:48
  15.9 0.7 collective-permute-start.5
  16.6 1.0 %collective-permute-done.3.refs_3_.refs_0_ = bf16[384,128]{1,0:T(8,128)(2,1)S(1)} collective-permute-done((bf16[384,128]{1,0:T(8,128)(2,1)S(1)}, bf16[384,128]{1,0:T(8,128)(2,1)S(1)}, u32[]{:S(2)}, u32[]{:S(2)}) %collective-permute-start.3) | collective-permute-done | bytes 98336 | tf_op jit(solution)/shard_map/ppermute | solution.py:654
  17.7 2.3 %collective-permute-start.4 = (bf16[448,128]{1,0:T(8,128)(2,1)S(1)}, bf16[448,128]{1,0:T(8,128)(2,1)S(1)}, u32[]{:S(2)}, u32[]{:S(2)}) collective-permute-start(bf16[448,128]{1,0:T(8,128)(2,1)S(1)} %get-tuple-element.86.refs_2_.refs_1_), channel_id=1, source_target_pairs={{0,8},{4,12},{8,0},{12,4},{16,24},{20,28},{24,16},{28,20},{1,9},{5... | collective-permute-start | bytes 344072 | tf_op jit(solution)/shard_map/ppermute | solution.py:654
  20.0 2.3 %collective-permute-start.7 = (bf16[2,72,384]{2,1,0:T(8,128)(2,1)S(1)}, bf16[2,72,384]{2,1,0:T(8,128)(2,1)S(1)}, u32[]{:S(2)}, u32[]{:S(2)}) collective-permute-start(bf16[2,72,384]{2,1,0:T(8,128)(2,1)S(1)} %get-tuple-element.93), channel_id=1, source_target_pairs={{0,4},{4,0},{8,12},{12,8},{16,20},{20,16},{24,28},{28,24},{1,5},{5... | collective-permute-start | bytes 331784 | tf_op jit(solution)/shard_map/ppermute | solution.py:654
  23.0 2.3 %act_kernel.1 = (bf16[1024,768]{1,0:T(8,128)(2,1)S(1)}, f32[1024,768]{1,0:T(8,128)S(1)}, f32[8,768]{1,0:T(8,128)S(1)}, bf16[1024,768]{1,0:T(8,128)(2,1)S(1)}) custom-call(bf16[1024,768]{1,0:T(8,128)(2,1)S(1)} %get-tuple-element.77.refs_0_.refs_1_, bf16[1024,768]{1,0:T(8,128)(2,1)} %refs_1_.3, bf16[448,128]{1,0:T(8,128)(2,1)S(1)} %get-tuple-element.86.refs_2_.refs_1_, ...), custom_call_target="tpu_custom_call" | custom-call | flops 1 | bytes 1 | tf_op jit(solution)/shard_map/act_kernel/pallas_call | solution.py:48
  25.3 0.6 upstream_kernel.1
  25.9 1.2 %collective-permute-done.8.refs_8_ = bf16[2,72,384]{2,1,0:T(8,128)(2,1)S(1)} collective-permute-done((bf16[2,72,384]{2,1,0:T(8,128)(2,1)S(1)}, bf16[2,72,384]{2,1,0:T(8,128)(2,1)S(1)}, u32[]{:S(2)}, u32[]{:S(2)}) %collective-permute-start.8) | collective-permute-done | bytes 110624 | tf_op jit(solution)/shard_map/ppermute | solution.py:654
  27.1 1.5 %conv_kernel.1 = (bf16[768,384]{1,0:T(8,128)(2,1)S(1)}, f32[1056,128]{1,0:T(8,128)S(1)}, f32[8,2,128]{2,1,0:T(2,128)S(1)}, bf16[2,48,768]{2,1,0:T(8,128)(2,1)S(1)}, bf16[11,72,384]{2,1,0:T(8,128)(2,1)S(1)}) custom-call(f32[3,1056,128]{2,1,0:T(8,128)S(1)} %get-tuple-element.84.refs_0_, bf16[1024,768]{1,0:T(8,128)(2,1)S(1)} %get-tuple-element.87.refs_1_.refs_2_, ...), custom_call_target="tpu_custom_call" | custom-call | flops 1 | bytes 1 | tf_op jit(solution)/shard_map/conv_kernel/pallas_call | solution.py:48
  28.5 1.6 %collective-permute-start.12 = (bf16[11,72,384]{2,1,0:T(8,128)(2,1)S(1)}, bf16[11,72,384]{2,1,0:T(8,128)(2,1)S(1)}, u32[]{:S(2)}, u32[]{:S(2)}) collective-permute-start(bf16[11,72,384]{2,1,0:T(8,128)(2,1)S(1)} %get-tuple-element.109), channel_id=1, source_target_pairs={{0,2},{1,3},{2,0},{3,1},{4,6},{5,7},{6,4},{7,5},{8,10},{9,11},{10,... | collective-permute-start | bytes 1824776 | tf_op jit(solution)/shard_map/ppermute | solution.py:654
  30.1 10.0 %all_to_all.10.refs_0_ = f32[8,2,128]{2,1,0:T(2,128)S(1)} all-to-all(f32[8,2,128]{2,1,0:T(2,128)S(1)} %get-tuple-element.96), channel_id=1, replica_groups=mesh['seq'=8,'ch'=4] {'seq'}, dimensions={0} | all-to-all | bytes 16384 | tf_op jit(solution)/shard_map/all_to_all | solution.py:665
  40.2 0.7 mid_kernel.1
  40.8 8.9 %all_to_all.11.refs_0_ = f32[8,2,128]{2,1,0:T(2,128)S(1)} all-to-all(f32[8,2,128]{2,1,0:T(2,128)S(1)} %get-tuple-element.101), channel_id=1, replica_groups=mesh['seq'=8,'ch'=4] {'seq'}, dimensions={0} | all-to-all | bytes 16384 | tf_op jit(solution)/shard_map/all_to_all | solution.py:665
  51.1 2.0 %weight_grad_kernel.1 = (bf16[1024,384]{1,0:T(8,128)(2,1)S(1)}, f32[4,96,384]{2,1,0:T(8,128)S(1)}, bf16[4,96,384]{2,1,0:T(8,128)(2,1)S(1)}, bf16[768,128]{1,0:T(8,128)(2,1)S(1)}, bf16[1344,128]{1,0:T(8,128)(2,1)S(1)}) custom-call(f32[3,1024,128]{2,1,0:T(8,128)S(1)} %get-tuple-element.83.refs_4_.refs_2_.refs_0_, ...), custom_call_target="tpu_custom_call" | custom-call | flops 1 | bytes 1 | tf_op jit(solution)/shard_map/weight_grad_kernel/pallas_call | solution.py:48
  53.3 0.6 collective-permute-start.23
  53.9 1.5 %first_half_kernel.1.refs_1_.refs_4_ = f32[1024,768]{1,0:T(8,128)S(1)} custom-call(f32[3,1024,128]{2,1,0:T(8,128)S(1)} %get-tuple-element.83.refs_4_.refs_2_.refs_0_, bf16[1024,384]{1,0:T(8,128)(2,1)S(1)} %get-tuple-element.112.refs_1_, bf16[792,128]{1,0:T(8,128)(2,1)S(1)} %collective-permute-done.13.refs_2_, ...), custom_call_target="tpu_custom_call" | custom-call | flops 1 | bytes 1 | tf_op jit(solution)/shard_map/first_half_kernel/pallas_call | solution.py:48
  56.0 1.7 %collective-permute-done.15.refs_0_ = bf16[792,128]{1,0:T(8,128)(2,1)S(1)} collective-permute-done((bf16[792,128]{1,0:T(8,128)(2,1)S(1)}, bf16[792,128]{1,0:T(8,128)(2,1)S(1)}, u32[]{:S(2)}, u32[]{:S(2)}) %collective-permute-start.15) | collective-permute-done | bytes 202784 | tf_op jit(solution)/shard_map/ppermute | solution.py:654
  58.3 0.9 %collective-permute-done.16.refs_7_ = bf16[792,128]{1,0:T(8,128)(2,1)S(1)} collective-permute-done((bf16[792,128]{1,0:T(8,128)(2,1)S(1)}, bf16[792,128]{1,0:T(8,128)(2,1)S(1)}, u32[]{:S(2)}, u32[]{:S(2)}) %collective-permute-start.16) | collective-permute-done | bytes 202784 | tf_op jit(solution)/shard_map/ppermute | solution.py:654
  59.2 2.1 %second_half_kernel.1 = (f32[1024,768]{1,0:T(8,128)S(1)}, f32[2,768]{1,0:T(2,128)S(1)}) custom-call(f32[3,1024,128]{2,1,0:T(8,128)S(1)} %get-tuple-element.83.refs_4_.refs_2_.refs_0_, bf16[1024,768]{1,0:T(8,128)(2,1)S(1)} %get-tuple-element.77.refs_0_.refs_1_, f32[1024,768]{1,0:T(8,128)S(1)} %get-tuple-element.111.refs_2_, ...), custom_call_target="tpu_custom_call" | custom-call | flops 1 | bytes 1 | tf_op jit(solution)/shard_map/second_half_kernel/pallas_call | solution.py:48
  61.2 0.6 collective-permute-start.17
  61.9 0.8 %collective-permute-done.23.refs_1_ = bf16[4,96,384]{2,1,0:T(8,128)(2,1)S(1)} collective-permute-done((bf16[4,96,384]{2,1,0:T(8,128)(2,1)S(1)}, bf16[4,96,384]{2,1,0:T(8,128)(2,1)S(1)}, u32[]{:S(2)}, u32[]{:S(2)}) %collective-permute-start.23) | collective-permute-done | bytes 294944 | tf_op jit(solution)/shard_map/ppermute | solution.py:654
  62.7 0.6 collective-permute-start.24
  63.3 2.6 %collective-permute-done.17.refs_1_ = f32[2,768]{1,0:T(2,128)S(1)} collective-permute-done((f32[2,768]{1,0:T(2,128)S(1)}, f32[2,768]{1,0:T(2,128)S(1)}, u32[]{:S(2)}, u32[]{:S(2)}) %collective-permute-start.17) | collective-permute-done | bytes 6176 | tf_op jit(solution)/shard_map/ppermute | solution.py:654
  66.7 1.6 %collective-permute-done.24.refs_1_ = bf16[2,96,384]{2,1,0:T(8,128)(2,1)S(1)} collective-permute-done((bf16[2,96,384]{2,1,0:T(8,128)(2,1)S(1)}, bf16[2,96,384]{2,1,0:T(8,128)(2,1)S(1)}, u32[]{:S(2)}, u32[]{:S(2)}) %collective-permute-start.24) | collective-permute-done | bytes 147488 | tf_op jit(solution)/shard_map/ppermute | solution.py:654
  68.3 1.7 %collective-permute-start.25 = (bf16[1,96,384]{2,1,0:T(8,128)(2,1)S(1)}, bf16[1,96,384]{2,1,0:T(8,128)(2,1)S(1)}, u32[]{:S(2)}, u32[]{:S(2)}) collective-permute-start(bf16[1,96,384]{2,1,0:T(8,128)(2,1)S(1)} %get-tuple-element.124), channel_id=1, source_target_pairs={{0,16},{4,20},{8,24},{12,28},{16,0},{20,4},{24,8},{28,12},{1,17},{... | collective-permute-start | bytes 221192 | tf_op jit(solution)/shard_map/ppermute | solution.py:654
  71.6 2.5 %out_kernel.1 = (bf16[1024,768]{1,0:T(8,128)(2,1)}, f32[8,128]{1,0:T(8,128)S(1)}) custom-call(bf16[1024,768]{1,0:T(8,128)(2,1)S(1)} %get-tuple-element.77.refs_0_.refs_1_, bf16[1344,128]{1,0:T(8,128)(2,1)S(1)} %get-tuple-element.107.refs_1_, bf16[1344,128]{1,0:T(8,128)(2,1)S(1)} %collective-permute-done.10.refs_8_.refs_2_, ...), custom_call_target="tpu_custom_call" | custom-call | flops 1 | bytes 1 | tf_op jit(solution)/shard_map/out_kernel/pallas_call | solution.py:48
  74.4 2.8 %final_kernel.1 = (f32[1024,768]{1,0:T(8,128)}, f32[2,768]{1,0:T(2,128)}, f32[2,768]{1,0:T(2,128)}, f32[2,768]{1,0:T(2,128)}, f32[3,96,96]{2,1,0:T(8,128)}, /*in...) custom-call(bf16[1024,768]{1,0:T(8,128)(2,1)S(1)} %get-tuple-element, ...), custom_call_target="tpu_custom_call" | custom-call | flops 1 | bytes 1 | tf_op jit(solution)/shard_map/final_kernel/pallas_call | solution.py:48
  (52 shorter events, 6.0 us)
Async XLA Ops:
  0.6 13.8 %copy-start.2 = (s32[8]{0:T(128)S(1)}, s32[8]{0:T(128)}, u32[]{:S(2)}) copy-start(s32[8]{0:T(128)} %refs_0_.3) | copy-start | bytes 100
  2.4 9.0 %collective-permute-start = (bf16[1,72,384]{2,1,0:T(8,128)(2,1)S(1)}, bf16[1,72,384]{2,1,0:T(8,128)(2,1)S(1)}, u32[]{:S(2)}, u32[]{:S(2)}) collective-permute-start(bf16[1,72,384]{2,1,0:T(8,128)(2,1)S(1)} %get-tuple-element.79.refs_0_), channel_id=1, source_target_pairs={{0,16},{4,20},{8,24},{12,28},{16,0},{20,4},{24,8},{28,12},{1,17},{... | collective-permute-start | bytes 165896 | tf_op jit(solution)/shard_map/ppermute | solution.py:654
  6.5 4.9 %collective-permute-start.1 = (bf16[144,128]{1,0:T(8,128)(2,1)S(1)}, bf16[144,128]{1,0:T(8,128)(2,1)S(1)}, u32[]{:S(2)}, u32[]{:S(2)}) collective-permute-start(bf16[144,128]{1,0:T(8,128)(2,1)S(1)} %get-tuple-element.80.refs_2_), channel_id=1, source_target_pairs={{0,16},{4,20},{8,24},{12,28},{16,0},{20,4},{24,8},{28,12},{1,17},{... | collective-permute-start | bytes 110600 | tf_op jit(solution)/shard_map/ppermute | solution.py:654
  11.4 6.3 %collective-permute-start.2 = (bf16[2,72,384]{2,1,0:T(8,128)(2,1)S(1)}, bf16[2,72,384]{2,1,0:T(8,128)(2,1)S(1)}, u32[]{:S(2)}, u32[]{:S(2)}) collective-permute-start(bf16[2,72,384]{2,1,0:T(8,128)(2,1)S(1)} %get-tuple-element.85.refs_0_), channel_id=1, source_target_pairs={{0,8},{4,12},{8,0},{12,4},{16,24},{20,28},{24,16},{28,20},{1,9},{5... | collective-permute-start | bytes 331784 | tf_op jit(solution)/shard_map/ppermute | solution.py:654
  13.0 4.6 %collective-permute-start.3 = (bf16[384,128]{1,0:T(8,128)(2,1)S(1)}, bf16[384,128]{1,0:T(8,128)(2,1)S(1)}, u32[]{:S(2)}, u32[]{:S(2)}) collective-permute-start(bf16[384,128]{1,0:T(8,128)(2,1)S(1)} %get-tuple-element.82.refs_2_), channel_id=1, source_target_pairs={{0,4},{4,0},{8,12},{12,8},{16,20},{20,16},{24,28},{28,24},{1,5},{5... | collective-permute-start | bytes 294920 | tf_op jit(solution)/shard_map/ppermute | solution.py:654
  15.9 6.4 %collective-permute-start.5 = (bf16[48,384]{1,0:T(8,128)(2,1)S(1)}, bf16[48,384]{1,0:T(8,128)(2,1)S(1)}, u32[]{:S(2)}, u32[]{:S(2)}) collective-permute-start(bf16[48,384]{1,0:T(8,128)(2,1)S(1)} %get-tuple-element.88), channel_id=1, source_target_pairs={{4,8},{12,16},{20,24},{8,4},{16,12},{24,20},{5,9},{13,17},{21,25},... | collective-permute-start | bytes 110600 | tf_op jit(solution)/shard_map/ppermute | solution.py:744
  17.6 5.4 %copy-start = (f32[2,768]{1,0:T(2,128)S(1)}, f32[2,768]{1,0:T(2,128)}, u32[]{:S(2)}) copy-start(f32[2,768]{1,0:T(2,128)} %refs_9_.1) | copy-start | bytes 18436
  17.7 5.3 %collective-permute-start.4 = (bf16[448,128]{1,0:T(8,128)(2,1)S(1)}, bf16[448,128]{1,0:T(8,128)(2,1)S(1)}, u32[]{:S(2)}, u32[]{:S(2)}) collective-permute-start(bf16[448,128]{1,0:T(8,128)(2,1)S(1)} %get-tuple-element.86.refs_2_.refs_1_), channel_id=1, source_target_pairs={{0,8},{4,12},{8,0},{12,4},{16,24},{20,28},{24,16},{28,20},{1,9},{5... | collective-permute-start | bytes 344072 | tf_op jit(solution)/shard_map/ppermute | solution.py:654
  20.0 5.9 %collective-permute-start.7 = (bf16[2,72,384]{2,1,0:T(8,128)(2,1)S(1)}, bf16[2,72,384]{2,1,0:T(8,128)(2,1)S(1)}, u32[]{:S(2)}, u32[]{:S(2)}) collective-permute-start(bf16[2,72,384]{2,1,0:T(8,128)(2,1)S(1)} %get-tuple-element.93), channel_id=1, source_target_pairs={{0,4},{4,0},{8,12},{12,8},{16,20},{20,16},{24,28},{28,24},{1,5},{5... | collective-permute-start | bytes 331784 | tf_op jit(solution)/shard_map/ppermute | solution.py:654
  22.3 4.7 %collective-permute-start.8 = (bf16[2,72,384]{2,1,0:T(8,128)(2,1)S(1)}, bf16[2,72,384]{2,1,0:T(8,128)(2,1)S(1)}, u32[]{:S(2)}, u32[]{:S(2)}) collective-permute-start(bf16[2,72,384]{2,1,0:T(8,128)(2,1)S(1)} %get-tuple-element.94), channel_id=1, source_target_pairs={{0,4},{4,0},{8,12},{12,8},{16,20},{20,16},{24,28},{28,24},{1,5},{5... | collective-permute-start | bytes 331784 | tf_op jit(solution)/shard_map/ppermute | solution.py:654
  22.4 3.5 %collective-permute-start.6 = (bf16[112,384]{1,0:T(8,128)(2,1)S(1)}, bf16[112,384]{1,0:T(8,128)(2,1)S(1)}, u32[]{:S(2)}, u32[]{:S(2)}) collective-permute-start(bf16[112,384]{1,0:T(8,128)(2,1)S(1)} %rim_kernel.1.refs_2_), channel_id=1, source_target_pairs={{0,1},{1,0},{2,3},{3,2},{4,5},{5,4},{6,7},{7,6},{8,9},{9,8},{10,11... | collective-permute-start | bytes 258056 | tf_op jit(solution)/shard_map/ppermute | solution.py:654
  27.1 13.1 %copy-start.1 = (f32[2,96]{1,0:T(2,128)S(1)}, f32[2,96]{1,0:T(2,128)}, u32[]{:S(2)}) copy-start(f32[2,96]{1,0:T(2,128)} %refs_18_.1) | copy-start | bytes 2308
  28.5 21.4 %collective-permute-start.12 = (bf16[11,72,384]{2,1,0:T(8,128)(2,1)S(1)}, bf16[11,72,384]{2,1,0:T(8,128)(2,1)S(1)}, u32[]{:S(2)}, u32[]{:S(2)}) collective-permute-start(bf16[11,72,384]{2,1,0:T(8,128)(2,1)S(1)} %get-tuple-element.109), channel_id=1, source_target_pairs={{0,2},{1,3},{2,0},{3,1},{4,6},{5,7},{6,4},{7,5},{8,10},{9,11},{10,... | collective-permute-start | bytes 1824776 | tf_op jit(solution)/shard_map/ppermute | solution.py:654
  30.1 10.0 %collective-permute-start.9 = (bf16[768,384]{1,0:T(8,128)(2,1)S(1)}, bf16[768,384]{1,0:T(8,128)(2,1)S(1)}, u32[]{:S(2)}, u32[]{:S(2)}) collective-permute-start(bf16[768,384]{1,0:T(8,128)(2,1)S(1)} %get-tuple-element.100.refs_3_), channel_id=1, source_target_pairs={{0,1},{1,0},{2,3},{3,2},{4,5},{5,4},{6,7},{7,6},{8,9},{9,8},{10,11... | collective-permute-start | bytes 1769480 | tf_op jit(solution)/shard_map/ppermute | solution.py:654
  50.0 5.4 %collective-permute-start.14 = (bf16[8,72,384]{2,1,0:T(8,128)(2,1)S(1)}, bf16[8,72,384]{2,1,0:T(8,128)(2,1)S(1)}, u32[]{:S(2)}, u32[]{:S(2)}) collective-permute-start(bf16[8,72,384]{2,1,0:T(8,128)(2,1)S(1)} %get-tuple-element.113.refs_0_), channel_id=1, source_target_pairs={{0,1},{1,0},{2,3},{3,2},{4,5},{5,4},{6,7},{7,6},{8,9},{9,8},{10,11... | collective-permute-start | bytes 1327112 | tf_op jit(solution)/shard_map/ppermute | solution.py:654
  50.1 3.7 %collective-permute-start.13 = (bf16[792,128]{1,0:T(8,128)(2,1)S(1)}, bf16[792,128]{1,0:T(8,128)(2,1)S(1)}, u32[]{:S(2)}, u32[]{:S(2)}) collective-permute-start(bf16[792,128]{1,0:T(8,128)(2,1)S(1)} %get-tuple-element.105.refs_1_), channel_id=1, source_target_pairs={{0,1},{1,0},{2,3},{3,2},{4,5},{5,4},{6,7},{7,6},{8,9},{9,8},{10,11... | collective-permute-start | bytes 608264 | tf_op jit(solution)/shard_map/ppermute | solution.py:654
  50.6 7.0 %collective-permute-start.15 = (bf16[792,128]{1,0:T(8,128)(2,1)S(1)}, bf16[792,128]{1,0:T(8,128)(2,1)S(1)}, u32[]{:S(2)}, u32[]{:S(2)}) collective-permute-start(bf16[792,128]{1,0:T(8,128)(2,1)S(1)} %get-tuple-element.105.refs_1_), channel_id=1, source_target_pairs={{0,2},{1,3},{2,0},{3,1},{4,6},{5,7},{6,4},{7,5},{8,10},{9,11},{10,... | collective-permute-start | bytes 608264 | tf_op jit(solution)/shard_map/ppermute | solution.py:654
  53.2 5.1 %collective-permute-start.10 = (bf16[1344,128]{1,0:T(8,128)(2,1)S(1)}, bf16[1344,128]{1,0:T(8,128)(2,1)S(1)}, u32[]{:S(2)}, u32[]{:S(2)}) collective-permute-start(bf16[1344,128]{1,0:T(8,128)(2,1)S(1)} %get-tuple-element.107.refs_1_), channel_id=1, source_target_pairs={{0,1},{1,0},{2,3},{3,2},{4,5},{5,4},{6,7},{7,6},{8,9},{9,8},{10,11... | collective-permute-start | bytes 1032200 | tf_op jit(solution)/shard_map/ppermute | solution.py:654
  53.3 9.4 %collective-permute-start.23 = (bf16[4,96,384]{2,1,0:T(8,128)(2,1)S(1)}, bf16[4,96,384]{2,1,0:T(8,128)(2,1)S(1)}, u32[]{:S(2)}, u32[]{:S(2)}) collective-permute-start(bf16[4,96,384]{2,1,0:T(8,128)(2,1)S(1)} %get-tuple-element.120), channel_id=1, source_target_pairs={{0,4},{4,0},{8,12},{12,8},{16,20},{20,16},{24,28},{28,24},{1,5},{5... | collective-permute-start | bytes 884744 | tf_op jit(solution)/shard_map/ppermute | solution.py:654
  57.7 1.5 %collective-permute-start.16 = (bf16[792,128]{1,0:T(8,128)(2,1)S(1)}, bf16[792,128]{1,0:T(8,128)(2,1)S(1)}, u32[]{:S(2)}, u32[]{:S(2)}) collective-permute-start(bf16[792,128]{1,0:T(8,128)(2,1)S(1)} %copy_kernel.1.refs_6_), channel_id=1, source_target_pairs={{0,1},{1,0},{2,3},{3,2},{4,5},{5,4},{6,7},{7,6},{8,9},{9,8},{10,11... | collective-permute-start | bytes 608264 | tf_op jit(solution)/shard_map/ppermute | solution.py:654
  57.7 8.2 %collective-permute-start.11 = (bf16[768,128]{1,0:T(8,128)(2,1)S(1)}, bf16[768,128]{1,0:T(8,128)(2,1)S(1)}, u32[]{:S(2)}, u32[]{:S(2)}) collective-permute-start(bf16[768,128]{1,0:T(8,128)(2,1)S(1)} %get-tuple-element.108), channel_id=1, source_target_pairs={{0,2},{1,3},{2,0},{3,1},{4,6},{5,7},{6,4},{7,5},{8,10},{9,11},{10,... | collective-permute-start | bytes 589832 | tf_op jit(solution)/shard_map/ppermute | solution.py:654
  61.2 4.7 %collective-permute-start.17 = (f32[2,768]{1,0:T(2,128)S(1)}, f32[2,768]{1,0:T(2,128)S(1)}, u32[]{:S(2)}, u32[]{:S(2)}) collective-permute-start(f32[2,768]{1,0:T(2,128)S(1)} %get-tuple-element.114.refs_0_), channel_id=1, source_target_pairs={{0,16},{4,20},{8,24},{12,28},{16,0},{20,4},{24,8},{28,12},{1,17},{... | collective-permute-start | bytes 18440 | tf_op jit(solution)/shard_map/ppermute | solution.py:654
  62.7 5.5 %collective-permute-start.24 = (bf16[2,96,384]{2,1,0:T(8,128)(2,1)S(1)}, bf16[2,96,384]{2,1,0:T(8,128)(2,1)S(1)}, u32[]{:S(2)}, u32[]{:S(2)}) collective-permute-start(bf16[2,96,384]{2,1,0:T(8,128)(2,1)S(1)} %get-tuple-element.122), channel_id=1, source_target_pairs={{0,8},{4,12},{8,0},{12,4},{16,24},{20,28},{24,16},{28,20},{1,9},{5... | collective-permute-start | bytes 442376 | tf_op jit(solution)/shard_map/ppermute | solution.py:654
  66.0 5.6 %collective-permute-start.19 = (bf16[848,128]{1,0:T(8,128)(2,1)S(1)}, bf16[848,128]{1,0:T(8,128)(2,1)S(1)}, u32[]{:S(2)}, u32[]{:S(2)}) collective-permute-start(bf16[848,128]{1,0:T(8,128)(2,1)S(1)} %get-tuple-element.115.refs_3_), channel_id=1, source_target_pairs={{0,1},{1,0},{2,3},{3,2},{4,5},{5,4},{6,7},{7,6},{8,9},{9,8},{10,11... | collective-permute-start | bytes 651272 | tf_op jit(solution)/shard_map/ppermute | solution.py:654
  66.1 4.0 %collective-permute-start.18 = (f32[2,768]{1,0:T(2,128)S(1)}, f32[2,768]{1,0:T(2,128)S(1)}, u32[]{:S(2)}, u32[]{:S(2)}) collective-permute-start(f32[2,768]{1,0:T(2,128)S(1)} %add_kernel.2.refs_3_.refs_0_.refs_2_), channel_id=1, source_target_pairs={{0,4},{4,0},{8,12},{12,8},{16,20},{20,16},{24,28},{28,24},{1,5},{5... | collective-permute-start | bytes 18440 | tf_op jit(solution)/shard_map/ppermute | solution.py:654
  68.3 6.1 %collective-permute-start.25 = (bf16[1,96,384]{2,1,0:T(8,128)(2,1)S(1)}, bf16[1,96,384]{2,1,0:T(8,128)(2,1)S(1)}, u32[]{:S(2)}, u32[]{:S(2)}) collective-permute-start(bf16[1,96,384]{2,1,0:T(8,128)(2,1)S(1)} %get-tuple-element.124), channel_id=1, source_target_pairs={{0,16},{4,20},{8,24},{12,28},{16,0},{20,4},{24,8},{28,12},{1,17},{... | collective-permute-start | bytes 221192 | tf_op jit(solution)/shard_map/ppermute | solution.py:654
  70.1 1.5 %collective-permute-start.21 = (bf16[272,128]{1,0:T(8,128)(2,1)S(1)}, bf16[272,128]{1,0:T(8,128)(2,1)S(1)}, u32[]{:S(2)}, u32[]{:S(2)}) collective-permute-start(bf16[272,128]{1,0:T(8,128)(2,1)S(1)} %pack_kernel.3.refs_5_), channel_id=1, source_target_pairs={{0,1},{1,0},{2,3},{3,2},{4,5},{5,4},{6,7},{7,6},{8,9},{9,8},{10,11... | collective-permute-start | bytes 208904 | tf_op jit(solution)/shard_map/ppermute | solution.py:654
  70.2 1.4 %collective-permute-start.20 = (bf16[224,128]{1,0:T(8,128)(2,1)S(1)}, bf16[224,128]{1,0:T(8,128)(2,1)S(1)}, u32[]{:S(2)}, u32[]{:S(2)}) collective-permute-start(bf16[224,128]{1,0:T(8,128)(2,1)S(1)} %get-tuple-element.116.refs_4_), channel_id=1, source_target_pairs={{0,1},{1,0},{2,3},{3,2},{4,5},{5,4},{6,7},{7,6},{8,9},{9,8},{10,11... | collective-permute-start | bytes 172040 | tf_op jit(solution)/shard_map/ppermute | solution.py:654
  70.7 3.7 %collective-permute-start.22 = (f32[2,768]{1,0:T(2,128)S(1)}, f32[2,768]{1,0:T(2,128)S(1)}, u32[]{:S(2)}, u32[]{:S(2)}) collective-permute-start(f32[2,768]{1,0:T(2,128)S(1)} %add_kernel.3.refs_1_.refs_9_.refs_4_), channel_id=1, source_target_pairs={{0,8},{4,12},{8,0},{12,4},{16,24},{20,28},{24,16},{28,20},{1,9},{5... | collective-permute-start | bytes 18440 | tf_op jit(solution)/shard_map/ppermute | solution.py:654

commit v10 on v9

--- a/solution.py
+++ b/solution.py
@@ -256,8 +256,7 @@
     out_ref[2 * height :, :] = jnp.zeros_like(out_ref[2 * height :, :])
 
 
-def mask_kernel(start_ref, rim_ref, ahead_ref, back_ref, far_ref):
-    far_ref[...] = rim_ref[...]
+def mask_kernel(start_ref, ahead_ref, back_ref):
     rows = back_ref.shape[1]
     first = lax.axis_index("seq") * rows
     for j, shift in enumerate(SHIFTS):
@@ -588,7 +587,11 @@
 
 
 def round_kernel(weight_one, weight_two, one_ref, two_ref, *refs, size, sides):
-    rims, (weight_ref, out_ref), halves = refs[: len(refs) - 2 - sides], refs[-2 - sides :][:2], refs[len(refs) - sides :]
+    count = (len(refs) - 2 - sides) // 3
+    rims, outs = refs[: 2 * count], refs[2 * count :]
+    weight_ref, out_ref, halves = outs[0], outs[1], outs[2 : 2 + sides]
+    if rims:
+        outs[-1][...] = rims[1][...]
     count = weight_one.shape[0]
     weight_ref[:count] = weight_one[...]
     weight_ref[count:] = weight_two[...]
@@ -597,7 +600,7 @@
     put_sums(out_ref, get_sums(one_ref) + get_sums(two_ref))
     out_ref[SUMS : SUMS + size, :] = one_ref[SUMS : SUMS + size, :]
     out_ref[SUMS + size : SUMS + 2 * size, :] = two_ref[SUMS : SUMS + size, :]
-    for rim in rims:
+    for rim in rims[:1]:
         height, width = rim.shape
         for k in range(width // LANES):
             at = SUMS + 2 * size + k * height
@@ -720,6 +723,13 @@
         sems=4 + chunks,
     )
     pairs = [(i, i + 1) for i in range(1, seq_size - 1, 2)]
+    ahead, back = call(
+        mask_kernel,
+        [((KERNEL_WIDTH, ext, LANES), F32), ((KERNEL_WIDTH, rows, LANES), F32)],
+        [starts],
+        smem=(0,),
+        after=[weight],
+    )
     parts = [weight]
     for k in range(rounds):
         weight_got = [swap(part, "seq", weight_order[k]) for part in parts]
@@ -733,23 +743,16 @@
             join = functools.partial(round_kernel, size=size, sides=sides)
             args = [weight, weight_got[0], near, near_got]
             if k == 0:
-                weight, near = call(join, outs, args + [rims[0]])
-                ahead, back, far = call(
-                    mask_kernel,
-                    [((KERNEL_WIDTH, ext, LANES), F32), ((KERNEL_WIDTH, rows, LANES), F32), (rim, BF16)],
-                    [starts, rims[1]],
-                    smem=(0,),
-                    after=[near],
-                )
+                weight, near, far = call(join, outs + [(rim, BF16)], args + rims, after=[back])
                 far = lax.ppermute(far, "seq", pairs + [(j, i) for i, j in pairs])
                 parts = [weight]
             else:
                 if k == 1:
                     (rims,) = call(
-                        rim_kernel, [((2 * rim[0] + 16, rim[1]), BF16)], [near_got, far], after=[back]
+                        rim_kernel, [((2 * rim[0] + 16, rim[1]), BF16)], [near_got, far]
                     )
                     other_rims = swap(rims, "ch", 1)
-                weight, near, *parts = call(join, outs, args, after=[back] if k == 1 else [])
+                weight, near, *parts = call(join, outs, args)
                 parts = parts or [weight]
     hidden_in, slope_in, vec_in, cotangent = call(
         functools.partial(act_kernel, bin_count=bin_count),

time: 77.6 us -> 76.9 us (level)
  starting transfers between devices: 21.4 us -> 19.9 us
    ppermute x25, starting transfers between devices: 20.7 us -> 19.2 us  [swap(): return lax.ppermute(x, axis, flip(axis, reach))]
where the time goes in v10:
time: 76.9 us; the launch traced here: 76.6 us
  Pallas kernels  20.2 us (26%)
  starting transfers between devices  19.9 us (26%)
  blocking collectives  19.6 us (25%)
  waiting for transfers between devices  15.9 us (21%)
  between operations  1.04 us (1%)
    pallas_call x24, Pallas kernels, call(): pl.pallas_call(kernel, out_shape=[jax.ShapeDtypeStruct(s, t) for s, t in...  20.2 us
    all_to_all x2, blocking collectives, spread(): return lax.all_to_all(copies, axes, 0, 0, tiled=True)  19.6 us
    ppermute x25, starting transfers between devices, swap(): return lax.ppermute(x, axis, flip(axis, reach))  19.2 us
    ppermute x25, waiting for transfers between devices, swap(): return lax.ppermute(x, axis, flip(axis, reach))  15.9 us
  transfers between devices with their start and end apart: 26, of which 11 were waited for; matrix products, arithmetic and copies ran while one was open for 0% of the time, Pallas kernels for 18%

profile of v10, /device:TPU:0, one launch (start us, length us, event | category | flops | bytes accessed | tf_op | source)
XLA Modules:
  0.0 76.6 jit_solution(11969444966057786840)
XLA Ops:
  0.7 1.7 %first_kernel.1 = (bf16[1024,768]{1,0:T(8,128)(2,1)S(1)}, bf16[1,72,384]{2,1,0:T(8,128)(2,1)S(1)}, bf16[144,128]{1,0:T(8,128)(2,1)S(1)}, bf16[48,384]{1,0:T(8,128)(2,1)S(1)}, bf16[48,384]{1,0:T(8,128)(2,1)S(1)}) custom-call(bf16[1024,768]{1,0:T(8,128)(2,1)} %refs_0_.2, bf16[1024,768]{1,0:T(8,128)(2,1)} %refs_1_.3, f32[3,96,96]{2,1,0:T(8,128)} %refs_12_.1, ...), custom_call_target="tpu_custom_call" | custom-call | flops 1 | bytes 1 | tf_op jit(solution)/shard_map/first_kernel/pallas_call | solution.py:48
  2.4 4.1 %collective-permute-start = (bf16[1,72,384]{2,1,0:T(8,128)(2,1)S(1)}, bf16[1,72,384]{2,1,0:T(8,128)(2,1)S(1)}, u32[]{:S(2)}, u32[]{:S(2)}) collective-permute-start(bf16[1,72,384]{2,1,0:T(8,128)(2,1)S(1)} %get-tuple-element.78.refs_1_.refs_0_), channel_id=1, source_target_pairs={{0,16},{4,20},{8,24},{12,28},{16,0},{20,4},{24,8},{28,12},{1,17},{... | collective-permute-start | bytes 165896 | tf_op jit(solution)/shard_map/ppermute | solution.py:657
  6.6 1.4 %mask_kernel.1 = (f32[3,1056,128]{2,1,0:T(8,128)S(1)}, f32[3,1024,128]{2,1,0:T(8,128)S(1)}) custom-call(s32[8]{0:T(128)S(1)} %copy-done.2, bf16[1,72,384]{2,1,0:T(8,128)(2,1)S(1)} %get-tuple-element.78.refs_1_.refs_0_), custom_call_target="tpu_custom_call" | custom-call | flops 1 | bytes 1 | tf_op jit(solution)/shard_map/mask_kernel/pallas_call | solution.py:48
  8.0 3.3 %collective-permute-done.1.refs_3_ = bf16[144,128]{1,0:T(8,128)(2,1)S(1)} collective-permute-done((bf16[144,128]{1,0:T(8,128)(2,1)S(1)}, bf16[144,128]{1,0:T(8,128)(2,1)S(1)}, u32[]{:S(2)}, u32[]{:S(2)}) %collective-permute-start.1) | collective-permute-done | bytes 36896 | tf_op jit(solution)/shard_map/ppermute | solution.py:657
  11.4 1.6 %collective-permute-start.2 = (bf16[2,72,384]{2,1,0:T(8,128)(2,1)S(1)}, bf16[2,72,384]{2,1,0:T(8,128)(2,1)S(1)}, u32[]{:S(2)}, u32[]{:S(2)}) collective-permute-start(bf16[2,72,384]{2,1,0:T(8,128)(2,1)S(1)} %get-tuple-element.84.refs_0_), channel_id=1, source_target_pairs={{0,8},{4,12},{8,0},{12,4},{16,24},{20,28},{24,16},{28,20},{1,9},{5... | collective-permute-start | bytes 331784 | tf_op jit(solution)/shard_map/ppermute | solution.py:657
  13.0 1.5 %collective-permute-start.3 = (bf16[384,128]{1,0:T(8,128)(2,1)S(1)}, bf16[384,128]{1,0:T(8,128)(2,1)S(1)}, u32[]{:S(2)}, u32[]{:S(2)}) collective-permute-start(bf16[384,128]{1,0:T(8,128)(2,1)S(1)} %get-tuple-element.85.refs_2_), channel_id=1, source_target_pairs={{0,4},{4,0},{8,12},{12,8},{16,20},{20,16},{24,28},{28,24},{1,5},{5... | collective-permute-start | bytes 294920 | tf_op jit(solution)/shard_map/ppermute | solution.py:657
  14.5 0.7 collective-permute-start.5
  15.2 2.5 %collective-permute-done.3.refs_3_.refs_0_ = bf16[384,128]{1,0:T(8,128)(2,1)S(1)} collective-permute-done((bf16[384,128]{1,0:T(8,128)(2,1)S(1)}, bf16[384,128]{1,0:T(8,128)(2,1)S(1)}, u32[]{:S(2)}, u32[]{:S(2)}) %collective-permute-start.3) | collective-permute-done | bytes 98336 | tf_op jit(solution)/shard_map/ppermute | solution.py:657
  17.7 0.9 %collective-permute-start.4 = (bf16[448,128]{1,0:T(8,128)(2,1)S(1)}, bf16[448,128]{1,0:T(8,128)(2,1)S(1)}, u32[]{:S(2)}, u32[]{:S(2)}) collective-permute-start(bf16[448,128]{1,0:T(8,128)(2,1)S(1)} %get-tuple-element.86.refs_2_.refs_1_), channel_id=1, source_target_pairs={{0,8},{4,12},{8,0},{12,4},{16,24},{20,28},{24,16},{28,20},{1,9},{5... | collective-permute-start | bytes 344072 | tf_op jit(solution)/shard_map/ppermute | solution.py:657
  18.5 2.3 %collective-permute-start.7 = (bf16[2,72,384]{2,1,0:T(8,128)(2,1)S(1)}, bf16[2,72,384]{2,1,0:T(8,128)(2,1)S(1)}, u32[]{:S(2)}, u32[]{:S(2)}) collective-permute-start(bf16[2,72,384]{2,1,0:T(8,128)(2,1)S(1)} %get-tuple-element.93), channel_id=1, source_target_pairs={{0,4},{4,0},{8,12},{12,8},{16,20},{20,16},{24,28},{28,24},{1,5},{5... | collective-permute-start | bytes 331784 | tf_op jit(solution)/shard_map/ppermute | solution.py:657
  21.0 1.5 %collective-permute-done.4.refs_3_.refs_2_ = bf16[448,128]{1,0:T(8,128)(2,1)S(1)} collective-permute-done((bf16[448,128]{1,0:T(8,128)(2,1)S(1)}, bf16[448,128]{1,0:T(8,128)(2,1)S(1)}, u32[]{:S(2)}, u32[]{:S(2)}) %collective-permute-start.4) | collective-permute-done | bytes 114720 | tf_op jit(solution)/shard_map/ppermute | solution.py:657
  22.5 2.3 %act_kernel.1 = (bf16[1024,768]{1,0:T(8,128)(2,1)S(1)}, f32[1024,768]{1,0:T(8,128)S(1)}, f32[8,768]{1,0:T(8,128)S(1)}, bf16[1024,768]{1,0:T(8,128)(2,1)S(1)}) custom-call(bf16[1024,768]{1,0:T(8,128)(2,1)S(1)} %get-tuple-element.77.refs_0_.refs_1_, bf16[1024,768]{1,0:T(8,128)(2,1)} %refs_1_.3, bf16[448,128]{1,0:T(8,128)(2,1)S(1)} %get-tuple-element.86.refs_2_.refs_1_, ...), custom_call_target="tpu_custom_call" | custom-call | flops 1 | bytes 1 | tf_op jit(solution)/shard_map/act_kernel/pallas_call | solution.py:48
  24.8 0.6 upstream_kernel.1
  25.6 1.4 %conv_kernel.1 = (bf16[768,384]{1,0:T(8,128)(2,1)S(1)}, f32[1056,128]{1,0:T(8,128)S(1)}, f32[8,2,128]{2,1,0:T(2,128)S(1)}, bf16[2,48,768]{2,1,0:T(8,128)(2,1)S(1)}, bf16[11,72,384]{2,1,0:T(8,128)(2,1)S(1)}) custom-call(f32[3,1056,128]{2,1,0:T(8,128)S(1)} %get-tuple-element.80.refs_0_, bf16[1024,768]{1,0:T(8,128)(2,1)S(1)} %get-tuple-element.87.refs_1_.refs_2_, ...), custom_call_target="tpu_custom_call" | custom-call | flops 1 | bytes 1 | tf_op jit(solution)/shard_map/conv_kernel/pallas_call | solution.py:48
  27.1 1.6 %collective-permute-start.12 = (bf16[11,72,384]{2,1,0:T(8,128)(2,1)S(1)}, bf16[11,72,384]{2,1,0:T(8,128)(2,1)S(1)}, u32[]{:S(2)}, u32[]{:S(2)}) collective-permute-start(bf16[11,72,384]{2,1,0:T(8,128)(2,1)S(1)} %get-tuple-element.109), channel_id=1, source_target_pairs={{0,2},{1,3},{2,0},{3,1},{4,6},{5,7},{6,4},{7,5},{8,10},{9,11},{10,... | collective-permute-start | bytes 1824776 | tf_op jit(solution)/shard_map/ppermute | solution.py:657
  28.7 10.7 %all_to_all.10.refs_0_ = f32[8,2,128]{2,1,0:T(2,128)S(1)} all-to-all(f32[8,2,128]{2,1,0:T(2,128)S(1)} %get-tuple-element.96), channel_id=1, replica_groups=mesh['seq'=8,'ch'=4] {'seq'}, dimensions={0} | all-to-all | bytes 16384 | tf_op jit(solution)/shard_map/all_to_all | solution.py:668
  39.3 0.7 mid_kernel.1
  40.0 8.9 %all_to_all.11.refs_0_ = f32[8,2,128]{2,1,0:T(2,128)S(1)} all-to-all(f32[8,2,128]{2,1,0:T(2,128)S(1)} %get-tuple-element.101), channel_id=1, replica_groups=mesh['seq'=8,'ch'=4] {'seq'}, dimensions={0} | all-to-all | bytes 16384 | tf_op jit(solution)/shard_map/all_to_all | solution.py:668
  50.3 2.1 %weight_grad_kernel.1 = (bf16[1024,384]{1,0:T(8,128)(2,1)S(1)}, f32[4,96,384]{2,1,0:T(8,128)S(1)}, bf16[4,96,384]{2,1,0:T(8,128)(2,1)S(1)}, bf16[768,128]{1,0:T(8,128)(2,1)S(1)}, bf16[1344,128]{1,0:T(8,128)(2,1)S(1)}) custom-call(f32[3,1024,128]{2,1,0:T(8,128)S(1)} %get-tuple-element.79.refs_6_.refs_0_, bf16[792,128]{1,0:T(8,128)(2,1)S(1)} %get-tuple-element.105.refs_1_, ...), custom_call_target="tpu_custom_call" | custom-call | flops 1 | bytes 1 | tf_op jit(solution)/shard_map/weight_grad_kernel/pallas_call | solution.py:48
  52.5 0.6 collective-permute-start.23
  53.1 1.6 %first_half_kernel.1.refs_1_.refs_4_ = f32[1024,768]{1,0:T(8,128)S(1)} custom-call(f32[3,1024,128]{2,1,0:T(8,128)S(1)} %get-tuple-element.79.refs_6_.refs_0_, bf16[1024,384]{1,0:T(8,128)(2,1)S(1)} %get-tuple-element.112.refs_1_, bf16[792,128]{1,0:T(8,128)(2,1)S(1)} %collective-permute-done.13.refs_2_, bf16[768,384]{1,0:T(8,128)(2,1)S(1)} %get-tuple-element.100.refs_3_, ...), custom_call_target="tpu_custom_call" | custom-call | flops 1 | bytes 1 | tf_op jit(solution)/shard_map/first_half_kernel/pallas_call | solution.py:48
  55.2 1.6 %collective-permute-done.15.refs_0_ = bf16[792,128]{1,0:T(8,128)(2,1)S(1)} collective-permute-done((bf16[792,128]{1,0:T(8,128)(2,1)S(1)}, bf16[792,128]{1,0:T(8,128)(2,1)S(1)}, u32[]{:S(2)}, u32[]{:S(2)}) %collective-permute-start.15) | collective-permute-done | bytes 202784 | tf_op jit(solution)/shard_map/ppermute | solution.py:657
  57.5 0.9 %collective-permute-done.16.refs_7_ = bf16[792,128]{1,0:T(8,128)(2,1)S(1)} collective-permute-done((bf16[792,128]{1,0:T(8,128)(2,1)S(1)}, bf16[792,128]{1,0:T(8,128)(2,1)S(1)}, u32[]{:S(2)}, u32[]{:S(2)}) %collective-permute-start.16) | collective-permute-done | bytes 202784 | tf_op jit(solution)/shard_map/ppermute | solution.py:657
  58.4 2.0 %second_half_kernel.1 = (f32[1024,768]{1,0:T(8,128)S(1)}, f32[2,768]{1,0:T(2,128)S(1)}) custom-call(f32[3,1024,128]{2,1,0:T(8,128)S(1)} %get-tuple-element.79.refs_6_.refs_0_, bf16[1024,768]{1,0:T(8,128)(2,1)S(1)} %get-tuple-element.77.refs_0_.refs_1_, f32[1024,768]{1,0:T(8,128)S(1)} %get-tuple-element.111.refs_2_, ...), custom_call_target="tpu_custom_call" | custom-call | flops 1 | bytes 1 | tf_op jit(solution)/shard_map/second_half_kernel/pallas_call | solution.py:48
  60.4 0.6 collective-permute-start.17
  61.0 0.9 %collective-permute-done.23.refs_1_ = bf16[4,96,384]{2,1,0:T(8,128)(2,1)S(1)} collective-permute-done((bf16[4,96,384]{2,1,0:T(8,128)(2,1)S(1)}, bf16[4,96,384]{2,1,0:T(8,128)(2,1)S(1)}, u32[]{:S(2)}, u32[]{:S(2)}) %collective-permute-start.23) | collective-permute-done | bytes 294944 | tf_op jit(solution)/shard_map/ppermute | solution.py:657
  62.0 0.6 collective-permute-start.24
  62.5 2.6 %collective-permute-done.17.refs_1_ = f32[2,768]{1,0:T(2,128)S(1)} collective-permute-done((f32[2,768]{1,0:T(2,128)S(1)}, f32[2,768]{1,0:T(2,128)S(1)}, u32[]{:S(2)}, u32[]{:S(2)}) %collective-permute-start.17) | collective-permute-done | bytes 6176 | tf_op jit(solution)/shard_map/ppermute | solution.py:657
  65.8 1.7 %collective-permute-done.24.refs_1_ = bf16[2,96,384]{2,1,0:T(8,128)(2,1)S(1)} collective-permute-done((bf16[2,96,384]{2,1,0:T(8,128)(2,1)S(1)}, bf16[2,96,384]{2,1,0:T(8,128)(2,1)S(1)}, u32[]{:S(2)}, u32[]{:S(2)}) %collective-permute-start.24) | collective-permute-done | bytes 147488 | tf_op jit(solution)/shard_map/ppermute | solution.py:657
  67.5 1.7 %collective-permute-start.25 = (bf16[1,96,384]{2,1,0:T(8,128)(2,1)S(1)}, bf16[1,96,384]{2,1,0:T(8,128)(2,1)S(1)}, u32[]{:S(2)}, u32[]{:S(2)}) collective-permute-start(bf16[1,96,384]{2,1,0:T(8,128)(2,1)S(1)} %get-tuple-element.124), channel_id=1, source_target_pairs={{0,16},{4,20},{8,24},{12,28},{16,0},{20,4},{24,8},{28,12},{1,17},{... | collective-permute-start | bytes 221192 | tf_op jit(solution)/shard_map/ppermute | solution.py:657
  70.7 2.5 %out_kernel.1 = (bf16[1024,768]{1,0:T(8,128)(2,1)}, f32[8,128]{1,0:T(8,128)S(1)}) custom-call(bf16[1024,768]{1,0:T(8,128)(2,1)S(1)} %get-tuple-element.77.refs_0_.refs_1_, bf16[1344,128]{1,0:T(8,128)(2,1)S(1)} %get-tuple-element.107.refs_1_, bf16[1344,128]{1,0:T(8,128)(2,1)S(1)} %collective-permute-done.10.refs_8_.refs_2_, ...), custom_call_target="tpu_custom_call" | custom-call | flops 1 | bytes 1 | tf_op jit(solution)/shard_map/out_kernel/pallas_call | solution.py:48
  73.6 2.8 %final_kernel.1 = (f32[1024,768]{1,0:T(8,128)}, f32[2,768]{1,0:T(2,128)}, f32[2,768]{1,0:T(2,128)}, f32[2,768]{1,0:T(2,128)}, f32[3,96,96]{2,1,0:T(8,128)}, /*in...) custom-call(bf16[1024,768]{1,0:T(8,128)(2,1)S(1)} %get-tuple-element, ...), custom_call_target="tpu_custom_call" | custom-call | flops 1 | bytes 1 | tf_op jit(solution)/shard_map/final_kernel/pallas_call | solution.py:48
  (52 shorter events, 5.7 us)
Async XLA Ops:
  0.6 5.9 %copy-start.2 = (s32[8]{0:T(128)S(1)}, s32[8]{0:T(128)}, u32[]{:S(2)}) copy-start(s32[8]{0:T(128)} %refs_0_.3) | copy-start | bytes 100
  2.4 20.2 %copy-start = (f32[2,768]{1,0:T(2,128)S(1)}, f32[2,768]{1,0:T(2,128)}, u32[]{:S(2)}) copy-start(f32[2,768]{1,0:T(2,128)} %refs_9_.1) | copy-start | bytes 18436
  2.4 9.0 %collective-permute-start = (bf16[1,72,384]{2,1,0:T(8,128)(2,1)S(1)}, bf16[1,72,384]{2,1,0:T(8,128)(2,1)S(1)}, u32[]{:S(2)}, u32[]{:S(2)}) collective-permute-start(bf16[1,72,384]{2,1,0:T(8,128)(2,1)S(1)} %get-tuple-element.78.refs_1_.refs_0_), channel_id=1, source_target_pairs={{0,16},{4,20},{8,24},{12,28},{16,0},{20,4},{24,8},{28,12},{1,17},{... | collective-permute-start | bytes 165896 | tf_op jit(solution)/shard_map/ppermute | solution.py:657
  6.5 4.9 %collective-permute-start.1 = (bf16[144,128]{1,0:T(8,128)(2,1)S(1)}, bf16[144,128]{1,0:T(8,128)(2,1)S(1)}, u32[]{:S(2)}, u32[]{:S(2)}) collective-permute-start(bf16[144,128]{1,0:T(8,128)(2,1)S(1)} %get-tuple-element.81.refs_2_), channel_id=1, source_target_pairs={{0,16},{4,20},{8,24},{12,28},{16,0},{20,4},{24,8},{28,12},{1,17},{... | collective-permute-start | bytes 110600 | tf_op jit(solution)/shard_map/ppermute | solution.py:657
  11.4 6.3 %collective-permute-start.2 = (bf16[2,72,384]{2,1,0:T(8,128)(2,1)S(1)}, bf16[2,72,384]{2,1,0:T(8,128)(2,1)S(1)}, u32[]{:S(2)}, u32[]{:S(2)}) collective-permute-start(bf16[2,72,384]{2,1,0:T(8,128)(2,1)S(1)} %get-tuple-element.84.refs_0_), channel_id=1, source_target_pairs={{0,8},{4,12},{8,0},{12,4},{16,24},{20,28},{24,16},{28,20},{1,9},{5... | collective-permute-start | bytes 331784 | tf_op jit(solution)/shard_map/ppermute | solution.py:657
  13.0 4.6 %collective-permute-start.3 = (bf16[384,128]{1,0:T(8,128)(2,1)S(1)}, bf16[384,128]{1,0:T(8,128)(2,1)S(1)}, u32[]{:S(2)}, u32[]{:S(2)}) collective-permute-start(bf16[384,128]{1,0:T(8,128)(2,1)S(1)} %get-tuple-element.85.refs_2_), channel_id=1, source_target_pairs={{0,4},{4,0},{8,12},{12,8},{16,20},{20,16},{24,28},{28,24},{1,5},{5... | collective-permute-start | bytes 294920 | tf_op jit(solution)/shard_map/ppermute | solution.py:657
  14.5 6.4 %collective-permute-start.5 = (bf16[48,384]{1,0:T(8,128)(2,1)S(1)}, bf16[48,384]{1,0:T(8,128)(2,1)S(1)}, u32[]{:S(2)}, u32[]{:S(2)}) collective-permute-start(bf16[48,384]{1,0:T(8,128)(2,1)S(1)} %get-tuple-element.88), channel_id=1, source_target_pairs={{4,8},{12,16},{20,24},{8,4},{16,12},{24,20},{5,9},{13,17},{21,25},... | collective-permute-start | bytes 110600 | tf_op jit(solution)/shard_map/ppermute | solution.py:747
  17.7 4.9 %collective-permute-start.4 = (bf16[448,128]{1,0:T(8,128)(2,1)S(1)}, bf16[448,128]{1,0:T(8,128)(2,1)S(1)}, u32[]{:S(2)}, u32[]{:S(2)}) collective-permute-start(bf16[448,128]{1,0:T(8,128)(2,1)S(1)} %get-tuple-element.86.refs_2_.refs_1_), channel_id=1, source_target_pairs={{0,8},{4,12},{8,0},{12,4},{16,24},{20,28},{24,16},{28,20},{1,9},{5... | collective-permute-start | bytes 344072 | tf_op jit(solution)/shard_map/ppermute | solution.py:657
  18.5 6.9 %collective-permute-start.7 = (bf16[2,72,384]{2,1,0:T(8,128)(2,1)S(1)}, bf16[2,72,384]{2,1,0:T(8,128)(2,1)S(1)}, u32[]{:S(2)}, u32[]{:S(2)}) collective-permute-start(bf16[2,72,384]{2,1,0:T(8,128)(2,1)S(1)} %get-tuple-element.93), channel_id=1, source_target_pairs={{0,4},{4,0},{8,12},{12,8},{16,20},{20,16},{24,28},{28,24},{1,5},{5... | collective-permute-start | bytes 331784 | tf_op jit(solution)/shard_map/ppermute | solution.py:657
  20.9 4.7 %collective-permute-start.8 = (bf16[2,72,384]{2,1,0:T(8,128)(2,1)S(1)}, bf16[2,72,384]{2,1,0:T(8,128)(2,1)S(1)}, u32[]{:S(2)}, u32[]{:S(2)}) collective-permute-start(bf16[2,72,384]{2,1,0:T(8,128)(2,1)S(1)} %get-tuple-element.94), channel_id=1, source_target_pairs={{0,4},{4,0},{8,12},{12,8},{16,20},{20,16},{24,28},{28,24},{1,5},{5... | collective-permute-start | bytes 331784 | tf_op jit(solution)/shard_map/ppermute | solution.py:657
  20.9 4.5 %collective-permute-start.6 = (bf16[112,384]{1,0:T(8,128)(2,1)S(1)}, bf16[112,384]{1,0:T(8,128)(2,1)S(1)}, u32[]{:S(2)}, u32[]{:S(2)}) collective-permute-start(bf16[112,384]{1,0:T(8,128)(2,1)S(1)} %rim_kernel.1.refs_2_), channel_id=1, source_target_pairs={{0,1},{1,0},{2,3},{3,2},{4,5},{5,4},{6,7},{7,6},{8,9},{9,8},{10,11... | collective-permute-start | bytes 258056 | tf_op jit(solution)/shard_map/ppermute | solution.py:657
  25.6 13.7 %copy-start.1 = (f32[2,96]{1,0:T(2,128)S(1)}, f32[2,96]{1,0:T(2,128)}, u32[]{:S(2)}) copy-start(f32[2,96]{1,0:T(2,128)} %refs_18_.1) | copy-start | bytes 2308
  27.1 22.1 %collective-permute-start.12 = (bf16[11,72,384]{2,1,0:T(8,128)(2,1)S(1)}, bf16[11,72,384]{2,1,0:T(8,128)(2,1)S(1)}, u32[]{:S(2)}, u32[]{:S(2)}) collective-permute-start(bf16[11,72,384]{2,1,0:T(8,128)(2,1)S(1)} %get-tuple-element.109), channel_id=1, source_target_pairs={{0,2},{1,3},{2,0},{3,1},{4,6},{5,7},{6,4},{7,5},{8,10},{9,11},{10,... | collective-permute-start | bytes 1824776 | tf_op jit(solution)/shard_map/ppermute | solution.py:657
  28.7 10.7 %collective-permute-start.9 = (bf16[768,384]{1,0:T(8,128)(2,1)S(1)}, bf16[768,384]{1,0:T(8,128)(2,1)S(1)}, u32[]{:S(2)}, u32[]{:S(2)}) collective-permute-start(bf16[768,384]{1,0:T(8,128)(2,1)S(1)} %get-tuple-element.100.refs_3_), channel_id=1, source_target_pairs={{0,1},{1,0},{2,3},{3,2},{4,5},{5,4},{6,7},{7,6},{8,9},{9,8},{10,11... | collective-permute-start | bytes 1769480 | tf_op jit(solution)/shard_map/ppermute | solution.py:657
  49.2 5.4 %collective-permute-start.14 = (bf16[8,72,384]{2,1,0:T(8,128)(2,1)S(1)}, bf16[8,72,384]{2,1,0:T(8,128)(2,1)S(1)}, u32[]{:S(2)}, u32[]{:S(2)}) collective-permute-start(bf16[8,72,384]{2,1,0:T(8,128)(2,1)S(1)} %get-tuple-element.113.refs_0_), channel_id=1, source_target_pairs={{0,1},{1,0},{2,3},{3,2},{4,5},{5,4},{6,7},{7,6},{8,9},{9,8},{10,11... | collective-permute-start | bytes 1327112 | tf_op jit(solution)/shard_map/ppermute | solution.py:657
  49.3 3.8 %collective-permute-start.13 = (bf16[792,128]{1,0:T(8,128)(2,1)S(1)}, bf16[792,128]{1,0:T(8,128)(2,1)S(1)}, u32[]{:S(2)}, u32[]{:S(2)}) collective-permute-start(bf16[792,128]{1,0:T(8,128)(2,1)S(1)} %get-tuple-element.105.refs_1_), channel_id=1, source_target_pairs={{0,1},{1,0},{2,3},{3,2},{4,5},{5,4},{6,7},{7,6},{8,9},{9,8},{10,11... | collective-permute-start | bytes 608264 | tf_op jit(solution)/shard_map/ppermute | solution.py:657
  49.8 7.0 %collective-permute-start.15 = (bf16[792,128]{1,0:T(8,128)(2,1)S(1)}, bf16[792,128]{1,0:T(8,128)(2,1)S(1)}, u32[]{:S(2)}, u32[]{:S(2)}) collective-permute-start(bf16[792,128]{1,0:T(8,128)(2,1)S(1)} %get-tuple-element.105.refs_1_), channel_id=1, source_target_pairs={{0,2},{1,3},{2,0},{3,1},{4,6},{5,7},{6,4},{7,5},{8,10},{9,11},{10,... | collective-permute-start | bytes 608264 | tf_op jit(solution)/shard_map/ppermute | solution.py:657
  52.4 5.1 %collective-permute-start.10 = (bf16[1344,128]{1,0:T(8,128)(2,1)S(1)}, bf16[1344,128]{1,0:T(8,128)(2,1)S(1)}, u32[]{:S(2)}, u32[]{:S(2)}) collective-permute-start(bf16[1344,128]{1,0:T(8,128)(2,1)S(1)} %get-tuple-element.107.refs_1_), channel_id=1, source_target_pairs={{0,1},{1,0},{2,3},{3,2},{4,5},{5,4},{6,7},{7,6},{8,9},{9,8},{10,11... | collective-permute-start | bytes 1032200 | tf_op jit(solution)/shard_map/ppermute | solution.py:657
  52.5 9.4 %collective-permute-start.23 = (bf16[4,96,384]{2,1,0:T(8,128)(2,1)S(1)}, bf16[4,96,384]{2,1,0:T(8,128)(2,1)S(1)}, u32[]{:S(2)}, u32[]{:S(2)}) collective-permute-start(bf16[4,96,384]{2,1,0:T(8,128)(2,1)S(1)} %get-tuple-element.120), channel_id=1, source_target_pairs={{0,4},{4,0},{8,12},{12,8},{16,20},{20,16},{24,28},{28,24},{1,5},{5... | collective-permute-start | bytes 884744 | tf_op jit(solution)/shard_map/ppermute | solution.py:657
  56.8 1.5 %collective-permute-start.16 = (bf16[792,128]{1,0:T(8,128)(2,1)S(1)}, bf16[792,128]{1,0:T(8,128)(2,1)S(1)}, u32[]{:S(2)}, u32[]{:S(2)}) collective-permute-start(bf16[792,128]{1,0:T(8,128)(2,1)S(1)} %copy_kernel.1.refs_6_), channel_id=1, source_target_pairs={{0,1},{1,0},{2,3},{3,2},{4,5},{5,4},{6,7},{7,6},{8,9},{9,8},{10,11... | collective-permute-start | bytes 608264 | tf_op jit(solution)/shard_map/ppermute | solution.py:657
  56.9 8.2 %collective-permute-start.11 = (bf16[768,128]{1,0:T(8,128)(2,1)S(1)}, bf16[768,128]{1,0:T(8,128)(2,1)S(1)}, u32[]{:S(2)}, u32[]{:S(2)}) collective-permute-start(bf16[768,128]{1,0:T(8,128)(2,1)S(1)} %get-tuple-element.108), channel_id=1, source_target_pairs={{0,2},{1,3},{2,0},{3,1},{4,6},{5,7},{6,4},{7,5},{8,10},{9,11},{10,... | collective-permute-start | bytes 589832 | tf_op jit(solution)/shard_map/ppermute | solution.py:657
  60.4 4.7 %collective-permute-start.17 = (f32[2,768]{1,0:T(2,128)S(1)}, f32[2,768]{1,0:T(2,128)S(1)}, u32[]{:S(2)}, u32[]{:S(2)}) collective-permute-start(f32[2,768]{1,0:T(2,128)S(1)} %get-tuple-element.114.refs_0_), channel_id=1, source_target_pairs={{0,16},{4,20},{8,24},{12,28},{16,0},{20,4},{24,8},{28,12},{1,17},{... | collective-permute-start | bytes 18440 | tf_op jit(solution)/shard_map/ppermute | solution.py:657
  62.0 5.5 %collective-permute-start.24 = (bf16[2,96,384]{2,1,0:T(8,128)(2,1)S(1)}, bf16[2,96,384]{2,1,0:T(8,128)(2,1)S(1)}, u32[]{:S(2)}, u32[]{:S(2)}) collective-permute-start(bf16[2,96,384]{2,1,0:T(8,128)(2,1)S(1)} %get-tuple-element.122), channel_id=1, source_target_pairs={{0,8},{4,12},{8,0},{12,4},{16,24},{20,28},{24,16},{28,20},{1,9},{5... | collective-permute-start | bytes 442376 | tf_op jit(solution)/shard_map/ppermute | solution.py:657
  65.2 5.6 %collective-permute-start.19 = (bf16[848,128]{1,0:T(8,128)(2,1)S(1)}, bf16[848,128]{1,0:T(8,128)(2,1)S(1)}, u32[]{:S(2)}, u32[]{:S(2)}) collective-permute-start(bf16[848,128]{1,0:T(8,128)(2,1)S(1)} %get-tuple-element.115.refs_3_), channel_id=1, source_target_pairs={{0,1},{1,0},{2,3},{3,2},{4,5},{5,4},{6,7},{7,6},{8,9},{9,8},{10,11... | collective-permute-start | bytes 651272 | tf_op jit(solution)/shard_map/ppermute | solution.py:657
  65.2 4.0 %collective-permute-start.18 = (f32[2,768]{1,0:T(2,128)S(1)}, f32[2,768]{1,0:T(2,128)S(1)}, u32[]{:S(2)}, u32[]{:S(2)}) collective-permute-start(f32[2,768]{1,0:T(2,128)S(1)} %add_kernel.2.refs_3_.refs_0_.refs_2_), channel_id=1, source_target_pairs={{0,4},{4,0},{8,12},{12,8},{16,20},{20,16},{24,28},{28,24},{1,5},{5... | collective-permute-start | bytes 18440 | tf_op jit(solution)/shard_map/ppermute | solution.py:657
  67.5 6.1 %collective-permute-start.25 = (bf16[1,96,384]{2,1,0:T(8,128)(2,1)S(1)}, bf16[1,96,384]{2,1,0:T(8,128)(2,1)S(1)}, u32[]{:S(2)}, u32[]{:S(2)}) collective-permute-start(bf16[1,96,384]{2,1,0:T(8,128)(2,1)S(1)} %get-tuple-element.124), channel_id=1, source_target_pairs={{0,16},{4,20},{8,24},{12,28},{16,0},{20,4},{24,8},{28,12},{1,17},{... | collective-permute-start | bytes 221192 | tf_op jit(solution)/shard_map/ppermute | solution.py:657
  69.3 1.5 %collective-permute-start.21 = (bf16[272,128]{1,0:T(8,128)(2,1)S(1)}, bf16[272,128]{1,0:T(8,128)(2,1)S(1)}, u32[]{:S(2)}, u32[]{:S(2)}) collective-permute-start(bf16[272,128]{1,0:T(8,128)(2,1)S(1)} %pack_kernel.3.refs_5_), channel_id=1, source_target_pairs={{0,1},{1,0},{2,3},{3,2},{4,5},{5,4},{6,7},{7,6},{8,9},{9,8},{10,11... | collective-permute-start | bytes 208904 | tf_op jit(solution)/shard_map/ppermute | solution.py:657
  69.3 1.4 %collective-permute-start.20 = (bf16[224,128]{1,0:T(8,128)(2,1)S(1)}, bf16[224,128]{1,0:T(8,128)(2,1)S(1)}, u32[]{:S(2)}, u32[]{:S(2)}) collective-permute-start(bf16[224,128]{1,0:T(8,128)(2,1)S(1)} %get-tuple-element.116.refs_4_), channel_id=1, source_target_pairs={{0,1},{1,0},{2,3},{3,2},{4,5},{5,4},{6,7},{7,6},{8,9},{9,8},{10,11... | collective-permute-start | bytes 172040 | tf_op jit(solution)/shard_map/ppermute | solution.py:657
  69.8 3.8 %collective-permute-start.22 = (f32[2,768]{1,0:T(2,128)S(1)}, f32[2,768]{1,0:T(2,128)S(1)}, u32[]{:S(2)}, u32[]{:S(2)}) collective-permute-start(f32[2,768]{1,0:T(2,128)S(1)} %add_kernel.3.refs_1_.refs_9_.refs_4_), channel_id=1, source_target_pairs={{0,8},{4,12},{8,0},{12,4},{16,24},{20,28},{24,16},{28,20},{1,9},{5... | collective-permute-start | bytes 18440 | tf_op jit(solution)/shard_map/ppermute | solution.py:657

commit v11 on v10

--- a/solution.py
+++ b/solution.py
@@ -398,27 +398,48 @@
         grad_ref[...] = grad[...].astype(BF16)
 
 
-def out_kernel(x_ref, *refs):
+def near_kernel(*refs, slim):
+    parts, (sum_ref, token_ref, hidden, point) = refs[:-4], refs[-4:]
+    token_ref[...] = jnp.zeros_like(token_ref)
+    rows, width = hidden.shape[0], point.shape[0]
+    count, end = folded_rows(rows, slim), folded_rows(rows, slim) + folded_rows(width, slim)
+    for r, part in enumerate(parts):
+        lanes = slice(r * LANES, (r + 1) * LANES)
+        hidden[:, lanes] = get_folded(part[:count, :], rows)
+        point[:, lanes] = get_folded(part[count:end, :], width)
+    for at in range(0, width, 256):
+        part = slice(at, at + 256)
+        sum_ref[:, part] = lax.dot_general(
+            hidden[...], point[part, :], LANE_DIMS, preferred_element_type=F32
+        )
+
+
+def out_kernel(x_ref, near_ref, *refs, slim):
     parts, (out_ref, token_ref, hidden, point) = refs[:-4], refs[-4:]
     token_ref[...] = jnp.zeros_like(token_ref)
-    rows = x_ref.shape[0]
-    side = hidden.shape[1] // LANES // 2
-    for r in range(2 * side):
-        if r < side:
-            part = parts[r][...]
-        else:
-            at = side + 3 * (r - side)
-            part = jnp.concatenate([piece[...] for piece in parts[at : at + 3]], axis=0)
-        width = point.shape[0]
-        count = part.shape[0] * rows // (rows + width)
-        hidden[:, r * LANES : (r + 1) * LANES] = get_folded(part[:count, :], rows)
-        point[:, r * LANES : (r + 1) * LANES] = get_folded(part[count:, :], width)
-    for at in range(0, x_ref.shape[1], 256):
+    rows, width = x_ref.shape
+    count, end = folded_rows(rows, slim), folded_rows(rows, slim) + folded_rows(width, slim)
+    for r in range(len(parts) // 3):
+        lanes = slice(r * LANES, (r + 1) * LANES)
+        first, middle, last = parts[3 * r : 3 * r + 3]
+        hidden[:, lanes] = get_folded(middle[:count, :], rows)
+        pieces = [first[end:, :], middle[count:, :], last[...]]
+        point[:, lanes] = get_folded(jnp.concatenate(pieces, axis=0), width)
+    for at in range(0, width, 256):
         part = slice(at, at + 256)
-        branch = lax.dot_general(
+        branch = near_ref[:, part] + lax.dot_general(
             hidden[...], point[part, :], LANE_DIMS, preferred_element_type=F32
         )
         out_ref[:, part] = (x_ref[:, part].astype(F32) + branch).astype(BF16)
+
+
+def operands_kernel(mid_ref, point_ref, far_ref, pack_ref, both_ref):
+    put_folded(mid_ref[...], pack_ref)
+    at = 0
+    for src in (pack_ref, point_ref):
+        both_ref[at : at + src.shape[0], :] = src[...]
+        at += src.shape[0]
+    both_ref[at:, :] = far_ref[: both_ref.shape[0] - at, :]
 
 
 def halve(blocks, kept_ref, sent_ref, high):
@@ -450,12 +471,8 @@
 
 
 def weight_grad_kernel(
-    mask_ref, part_ref, hid_ref, cot_ref, mid_ref, point_ref, term_ref, kept_ref, sent_ref, pack_ref, both_ref, grad, full, *, depth, slim
+    mask_ref, part_ref, hid_ref, cot_ref, mid_ref, term_ref, kept_ref, sent_ref, grad, full, *, depth, slim
 ):
-    put_folded(mid_ref[...], pack_ref)
-    both_ref[: pack_ref.shape[0], :] = pack_ref[...]
-    both_ref[pack_ref.shape[0] :, :] = point_ref[...]
-
     rows = term_ref.shape[0]
     terms_of(part_ref, grad, term_ref, 0, mask_ref)
     taps = lax.dot_general(
@@ -693,7 +710,7 @@
     wide = KERNEL_WIDTH * LANES
     weight_order = descending(seq_size)
     sum_order = weight_order[::-1]
-    last_order = weight_order[:1] + sum_order[:-1]
+    last_order = weight_order[1::-1] + weight_order[2:]
     point_order = weight_order[:1] + [1] + weight_order[1:-1]
     ch_order = descending(ch_size)
     ext = rows + 2 * EDGE
@@ -827,16 +844,14 @@
     )
     half = seq_size // 2
     hidden_rows = folded_rows(rows, slim)
-    terms, kept, sent, hidden_pack, both = call(
+    terms, kept, sent = call(
         functools.partial(weight_grad_kernel, depth=depth, slim=slim),
         [
             ((rows, wide), BF16),
             ((half, depth, 4 * slim), F32),
             ((half, depth, 4 * slim), BF16),
-            ((hidden_rows, LANES), BF16),
-            ((hidden_rows + point_pack.shape[0], LANES), BF16),
         ],
-        [back, grad_own, hidden_in, cotangent, hidden_mid, point_pack],
+        [back, grad_own, hidden_in, cotangent, hidden_mid],
         scratch=[((ext, LANES), F32), ((width, 4 * slim), F32)],
     )
     (up_part,) = call(
@@ -846,18 +861,25 @@
         scratch=[((rows, side), BF16), ((width, side), BF16), ((ext, LANES), F32)],
     )
     grad_far = gather_parts(copies([grad_far], [up_part, conv_far])[0], lower)
+    count = point_far.shape[0]
+    cuts = [up_to(k * count // 100, 16) for k in (39, 52)]
+    hidden_pack, both = call(
+        operands_kernel,
+        [((hidden_rows, LANES), BF16), ((hidden_rows + count + cuts[0], LANES), BF16)],
+        [hidden_mid, point_pack, point_far],
+        after=[sent],
+    )
     both_parts = gather_parts(both, lower)
     d_in, sums_back = call(
         second_half_kernel,
         [((rows, width), F32), ((2, width), F32)],
         [back, inputs, slope_in, vec_in, up_part, conv_far, *grad_far],
         scratch=[((rows, side), BF16), ((ext, LANES), F32)],
-        after=both_parts[1:],
     )
     total_back = sums_back
     hidden_far = swap(hidden_pack, "ch", top)
-    count = point_far.shape[0]
-    cuts = [0, up_to(13 * count // 100, 16), up_to(52 * count // 100, 16), count]
+    placed = []
+    scratch = [((size, ch_size // 2 * LANES), BF16) for size in (rows, width)]
     for k, reach in enumerate(sum_order):
         total_got = swap(total_back, "seq", last_order[k])
         got = swap(sent, "seq", reach)
@@ -867,21 +889,28 @@
                 functools.partial(fold_kernel, reach=2 * reach),
                 [((half, depth, 4 * slim), F32), ((half, depth, 4 * slim), BF16)],
                 [kept, got],
-                after=[total_back] if k else [],
+                after=[total_back, *placed] if k else [],
             )
             total_back = add(total_back, total_got)
         if k == rounds - 3:
-            wanted = [[hidden_far, (point_far, *cuts[:2])], [(point_far, *cuts[1:3])]]
-            far_parts = [gather_parts(x, lower) for x in packs(wanted, [total_back])]
+            (first,) = packs([[hidden_far, (point_far, *cuts)]], [total_back])
+            first_parts = gather_parts(first, lower)
+            near_sum, *placed = call(
+                functools.partial(near_kernel, slim=slim),
+                [((rows, width), F32), ((8, LANES), F32)],
+                both_parts,
+                scratch=scratch,
+                after=[total_back],
+            )
         if k == rounds - 2:
-            (last,) = packs([[(point_far, *cuts[2:])]], [total_back])
-            far_parts.append(gather_parts(last, lower))
-    both_parts += [part for group in zip(*far_parts) for part in group]
+            (last,) = packs([[(point_far, cuts[1], count)]], [total_back])
+            last_parts = gather_parts(last, lower)
+    far_parts = [x for group in zip(both_parts, first_parts, last_parts) for x in group]
     block_out, token = call(
-        out_kernel,
+        functools.partial(out_kernel, slim=slim),
         [((rows, width), BF16), ((8, LANES), F32)],
-        [inputs, *both_parts],
-        scratch=[((rows, ch_size * LANES), BF16), ((width, ch_size * LANES), BF16)],
+        [inputs, near_sum, *far_parts],
+        scratch=scratch,
         after=[total_back],
     )
     states = [norm_in, first_in, second_in, master_conv, first_conv, second_conv]

time: 76.9 us -> 76 us (0.988)
  waiting for transfers between devices: 15.9 us -> 14.3 us
    ppermute x25 -> x24, waiting for transfers between devices: 15.9 us -> 14.3 us  [swap(): return lax.ppermute(x, axis, flip(axis, reach))]
    pallas_call x24 -> x26, Pallas kernels: 20.2 us -> 20.6 us  [call(): pl.pallas_call(kernel, out_shape=[jax.ShapeDtypeStruct(s, t) for s, t in...]
    ppermute x25 -> x24, starting transfers between devices: 19.2 us -> 19.5 us  [swap(): return lax.ppermute(x, axis, flip(axis, reach))]
  transfers between devices with their start and end apart: 26 -> 25, of which waited for: 11 -> 13; matrix products, arithmetic and copies ran while one was open for 0% -> 0% of each run, Pallas kernels for 18% -> 19%
where the time goes in v11:
time: 76 us; the launch traced here: 75.7 us
  Pallas kernels  20.6 us (27%)
  starting transfers between devices  20.2 us (27%)
  blocking collectives  19.6 us (26%)
  waiting for transfers between devices  14.3 us (19%)
  between operations  1.05 us (1%)
    pallas_call x26, Pallas kernels, call(): pl.pallas_call(kernel, out_shape=[jax.ShapeDtypeStruct(s, t) for s, t in...  20.6 us
    all_to_all x2, blocking collectives, spread(): return lax.all_to_all(copies, axes, 0, 0, tiled=True)  19.6 us
    ppermute x24, starting transfers between devices, swap(): return lax.ppermute(x, axis, flip(axis, reach))  19.5 us
    ppermute x24, waiting for transfers between devices, swap(): return lax.ppermute(x, axis, flip(axis, reach))  14.3 us
  transfers between devices with their start and end apart: 25, of which 13 were waited for; matrix products, arithmetic and copies ran while one was open for 0% of the time, Pallas kernels for 19%

profile of v11, /device:TPU:0, one launch (start us, length us, event | category | flops | bytes accessed | tf_op | source)
XLA Modules:
  0.0 75.7 jit_solution(4598393822401696150)
XLA Ops:
  0.7 1.7 %first_kernel.1 = (bf16[1024,768]{1,0:T(8,128)(2,1)S(1)}, bf16[1,72,384]{2,1,0:T(8,128)(2,1)S(1)}, bf16[144,128]{1,0:T(8,128)(2,1)S(1)}, bf16[48,384]{1,0:T(8,128)(2,1)S(1)}, bf16[48,384]{1,0:T(8,128)(2,1)S(1)}) custom-call(bf16[1024,768]{1,0:T(8,128)(2,1)} %refs_0_.2, bf16[1024,768]{1,0:T(8,128)(2,1)} %refs_1_.3, f32[3,96,96]{2,1,0:T(8,128)} %refs_12_.1, ...), custom_call_target="tpu_custom_call" | custom-call | flops 1 | bytes 1 | tf_op jit(solution)/shard_map/first_kernel/pallas_call | solution.py:48
  2.4 4.1 %collective-permute-start = (bf16[1,72,384]{2,1,0:T(8,128)(2,1)S(1)}, bf16[1,72,384]{2,1,0:T(8,128)(2,1)S(1)}, u32[]{:S(2)}, u32[]{:S(2)}) collective-permute-start(bf16[1,72,384]{2,1,0:T(8,128)(2,1)S(1)} %get-tuple-element.78.refs_1_.refs_0_), channel_id=1, source_target_pairs={{0,16},{4,20},{8,24},{12,28},{16,0},{20,4},{24,8},{28,12},{1,17},{... | collective-permute-start | bytes 165896 | tf_op jit(solution)/shard_map/ppermute | solution.py:674
  6.6 1.4 %mask_kernel.1 = (f32[3,1056,128]{2,1,0:T(8,128)S(1)}, f32[3,1024,128]{2,1,0:T(8,128)S(1)}) custom-call(s32[8]{0:T(128)S(1)} %copy-done.2, bf16[1,72,384]{2,1,0:T(8,128)(2,1)S(1)} %get-tuple-element.78.refs_1_.refs_0_), custom_call_target="tpu_custom_call" | custom-call | flops 1 | bytes 1 | tf_op jit(solution)/shard_map/mask_kernel/pallas_call | solution.py:48
  8.0 3.3 %collective-permute-done.1.refs_3_ = bf16[144,128]{1,0:T(8,128)(2,1)S(1)} collective-permute-done((bf16[144,128]{1,0:T(8,128)(2,1)S(1)}, bf16[144,128]{1,0:T(8,128)(2,1)S(1)}, u32[]{:S(2)}, u32[]{:S(2)}) %collective-permute-start.1) | collective-permute-done | bytes 36896 | tf_op jit(solution)/shard_map/ppermute | solution.py:674
  11.4 1.6 %collective-permute-start.2 = (bf16[2,72,384]{2,1,0:T(8,128)(2,1)S(1)}, bf16[2,72,384]{2,1,0:T(8,128)(2,1)S(1)}, u32[]{:S(2)}, u32[]{:S(2)}) collective-permute-start(bf16[2,72,384]{2,1,0:T(8,128)(2,1)S(1)} %get-tuple-element.84.refs_0_), channel_id=1, source_target_pairs={{0,8},{4,12},{8,0},{12,4},{16,24},{20,28},{24,16},{28,20},{1,9},{5... | collective-permute-start | bytes 331784 | tf_op jit(solution)/shard_map/ppermute | solution.py:674
  13.0 1.5 %collective-permute-start.3 = (bf16[384,128]{1,0:T(8,128)(2,1)S(1)}, bf16[384,128]{1,0:T(8,128)(2,1)S(1)}, u32[]{:S(2)}, u32[]{:S(2)}) collective-permute-start(bf16[384,128]{1,0:T(8,128)(2,1)S(1)} %get-tuple-element.85.refs_2_), channel_id=1, source_target_pairs={{0,4},{4,0},{8,12},{12,8},{16,20},{20,16},{24,28},{28,24},{1,5},{5... | collective-permute-start | bytes 294920 | tf_op jit(solution)/shard_map/ppermute | solution.py:674
  14.5 0.7 collective-permute-start.5
  15.2 2.5 %collective-permute-done.3.refs_3_.refs_0_ = bf16[384,128]{1,0:T(8,128)(2,1)S(1)} collective-permute-done((bf16[384,128]{1,0:T(8,128)(2,1)S(1)}, bf16[384,128]{1,0:T(8,128)(2,1)S(1)}, u32[]{:S(2)}, u32[]{:S(2)}) %collective-permute-start.3) | collective-permute-done | bytes 98336 | tf_op jit(solution)/shard_map/ppermute | solution.py:674
  17.7 0.9 %collective-permute-start.4 = (bf16[448,128]{1,0:T(8,128)(2,1)S(1)}, bf16[448,128]{1,0:T(8,128)(2,1)S(1)}, u32[]{:S(2)}, u32[]{:S(2)}) collective-permute-start(bf16[448,128]{1,0:T(8,128)(2,1)S(1)} %get-tuple-element.86.refs_2_.refs_1_), channel_id=1, source_target_pairs={{0,8},{4,12},{8,0},{12,4},{16,24},{20,28},{24,16},{28,20},{1,9},{5... | collective-permute-start | bytes 344072 | tf_op jit(solution)/shard_map/ppermute | solution.py:674
  18.5 2.3 %collective-permute-start.7 = (bf16[2,72,384]{2,1,0:T(8,128)(2,1)S(1)}, bf16[2,72,384]{2,1,0:T(8,128)(2,1)S(1)}, u32[]{:S(2)}, u32[]{:S(2)}) collective-permute-start(bf16[2,72,384]{2,1,0:T(8,128)(2,1)S(1)} %get-tuple-element.93), channel_id=1, source_target_pairs={{0,4},{4,0},{8,12},{12,8},{16,20},{20,16},{24,28},{28,24},{1,5},{5... | collective-permute-start | bytes 331784 | tf_op jit(solution)/shard_map/ppermute | solution.py:674
  21.0 1.5 %collective-permute-done.4.refs_3_.refs_2_ = bf16[448,128]{1,0:T(8,128)(2,1)S(1)} collective-permute-done((bf16[448,128]{1,0:T(8,128)(2,1)S(1)}, bf16[448,128]{1,0:T(8,128)(2,1)S(1)}, u32[]{:S(2)}, u32[]{:S(2)}) %collective-permute-start.4) | collective-permute-done | bytes 114720 | tf_op jit(solution)/shard_map/ppermute | solution.py:674
  22.5 2.3 %act_kernel.1 = (bf16[1024,768]{1,0:T(8,128)(2,1)S(1)}, f32[1024,768]{1,0:T(8,128)S(1)}, f32[8,768]{1,0:T(8,128)S(1)}, bf16[1024,768]{1,0:T(8,128)(2,1)S(1)}) custom-call(bf16[1024,768]{1,0:T(8,128)(2,1)S(1)} %get-tuple-element.77.refs_0_.refs_1_, bf16[1024,768]{1,0:T(8,128)(2,1)} %refs_1_.3, bf16[448,128]{1,0:T(8,128)(2,1)S(1)} %get-tuple-element.86.refs_2_.refs_1_, ...), custom_call_target="tpu_custom_call" | custom-call | flops 1 | bytes 1 | tf_op jit(solution)/shard_map/act_kernel/pallas_call | solution.py:48
  25.6 1.4 %conv_kernel.1 = (bf16[768,384]{1,0:T(8,128)(2,1)S(1)}, f32[1056,128]{1,0:T(8,128)S(1)}, f32[8,2,128]{2,1,0:T(2,128)S(1)}, bf16[2,48,768]{2,1,0:T(8,128)(2,1)S(1)}, bf16[11,72,384]{2,1,0:T(8,128)(2,1)S(1)}) custom-call(f32[3,1056,128]{2,1,0:T(8,128)S(1)} %get-tuple-element.79.refs_0_, bf16[1024,768]{1,0:T(8,128)(2,1)S(1)} %get-tuple-element.87.refs_1_.refs_2_, ...), custom_call_target="tpu_custom_call" | custom-call | flops 1 | bytes 1 | tf_op jit(solution)/shard_map/conv_kernel/pallas_call | solution.py:48
  27.1 1.6 %collective-permute-start.10 = (bf16[11,72,384]{2,1,0:T(8,128)(2,1)S(1)}, bf16[11,72,384]{2,1,0:T(8,128)(2,1)S(1)}, u32[]{:S(2)}, u32[]{:S(2)}) collective-permute-start(bf16[11,72,384]{2,1,0:T(8,128)(2,1)S(1)} %get-tuple-element.102), channel_id=1, source_target_pairs={{0,2},{1,3},{2,0},{3,1},{4,6},{5,7},{6,4},{7,5},{8,10},{9,11},{10,... | collective-permute-start | bytes 1824776 | tf_op jit(solution)/shard_map/ppermute | solution.py:674
  28.7 10.7 %all_to_all.10.refs_0_ = f32[8,2,128]{2,1,0:T(2,128)S(1)} all-to-all(f32[8,2,128]{2,1,0:T(2,128)S(1)} %get-tuple-element.96), channel_id=1, replica_groups=mesh['seq'=8,'ch'=4] {'seq'}, dimensions={0} | all-to-all | bytes 16384 | tf_op jit(solution)/shard_map/all_to_all | solution.py:685
  39.3 0.7 mid_kernel.1
  40.0 8.9 %all_to_all.11.refs_0_ = f32[8,2,128]{2,1,0:T(2,128)S(1)} all-to-all(f32[8,2,128]{2,1,0:T(2,128)S(1)} %get-tuple-element.103), channel_id=1, replica_groups=mesh['seq'=8,'ch'=4] {'seq'}, dimensions={0} | all-to-all | bytes 16384 | tf_op jit(solution)/shard_map/all_to_all | solution.py:685
  50.3 2.0 %weight_grad_kernel.1 = (bf16[1024,384]{1,0:T(8,128)(2,1)S(1)}, f32[4,96,384]{2,1,0:T(8,128)S(1)}, bf16[4,96,384]{2,1,0:T(8,128)(2,1)S(1)}) custom-call(f32[3,1024,128]{2,1,0:T(8,128)S(1)} %get-tuple-element.83.refs_6_.refs_0_, bf16[792,128]{1,0:T(8,128)(2,1)S(1)} %get-tuple-element.107.refs_1_, bf16[1024,768]{1,0:T(8,128)(2,1)S(1)} %get-tuple-element.87.refs_1_.refs_2_, ...), custom_call_target="tpu_custom_call" | custom-call | flops 1 | bytes 1 | tf_op jit(solution)/shard_map/weight_grad_kernel/pallas_call | solution.py:48
  53.2 1.6 %first_half_kernel.1.refs_1_.refs_4_ = f32[1024,768]{1,0:T(8,128)S(1)} custom-call(f32[3,1024,128]{2,1,0:T(8,128)S(1)} %get-tuple-element.83.refs_6_.refs_0_, bf16[1024,384]{1,0:T(8,128)(2,1)S(1)} %get-tuple-element.112.refs_1_, bf16[792,128]{1,0:T(8,128)(2,1)S(1)} %collective-permute-done.12.refs_2_, bf16[768,384]{1,0:T(8,128)(2,1)S(1)} %get-tuple-element.100.refs_3_, ...), custom_call_target="tpu_custom_call" | custom-call | flops 1 | bytes 1 | tf_op jit(solution)/shard_map/first_half_kernel/pallas_call | solution.py:48
  55.3 1.5 %collective-permute-done.14.refs_0_ = bf16[792,128]{1,0:T(8,128)(2,1)S(1)} collective-permute-done((bf16[792,128]{1,0:T(8,128)(2,1)S(1)}, bf16[792,128]{1,0:T(8,128)(2,1)S(1)}, u32[]{:S(2)}, u32[]{:S(2)}) %collective-permute-start.14) | collective-permute-done | bytes 202784 | tf_op jit(solution)/shard_map/ppermute | solution.py:674
  57.5 0.9 %collective-permute-done.15.refs_7_ = bf16[792,128]{1,0:T(8,128)(2,1)S(1)} collective-permute-done((bf16[792,128]{1,0:T(8,128)(2,1)S(1)}, bf16[792,128]{1,0:T(8,128)(2,1)S(1)}, u32[]{:S(2)}, u32[]{:S(2)}) %collective-permute-start.15) | collective-permute-done | bytes 202784 | tf_op jit(solution)/shard_map/ppermute | solution.py:674
  58.4 2.0 %second_half_kernel.1 = (f32[1024,768]{1,0:T(8,128)S(1)}, f32[2,768]{1,0:T(2,128)S(1)}) custom-call(f32[3,1024,128]{2,1,0:T(8,128)S(1)} %get-tuple-element.83.refs_6_.refs_0_, bf16[1024,768]{1,0:T(8,128)(2,1)S(1)} %get-tuple-element.77.refs_0_.refs_1_, f32[1024,768]{1,0:T(8,128)S(1)} %get-tuple-element.111.refs_2_, ...), custom_call_target="tpu_custom_call" | custom-call | flops 1 | bytes 1 | tf_op jit(solution)/shard_map/second_half_kernel/pallas_call | solution.py:48
  61.1 1.5 %collective-permute-start.23 = (bf16[2,96,384]{2,1,0:T(8,128)(2,1)S(1)}, bf16[2,96,384]{2,1,0:T(8,128)(2,1)S(1)}, u32[]{:S(2)}, u32[]{:S(2)}) collective-permute-start(bf16[2,96,384]{2,1,0:T(8,128)(2,1)S(1)} %get-tuple-element.121), channel_id=1, source_target_pairs={{0,8},{4,12},{8,0},{12,4},{16,24},{20,28},{24,16},{28,20},{1,9},{5... | collective-permute-start | bytes 442376 | tf_op jit(solution)/shard_map/ppermute | solution.py:674
  62.6 1.5 %collective-permute-done.16.refs_1_ = f32[2,768]{1,0:T(2,128)S(1)} collective-permute-done((f32[2,768]{1,0:T(2,128)S(1)}, f32[2,768]{1,0:T(2,128)S(1)}, u32[]{:S(2)}, u32[]{:S(2)}) %collective-permute-start.16) | collective-permute-done | bytes 6176 | tf_op jit(solution)/shard_map/ppermute | solution.py:674
  64.3 0.6 collective-permute-start.18
  65.0 0.8 %near_kernel.1 = (f32[1024,768]{1,0:T(8,128)S(1)}, f32[8,128]{1,0:T(8,128)S(1)}) custom-call(bf16[1568,128]{1,0:T(8,128)(2,1)S(1)} %get-tuple-element.110.refs_0_.refs_2_, bf16[1568,128]{1,0:T(8,128)(2,1)S(1)} %collective-permute-done.11.refs_1_.refs_5_, f32[2,768]{1,0:T(2,128)S(1)} %add_kernel.2.refs_2_.refs_0_), custom_call_target="tpu_custom_call" | custom-call | flops 1 | bytes 1 | tf_op jit(solution)/shard_map/near_kernel/pallas_call | solution.py:48
  65.8 1.0 %collective-permute-done.23.refs_1_ = bf16[2,96,384]{2,1,0:T(8,128)(2,1)S(1)} collective-permute-done((bf16[2,96,384]{2,1,0:T(8,128)(2,1)S(1)}, bf16[2,96,384]{2,1,0:T(8,128)(2,1)S(1)}, u32[]{:S(2)}, u32[]{:S(2)}) %collective-permute-start.23) | collective-permute-done | bytes 147488 | tf_op jit(solution)/shard_map/ppermute | solution.py:674
  66.8 1.5 %collective-permute-start.24 = (bf16[1,96,384]{2,1,0:T(8,128)(2,1)S(1)}, bf16[1,96,384]{2,1,0:T(8,128)(2,1)S(1)}, u32[]{:S(2)}, u32[]{:S(2)}) collective-permute-start(bf16[1,96,384]{2,1,0:T(8,128)(2,1)S(1)} %get-tuple-element.124), channel_id=1, source_target_pairs={{0,16},{4,20},{8,24},{12,28},{16,0},{20,4},{24,8},{28,12},{1,17},{... | collective-permute-start | bytes 221192 | tf_op jit(solution)/shard_map/ppermute | solution.py:674
  68.3 0.7 collective-permute-done.18.refs_1_
  69.0 0.7 collective-permute-start.21
  70.3 2.0 %out_kernel.1 = (bf16[1024,768]{1,0:T(8,128)(2,1)}, f32[8,128]{1,0:T(8,128)S(1)}) custom-call(bf16[1024,768]{1,0:T(8,128)(2,1)S(1)} %get-tuple-element.77.refs_0_.refs_1_, f32[1024,768]{1,0:T(8,128)S(1)} %get-tuple-element.115.refs_1_, bf16[1568,128]{1,0:T(8,128)(2,1)S(1)} %get-tuple-element.110.refs_0_.refs_2_, bf16[848,128]{1,0:T(8,128)(2,1)S(1)} %pack_kernel.2.refs_3_, ...), custom_call_target="tpu_custom_call" | custom-call | flops 1 | bytes 1 | tf_op jit(solution)/shard_map/out_kernel/pallas_call | solution.py:48
  72.7 2.8 %final_kernel.1 = (f32[1024,768]{1,0:T(8,128)}, f32[2,768]{1,0:T(2,128)}, f32[2,768]{1,0:T(2,128)}, f32[2,768]{1,0:T(2,128)}, f32[3,96,96]{2,1,0:T(8,128)}, /*in...) custom-call(bf16[1024,768]{1,0:T(8,128)(2,1)S(1)} %get-tuple-element, ...), custom_call_target="tpu_custom_call" | custom-call | flops 1 | bytes 1 | tf_op jit(solution)/shard_map/final_kernel/pallas_call | solution.py:48
  (52 shorter events, 6.7 us)
Async XLA Ops:
  0.6 5.9 %copy-start.2 = (s32[8]{0:T(128)S(1)}, s32[8]{0:T(128)}, u32[]{:S(2)}) copy-start(s32[8]{0:T(128)} %refs_0_.3) | copy-start | bytes 100
  2.4 20.2 %copy-start = (f32[2,768]{1,0:T(2,128)S(1)}, f32[2,768]{1,0:T(2,128)}, u32[]{:S(2)}) copy-start(f32[2,768]{1,0:T(2,128)} %refs_9_.1) | copy-start | bytes 18436
  2.4 9.0 %collective-permute-start = (bf16[1,72,384]{2,1,0:T(8,128)(2,1)S(1)}, bf16[1,72,384]{2,1,0:T(8,128)(2,1)S(1)}, u32[]{:S(2)}, u32[]{:S(2)}) collective-permute-start(bf16[1,72,384]{2,1,0:T(8,128)(2,1)S(1)} %get-tuple-element.78.refs_1_.refs_0_), channel_id=1, source_target_pairs={{0,16},{4,20},{8,24},{12,28},{16,0},{20,4},{24,8},{28,12},{1,17},{... | collective-permute-start | bytes 165896 | tf_op jit(solution)/shard_map/ppermute | solution.py:674
  6.5 4.9 %collective-permute-start.1 = (bf16[144,128]{1,0:T(8,128)(2,1)S(1)}, bf16[144,128]{1,0:T(8,128)(2,1)S(1)}, u32[]{:S(2)}, u32[]{:S(2)}) collective-permute-start(bf16[144,128]{1,0:T(8,128)(2,1)S(1)} %get-tuple-element.80.refs_2_), channel_id=1, source_target_pairs={{0,16},{4,20},{8,24},{12,28},{16,0},{20,4},{24,8},{28,12},{1,17},{... | collective-permute-start | bytes 110600 | tf_op jit(solution)/shard_map/ppermute | solution.py:674
  11.4 6.3 %collective-permute-start.2 = (bf16[2,72,384]{2,1,0:T(8,128)(2,1)S(1)}, bf16[2,72,384]{2,1,0:T(8,128)(2,1)S(1)}, u32[]{:S(2)}, u32[]{:S(2)}) collective-permute-start(bf16[2,72,384]{2,1,0:T(8,128)(2,1)S(1)} %get-tuple-element.84.refs_0_), channel_id=1, source_target_pairs={{0,8},{4,12},{8,0},{12,4},{16,24},{20,28},{24,16},{28,20},{1,9},{5... | collective-permute-start | bytes 331784 | tf_op jit(solution)/shard_map/ppermute | solution.py:674
  13.0 4.6 %collective-permute-start.3 = (bf16[384,128]{1,0:T(8,128)(2,1)S(1)}, bf16[384,128]{1,0:T(8,128)(2,1)S(1)}, u32[]{:S(2)}, u32[]{:S(2)}) collective-permute-start(bf16[384,128]{1,0:T(8,128)(2,1)S(1)} %get-tuple-element.85.refs_2_), channel_id=1, source_target_pairs={{0,4},{4,0},{8,12},{12,8},{16,20},{20,16},{24,28},{28,24},{1,5},{5... | collective-permute-start | bytes 294920 | tf_op jit(solution)/shard_map/ppermute | solution.py:674
  14.5 6.4 %collective-permute-start.5 = (bf16[48,384]{1,0:T(8,128)(2,1)S(1)}, bf16[48,384]{1,0:T(8,128)(2,1)S(1)}, u32[]{:S(2)}, u32[]{:S(2)}) collective-permute-start(bf16[48,384]{1,0:T(8,128)(2,1)S(1)} %get-tuple-element.88), channel_id=1, source_target_pairs={{4,8},{12,16},{20,24},{8,4},{16,12},{24,20},{5,9},{13,17},{21,25},... | collective-permute-start | bytes 110600 | tf_op jit(solution)/shard_map/ppermute | solution.py:764
  17.7 4.9 %collective-permute-start.4 = (bf16[448,128]{1,0:T(8,128)(2,1)S(1)}, bf16[448,128]{1,0:T(8,128)(2,1)S(1)}, u32[]{:S(2)}, u32[]{:S(2)}) collective-permute-start(bf16[448,128]{1,0:T(8,128)(2,1)S(1)} %get-tuple-element.86.refs_2_.refs_1_), channel_id=1, source_target_pairs={{0,8},{4,12},{8,0},{12,4},{16,24},{20,28},{24,16},{28,20},{1,9},{5... | collective-permute-start | bytes 344072 | tf_op jit(solution)/shard_map/ppermute | solution.py:674
  18.5 6.9 %collective-permute-start.7 = (bf16[2,72,384]{2,1,0:T(8,128)(2,1)S(1)}, bf16[2,72,384]{2,1,0:T(8,128)(2,1)S(1)}, u32[]{:S(2)}, u32[]{:S(2)}) collective-permute-start(bf16[2,72,384]{2,1,0:T(8,128)(2,1)S(1)} %get-tuple-element.93), channel_id=1, source_target_pairs={{0,4},{4,0},{8,12},{12,8},{16,20},{20,16},{24,28},{28,24},{1,5},{5... | collective-permute-start | bytes 331784 | tf_op jit(solution)/shard_map/ppermute | solution.py:674
  20.9 4.7 %collective-permute-start.8 = (bf16[2,72,384]{2,1,0:T(8,128)(2,1)S(1)}, bf16[2,72,384]{2,1,0:T(8,128)(2,1)S(1)}, u32[]{:S(2)}, u32[]{:S(2)}) collective-permute-start(bf16[2,72,384]{2,1,0:T(8,128)(2,1)S(1)} %get-tuple-element.94), channel_id=1, source_target_pairs={{0,4},{4,0},{8,12},{12,8},{16,20},{20,16},{24,28},{28,24},{1,5},{5... | collective-permute-start | bytes 331784 | tf_op jit(solution)/shard_map/ppermute | solution.py:674
  20.9 4.5 %collective-permute-start.6 = (bf16[112,384]{1,0:T(8,128)(2,1)S(1)}, bf16[112,384]{1,0:T(8,128)(2,1)S(1)}, u32[]{:S(2)}, u32[]{:S(2)}) collective-permute-start(bf16[112,384]{1,0:T(8,128)(2,1)S(1)} %rim_kernel.1.refs_2_), channel_id=1, source_target_pairs={{0,1},{1,0},{2,3},{3,2},{4,5},{5,4},{6,7},{7,6},{8,9},{9,8},{10,11... | collective-permute-start | bytes 258056 | tf_op jit(solution)/shard_map/ppermute | solution.py:674
  25.6 13.7 %copy-start.1 = (f32[2,96]{1,0:T(2,128)S(1)}, f32[2,96]{1,0:T(2,128)}, u32[]{:S(2)}) copy-start(f32[2,96]{1,0:T(2,128)} %refs_18_.1) | copy-start | bytes 2308
  27.1 22.1 %collective-permute-start.10 = (bf16[11,72,384]{2,1,0:T(8,128)(2,1)S(1)}, bf16[11,72,384]{2,1,0:T(8,128)(2,1)S(1)}, u32[]{:S(2)}, u32[]{:S(2)}) collective-permute-start(bf16[11,72,384]{2,1,0:T(8,128)(2,1)S(1)} %get-tuple-element.102), channel_id=1, source_target_pairs={{0,2},{1,3},{2,0},{3,1},{4,6},{5,7},{6,4},{7,5},{8,10},{9,11},{10,... | collective-permute-start | bytes 1824776 | tf_op jit(solution)/shard_map/ppermute | solution.py:674
  28.7 10.7 %collective-permute-start.9 = (bf16[768,384]{1,0:T(8,128)(2,1)S(1)}, bf16[768,384]{1,0:T(8,128)(2,1)S(1)}, u32[]{:S(2)}, u32[]{:S(2)}) collective-permute-start(bf16[768,384]{1,0:T(8,128)(2,1)S(1)} %get-tuple-element.100.refs_3_), channel_id=1, source_target_pairs={{0,1},{1,0},{2,3},{3,2},{4,5},{5,4},{6,7},{7,6},{8,9},{9,8},{10,11... | collective-permute-start | bytes 1769480 | tf_op jit(solution)/shard_map/ppermute | solution.py:674
  49.2 5.6 %collective-permute-start.13 = (bf16[8,72,384]{2,1,0:T(8,128)(2,1)S(1)}, bf16[8,72,384]{2,1,0:T(8,128)(2,1)S(1)}, u32[]{:S(2)}, u32[]{:S(2)}) collective-permute-start(bf16[8,72,384]{2,1,0:T(8,128)(2,1)S(1)} %get-tuple-element.113.refs_0_), channel_id=1, source_target_pairs={{0,1},{1,0},{2,3},{3,2},{4,5},{5,4},{6,7},{7,6},{8,9},{9,8},{10,11... | collective-permute-start | bytes 1327112 | tf_op jit(solution)/shard_map/ppermute | solution.py:674
  49.3 3.9 %collective-permute-start.12 = (bf16[792,128]{1,0:T(8,128)(2,1)S(1)}, bf16[792,128]{1,0:T(8,128)(2,1)S(1)}, u32[]{:S(2)}, u32[]{:S(2)}) collective-permute-start(bf16[792,128]{1,0:T(8,128)(2,1)S(1)} %get-tuple-element.107.refs_1_), channel_id=1, source_target_pairs={{0,1},{1,0},{2,3},{3,2},{4,5},{5,4},{6,7},{7,6},{8,9},{9,8},{10,11... | collective-permute-start | bytes 608264 | tf_op jit(solution)/shard_map/ppermute | solution.py:674
  49.8 7.0 %collective-permute-start.14 = (bf16[792,128]{1,0:T(8,128)(2,1)S(1)}, bf16[792,128]{1,0:T(8,128)(2,1)S(1)}, u32[]{:S(2)}, u32[]{:S(2)}) collective-permute-start(bf16[792,128]{1,0:T(8,128)(2,1)S(1)} %get-tuple-element.107.refs_1_), channel_id=1, source_target_pairs={{0,2},{1,3},{2,0},{3,1},{4,6},{5,7},{6,4},{7,5},{8,10},{9,11},{10,... | collective-permute-start | bytes 608264 | tf_op jit(solution)/shard_map/ppermute | solution.py:674
  52.3 8.8 %collective-permute-start.22 = (bf16[4,96,384]{2,1,0:T(8,128)(2,1)S(1)}, bf16[4,96,384]{2,1,0:T(8,128)(2,1)S(1)}, u32[]{:S(2)}, u32[]{:S(2)}) collective-permute-start(bf16[4,96,384]{2,1,0:T(8,128)(2,1)S(1)} %get-tuple-element.109.refs_3_), channel_id=1, source_target_pairs={{0,4},{4,0},{8,12},{12,8},{16,20},{20,16},{24,28},{28,24},{1,5},{5... | collective-permute-start | bytes 884744 | tf_op jit(solution)/shard_map/ppermute | solution.py:674
  53.1 11.8 %collective-permute-start.11 = (bf16[1568,128]{1,0:T(8,128)(2,1)S(1)}, bf16[1568,128]{1,0:T(8,128)(2,1)S(1)}, u32[]{:S(2)}, u32[]{:S(2)}) collective-permute-start(bf16[1568,128]{1,0:T(8,128)(2,1)S(1)} %get-tuple-element.110.refs_0_.refs_2_), channel_id=1, source_target_pairs={{0,1},{1,0},{2,3},{3,2},{4,5},{5,4},{6,7},{7,6},{8,9},{9,8},{10,11... | collective-permute-start | bytes 1204232 | tf_op jit(solution)/shard_map/ppermute | solution.py:674
  56.8 1.5 %collective-permute-start.15 = (bf16[792,128]{1,0:T(8,128)(2,1)S(1)}, bf16[792,128]{1,0:T(8,128)(2,1)S(1)}, u32[]{:S(2)}, u32[]{:S(2)}) collective-permute-start(bf16[792,128]{1,0:T(8,128)(2,1)S(1)} %copy_kernel.1.refs_6_), channel_id=1, source_target_pairs={{0,1},{1,0},{2,3},{3,2},{4,5},{5,4},{6,7},{7,6},{8,9},{9,8},{10,11... | collective-permute-start | bytes 608264 | tf_op jit(solution)/shard_map/ppermute | solution.py:674
  56.9 7.3 %collective-permute-start.17 = (bf16[768,128]{1,0:T(8,128)(2,1)S(1)}, bf16[768,128]{1,0:T(8,128)(2,1)S(1)}, u32[]{:S(2)}, u32[]{:S(2)}) collective-permute-start(bf16[768,128]{1,0:T(8,128)(2,1)S(1)} %get-tuple-element.116), channel_id=1, source_target_pairs={{0,2},{1,3},{2,0},{3,1},{4,6},{5,7},{6,4},{7,5},{8,10},{9,11},{10,... | collective-permute-start | bytes 589832 | tf_op jit(solution)/shard_map/ppermute | solution.py:674
  60.4 3.7 %collective-permute-start.16 = (f32[2,768]{1,0:T(2,128)S(1)}, f32[2,768]{1,0:T(2,128)S(1)}, u32[]{:S(2)}, u32[]{:S(2)}) collective-permute-start(f32[2,768]{1,0:T(2,128)S(1)} %get-tuple-element.114.refs_0_), channel_id=1, source_target_pairs={{0,8},{4,12},{8,0},{12,4},{16,24},{20,28},{24,16},{28,20},{1,9},{5... | collective-permute-start | bytes 18440 | tf_op jit(solution)/shard_map/ppermute | solution.py:674
  61.1 5.6 %collective-permute-start.23 = (bf16[2,96,384]{2,1,0:T(8,128)(2,1)S(1)}, bf16[2,96,384]{2,1,0:T(8,128)(2,1)S(1)}, u32[]{:S(2)}, u32[]{:S(2)}) collective-permute-start(bf16[2,96,384]{2,1,0:T(8,128)(2,1)S(1)} %get-tuple-element.121), channel_id=1, source_target_pairs={{0,8},{4,12},{8,0},{12,4},{16,24},{20,28},{24,16},{28,20},{1,9},{5... | collective-permute-start | bytes 442376 | tf_op jit(solution)/shard_map/ppermute | solution.py:674
  64.3 6.0 %collective-permute-start.19 = (bf16[848,128]{1,0:T(8,128)(2,1)S(1)}, bf16[848,128]{1,0:T(8,128)(2,1)S(1)}, u32[]{:S(2)}, u32[]{:S(2)}) collective-permute-start(bf16[848,128]{1,0:T(8,128)(2,1)S(1)} %pack_kernel.2.refs_3_), channel_id=1, source_target_pairs={{0,1},{1,0},{2,3},{3,2},{4,5},{5,4},{6,7},{7,6},{8,9},{9,8},{10,11... | collective-permute-start | bytes 651272 | tf_op jit(solution)/shard_map/ppermute | solution.py:674
  64.3 4.6 %collective-permute-start.18 = (f32[2,768]{1,0:T(2,128)S(1)}, f32[2,768]{1,0:T(2,128)S(1)}, u32[]{:S(2)}, u32[]{:S(2)}) collective-permute-start(f32[2,768]{1,0:T(2,128)S(1)} %add_kernel.2.refs_2_.refs_0_), channel_id=1, source_target_pairs={{0,16},{4,20},{8,24},{12,28},{16,0},{20,4},{24,8},{28,12},{1,17},{... | collective-permute-start | bytes 18440 | tf_op jit(solution)/shard_map/ppermute | solution.py:674
  66.8 5.9 %collective-permute-start.24 = (bf16[1,96,384]{2,1,0:T(8,128)(2,1)S(1)}, bf16[1,96,384]{2,1,0:T(8,128)(2,1)S(1)}, u32[]{:S(2)}, u32[]{:S(2)}) collective-permute-start(bf16[1,96,384]{2,1,0:T(8,128)(2,1)S(1)} %get-tuple-element.124), channel_id=1, source_target_pairs={{0,16},{4,20},{8,24},{12,28},{16,0},{20,4},{24,8},{28,12},{1,17},{... | collective-permute-start | bytes 221192 | tf_op jit(solution)/shard_map/ppermute | solution.py:674
  69.0 1.3 %collective-permute-start.20 = (bf16[272,128]{1,0:T(8,128)(2,1)S(1)}, bf16[272,128]{1,0:T(8,128)(2,1)S(1)}, u32[]{:S(2)}, u32[]{:S(2)}) collective-permute-start(bf16[272,128]{1,0:T(8,128)(2,1)S(1)} %pack_kernel.3.refs_4_), channel_id=1, source_target_pairs={{0,1},{1,0},{2,3},{3,2},{4,5},{5,4},{6,7},{7,6},{8,9},{9,8},{10,11... | collective-permute-start | bytes 208904 | tf_op jit(solution)/shard_map/ppermute | solution.py:674
  69.0 3.7 %collective-permute-start.21 = (f32[2,768]{1,0:T(2,128)S(1)}, f32[2,768]{1,0:T(2,128)S(1)}, u32[]{:S(2)}, u32[]{:S(2)}) collective-permute-start(f32[2,768]{1,0:T(2,128)S(1)} %add_kernel.3.refs_1_.refs_8_.refs_4_), channel_id=1, source_target_pairs={{0,4},{4,0},{8,12},{12,8},{16,20},{20,16},{24,28},{28,24},{1,5},{5... | collective-permute-start | bytes 18440 | tf_op jit(solution)/shard_map/ppermute | solution.py:674

commit v12 on v11

--- a/solution.py
+++ b/solution.py
@@ -211,9 +211,11 @@
         vec_ref[2:3, lanes] = gain
         vec_ref[3:4, lanes] = norm_ref[1:2, lanes] - mean * gain
 
+    gain, offset = vec_ref[2:3, :], vec_ref[3:4, :]
+
     def step(k, carry):
         at = pl.multiple_of(k * 16, 16)
-        v = x_ref[pl.ds(at, 16), :].astype(F32) * vec_ref[2:3, :] + vec_ref[3:4, :]
+        v = x_ref[pl.ds(at, 16), :].astype(F32) * gain + offset
         hidden, slope = gelu_and_slope(v)
         hid_ref[pl.ds(at, 16), :] = hidden.astype(BF16)
         slope_ref[pl.ds(at, 16), :] = slope
@@ -478,7 +480,7 @@
     taps = lax.dot_general(
         hid_ref[...], term_ref[...], ROW_DIMS, preferred_element_type=F32
     )
-    point = lax.dot_general(cot_ref[...], mid_ref[...], ROW_DIMS, preferred_element_type=F32)
+    point = lax.dot_general(mid_ref[...], cot_ref[...], ROW_DIMS, preferred_element_type=F32).T
     parts = [taps[:, j * LANES : j * LANES + slim] for j in range(KERNEL_WIDTH)] + [point[:, :slim]]
     full[...] = jnp.concatenate(parts, axis=1)
     halve(
@@ -918,13 +920,13 @@
     arrays = [inputs, cotangent, d_in, vec_in, total_back, total_got, kept, got, total_mid]
     small = [(x.shape, F32) for x in states]
     input_grad, *news = call(
-        functools.partial(final_kernel, bin_count=bin_count, chunks=8),
+        functools.partial(final_kernel, bin_count=bin_count, chunks=4),
         [((rows, width), F32)] + small,
         arrays + states,
         scratch=small + small + [((rows, width), F32)],
         away=range(len(arrays), len(arrays) + 12),
         away_outs=range(13),
-        sems=24 + 8,
+        sems=24 + 4,
         after=[token],
     )
     return (block_out, input_grad, *news[3:9], *news[:3], *news[9:])

time: 76 us -> 75.6 us (level)
  transfers between devices with their start and end apart: 25 -> 25, of which waited for: 13 -> 12; matrix products, arithmetic and copies ran while one was open for 0% -> 0% of each run, Pallas kernels for 19% -> 19%
where the time goes in v12:
time: 75.6 us; the launch traced here: 75.3 us
  starting transfers between devices  20.3 us (27%)
  Pallas kernels  20 us (26%)
  blocking collectives  19.5 us (26%)
  waiting for transfers between devices  14.4 us (19%)
  between operations  1.05 us (1%)
    pallas_call x26, Pallas kernels, call(): pl.pallas_call(kernel, out_shape=[jax.ShapeDtypeStruct(s, t) for s, t in...  20 us
    ppermute x24, starting transfers between devices, swap(): return lax.ppermute(x, axis, flip(axis, reach))  19.6 us
    all_to_all x2, blocking collectives, spread(): return lax.all_to_all(copies, axes, 0, 0, tiled=True)  19.5 us
    ppermute x24, waiting for transfers between devices, swap(): return lax.ppermute(x, axis, flip(axis, reach))  14.4 us
  transfers between devices with their start and end apart: 25, of which 12 were waited for; matrix products, arithmetic and copies ran while one was open for 0% of the time, Pallas kernels for 19%

profile of v12, /device:TPU:0, one launch (start us, length us, event | category | flops | bytes accessed | tf_op | source)
XLA Modules:
  0.0 75.3 jit_solution(12244508800984012857)
XLA Ops:
  0.7 1.7 %first_kernel.1 = (bf16[1024,768]{1,0:T(8,128)(2,1)S(1)}, bf16[1,72,384]{2,1,0:T(8,128)(2,1)S(1)}, bf16[144,128]{1,0:T(8,128)(2,1)S(1)}, bf16[48,384]{1,0:T(8,128)(2,1)S(1)}, bf16[48,384]{1,0:T(8,128)(2,1)S(1)}) custom-call(bf16[1024,768]{1,0:T(8,128)(2,1)} %refs_0_.2, bf16[1024,768]{1,0:T(8,128)(2,1)} %refs_1_.3, f32[3,96,96]{2,1,0:T(8,128)} %refs_12_.1, ...), custom_call_target="tpu_custom_call" | custom-call | flops 1 | bytes 1 | tf_op jit(solution)/shard_map/first_kernel/pallas_call | solution.py:48
  2.4 4.1 %collective-permute-start = (bf16[1,72,384]{2,1,0:T(8,128)(2,1)S(1)}, bf16[1,72,384]{2,1,0:T(8,128)(2,1)S(1)}, u32[]{:S(2)}, u32[]{:S(2)}) collective-permute-start(bf16[1,72,384]{2,1,0:T(8,128)(2,1)S(1)} %get-tuple-element.78.refs_1_.refs_0_), channel_id=1, source_target_pairs={{0,16},{4,20},{8,24},{12,28},{16,0},{20,4},{24,8},{28,12},{1,17},{... | collective-permute-start | bytes 165896 | tf_op jit(solution)/shard_map/ppermute | solution.py:676
  6.6 1.4 %mask_kernel.1 = (f32[3,1056,128]{2,1,0:T(8,128)S(1)}, f32[3,1024,128]{2,1,0:T(8,128)S(1)}) custom-call(s32[8]{0:T(128)S(1)} %copy-done.2, bf16[1,72,384]{2,1,0:T(8,128)(2,1)S(1)} %get-tuple-element.78.refs_1_.refs_0_), custom_call_target="tpu_custom_call" | custom-call | flops 1 | bytes 1 | tf_op jit(solution)/shard_map/mask_kernel/pallas_call | solution.py:48
  8.0 3.3 %collective-permute-done.1.refs_3_ = bf16[144,128]{1,0:T(8,128)(2,1)S(1)} collective-permute-done((bf16[144,128]{1,0:T(8,128)(2,1)S(1)}, bf16[144,128]{1,0:T(8,128)(2,1)S(1)}, u32[]{:S(2)}, u32[]{:S(2)}) %collective-permute-start.1) | collective-permute-done | bytes 36896 | tf_op jit(solution)/shard_map/ppermute | solution.py:676
  11.4 1.6 %collective-permute-start.2 = (bf16[2,72,384]{2,1,0:T(8,128)(2,1)S(1)}, bf16[2,72,384]{2,1,0:T(8,128)(2,1)S(1)}, u32[]{:S(2)}, u32[]{:S(2)}) collective-permute-start(bf16[2,72,384]{2,1,0:T(8,128)(2,1)S(1)} %get-tuple-element.84.refs_0_), channel_id=1, source_target_pairs={{0,8},{4,12},{8,0},{12,4},{16,24},{20,28},{24,16},{28,20},{1,9},{5... | collective-permute-start | bytes 331784 | tf_op jit(solution)/shard_map/ppermute | solution.py:676
  13.0 1.5 %collective-permute-start.3 = (bf16[384,128]{1,0:T(8,128)(2,1)S(1)}, bf16[384,128]{1,0:T(8,128)(2,1)S(1)}, u32[]{:S(2)}, u32[]{:S(2)}) collective-permute-start(bf16[384,128]{1,0:T(8,128)(2,1)S(1)} %get-tuple-element.85.refs_2_), channel_id=1, source_target_pairs={{0,4},{4,0},{8,12},{12,8},{16,20},{20,16},{24,28},{28,24},{1,5},{5... | collective-permute-start | bytes 294920 | tf_op jit(solution)/shard_map/ppermute | solution.py:676
  14.5 0.7 collective-permute-start.5
  15.2 2.5 %collective-permute-done.3.refs_3_.refs_0_ = bf16[384,128]{1,0:T(8,128)(2,1)S(1)} collective-permute-done((bf16[384,128]{1,0:T(8,128)(2,1)S(1)}, bf16[384,128]{1,0:T(8,128)(2,1)S(1)}, u32[]{:S(2)}, u32[]{:S(2)}) %collective-permute-start.3) | collective-permute-done | bytes 98336 | tf_op jit(solution)/shard_map/ppermute | solution.py:676
  17.7 0.9 %collective-permute-start.4 = (bf16[448,128]{1,0:T(8,128)(2,1)S(1)}, bf16[448,128]{1,0:T(8,128)(2,1)S(1)}, u32[]{:S(2)}, u32[]{:S(2)}) collective-permute-start(bf16[448,128]{1,0:T(8,128)(2,1)S(1)} %get-tuple-element.86.refs_2_.refs_1_), channel_id=1, source_target_pairs={{0,8},{4,12},{8,0},{12,4},{16,24},{20,28},{24,16},{28,20},{1,9},{5... | collective-permute-start | bytes 344072 | tf_op jit(solution)/shard_map/ppermute | solution.py:676
  18.5 2.3 %collective-permute-start.7 = (bf16[2,72,384]{2,1,0:T(8,128)(2,1)S(1)}, bf16[2,72,384]{2,1,0:T(8,128)(2,1)S(1)}, u32[]{:S(2)}, u32[]{:S(2)}) collective-permute-start(bf16[2,72,384]{2,1,0:T(8,128)(2,1)S(1)} %get-tuple-element.93), channel_id=1, source_target_pairs={{0,4},{4,0},{8,12},{12,8},{16,20},{20,16},{24,28},{28,24},{1,5},{5... | collective-permute-start | bytes 331784 | tf_op jit(solution)/shard_map/ppermute | solution.py:676
  21.0 1.5 %collective-permute-done.4.refs_3_.refs_2_ = bf16[448,128]{1,0:T(8,128)(2,1)S(1)} collective-permute-done((bf16[448,128]{1,0:T(8,128)(2,1)S(1)}, bf16[448,128]{1,0:T(8,128)(2,1)S(1)}, u32[]{:S(2)}, u32[]{:S(2)}) %collective-permute-start.4) | collective-permute-done | bytes 114720 | tf_op jit(solution)/shard_map/ppermute | solution.py:676
  22.5 2.3 %act_kernel.1 = (bf16[1024,768]{1,0:T(8,128)(2,1)S(1)}, f32[1024,768]{1,0:T(8,128)S(1)}, f32[8,768]{1,0:T(8,128)S(1)}, bf16[1024,768]{1,0:T(8,128)(2,1)S(1)}) custom-call(bf16[1024,768]{1,0:T(8,128)(2,1)S(1)} %get-tuple-element.77.refs_0_.refs_1_, bf16[1024,768]{1,0:T(8,128)(2,1)} %refs_1_.3, bf16[448,128]{1,0:T(8,128)(2,1)S(1)} %get-tuple-element.86.refs_2_.refs_1_, ...), custom_call_target="tpu_custom_call" | custom-call | flops 1 | bytes 1 | tf_op jit(solution)/shard_map/act_kernel/pallas_call | solution.py:48
  25.6 1.4 %conv_kernel.1 = (bf16[768,384]{1,0:T(8,128)(2,1)S(1)}, f32[1056,128]{1,0:T(8,128)S(1)}, f32[8,2,128]{2,1,0:T(2,128)S(1)}, bf16[2,48,768]{2,1,0:T(8,128)(2,1)S(1)}, bf16[11,72,384]{2,1,0:T(8,128)(2,1)S(1)}) custom-call(f32[3,1056,128]{2,1,0:T(8,128)S(1)} %get-tuple-element.79.refs_0_, bf16[1024,768]{1,0:T(8,128)(2,1)S(1)} %get-tuple-element.87.refs_1_.refs_2_, ...), custom_call_target="tpu_custom_call" | custom-call | flops 1 | bytes 1 | tf_op jit(solution)/shard_map/conv_kernel/pallas_call | solution.py:48
  27.1 1.6 %collective-permute-start.10 = (bf16[11,72,384]{2,1,0:T(8,128)(2,1)S(1)}, bf16[11,72,384]{2,1,0:T(8,128)(2,1)S(1)}, u32[]{:S(2)}, u32[]{:S(2)}) collective-permute-start(bf16[11,72,384]{2,1,0:T(8,128)(2,1)S(1)} %get-tuple-element.102), channel_id=1, source_target_pairs={{0,2},{1,3},{2,0},{3,1},{4,6},{5,7},{6,4},{7,5},{8,10},{9,11},{10,... | collective-permute-start | bytes 1824776 | tf_op jit(solution)/shard_map/ppermute | solution.py:676
  28.7 10.7 %all_to_all.10.refs_0_ = f32[8,2,128]{2,1,0:T(2,128)S(1)} all-to-all(f32[8,2,128]{2,1,0:T(2,128)S(1)} %get-tuple-element.96), channel_id=1, replica_groups=mesh['seq'=8,'ch'=4] {'seq'}, dimensions={0} | all-to-all | bytes 16384 | tf_op jit(solution)/shard_map/all_to_all | solution.py:687
  39.3 0.7 mid_kernel.1
  40.0 8.9 %all_to_all.11.refs_0_ = f32[8,2,128]{2,1,0:T(2,128)S(1)} all-to-all(f32[8,2,128]{2,1,0:T(2,128)S(1)} %get-tuple-element.103), channel_id=1, replica_groups=mesh['seq'=8,'ch'=4] {'seq'}, dimensions={0} | all-to-all | bytes 16384 | tf_op jit(solution)/shard_map/all_to_all | solution.py:687
  50.3 1.8 %weight_grad_kernel.1 = (bf16[1024,384]{1,0:T(8,128)(2,1)S(1)}, f32[4,96,384]{2,1,0:T(8,128)S(1)}, bf16[4,96,384]{2,1,0:T(8,128)(2,1)S(1)}) custom-call(f32[3,1024,128]{2,1,0:T(8,128)S(1)} %get-tuple-element.83.refs_6_.refs_0_, bf16[792,128]{1,0:T(8,128)(2,1)S(1)} %get-tuple-element.107.refs_1_, bf16[1024,768]{1,0:T(8,128)(2,1)S(1)} %get-tuple-element.87.refs_1_.refs_2_, ...), custom_call_target="tpu_custom_call" | custom-call | flops 1 | bytes 1 | tf_op jit(solution)/shard_map/weight_grad_kernel/pallas_call | solution.py:48
  53.0 1.6 %first_half_kernel.1.refs_1_.refs_4_ = f32[1024,768]{1,0:T(8,128)S(1)} custom-call(f32[3,1024,128]{2,1,0:T(8,128)S(1)} %get-tuple-element.83.refs_6_.refs_0_, bf16[1024,384]{1,0:T(8,128)(2,1)S(1)} %get-tuple-element.112.refs_1_, bf16[792,128]{1,0:T(8,128)(2,1)S(1)} %collective-permute-done.12.refs_2_, bf16[768,384]{1,0:T(8,128)(2,1)S(1)} %get-tuple-element.100.refs_3_, ...), custom_call_target="tpu_custom_call" | custom-call | flops 1 | bytes 1 | tf_op jit(solution)/shard_map/first_half_kernel/pallas_call | solution.py:48
  55.2 1.6 %collective-permute-done.14.refs_0_ = bf16[792,128]{1,0:T(8,128)(2,1)S(1)} collective-permute-done((bf16[792,128]{1,0:T(8,128)(2,1)S(1)}, bf16[792,128]{1,0:T(8,128)(2,1)S(1)}, u32[]{:S(2)}, u32[]{:S(2)}) %collective-permute-start.14) | collective-permute-done | bytes 202784 | tf_op jit(solution)/shard_map/ppermute | solution.py:676
  57.5 0.9 %collective-permute-done.15.refs_7_ = bf16[792,128]{1,0:T(8,128)(2,1)S(1)} collective-permute-done((bf16[792,128]{1,0:T(8,128)(2,1)S(1)}, bf16[792,128]{1,0:T(8,128)(2,1)S(1)}, u32[]{:S(2)}, u32[]{:S(2)}) %collective-permute-start.15) | collective-permute-done | bytes 202784 | tf_op jit(solution)/shard_map/ppermute | solution.py:676
  58.3 2.0 %second_half_kernel.1 = (f32[1024,768]{1,0:T(8,128)S(1)}, f32[2,768]{1,0:T(2,128)S(1)}) custom-call(f32[3,1024,128]{2,1,0:T(8,128)S(1)} %get-tuple-element.83.refs_6_.refs_0_, bf16[1024,768]{1,0:T(8,128)(2,1)S(1)} %get-tuple-element.77.refs_0_.refs_1_, f32[1024,768]{1,0:T(8,128)S(1)} %get-tuple-element.111.refs_2_, ...), custom_call_target="tpu_custom_call" | custom-call | flops 1 | bytes 1 | tf_op jit(solution)/shard_map/second_half_kernel/pallas_call | solution.py:48
  61.0 1.6 %collective-permute-start.23 = (bf16[2,96,384]{2,1,0:T(8,128)(2,1)S(1)}, bf16[2,96,384]{2,1,0:T(8,128)(2,1)S(1)}, u32[]{:S(2)}, u32[]{:S(2)}) collective-permute-start(bf16[2,96,384]{2,1,0:T(8,128)(2,1)S(1)} %get-tuple-element.121), channel_id=1, source_target_pairs={{0,8},{4,12},{8,0},{12,4},{16,24},{20,28},{24,16},{28,20},{1,9},{5... | collective-permute-start | bytes 442376 | tf_op jit(solution)/shard_map/ppermute | solution.py:676
  62.6 1.5 %collective-permute-done.16.refs_1_ = f32[2,768]{1,0:T(2,128)S(1)} collective-permute-done((f32[2,768]{1,0:T(2,128)S(1)}, f32[2,768]{1,0:T(2,128)S(1)}, u32[]{:S(2)}, u32[]{:S(2)}) %collective-permute-start.16) | collective-permute-done | bytes 6176 | tf_op jit(solution)/shard_map/ppermute | solution.py:676
  64.3 0.6 collective-permute-start.18
  64.9 0.8 %near_kernel.1 = (f32[1024,768]{1,0:T(8,128)S(1)}, f32[8,128]{1,0:T(8,128)S(1)}) custom-call(bf16[1568,128]{1,0:T(8,128)(2,1)S(1)} %get-tuple-element.110.refs_0_.refs_2_, bf16[1568,128]{1,0:T(8,128)(2,1)S(1)} %collective-permute-done.11.refs_1_.refs_5_, f32[2,768]{1,0:T(2,128)S(1)} %add_kernel.2.refs_2_.refs_0_), custom_call_target="tpu_custom_call" | custom-call | flops 1 | bytes 1 | tf_op jit(solution)/shard_map/near_kernel/pallas_call | solution.py:48
  65.7 1.0 %collective-permute-done.23.refs_1_ = bf16[2,96,384]{2,1,0:T(8,128)(2,1)S(1)} collective-permute-done((bf16[2,96,384]{2,1,0:T(8,128)(2,1)S(1)}, bf16[2,96,384]{2,1,0:T(8,128)(2,1)S(1)}, u32[]{:S(2)}, u32[]{:S(2)}) %collective-permute-start.23) | collective-permute-done | bytes 147488 | tf_op jit(solution)/shard_map/ppermute | solution.py:676
  66.8 1.5 %collective-permute-start.24 = (bf16[1,96,384]{2,1,0:T(8,128)(2,1)S(1)}, bf16[1,96,384]{2,1,0:T(8,128)(2,1)S(1)}, u32[]{:S(2)}, u32[]{:S(2)}) collective-permute-start(bf16[1,96,384]{2,1,0:T(8,128)(2,1)S(1)} %get-tuple-element.124), channel_id=1, source_target_pairs={{0,16},{4,20},{8,24},{12,28},{16,0},{20,4},{24,8},{28,12},{1,17},{... | collective-permute-start | bytes 221192 | tf_op jit(solution)/shard_map/ppermute | solution.py:676
  68.2 0.7 collective-permute-done.18.refs_1_
  69.0 0.7 collective-permute-start.21
  70.3 2.0 %out_kernel.1 = (bf16[1024,768]{1,0:T(8,128)(2,1)}, f32[8,128]{1,0:T(8,128)S(1)}) custom-call(bf16[1024,768]{1,0:T(8,128)(2,1)S(1)} %get-tuple-element.77.refs_0_.refs_1_, f32[1024,768]{1,0:T(8,128)S(1)} %get-tuple-element.115.refs_1_, bf16[1568,128]{1,0:T(8,128)(2,1)S(1)} %get-tuple-element.110.refs_0_.refs_2_, bf16[848,128]{1,0:T(8,128)(2,1)S(1)} %pack_kernel.2.refs_3_, ...), custom_call_target="tpu_custom_call" | custom-call | flops 1 | bytes 1 | tf_op jit(solution)/shard_map/out_kernel/pallas_call | solution.py:48
  72.7 2.5 %final_kernel.1 = (f32[1024,768]{1,0:T(8,128)}, f32[2,768]{1,0:T(2,128)}, f32[2,768]{1,0:T(2,128)}, f32[2,768]{1,0:T(2,128)}, f32[3,96,96]{2,1,0:T(8,128)}, /*in...) custom-call(bf16[1024,768]{1,0:T(8,128)(2,1)S(1)} %get-tuple-element, ...), custom_call_target="tpu_custom_call" | custom-call | flops 1 | bytes 1 | tf_op jit(solution)/shard_map/final_kernel/pallas_call | solution.py:48
  (52 shorter events, 6.6 us)
Async XLA Ops:
  0.6 5.9 %copy-start.2 = (s32[8]{0:T(128)S(1)}, s32[8]{0:T(128)}, u32[]{:S(2)}) copy-start(s32[8]{0:T(128)} %refs_0_.3) | copy-start | bytes 100
  2.4 20.2 %copy-start = (f32[2,768]{1,0:T(2,128)S(1)}, f32[2,768]{1,0:T(2,128)}, u32[]{:S(2)}) copy-start(f32[2,768]{1,0:T(2,128)} %refs_9_.1) | copy-start | bytes 18436
  2.4 9.0 %collective-permute-start = (bf16[1,72,384]{2,1,0:T(8,128)(2,1)S(1)}, bf16[1,72,384]{2,1,0:T(8,128)(2,1)S(1)}, u32[]{:S(2)}, u32[]{:S(2)}) collective-permute-start(bf16[1,72,384]{2,1,0:T(8,128)(2,1)S(1)} %get-tuple-element.78.refs_1_.refs_0_), channel_id=1, source_target_pairs={{0,16},{4,20},{8,24},{12,28},{16,0},{20,4},{24,8},{28,12},{1,17},{... | collective-permute-start | bytes 165896 | tf_op jit(solution)/shard_map/ppermute | solution.py:676
  6.5 4.9 %collective-permute-start.1 = (bf16[144,128]{1,0:T(8,128)(2,1)S(1)}, bf16[144,128]{1,0:T(8,128)(2,1)S(1)}, u32[]{:S(2)}, u32[]{:S(2)}) collective-permute-start(bf16[144,128]{1,0:T(8,128)(2,1)S(1)} %get-tuple-element.80.refs_2_), channel_id=1, source_target_pairs={{0,16},{4,20},{8,24},{12,28},{16,0},{20,4},{24,8},{28,12},{1,17},{... | collective-permute-start | bytes 110600 | tf_op jit(solution)/shard_map/ppermute | solution.py:676
  11.4 6.3 %collective-permute-start.2 = (bf16[2,72,384]{2,1,0:T(8,128)(2,1)S(1)}, bf16[2,72,384]{2,1,0:T(8,128)(2,1)S(1)}, u32[]{:S(2)}, u32[]{:S(2)}) collective-permute-start(bf16[2,72,384]{2,1,0:T(8,128)(2,1)S(1)} %get-tuple-element.84.refs_0_), channel_id=1, source_target_pairs={{0,8},{4,12},{8,0},{12,4},{16,24},{20,28},{24,16},{28,20},{1,9},{5... | collective-permute-start | bytes 331784 | tf_op jit(solution)/shard_map/ppermute | solution.py:676
  13.0 4.6 %collective-permute-start.3 = (bf16[384,128]{1,0:T(8,128)(2,1)S(1)}, bf16[384,128]{1,0:T(8,128)(2,1)S(1)}, u32[]{:S(2)}, u32[]{:S(2)}) collective-permute-start(bf16[384,128]{1,0:T(8,128)(2,1)S(1)} %get-tuple-element.85.refs_2_), channel_id=1, source_target_pairs={{0,4},{4,0},{8,12},{12,8},{16,20},{20,16},{24,28},{28,24},{1,5},{5... | collective-permute-start | bytes 294920 | tf_op jit(solution)/shard_map/ppermute | solution.py:676
  14.5 6.4 %collective-permute-start.5 = (bf16[48,384]{1,0:T(8,128)(2,1)S(1)}, bf16[48,384]{1,0:T(8,128)(2,1)S(1)}, u32[]{:S(2)}, u32[]{:S(2)}) collective-permute-start(bf16[48,384]{1,0:T(8,128)(2,1)S(1)} %get-tuple-element.88), channel_id=1, source_target_pairs={{4,8},{12,16},{20,24},{8,4},{16,12},{24,20},{5,9},{13,17},{21,25},... | collective-permute-start | bytes 110600 | tf_op jit(solution)/shard_map/ppermute | solution.py:766
  17.7 4.9 %collective-permute-start.4 = (bf16[448,128]{1,0:T(8,128)(2,1)S(1)}, bf16[448,128]{1,0:T(8,128)(2,1)S(1)}, u32[]{:S(2)}, u32[]{:S(2)}) collective-permute-start(bf16[448,128]{1,0:T(8,128)(2,1)S(1)} %get-tuple-element.86.refs_2_.refs_1_), channel_id=1, source_target_pairs={{0,8},{4,12},{8,0},{12,4},{16,24},{20,28},{24,16},{28,20},{1,9},{5... | collective-permute-start | bytes 344072 | tf_op jit(solution)/shard_map/ppermute | solution.py:676
  18.5 6.9 %collective-permute-start.7 = (bf16[2,72,384]{2,1,0:T(8,128)(2,1)S(1)}, bf16[2,72,384]{2,1,0:T(8,128)(2,1)S(1)}, u32[]{:S(2)}, u32[]{:S(2)}) collective-permute-start(bf16[2,72,384]{2,1,0:T(8,128)(2,1)S(1)} %get-tuple-element.93), channel_id=1, source_target_pairs={{0,4},{4,0},{8,12},{12,8},{16,20},{20,16},{24,28},{28,24},{1,5},{5... | collective-permute-start | bytes 331784 | tf_op jit(solution)/shard_map/ppermute | solution.py:676
  20.9 4.7 %collective-permute-start.8 = (bf16[2,72,384]{2,1,0:T(8,128)(2,1)S(1)}, bf16[2,72,384]{2,1,0:T(8,128)(2,1)S(1)}, u32[]{:S(2)}, u32[]{:S(2)}) collective-permute-start(bf16[2,72,384]{2,1,0:T(8,128)(2,1)S(1)} %get-tuple-element.94), channel_id=1, source_target_pairs={{0,4},{4,0},{8,12},{12,8},{16,20},{20,16},{24,28},{28,24},{1,5},{5... | collective-permute-start | bytes 331784 | tf_op jit(solution)/shard_map/ppermute | solution.py:676
  20.9 4.5 %collective-permute-start.6 = (bf16[112,384]{1,0:T(8,128)(2,1)S(1)}, bf16[112,384]{1,0:T(8,128)(2,1)S(1)}, u32[]{:S(2)}, u32[]{:S(2)}) collective-permute-start(bf16[112,384]{1,0:T(8,128)(2,1)S(1)} %rim_kernel.1.refs_2_), channel_id=1, source_target_pairs={{0,1},{1,0},{2,3},{3,2},{4,5},{5,4},{6,7},{7,6},{8,9},{9,8},{10,11... | collective-permute-start | bytes 258056 | tf_op jit(solution)/shard_map/ppermute | solution.py:676
  25.6 13.7 %copy-start.1 = (f32[2,96]{1,0:T(2,128)S(1)}, f32[2,96]{1,0:T(2,128)}, u32[]{:S(2)}) copy-start(f32[2,96]{1,0:T(2,128)} %refs_18_.1) | copy-start | bytes 2308
  27.1 22.0 %collective-permute-start.10 = (bf16[11,72,384]{2,1,0:T(8,128)(2,1)S(1)}, bf16[11,72,384]{2,1,0:T(8,128)(2,1)S(1)}, u32[]{:S(2)}, u32[]{:S(2)}) collective-permute-start(bf16[11,72,384]{2,1,0:T(8,128)(2,1)S(1)} %get-tuple-element.102), channel_id=1, source_target_pairs={{0,2},{1,3},{2,0},{3,1},{4,6},{5,7},{6,4},{7,5},{8,10},{9,11},{10,... | collective-permute-start | bytes 1824776 | tf_op jit(solution)/shard_map/ppermute | solution.py:676
  28.7 10.7 %collective-permute-start.9 = (bf16[768,384]{1,0:T(8,128)(2,1)S(1)}, bf16[768,384]{1,0:T(8,128)(2,1)S(1)}, u32[]{:S(2)}, u32[]{:S(2)}) collective-permute-start(bf16[768,384]{1,0:T(8,128)(2,1)S(1)} %get-tuple-element.100.refs_3_), channel_id=1, source_target_pairs={{0,1},{1,0},{2,3},{3,2},{4,5},{5,4},{6,7},{7,6},{8,9},{9,8},{10,11... | collective-permute-start | bytes 1769480 | tf_op jit(solution)/shard_map/ppermute | solution.py:676
  49.2 5.4 %collective-permute-start.13 = (bf16[8,72,384]{2,1,0:T(8,128)(2,1)S(1)}, bf16[8,72,384]{2,1,0:T(8,128)(2,1)S(1)}, u32[]{:S(2)}, u32[]{:S(2)}) collective-permute-start(bf16[8,72,384]{2,1,0:T(8,128)(2,1)S(1)} %get-tuple-element.113.refs_0_), channel_id=1, source_target_pairs={{0,1},{1,0},{2,3},{3,2},{4,5},{5,4},{6,7},{7,6},{8,9},{9,8},{10,11... | collective-permute-start | bytes 1327112 | tf_op jit(solution)/shard_map/ppermute | solution.py:676
  49.3 3.7 %collective-permute-start.12 = (bf16[792,128]{1,0:T(8,128)(2,1)S(1)}, bf16[792,128]{1,0:T(8,128)(2,1)S(1)}, u32[]{:S(2)}, u32[]{:S(2)}) collective-permute-start(bf16[792,128]{1,0:T(8,128)(2,1)S(1)} %get-tuple-element.107.refs_1_), channel_id=1, source_target_pairs={{0,1},{1,0},{2,3},{3,2},{4,5},{5,4},{6,7},{7,6},{8,9},{9,8},{10,11... | collective-permute-start | bytes 608264 | tf_op jit(solution)/shard_map/ppermute | solution.py:676
  49.8 7.0 %collective-permute-start.14 = (bf16[792,128]{1,0:T(8,128)(2,1)S(1)}, bf16[792,128]{1,0:T(8,128)(2,1)S(1)}, u32[]{:S(2)}, u32[]{:S(2)}) collective-permute-start(bf16[792,128]{1,0:T(8,128)(2,1)S(1)} %get-tuple-element.107.refs_1_), channel_id=1, source_target_pairs={{0,2},{1,3},{2,0},{3,1},{4,6},{5,7},{6,4},{7,5},{8,10},{9,11},{10,... | collective-permute-start | bytes 608264 | tf_op jit(solution)/shard_map/ppermute | solution.py:676
  52.1 8.8 %collective-permute-start.22 = (bf16[4,96,384]{2,1,0:T(8,128)(2,1)S(1)}, bf16[4,96,384]{2,1,0:T(8,128)(2,1)S(1)}, u32[]{:S(2)}, u32[]{:S(2)}) collective-permute-start(bf16[4,96,384]{2,1,0:T(8,128)(2,1)S(1)} %get-tuple-element.109.refs_3_), channel_id=1, source_target_pairs={{0,4},{4,0},{8,12},{12,8},{16,20},{20,16},{24,28},{28,24},{1,5},{5... | collective-permute-start | bytes 884744 | tf_op jit(solution)/shard_map/ppermute | solution.py:676
  52.9 12.0 %collective-permute-start.11 = (bf16[1568,128]{1,0:T(8,128)(2,1)S(1)}, bf16[1568,128]{1,0:T(8,128)(2,1)S(1)}, u32[]{:S(2)}, u32[]{:S(2)}) collective-permute-start(bf16[1568,128]{1,0:T(8,128)(2,1)S(1)} %get-tuple-element.110.refs_0_.refs_2_), channel_id=1, source_target_pairs={{0,1},{1,0},{2,3},{3,2},{4,5},{5,4},{6,7},{7,6},{8,9},{9,8},{10,11... | collective-permute-start | bytes 1204232 | tf_op jit(solution)/shard_map/ppermute | solution.py:676
  56.8 1.5 %collective-permute-start.15 = (bf16[792,128]{1,0:T(8,128)(2,1)S(1)}, bf16[792,128]{1,0:T(8,128)(2,1)S(1)}, u32[]{:S(2)}, u32[]{:S(2)}) collective-permute-start(bf16[792,128]{1,0:T(8,128)(2,1)S(1)} %copy_kernel.1.refs_6_), channel_id=1, source_target_pairs={{0,1},{1,0},{2,3},{3,2},{4,5},{5,4},{6,7},{7,6},{8,9},{9,8},{10,11... | collective-permute-start | bytes 608264 | tf_op jit(solution)/shard_map/ppermute | solution.py:676
  56.9 7.3 %collective-permute-start.17 = (bf16[768,128]{1,0:T(8,128)(2,1)S(1)}, bf16[768,128]{1,0:T(8,128)(2,1)S(1)}, u32[]{:S(2)}, u32[]{:S(2)}) collective-permute-start(bf16[768,128]{1,0:T(8,128)(2,1)S(1)} %get-tuple-element.116), channel_id=1, source_target_pairs={{0,2},{1,3},{2,0},{3,1},{4,6},{5,7},{6,4},{7,5},{8,10},{9,11},{10,... | collective-permute-start | bytes 589832 | tf_op jit(solution)/shard_map/ppermute | solution.py:676
  60.4 3.7 %collective-permute-start.16 = (f32[2,768]{1,0:T(2,128)S(1)}, f32[2,768]{1,0:T(2,128)S(1)}, u32[]{:S(2)}, u32[]{:S(2)}) collective-permute-start(f32[2,768]{1,0:T(2,128)S(1)} %get-tuple-element.114.refs_0_), channel_id=1, source_target_pairs={{0,8},{4,12},{8,0},{12,4},{16,24},{20,28},{24,16},{28,20},{1,9},{5... | collective-permute-start | bytes 18440 | tf_op jit(solution)/shard_map/ppermute | solution.py:676
  61.0 5.7 %collective-permute-start.23 = (bf16[2,96,384]{2,1,0:T(8,128)(2,1)S(1)}, bf16[2,96,384]{2,1,0:T(8,128)(2,1)S(1)}, u32[]{:S(2)}, u32[]{:S(2)}) collective-permute-start(bf16[2,96,384]{2,1,0:T(8,128)(2,1)S(1)} %get-tuple-element.121), channel_id=1, source_target_pairs={{0,8},{4,12},{8,0},{12,4},{16,24},{20,28},{24,16},{28,20},{1,9},{5... | collective-permute-start | bytes 442376 | tf_op jit(solution)/shard_map/ppermute | solution.py:676
  64.2 6.0 %collective-permute-start.19 = (bf16[848,128]{1,0:T(8,128)(2,1)S(1)}, bf16[848,128]{1,0:T(8,128)(2,1)S(1)}, u32[]{:S(2)}, u32[]{:S(2)}) collective-permute-start(bf16[848,128]{1,0:T(8,128)(2,1)S(1)} %pack_kernel.2.refs_3_), channel_id=1, source_target_pairs={{0,1},{1,0},{2,3},{3,2},{4,5},{5,4},{6,7},{7,6},{8,9},{9,8},{10,11... | collective-permute-start | bytes 651272 | tf_op jit(solution)/shard_map/ppermute | solution.py:676
  64.3 4.6 %collective-permute-start.18 = (f32[2,768]{1,0:T(2,128)S(1)}, f32[2,768]{1,0:T(2,128)S(1)}, u32[]{:S(2)}, u32[]{:S(2)}) collective-permute-start(f32[2,768]{1,0:T(2,128)S(1)} %add_kernel.2.refs_2_.refs_0_), channel_id=1, source_target_pairs={{0,16},{4,20},{8,24},{12,28},{16,0},{20,4},{24,8},{28,12},{1,17},{... | collective-permute-start | bytes 18440 | tf_op jit(solution)/shard_map/ppermute | solution.py:676
  66.8 5.9 %collective-permute-start.24 = (bf16[1,96,384]{2,1,0:T(8,128)(2,1)S(1)}, bf16[1,96,384]{2,1,0:T(8,128)(2,1)S(1)}, u32[]{:S(2)}, u32[]{:S(2)}) collective-permute-start(bf16[1,96,384]{2,1,0:T(8,128)(2,1)S(1)} %get-tuple-element.124), channel_id=1, source_target_pairs={{0,16},{4,20},{8,24},{12,28},{16,0},{20,4},{24,8},{28,12},{1,17},{... | collective-permute-start | bytes 221192 | tf_op jit(solution)/shard_map/ppermute | solution.py:676
  68.9 1.3 %collective-permute-start.20 = (bf16[272,128]{1,0:T(8,128)(2,1)S(1)}, bf16[272,128]{1,0:T(8,128)(2,1)S(1)}, u32[]{:S(2)}, u32[]{:S(2)}) collective-permute-start(bf16[272,128]{1,0:T(8,128)(2,1)S(1)} %pack_kernel.3.refs_4_), channel_id=1, source_target_pairs={{0,1},{1,0},{2,3},{3,2},{4,5},{5,4},{6,7},{7,6},{8,9},{9,8},{10,11... | collective-permute-start | bytes 208904 | tf_op jit(solution)/shard_map/ppermute | solution.py:676
  69.0 3.7 %collective-permute-start.21 = (f32[2,768]{1,0:T(2,128)S(1)}, f32[2,768]{1,0:T(2,128)S(1)}, u32[]{:S(2)}, u32[]{:S(2)}) collective-permute-start(f32[2,768]{1,0:T(2,128)S(1)} %add_kernel.3.refs_1_.refs_8_.refs_4_), channel_id=1, source_target_pairs={{0,4},{4,0},{8,12},{12,8},{16,20},{20,16},{24,28},{28,24},{1,5},{5... | collective-permute-start | bytes 18440 | tf_op jit(solution)/shard_map/ppermute | solution.py:676

commit v13 on v12

--- a/solution.py
+++ b/solution.py
@@ -719,7 +719,7 @@
 
     rounds = len(weight_order)
     top, lower = ch_order[0], ch_order[1:]
-    chunks = 4
+    chunks = 2
     rim = (RIM + EDGE, width // 2)
     packed = 3 * depth // 4 if folds(depth, slim) else depth
     inputs, weight, near, *rims = call(

time: 75.6 us -> 75.7 us (level)
  no operation moved by 1% of the time
where the time goes in v13:
time: 75.7 us; the launch traced here: 75.4 us
  starting transfers between devices  20.3 us (27%)
  Pallas kernels  20.1 us (27%)
  blocking collectives  19.5 us (26%)
  waiting for transfers between devices  14.4 us (19%)
  between operations  1.05 us (1%)
    pallas_call x26, Pallas kernels, call(): pl.pallas_call(kernel, out_shape=[jax.ShapeDtypeStruct(s, t) for s, t in...  20.1 us
    ppermute x24, starting transfers between devices, swap(): return lax.ppermute(x, axis, flip(axis, reach))  19.6 us
    all_to_all x2, blocking collectives, spread(): return lax.all_to_all(copies, axes, 0, 0, tiled=True)  19.5 us
    ppermute x24, waiting for transfers between devices, swap(): return lax.ppermute(x, axis, flip(axis, reach))  14.4 us
  transfers between devices with their start and end apart: 25, of which 12 were waited for; matrix products, arithmetic and copies ran while one was open for 0% of the time, Pallas kernels for 19%

profile of v13, /device:TPU:0, one launch (start us, length us, event | category | flops | bytes accessed | tf_op | source)
XLA Modules:
  0.0 75.4 jit_solution(3411072951206533696)
XLA Ops:
  0.7 1.8 %first_kernel.1 = (bf16[1024,768]{1,0:T(8,128)(2,1)S(1)}, bf16[1,72,384]{2,1,0:T(8,128)(2,1)S(1)}, bf16[144,128]{1,0:T(8,128)(2,1)S(1)}, bf16[48,384]{1,0:T(8,128)(2,1)S(1)}, bf16[48,384]{1,0:T(8,128)(2,1)S(1)}) custom-call(bf16[1024,768]{1,0:T(8,128)(2,1)} %refs_0_.2, bf16[1024,768]{1,0:T(8,128)(2,1)} %refs_1_.3, f32[3,96,96]{2,1,0:T(8,128)} %refs_12_.1, ...), custom_call_target="tpu_custom_call" | custom-call | flops 1 | bytes 1 | tf_op jit(solution)/shard_map/first_kernel/pallas_call | solution.py:48
  2.5 4.1 %collective-permute-start = (bf16[1,72,384]{2,1,0:T(8,128)(2,1)S(1)}, bf16[1,72,384]{2,1,0:T(8,128)(2,1)S(1)}, u32[]{:S(2)}, u32[]{:S(2)}) collective-permute-start(bf16[1,72,384]{2,1,0:T(8,128)(2,1)S(1)} %get-tuple-element.78.refs_1_.refs_0_), channel_id=1, source_target_pairs={{0,16},{4,20},{8,24},{12,28},{16,0},{20,4},{24,8},{28,12},{1,17},{... | collective-permute-start | bytes 165896 | tf_op jit(solution)/shard_map/ppermute | solution.py:676
  6.7 1.4 %mask_kernel.1 = (f32[3,1056,128]{2,1,0:T(8,128)S(1)}, f32[3,1024,128]{2,1,0:T(8,128)S(1)}) custom-call(s32[8]{0:T(128)S(1)} %copy-done.2, bf16[1,72,384]{2,1,0:T(8,128)(2,1)S(1)} %get-tuple-element.78.refs_1_.refs_0_), custom_call_target="tpu_custom_call" | custom-call | flops 1 | bytes 1 | tf_op jit(solution)/shard_map/mask_kernel/pallas_call | solution.py:48
  8.1 3.3 %collective-permute-done.1.refs_3_ = bf16[144,128]{1,0:T(8,128)(2,1)S(1)} collective-permute-done((bf16[144,128]{1,0:T(8,128)(2,1)S(1)}, bf16[144,128]{1,0:T(8,128)(2,1)S(1)}, u32[]{:S(2)}, u32[]{:S(2)}) %collective-permute-start.1) | collective-permute-done | bytes 36896 | tf_op jit(solution)/shard_map/ppermute | solution.py:676
  11.5 1.6 %collective-permute-start.2 = (bf16[2,72,384]{2,1,0:T(8,128)(2,1)S(1)}, bf16[2,72,384]{2,1,0:T(8,128)(2,1)S(1)}, u32[]{:S(2)}, u32[]{:S(2)}) collective-permute-start(bf16[2,72,384]{2,1,0:T(8,128)(2,1)S(1)} %get-tuple-element.84.refs_0_), channel_id=1, source_target_pairs={{0,8},{4,12},{8,0},{12,4},{16,24},{20,28},{24,16},{28,20},{1,9},{5... | collective-permute-start | bytes 331784 | tf_op jit(solution)/shard_map/ppermute | solution.py:676
  13.1 1.5 %collective-permute-start.3 = (bf16[384,128]{1,0:T(8,128)(2,1)S(1)}, bf16[384,128]{1,0:T(8,128)(2,1)S(1)}, u32[]{:S(2)}, u32[]{:S(2)}) collective-permute-start(bf16[384,128]{1,0:T(8,128)(2,1)S(1)} %get-tuple-element.85.refs_2_), channel_id=1, source_target_pairs={{0,4},{4,0},{8,12},{12,8},{16,20},{20,16},{24,28},{28,24},{1,5},{5... | collective-permute-start | bytes 294920 | tf_op jit(solution)/shard_map/ppermute | solution.py:676
  14.6 0.7 collective-permute-start.5
  15.3 2.5 %collective-permute-done.3.refs_3_.refs_0_ = bf16[384,128]{1,0:T(8,128)(2,1)S(1)} collective-permute-done((bf16[384,128]{1,0:T(8,128)(2,1)S(1)}, bf16[384,128]{1,0:T(8,128)(2,1)S(1)}, u32[]{:S(2)}, u32[]{:S(2)}) %collective-permute-start.3) | collective-permute-done | bytes 98336 | tf_op jit(solution)/shard_map/ppermute | solution.py:676
  17.8 0.9 %collective-permute-start.4 = (bf16[448,128]{1,0:T(8,128)(2,1)S(1)}, bf16[448,128]{1,0:T(8,128)(2,1)S(1)}, u32[]{:S(2)}, u32[]{:S(2)}) collective-permute-start(bf16[448,128]{1,0:T(8,128)(2,1)S(1)} %get-tuple-element.86.refs_2_.refs_1_), channel_id=1, source_target_pairs={{0,8},{4,12},{8,0},{12,4},{16,24},{20,28},{24,16},{28,20},{1,9},{5... | collective-permute-start | bytes 344072 | tf_op jit(solution)/shard_map/ppermute | solution.py:676
  18.6 2.3 %collective-permute-start.7 = (bf16[2,72,384]{2,1,0:T(8,128)(2,1)S(1)}, bf16[2,72,384]{2,1,0:T(8,128)(2,1)S(1)}, u32[]{:S(2)}, u32[]{:S(2)}) collective-permute-start(bf16[2,72,384]{2,1,0:T(8,128)(2,1)S(1)} %get-tuple-element.93), channel_id=1, source_target_pairs={{0,4},{4,0},{8,12},{12,8},{16,20},{20,16},{24,28},{28,24},{1,5},{5... | collective-permute-start | bytes 331784 | tf_op jit(solution)/shard_map/ppermute | solution.py:676
  21.1 1.5 %collective-permute-done.4.refs_3_.refs_2_ = bf16[448,128]{1,0:T(8,128)(2,1)S(1)} collective-permute-done((bf16[448,128]{1,0:T(8,128)(2,1)S(1)}, bf16[448,128]{1,0:T(8,128)(2,1)S(1)}, u32[]{:S(2)}, u32[]{:S(2)}) %collective-permute-start.4) | collective-permute-done | bytes 114720 | tf_op jit(solution)/shard_map/ppermute | solution.py:676
  22.6 2.3 %act_kernel.1 = (bf16[1024,768]{1,0:T(8,128)(2,1)S(1)}, f32[1024,768]{1,0:T(8,128)S(1)}, f32[8,768]{1,0:T(8,128)S(1)}, bf16[1024,768]{1,0:T(8,128)(2,1)S(1)}) custom-call(bf16[1024,768]{1,0:T(8,128)(2,1)S(1)} %get-tuple-element.77.refs_0_.refs_1_, bf16[1024,768]{1,0:T(8,128)(2,1)} %refs_1_.3, bf16[448,128]{1,0:T(8,128)(2,1)S(1)} %get-tuple-element.86.refs_2_.refs_1_, ...), custom_call_target="tpu_custom_call" | custom-call | flops 1 | bytes 1 | tf_op jit(solution)/shard_map/act_kernel/pallas_call | solution.py:48
  25.7 1.4 %conv_kernel.1 = (bf16[768,384]{1,0:T(8,128)(2,1)S(1)}, f32[1056,128]{1,0:T(8,128)S(1)}, f32[8,2,128]{2,1,0:T(2,128)S(1)}, bf16[2,48,768]{2,1,0:T(8,128)(2,1)S(1)}, bf16[11,72,384]{2,1,0:T(8,128)(2,1)S(1)}) custom-call(f32[3,1056,128]{2,1,0:T(8,128)S(1)} %get-tuple-element.79.refs_0_, bf16[1024,768]{1,0:T(8,128)(2,1)S(1)} %get-tuple-element.87.refs_1_.refs_2_, ...), custom_call_target="tpu_custom_call" | custom-call | flops 1 | bytes 1 | tf_op jit(solution)/shard_map/conv_kernel/pallas_call | solution.py:48
  27.2 1.6 %collective-permute-start.10 = (bf16[11,72,384]{2,1,0:T(8,128)(2,1)S(1)}, bf16[11,72,384]{2,1,0:T(8,128)(2,1)S(1)}, u32[]{:S(2)}, u32[]{:S(2)}) collective-permute-start(bf16[11,72,384]{2,1,0:T(8,128)(2,1)S(1)} %get-tuple-element.102), channel_id=1, source_target_pairs={{0,2},{1,3},{2,0},{3,1},{4,6},{5,7},{6,4},{7,5},{8,10},{9,11},{10,... | collective-permute-start | bytes 1824776 | tf_op jit(solution)/shard_map/ppermute | solution.py:676
  28.8 10.7 %all_to_all.10.refs_0_ = f32[8,2,128]{2,1,0:T(2,128)S(1)} all-to-all(f32[8,2,128]{2,1,0:T(2,128)S(1)} %get-tuple-element.96), channel_id=1, replica_groups=mesh['seq'=8,'ch'=4] {'seq'}, dimensions={0} | all-to-all | bytes 16384 | tf_op jit(solution)/shard_map/all_to_all | solution.py:687
  39.4 0.7 mid_kernel.1
  40.1 8.9 %all_to_all.11.refs_0_ = f32[8,2,128]{2,1,0:T(2,128)S(1)} all-to-all(f32[8,2,128]{2,1,0:T(2,128)S(1)} %get-tuple-element.103), channel_id=1, replica_groups=mesh['seq'=8,'ch'=4] {'seq'}, dimensions={0} | all-to-all | bytes 16384 | tf_op jit(solution)/shard_map/all_to_all | solution.py:687
  50.4 1.8 %weight_grad_kernel.1 = (bf16[1024,384]{1,0:T(8,128)(2,1)S(1)}, f32[4,96,384]{2,1,0:T(8,128)S(1)}, bf16[4,96,384]{2,1,0:T(8,128)(2,1)S(1)}) custom-call(f32[3,1024,128]{2,1,0:T(8,128)S(1)} %get-tuple-element.83.refs_6_.refs_0_, bf16[792,128]{1,0:T(8,128)(2,1)S(1)} %get-tuple-element.107.refs_1_, bf16[1024,768]{1,0:T(8,128)(2,1)S(1)} %get-tuple-element.87.refs_1_.refs_2_, ...), custom_call_target="tpu_custom_call" | custom-call | flops 1 | bytes 1 | tf_op jit(solution)/shard_map/weight_grad_kernel/pallas_call | solution.py:48
  53.1 1.6 %first_half_kernel.1.refs_1_.refs_4_ = f32[1024,768]{1,0:T(8,128)S(1)} custom-call(f32[3,1024,128]{2,1,0:T(8,128)S(1)} %get-tuple-element.83.refs_6_.refs_0_, bf16[1024,384]{1,0:T(8,128)(2,1)S(1)} %get-tuple-element.112.refs_1_, bf16[792,128]{1,0:T(8,128)(2,1)S(1)} %collective-permute-done.12.refs_2_, bf16[768,384]{1,0:T(8,128)(2,1)S(1)} %get-tuple-element.100.refs_3_, ...), custom_call_target="tpu_custom_call" | custom-call | flops 1 | bytes 1 | tf_op jit(solution)/shard_map/first_half_kernel/pallas_call | solution.py:48
  55.2 1.6 %collective-permute-done.14.refs_0_ = bf16[792,128]{1,0:T(8,128)(2,1)S(1)} collective-permute-done((bf16[792,128]{1,0:T(8,128)(2,1)S(1)}, bf16[792,128]{1,0:T(8,128)(2,1)S(1)}, u32[]{:S(2)}, u32[]{:S(2)}) %collective-permute-start.14) | collective-permute-done | bytes 202784 | tf_op jit(solution)/shard_map/ppermute | solution.py:676
  57.6 0.9 %collective-permute-done.15.refs_7_ = bf16[792,128]{1,0:T(8,128)(2,1)S(1)} collective-permute-done((bf16[792,128]{1,0:T(8,128)(2,1)S(1)}, bf16[792,128]{1,0:T(8,128)(2,1)S(1)}, u32[]{:S(2)}, u32[]{:S(2)}) %collective-permute-start.15) | collective-permute-done | bytes 202784 | tf_op jit(solution)/shard_map/ppermute | solution.py:676
  58.4 2.0 %second_half_kernel.1 = (f32[1024,768]{1,0:T(8,128)S(1)}, f32[2,768]{1,0:T(2,128)S(1)}) custom-call(f32[3,1024,128]{2,1,0:T(8,128)S(1)} %get-tuple-element.83.refs_6_.refs_0_, bf16[1024,768]{1,0:T(8,128)(2,1)S(1)} %get-tuple-element.77.refs_0_.refs_1_, f32[1024,768]{1,0:T(8,128)S(1)} %get-tuple-element.111.refs_2_, ...), custom_call_target="tpu_custom_call" | custom-call | flops 1 | bytes 1 | tf_op jit(solution)/shard_map/second_half_kernel/pallas_call | solution.py:48
  61.1 1.6 %collective-permute-start.23 = (bf16[2,96,384]{2,1,0:T(8,128)(2,1)S(1)}, bf16[2,96,384]{2,1,0:T(8,128)(2,1)S(1)}, u32[]{:S(2)}, u32[]{:S(2)}) collective-permute-start(bf16[2,96,384]{2,1,0:T(8,128)(2,1)S(1)} %get-tuple-element.121), channel_id=1, source_target_pairs={{0,8},{4,12},{8,0},{12,4},{16,24},{20,28},{24,16},{28,20},{1,9},{5... | collective-permute-start | bytes 442376 | tf_op jit(solution)/shard_map/ppermute | solution.py:676
  62.7 1.5 %collective-permute-done.16.refs_1_ = f32[2,768]{1,0:T(2,128)S(1)} collective-permute-done((f32[2,768]{1,0:T(2,128)S(1)}, f32[2,768]{1,0:T(2,128)S(1)}, u32[]{:S(2)}, u32[]{:S(2)}) %collective-permute-start.16) | collective-permute-done | bytes 6176 | tf_op jit(solution)/shard_map/ppermute | solution.py:676
  64.4 0.6 collective-permute-start.18
  65.0 0.8 %near_kernel.1 = (f32[1024,768]{1,0:T(8,128)S(1)}, f32[8,128]{1,0:T(8,128)S(1)}) custom-call(bf16[1568,128]{1,0:T(8,128)(2,1)S(1)} %get-tuple-element.110.refs_0_.refs_2_, bf16[1568,128]{1,0:T(8,128)(2,1)S(1)} %collective-permute-done.11.refs_1_.refs_5_, f32[2,768]{1,0:T(2,128)S(1)} %add_kernel.2.refs_2_.refs_0_), custom_call_target="tpu_custom_call" | custom-call | flops 1 | bytes 1 | tf_op jit(solution)/shard_map/near_kernel/pallas_call | solution.py:48
  65.8 1.0 %collective-permute-done.23.refs_1_ = bf16[2,96,384]{2,1,0:T(8,128)(2,1)S(1)} collective-permute-done((bf16[2,96,384]{2,1,0:T(8,128)(2,1)S(1)}, bf16[2,96,384]{2,1,0:T(8,128)(2,1)S(1)}, u32[]{:S(2)}, u32[]{:S(2)}) %collective-permute-start.23) | collective-permute-done | bytes 147488 | tf_op jit(solution)/shard_map/ppermute | solution.py:676
  66.9 1.4 %collective-permute-start.24 = (bf16[1,96,384]{2,1,0:T(8,128)(2,1)S(1)}, bf16[1,96,384]{2,1,0:T(8,128)(2,1)S(1)}, u32[]{:S(2)}, u32[]{:S(2)}) collective-permute-start(bf16[1,96,384]{2,1,0:T(8,128)(2,1)S(1)} %get-tuple-element.124), channel_id=1, source_target_pairs={{0,16},{4,20},{8,24},{12,28},{16,0},{20,4},{24,8},{28,12},{1,17},{... | collective-permute-start | bytes 221192 | tf_op jit(solution)/shard_map/ppermute | solution.py:676
  68.3 0.7 collective-permute-done.18.refs_1_
  69.1 0.7 collective-permute-start.21
  70.4 2.0 %out_kernel.1 = (bf16[1024,768]{1,0:T(8,128)(2,1)}, f32[8,128]{1,0:T(8,128)S(1)}) custom-call(bf16[1024,768]{1,0:T(8,128)(2,1)S(1)} %get-tuple-element.77.refs_0_.refs_1_, f32[1024,768]{1,0:T(8,128)S(1)} %get-tuple-element.115.refs_1_, bf16[1568,128]{1,0:T(8,128)(2,1)S(1)} %get-tuple-element.110.refs_0_.refs_2_, bf16[848,128]{1,0:T(8,128)(2,1)S(1)} %pack_kernel.2.refs_3_, ...), custom_call_target="tpu_custom_call" | custom-call | flops 1 | bytes 1 | tf_op jit(solution)/shard_map/out_kernel/pallas_call | solution.py:48
  72.8 2.5 %final_kernel.1 = (f32[1024,768]{1,0:T(8,128)}, f32[2,768]{1,0:T(2,128)}, f32[2,768]{1,0:T(2,128)}, f32[2,768]{1,0:T(2,128)}, f32[3,96,96]{2,1,0:T(8,128)}, /*in...) custom-call(bf16[1024,768]{1,0:T(8,128)(2,1)S(1)} %get-tuple-element, ...), custom_call_target="tpu_custom_call" | custom-call | flops 1 | bytes 1 | tf_op jit(solution)/shard_map/final_kernel/pallas_call | solution.py:48
  (52 shorter events, 6.6 us)
Async XLA Ops:
  0.6 6.0 %copy-start.2 = (s32[8]{0:T(128)S(1)}, s32[8]{0:T(128)}, u32[]{:S(2)}) copy-start(s32[8]{0:T(128)} %refs_0_.3) | copy-start | bytes 100
  2.5 20.2 %copy-start = (f32[2,768]{1,0:T(2,128)S(1)}, f32[2,768]{1,0:T(2,128)}, u32[]{:S(2)}) copy-start(f32[2,768]{1,0:T(2,128)} %refs_9_.1) | copy-start | bytes 18436
  2.5 9.0 %collective-permute-start = (bf16[1,72,384]{2,1,0:T(8,128)(2,1)S(1)}, bf16[1,72,384]{2,1,0:T(8,128)(2,1)S(1)}, u32[]{:S(2)}, u32[]{:S(2)}) collective-permute-start(bf16[1,72,384]{2,1,0:T(8,128)(2,1)S(1)} %get-tuple-element.78.refs_1_.refs_0_), channel_id=1, source_target_pairs={{0,16},{4,20},{8,24},{12,28},{16,0},{20,4},{24,8},{28,12},{1,17},{... | collective-permute-start | bytes 165896 | tf_op jit(solution)/shard_map/ppermute | solution.py:676
  6.6 4.9 %collective-permute-start.1 = (bf16[144,128]{1,0:T(8,128)(2,1)S(1)}, bf16[144,128]{1,0:T(8,128)(2,1)S(1)}, u32[]{:S(2)}, u32[]{:S(2)}) collective-permute-start(bf16[144,128]{1,0:T(8,128)(2,1)S(1)} %get-tuple-element.80.refs_2_), channel_id=1, source_target_pairs={{0,16},{4,20},{8,24},{12,28},{16,0},{20,4},{24,8},{28,12},{1,17},{... | collective-permute-start | bytes 110600 | tf_op jit(solution)/shard_map/ppermute | solution.py:676
  11.5 6.3 %collective-permute-start.2 = (bf16[2,72,384]{2,1,0:T(8,128)(2,1)S(1)}, bf16[2,72,384]{2,1,0:T(8,128)(2,1)S(1)}, u32[]{:S(2)}, u32[]{:S(2)}) collective-permute-start(bf16[2,72,384]{2,1,0:T(8,128)(2,1)S(1)} %get-tuple-element.84.refs_0_), channel_id=1, source_target_pairs={{0,8},{4,12},{8,0},{12,4},{16,24},{20,28},{24,16},{28,20},{1,9},{5... | collective-permute-start | bytes 331784 | tf_op jit(solution)/shard_map/ppermute | solution.py:676
  13.1 4.6 %collective-permute-start.3 = (bf16[384,128]{1,0:T(8,128)(2,1)S(1)}, bf16[384,128]{1,0:T(8,128)(2,1)S(1)}, u32[]{:S(2)}, u32[]{:S(2)}) collective-permute-start(bf16[384,128]{1,0:T(8,128)(2,1)S(1)} %get-tuple-element.85.refs_2_), channel_id=1, source_target_pairs={{0,4},{4,0},{8,12},{12,8},{16,20},{20,16},{24,28},{28,24},{1,5},{5... | collective-permute-start | bytes 294920 | tf_op jit(solution)/shard_map/ppermute | solution.py:676
  14.6 6.4 %collective-permute-start.5 = (bf16[48,384]{1,0:T(8,128)(2,1)S(1)}, bf16[48,384]{1,0:T(8,128)(2,1)S(1)}, u32[]{:S(2)}, u32[]{:S(2)}) collective-permute-start(bf16[48,384]{1,0:T(8,128)(2,1)S(1)} %get-tuple-element.88), channel_id=1, source_target_pairs={{4,8},{12,16},{20,24},{8,4},{16,12},{24,20},{5,9},{13,17},{21,25},... | collective-permute-start | bytes 110600 | tf_op jit(solution)/shard_map/ppermute | solution.py:766
  17.8 4.9 %collective-permute-start.4 = (bf16[448,128]{1,0:T(8,128)(2,1)S(1)}, bf16[448,128]{1,0:T(8,128)(2,1)S(1)}, u32[]{:S(2)}, u32[]{:S(2)}) collective-permute-start(bf16[448,128]{1,0:T(8,128)(2,1)S(1)} %get-tuple-element.86.refs_2_.refs_1_), channel_id=1, source_target_pairs={{0,8},{4,12},{8,0},{12,4},{16,24},{20,28},{24,16},{28,20},{1,9},{5... | collective-permute-start | bytes 344072 | tf_op jit(solution)/shard_map/ppermute | solution.py:676
  18.6 6.9 %collective-permute-start.7 = (bf16[2,72,384]{2,1,0:T(8,128)(2,1)S(1)}, bf16[2,72,384]{2,1,0:T(8,128)(2,1)S(1)}, u32[]{:S(2)}, u32[]{:S(2)}) collective-permute-start(bf16[2,72,384]{2,1,0:T(8,128)(2,1)S(1)} %get-tuple-element.93), channel_id=1, source_target_pairs={{0,4},{4,0},{8,12},{12,8},{16,20},{20,16},{24,28},{28,24},{1,5},{5... | collective-permute-start | bytes 331784 | tf_op jit(solution)/shard_map/ppermute | solution.py:676
  21.0 4.7 %collective-permute-start.8 = (bf16[2,72,384]{2,1,0:T(8,128)(2,1)S(1)}, bf16[2,72,384]{2,1,0:T(8,128)(2,1)S(1)}, u32[]{:S(2)}, u32[]{:S(2)}) collective-permute-start(bf16[2,72,384]{2,1,0:T(8,128)(2,1)S(1)} %get-tuple-element.94), channel_id=1, source_target_pairs={{0,4},{4,0},{8,12},{12,8},{16,20},{20,16},{24,28},{28,24},{1,5},{5... | collective-permute-start | bytes 331784 | tf_op jit(solution)/shard_map/ppermute | solution.py:676
  21.0 4.5 %collective-permute-start.6 = (bf16[112,384]{1,0:T(8,128)(2,1)S(1)}, bf16[112,384]{1,0:T(8,128)(2,1)S(1)}, u32[]{:S(2)}, u32[]{:S(2)}) collective-permute-start(bf16[112,384]{1,0:T(8,128)(2,1)S(1)} %rim_kernel.1.refs_2_), channel_id=1, source_target_pairs={{0,1},{1,0},{2,3},{3,2},{4,5},{5,4},{6,7},{7,6},{8,9},{9,8},{10,11... | collective-permute-start | bytes 258056 | tf_op jit(solution)/shard_map/ppermute | solution.py:676
  25.7 13.7 %copy-start.1 = (f32[2,96]{1,0:T(2,128)S(1)}, f32[2,96]{1,0:T(2,128)}, u32[]{:S(2)}) copy-start(f32[2,96]{1,0:T(2,128)} %refs_18_.1) | copy-start | bytes 2308
  27.2 22.1 %collective-permute-start.10 = (bf16[11,72,384]{2,1,0:T(8,128)(2,1)S(1)}, bf16[11,72,384]{2,1,0:T(8,128)(2,1)S(1)}, u32[]{:S(2)}, u32[]{:S(2)}) collective-permute-start(bf16[11,72,384]{2,1,0:T(8,128)(2,1)S(1)} %get-tuple-element.102), channel_id=1, source_target_pairs={{0,2},{1,3},{2,0},{3,1},{4,6},{5,7},{6,4},{7,5},{8,10},{9,11},{10,... | collective-permute-start | bytes 1824776 | tf_op jit(solution)/shard_map/ppermute | solution.py:676
  28.7 10.7 %collective-permute-start.9 = (bf16[768,384]{1,0:T(8,128)(2,1)S(1)}, bf16[768,384]{1,0:T(8,128)(2,1)S(1)}, u32[]{:S(2)}, u32[]{:S(2)}) collective-permute-start(bf16[768,384]{1,0:T(8,128)(2,1)S(1)} %get-tuple-element.100.refs_3_), channel_id=1, source_target_pairs={{0,1},{1,0},{2,3},{3,2},{4,5},{5,4},{6,7},{7,6},{8,9},{9,8},{10,11... | collective-permute-start | bytes 1769480 | tf_op jit(solution)/shard_map/ppermute | solution.py:676
  49.3 5.4 %collective-permute-start.13 = (bf16[8,72,384]{2,1,0:T(8,128)(2,1)S(1)}, bf16[8,72,384]{2,1,0:T(8,128)(2,1)S(1)}, u32[]{:S(2)}, u32[]{:S(2)}) collective-permute-start(bf16[8,72,384]{2,1,0:T(8,128)(2,1)S(1)} %get-tuple-element.113.refs_0_), channel_id=1, source_target_pairs={{0,1},{1,0},{2,3},{3,2},{4,5},{5,4},{6,7},{7,6},{8,9},{9,8},{10,11... | collective-permute-start | bytes 1327112 | tf_op jit(solution)/shard_map/ppermute | solution.py:676
  49.4 3.7 %collective-permute-start.12 = (bf16[792,128]{1,0:T(8,128)(2,1)S(1)}, bf16[792,128]{1,0:T(8,128)(2,1)S(1)}, u32[]{:S(2)}, u32[]{:S(2)}) collective-permute-start(bf16[792,128]{1,0:T(8,128)(2,1)S(1)} %get-tuple-element.107.refs_1_), channel_id=1, source_target_pairs={{0,1},{1,0},{2,3},{3,2},{4,5},{5,4},{6,7},{7,6},{8,9},{9,8},{10,11... | collective-permute-start | bytes 608264 | tf_op jit(solution)/shard_map/ppermute | solution.py:676
  49.9 7.0 %collective-permute-start.14 = (bf16[792,128]{1,0:T(8,128)(2,1)S(1)}, bf16[792,128]{1,0:T(8,128)(2,1)S(1)}, u32[]{:S(2)}, u32[]{:S(2)}) collective-permute-start(bf16[792,128]{1,0:T(8,128)(2,1)S(1)} %get-tuple-element.107.refs_1_), channel_id=1, source_target_pairs={{0,2},{1,3},{2,0},{3,1},{4,6},{5,7},{6,4},{7,5},{8,10},{9,11},{10,... | collective-permute-start | bytes 608264 | tf_op jit(solution)/shard_map/ppermute | solution.py:676
  52.2 8.8 %collective-permute-start.22 = (bf16[4,96,384]{2,1,0:T(8,128)(2,1)S(1)}, bf16[4,96,384]{2,1,0:T(8,128)(2,1)S(1)}, u32[]{:S(2)}, u32[]{:S(2)}) collective-permute-start(bf16[4,96,384]{2,1,0:T(8,128)(2,1)S(1)} %get-tuple-element.109.refs_3_), channel_id=1, source_target_pairs={{0,4},{4,0},{8,12},{12,8},{16,20},{20,16},{24,28},{28,24},{1,5},{5... | collective-permute-start | bytes 884744 | tf_op jit(solution)/shard_map/ppermute | solution.py:676
  53.0 12.0 %collective-permute-start.11 = (bf16[1568,128]{1,0:T(8,128)(2,1)S(1)}, bf16[1568,128]{1,0:T(8,128)(2,1)S(1)}, u32[]{:S(2)}, u32[]{:S(2)}) collective-permute-start(bf16[1568,128]{1,0:T(8,128)(2,1)S(1)} %get-tuple-element.110.refs_0_.refs_2_), channel_id=1, source_target_pairs={{0,1},{1,0},{2,3},{3,2},{4,5},{5,4},{6,7},{7,6},{8,9},{9,8},{10,11... | collective-permute-start | bytes 1204232 | tf_op jit(solution)/shard_map/ppermute | solution.py:676
  56.9 1.5 %collective-permute-start.15 = (bf16[792,128]{1,0:T(8,128)(2,1)S(1)}, bf16[792,128]{1,0:T(8,128)(2,1)S(1)}, u32[]{:S(2)}, u32[]{:S(2)}) collective-permute-start(bf16[792,128]{1,0:T(8,128)(2,1)S(1)} %copy_kernel.1.refs_6_), channel_id=1, source_target_pairs={{0,1},{1,0},{2,3},{3,2},{4,5},{5,4},{6,7},{7,6},{8,9},{9,8},{10,11... | collective-permute-start | bytes 608264 | tf_op jit(solution)/shard_map/ppermute | solution.py:676
  57.0 7.3 %collective-permute-start.17 = (bf16[768,128]{1,0:T(8,128)(2,1)S(1)}, bf16[768,128]{1,0:T(8,128)(2,1)S(1)}, u32[]{:S(2)}, u32[]{:S(2)}) collective-permute-start(bf16[768,128]{1,0:T(8,128)(2,1)S(1)} %get-tuple-element.116), channel_id=1, source_target_pairs={{0,2},{1,3},{2,0},{3,1},{4,6},{5,7},{6,4},{7,5},{8,10},{9,11},{10,... | collective-permute-start | bytes 589832 | tf_op jit(solution)/shard_map/ppermute | solution.py:676
  60.5 3.7 %collective-permute-start.16 = (f32[2,768]{1,0:T(2,128)S(1)}, f32[2,768]{1,0:T(2,128)S(1)}, u32[]{:S(2)}, u32[]{:S(2)}) collective-permute-start(f32[2,768]{1,0:T(2,128)S(1)} %get-tuple-element.114.refs_0_), channel_id=1, source_target_pairs={{0,8},{4,12},{8,0},{12,4},{16,24},{20,28},{24,16},{28,20},{1,9},{5... | collective-permute-start | bytes 18440 | tf_op jit(solution)/shard_map/ppermute | solution.py:676
  61.1 5.7 %collective-permute-start.23 = (bf16[2,96,384]{2,1,0:T(8,128)(2,1)S(1)}, bf16[2,96,384]{2,1,0:T(8,128)(2,1)S(1)}, u32[]{:S(2)}, u32[]{:S(2)}) collective-permute-start(bf16[2,96,384]{2,1,0:T(8,128)(2,1)S(1)} %get-tuple-element.121), channel_id=1, source_target_pairs={{0,8},{4,12},{8,0},{12,4},{16,24},{20,28},{24,16},{28,20},{1,9},{5... | collective-permute-start | bytes 442376 | tf_op jit(solution)/shard_map/ppermute | solution.py:676
  64.3 6.0 %collective-permute-start.19 = (bf16[848,128]{1,0:T(8,128)(2,1)S(1)}, bf16[848,128]{1,0:T(8,128)(2,1)S(1)}, u32[]{:S(2)}, u32[]{:S(2)}) collective-permute-start(bf16[848,128]{1,0:T(8,128)(2,1)S(1)} %pack_kernel.2.refs_3_), channel_id=1, source_target_pairs={{0,1},{1,0},{2,3},{3,2},{4,5},{5,4},{6,7},{7,6},{8,9},{9,8},{10,11... | collective-permute-start | bytes 651272 | tf_op jit(solution)/shard_map/ppermute | solution.py:676
  64.4 4.6 %collective-permute-start.18 = (f32[2,768]{1,0:T(2,128)S(1)}, f32[2,768]{1,0:T(2,128)S(1)}, u32[]{:S(2)}, u32[]{:S(2)}) collective-permute-start(f32[2,768]{1,0:T(2,128)S(1)} %add_kernel.2.refs_2_.refs_0_), channel_id=1, source_target_pairs={{0,16},{4,20},{8,24},{12,28},{16,0},{20,4},{24,8},{28,12},{1,17},{... | collective-permute-start | bytes 18440 | tf_op jit(solution)/shard_map/ppermute | solution.py:676
  66.9 5.9 %collective-permute-start.24 = (bf16[1,96,384]{2,1,0:T(8,128)(2,1)S(1)}, bf16[1,96,384]{2,1,0:T(8,128)(2,1)S(1)}, u32[]{:S(2)}, u32[]{:S(2)}) collective-permute-start(bf16[1,96,384]{2,1,0:T(8,128)(2,1)S(1)} %get-tuple-element.124), channel_id=1, source_target_pairs={{0,16},{4,20},{8,24},{12,28},{16,0},{20,4},{24,8},{28,12},{1,17},{... | collective-permute-start | bytes 221192 | tf_op jit(solution)/shard_map/ppermute | solution.py:676
  69.0 1.3 %collective-permute-start.20 = (bf16[272,128]{1,0:T(8,128)(2,1)S(1)}, bf16[272,128]{1,0:T(8,128)(2,1)S(1)}, u32[]{:S(2)}, u32[]{:S(2)}) collective-permute-start(bf16[272,128]{1,0:T(8,128)(2,1)S(1)} %pack_kernel.3.refs_4_), channel_id=1, source_target_pairs={{0,1},{1,0},{2,3},{3,2},{4,5},{5,4},{6,7},{7,6},{8,9},{9,8},{10,11... | collective-permute-start | bytes 208904 | tf_op jit(solution)/shard_map/ppermute | solution.py:676
  69.1 3.7 %collective-permute-start.21 = (f32[2,768]{1,0:T(2,128)S(1)}, f32[2,768]{1,0:T(2,128)S(1)}, u32[]{:S(2)}, u32[]{:S(2)}) collective-permute-start(f32[2,768]{1,0:T(2,128)S(1)} %add_kernel.3.refs_1_.refs_8_.refs_4_), channel_id=1, source_target_pairs={{0,4},{4,0},{8,12},{12,8},{16,20},{20,16},{24,28},{28,24},{1,5},{5... | collective-permute-start | bytes 18440 | tf_op jit(solution)/shard_map/ppermute | solution.py:676
